TPU v7x, 256 devices: a whole 4x4x8 slice. The times are simulated.
256 devices in a mesh: dp: 64 (over x, z, core), mp: 4 (over y).
Axes of the slice: x: 4, y: 4, z: 8, core: 2. Of those that a mesh axis runs over, the one named last changes fastest.
Arguments:
- pool_inputs: bfloat16 [8192, 8, 4096], P('dp', None, 'mp'), may hold values from -6 to 6
- pool_targets: bfloat16 [8192, 8, 4096], P('dp', None, 'mp'), may hold values from -6 to 6
- frozen: bfloat16 [4096, 4096], P(None, 'mp'), may hold values from -0.09375 to 0.09375
- gain: float32 [4096], P('mp'), may hold values from 0.5 to 1.5
- adapter_down: bfloat16 [64, 64, 4096], P('dp', None, 'mp'), may hold values from -0.09375 to 0.09375
- adapter_up: bfloat16 [64, 64, 4096], P('dp', None, 'mp'), may hold values from -0.75 to 0.75
- sample_ids: int32 [4096], P('dp'), may hold values from 0 to 127
- buckets: int32 [8192], P('dp'), may hold values from 0 to 15
- lengths: int32 [8192], P('dp'), may hold values from 1 to 8
- destinations: int32 [4096, 1], P('dp'), may hold values from 0 to 63; in each aligned block of 64 rows (0 to 63, 64 to 127, ...) at most 2 rows name the same one
- competence: float32 [1], replicated, may hold values from 0.3 to 0.7
Outputs:
- grad_down: float32 [64, 64, 4096], P('dp', None, 'mp')
- grad_up: float32 [64, 64, 4096], P('dp', None, 'mp')
- bucket_loss: float32 [16], replicated
- competence_next: float32 [1], replicated
Inputs may be any that keep to these rules, and one draw needn't show every extreme that they name: `destinations`: of the 64 sampled slots of one holder, at most 2 name the same trainer. `sample_ids`: an index into the holder's own 128 stored blocks.
All inputs are finite; a program needn't handle non-finite values.
Results may differ from a plain program's by a relative error of at most 0.0056.
Values may be sent and summed in bfloat16 or wider, within the bound.
No kernel may reach another device: no remote copies, remote signals or barrier semaphores. Data moves between devices by JAX's collectives and lax.ppermute only.
A program may use at most 128 MiB of HBM per device.

v0:
```python
import functools

import jax
import jax.numpy as jnp
from jax import lax
from jax.sharding import Mesh
from jax.sharding import PartitionSpec as P

NB = 16
DP = ("dp_0", "dp_1", "dp_2")
DP_MP = ("dp_0", "dp_1", "dp_2", "mp")


RMS_EPSILON = 1e-05
SHARPNESS = 12.0
ADAPTER_SCALING = 2.0


def sent_to_all(value, axis):
    peers = lax.axis_size(axis)
    return lax.all_to_all(
        jnp.broadcast_to(value[None], (peers, *value.shape)), axis, 0, 0, tiled=True
    )


def of_everyone(value, axis):
    everything = sent_to_all(value, axis)
    return jnp.sum(everything, axis=0)


def over_axes(value, axes):
    return functools.reduce(lax.psum, axes, value)


def normalize(values, gain, model_width):
    partial_value = jnp.sum(values * values, axis=1)
    square_total = of_everyone(partial_value, "mp")
    inverse_rms = lax.rsqrt(square_total / model_width + RMS_EPSILON)
    return (values * inverse_rms[:, None] * gain[None, :]).astype(jnp.bfloat16)


def frozen_gap(values, normed, targets, frozen):
    projected = jnp.dot(
        lax.all_gather(normed, "mp", axis=1, tiled=True), frozen, preferred_element_type=jnp.float32
    )
    return (values + projected - targets.astype(jnp.float32)).astype(jnp.bfloat16)


def place_blocks(placing, sequence_blocks):
    flat_blocks = sequence_blocks.reshape(sequence_blocks.shape[0], -1)
    return jnp.dot(placing, flat_blocks, preferred_element_type=jnp.float32).astype(jnp.bfloat16)


def on_device(
    pool_inputs,
    pool_targets,
    frozen,
    gain,
    adapter_down,
    adapter_up,
    sample_ids,
    buckets,
    lengths,
    destinations,
    competence,
):
    trainers = lax.axis_size(DP)
    sampled = sample_ids.shape[0]
    pool_rows, block_len, feature_part = pool_inputs.shape
    model_width = frozen.shape[0]
    per_pair = max(2, 3 * sampled // (2 * trainers))
    block_capacity = trainers * per_pair
    choosing = sample_ids[:, None] == jnp.arange(pool_rows, dtype=jnp.int32)[None, :]
    chosen_buckets = jnp.sum(jnp.where(choosing, buckets[None, :], 0), axis=1)
    chosen_lengths = jnp.sum(jnp.where(choosing, lengths[None, :], 0), axis=1)
    chosen_inputs = jnp.take(pool_inputs, sample_ids, axis=0)
    chosen_targets = jnp.take(pool_targets, sample_ids, axis=0)
    bucket_range = jnp.arange(NB, dtype=jnp.int32)
    local_onehot = (chosen_buckets[:, None] == bucket_range[None, :]).astype(jnp.float32)
    local_counts = jnp.sum(local_onehot * chosen_lengths[:, None].astype(jnp.float32), axis=0)
    counts = of_everyone(local_counts, DP)
    floor_counts = jnp.maximum(counts, 1.0)
    weights = jax.nn.sigmoid(
        SHARPNESS * (competence[0] - (bucket_range.astype(jnp.float32) + 0.5) / NB)
    )
    target_trainer = destinations[:, 0]
    same_dest = target_trainer[:, None] == target_trainer[None, :]
    earlier = jnp.arange(sampled)[None, :] < jnp.arange(sampled)[:, None]
    arrival = jnp.sum((same_dest & earlier).astype(jnp.int32), axis=1)
    slot_index = target_trainer * per_pair + arrival
    slot_match = jnp.arange(block_capacity, dtype=jnp.int32)[:, None] == slot_index[None, :]
    placing = slot_match.astype(jnp.bfloat16)
    slot_bucket = jnp.sum(jnp.where(slot_match, chosen_buckets[None, :], 0), axis=1)
    slot_length = jnp.sum(jnp.where(slot_match, chosen_lengths[None, :], 0), axis=1)
    slot_info = jnp.stack([slot_bucket, slot_length], axis=1)
    values = chosen_inputs.reshape(sampled * block_len, feature_part).astype(jnp.float32)
    local_normed = normalize(values, gain, model_width)
    local_gap = frozen_gap(
        values, local_normed, chosen_targets.reshape(sampled * block_len, feature_part), frozen
    )
    send_normed = place_blocks(placing, local_normed.reshape(sampled, block_len, feature_part))
    send_gap = place_blocks(placing, local_gap.reshape(sampled, block_len, feature_part))
    got_normed, got_gap, got_info = (
        lax.all_to_all(send_normed, DP, split_axis=0, concat_axis=0, tiled=True),
        lax.all_to_all(send_gap, DP, split_axis=0, concat_axis=0, tiled=True),
        lax.all_to_all(slot_info, DP, split_axis=0, concat_axis=0, tiled=True),
    )
    normed = got_normed.reshape(block_capacity * block_len, feature_part)
    base_gap = got_gap.reshape(block_capacity * block_len, feature_part)
    slot_onehot = (got_info[:, 0][:, None] == bucket_range[None, :]).astype(jnp.float32)
    live_mask = (
        (jnp.arange(block_len, dtype=jnp.int32)[None, :] < got_info[:, 1][:, None])
        .astype(jnp.float32)
        .reshape(-1)
    )
    block_coefficient = jnp.sum(slot_onehot * (weights / floor_counts)[None, :], axis=1)
    row_coefficient = jnp.repeat(block_coefficient, block_len)
    down_map = adapter_down[0]
    up_map = adapter_up[0]
    contract_last = (((1,), (1,)), ((), ()))
    contract_first = (((0,), (0,)), ((), ()))
    latent_part = lax.dot_general(
        normed, down_map, contract_last, preferred_element_type=jnp.float32
    )
    latent_rows = of_everyone(latent_part, "mp")
    lowered_rows = (ADAPTER_SCALING * latent_rows).astype(jnp.bfloat16)
    distance = base_gap.astype(jnp.float32) + jnp.dot(
        lowered_rows, up_map, preferred_element_type=jnp.float32
    )
    output_grad = ((2.0 * row_coefficient * live_mask)[:, None] * distance).astype(jnp.bfloat16)
    back_part = lax.dot_general(
        output_grad, up_map, contract_last, preferred_element_type=jnp.float32
    )
    latent_gradient = of_everyone(back_part, "mp")
    lowered_gradient = (ADAPTER_SCALING * latent_gradient).astype(jnp.bfloat16)
    up_gradient = lax.dot_general(
        lowered_rows, output_grad, contract_first, preferred_element_type=jnp.float32
    )
    down_gradient = lax.dot_general(
        lowered_gradient, normed, contract_first, preferred_element_type=jnp.float32
    )
    block_square = jnp.sum(
        (jnp.sum(distance * distance, axis=1) * live_mask).reshape(block_capacity, block_len),
        axis=1,
    )
    partial_value = jnp.sum(slot_onehot * block_square[:, None], axis=0)
    loss_sum = over_axes(partial_value, DP_MP)
    bucket_loss = loss_sum / (floor_counts * model_width)
    progress = jnp.sum(weights * bucket_loss) / jnp.sum(bucket_loss)
    competence_next = competence + 0.5 * (1.0 - competence) * progress
    return (down_gradient[None], up_gradient[None], bucket_loss, competence_next)


def solution(mesh):
    split = Mesh(mesh.devices.reshape(4, 8, 2, mesh.shape["mp"]), ("dp_0", "dp_1", "dp_2", "mp"))
    placed = (
        P(DP, None, "mp"),
        P(DP, None, "mp"),
        P(None, "mp"),
        P("mp"),
        P(DP, None, "mp"),
        P(DP, None, "mp"),
        P(DP),
        P(DP),
        P(DP),
        P(DP, None),
        P(),
    )
    return jax.shard_map(
        on_device,
        mesh=split,
        in_specs=placed,
        out_specs=(P(DP, None, "mp"), P(DP, None, "mp"), P(), P()),
        check_vma=False,
    )
```

profile of v0, /device:TPU:1, one launch (start us, length us, event | category | flops | bytes accessed | tf_op | source)
XLA Modules:
  0.0 286.0 jit_solution(10757932333468929910)
XLA Ops:
  9.9 9.0 %all_to_all.49 = f32[4,1,512]{2,1,0:T(1,128)S(1)} all-to-all(f32[4,1,512]{2,1,0:T(1,128)S(1)} %broadcast_in_dim.109), channel_id=1, replica_groups=mesh['dp_0'=4,'dp_1'=8,'dp_2'=2,'mp'=4] {'mp'}, dimensions={0} | all-to-all | bytes 16384 | tf_op jit(solution)/shard_map/all_to_all | solution.py:21
  19.0 1.4 fusion.3
  22.3 2.2 convolution_convert_fusion
  24.5 4.4 %all_to_all.38 = bf16[64,2,8192]{2,1,0:T(2,128)(2,1)} reshape(bf16[128,8192]{1,0:T(8,128)(2,1)} %convolution_convert_fusion) | data formatting | bytes 4194304 | tf_op jit(solution)/shard_map/all_to_all | solution.py:104
  28.9 13.9 %all-to-all-start.4 = ((bf16[64,2,8192]{2,1,0:T(2,128)(2,1)}), bf16[64,2,8192]{2,1,0:T(2,128)(2,1)}, u32[]{:S(2)}, u32[]{:S(2)}) async-start(bf16[64,2,8192]{2,1,0:T(2,128)(2,1)} %all_to_all.38), calls=%async_computation.4 | async-start | bytes 4194304 | tf_op jit(solution)/shard_map/all_to_all | solution.py:104
  44.1 49.9 %all-to-all-done.4 = bf16[64,2,8192]{2,1,0:T(2,128)(2,1)} async-done(((bf16[64,2,8192]{2,1,0:T(2,128)(2,1)}), bf16[64,2,8192]{2,1,0:T(2,128)(2,1)}, u32[]{:S(2)}, u32[]{:S(2)}) %all-to-all-start.4) | async-done | bytes 2097184 | tf_op jit(solution)/shard_map/all_to_all | solution.py:104
  94.0 5.8 %all-to-all-start = ((s32[64,2,2]{1,2,0:T(2,128)}), s32[64,2,2]{1,2,0:T(2,128)S(1)}, u32[]{:S(2)}, u32[]{:S(2)}) async-start(s32[64,2,2]{1,2,0:T(2,128)} %copy.31), calls=%async_computation | async-start | bytes 131072 | tf_op jit(solution)/shard_map/all_to_all | solution.py:106
  99.9 3.2 %gather_fusion.1 = bf16[64,8,1024]{2,1,0:T(8,128)(2,1)} fusion(bf16[128,8,1024]{2,1,0:T(8,128)(2,1)} %param.14, s32[1024]{0:T(1024)S(1)} %pad_clamp_fusion), kind=kCustom, calls=%fused_computation.1.clone | custom fusion | bytes 2097408 | tf_op jit(solution)/shard_map/jit(_take)/gather | solution.py:77
  103.1 4.5 %reshape.136 = bf16[1024,1024]{1,0:T(8,128)(2,1)} reshape(bf16[64,2,8192]{2,1,0:T(2,128)(2,1)} %all-to-all-done.4) | data formatting | bytes 4194304 | tf_op jit(solution)/shard_map/reshape | solution.py:108
  107.6 2.0 all-to-all-done
  110.2 8.3 %all-to-all-start.1 = ((f32[64,1,16]{2,1,0:T(1,128)}), f32[64,1,16]{2,1,0:T(1,128)S(1)}, u32[]{:S(2)}, u32[]{:S(2)}) async-start(f32[64,1,16]{2,1,0:T(1,128)} %broadcast_in_dim.106), calls=%async_computation.1 | async-start | bytes 65536 | tf_op jit(solution)/shard_map/all_to_all | solution.py:21
  118.5 2.4 fusion.11
  120.9 6.9 %all-to-all-done.1 = f32[64,1,16]{2,1,0:T(1,128)S(1)} async-done(((f32[64,1,16]{2,1,0:T(1,128)}), f32[64,1,16]{2,1,0:T(1,128)S(1)}, u32[]{:S(2)}, u32[]{:S(2)}) %all-to-all-start.1) | async-done | bytes 4128 | tf_op jit(solution)/shard_map/all_to_all | solution.py:21
  128.9 4.4 %all-to-all-start.5 = ((f32[4,1024,64]{1,2,0:T(8,128)}), f32[4,1024,64]{1,2,0:T(8,128)}, u32[]{:S(2)}, u32[]{:S(2)}) async-start(f32[4,1024,64]{1,2,0:T(8,128)} %broadcast_in_dim.110), calls=%async_computation.5 | async-start | bytes 2097152 | tf_op jit(solution)/shard_map/all_to_all | solution.py:21
  133.4 10.4 %fusion.5 = bf16[512,1024]{1,0:T(8,128)(2,1)} fusion(bf16[512,4096]{1,0:T(8,128)(2,1)} %all-gather.2.cloned.1.call-done, bf16[4096,1024]{1,0:T(8,128)(2,1)} %param.15, bf16[64,8,1024]{2,1,0:T(8,128)(2,1)} %gather_fusion.1, pred[64]{0:T(512)(128)(4,1)S(1)} %compare_and_fusion, bf16[64,8,1024]{2,1,0:T(8,128)(2,1)S(1)} %gather_fusion), kind=kOutput, calls=%fused_computation.15 | convolution fusion | flops 4298637312 | bytes 15728704 | tf_op jit(solution)/shard_map/dot_general | solution.py:43
  143.8 1.6 reshape_reshape.4
  145.4 2.2 convolution_convert_fusion.1
  147.5 4.4 %all_to_all.36 = bf16[64,2,8192]{2,1,0:T(2,128)(2,1)} reshape(bf16[128,8192]{1,0:T(8,128)(2,1)} %convolution_convert_fusion.1) | data formatting | bytes 4194304 | tf_op jit(solution)/shard_map/all_to_all | solution.py:105
  151.9 5.6 %all-to-all-start.3 = ((bf16[64,2,8192]{2,1,0:T(2,128)(2,1)}), bf16[64,2,8192]{2,1,0:T(2,128)(2,1)}, u32[]{:S(2)}, u32[]{:S(2)}) async-start(bf16[64,2,8192]{2,1,0:T(2,128)(2,1)} %all_to_all.36), calls=%async_computation.3 | async-start | bytes 4194304 | tf_op jit(solution)/shard_map/all_to_all | solution.py:105
  158.4 1.3 reduce_sum.165
  159.8 49.0 %all-to-all-done.3 = bf16[64,2,8192]{2,1,0:T(2,128)(2,1)} async-done(((bf16[64,2,8192]{2,1,0:T(2,128)(2,1)}), bf16[64,2,8192]{2,1,0:T(2,128)(2,1)}, u32[]{:S(2)}, u32[]{:S(2)}) %all-to-all-start.3) | async-done | bytes 2097184 | tf_op jit(solution)/shard_map/all_to_all | solution.py:105
  208.8 4.6 %reshape.139 = f32[1024,1024]{1,0:T(8,128)} reshape(bf16[64,2,8192]{2,1,0:T(2,128)(2,1)} %all-to-all-done.3) | data formatting | bytes 6291456 | tf_op jit(solution)/shard_map/convert_element_type | solution.py:127
  213.4 5.4 %copy.35 = f32[1024,1024]{0,1:T(8,128)} copy(f32[1024,1024]{1,0:T(8,128)} %reshape.139) | data formatting | bytes 8388608 | tf_op jit(solution)/shard_map/convert_element_type | solution.py:127
  218.9 5.0 %multiply_reduce_fusion = (f32[1024]{0:T(1024)S(1)}, f32[1024,1024]{0,1:T(8,128)}) fusion(f32[1024,1024]{0,1:T(8,128)} %copy.35, bf16[1,64,1024]{2,1,0:T(8,128)(2,1)S(1)} %copy-done.1, f32[1024,64]{0,1:T(8,128)S(1)} %reduce_sum.165), kind=kOutput, calls=%fused_computation.4 | convolution fusion | flops 137493504 | bytes 8785920 | tf_op jit(solution)/shard_map/dot_general | solution.py:127
  224.4 2.7 fusion.8
  228.2 4.3 %all-to-all-start.6 = ((f32[4,1024,64]{1,2,0:T(8,128)}), f32[4,1024,64]{1,2,0:T(8,128)S(1)}, u32[]{:S(2)}, u32[]{:S(2)}) async-start(f32[4,1024,64]{1,2,0:T(8,128)} %broadcast_in_dim.111), calls=%async_computation.6 | async-start | bytes 2097152 | tf_op jit(solution)/shard_map/all_to_all | solution.py:21
  232.5 9.0 %psum.28 = f32[16]{0:T(128)S(1)} all-reduce(f32[16]{0:T(128)S(1)} %get-tuple-element.7), channel_id=1, replica_groups=mesh['dp_0'=4,'dp_1'=8,'dp_2'=2,'mp'=4] {'dp_0'}, use_global_device_ids=true, to_apply=%region_15.17 | all-reduce | flops 16 | bytes 128 | tf_op jit(solution)/shard_map/psum | solution.py:32
  241.5 11.4 %psum.29 = f32[16]{0:T(128)S(1)} all-reduce(f32[16]{0:T(128)S(1)} %psum.28), channel_id=1, replica_groups=mesh['dp_0'=4,'dp_1'=8,'dp_2'=2,'mp'=4] {'dp_1'}, use_global_device_ids=true, to_apply=%region_16.18 | all-reduce | flops 16 | bytes 128 | tf_op jit(solution)/shard_map/psum | solution.py:32
  252.9 7.2 %psum.30 = f32[16]{0:T(128)S(1)} all-reduce(f32[16]{0:T(128)S(1)} %psum.29), channel_id=1, replica_groups=mesh['dp_0'=4,'dp_1'=8,'dp_2'=2,'mp'=4] {'dp_2'}, use_global_device_ids=true, to_apply=%region_17.19 | all-reduce | flops 16 | bytes 128 | tf_op jit(solution)/shard_map/psum | solution.py:32
  260.2 8.9 %psum.31 = f32[16]{0:T(128)S(1)} all-reduce(f32[16]{0:T(128)S(1)} %psum.30), channel_id=1, replica_groups=mesh['dp_0'=4,'dp_1'=8,'dp_2'=2,'mp'=4] {'mp'}, use_global_device_ids=true, to_apply=%region_18.20 | all-reduce | flops 16 | bytes 128 | tf_op jit(solution)/shard_map/psum | solution.py:32
  271.5 3.7 %convolution_bitcast_fusion = f32[1,64,1024]{2,1,0:T(8,128)} fusion(f32[1024,1024]{0,1:T(8,128)} %get-tuple-element.17, f32[1024]{0:T(1024)S(1)} %mul.142, f32[1024,64]{0,1:T(8,128)S(1)} %reduce_sum.165), kind=kOutput, calls=%fused_computation.18 | convolution fusion | flops 136445952 | bytes 4722688 | tf_op jit(solution)/shard_map/dot_general | solution.py:136
  275.3 2.8 convolution_bitcast_fusion.1
  (59 shorter events, 11.0 us)
Async XLA Ops:
  7.2 1.6 copy-start
  7.2 11.8 %copy-start.2 = (f32[1024]{0:T(1024)S(1)}, f32[1024]{0:T(1024)}, u32[]{:S(2)}) copy-start(f32[1024]{0:T(1024)} %param.16) | copy-start | bytes 12292
  7.2 126.2 %all-gather.2.cloned.1.call-start = ((), (), s32[]{:S(2)}) async-start(), calls=%async_computation.7 | async-start | bytes 5242880 | tf_op jit(solution)/shard_map/all_gather | solution.py:44
  9.4 11.0 %copy-start.6 = (s32[64,1]{0,1:T(1,128)S(1)}, s32[64,1]{0,1:T(1,128)}, u32[]{:S(2)}) copy-start(s32[64,1]{0,1:T(1,128)} %param.22) | copy-start | bytes 772
  28.9 13.9 %copy-start.3 = (s32[64]{0:T(128)S(1)}, s32[64]{0:T(128)}, u32[]{:S(2)}) copy-start(s32[64]{0:T(128)} %param.19) | copy-start | bytes 772
  28.9 13.9 %copy-start.4 = (s32[128]{0:T(128)S(1)}, s32[128]{0:T(128)}, u32[]{:S(2)}) copy-start(s32[128]{0:T(128)} %param.20) | copy-start | bytes 1540
  28.9 13.9 %copy-start.5 = (s32[128]{0:T(128)S(1)}, s32[128]{0:T(128)}, u32[]{:S(2)}) copy-start(s32[128]{0:T(128)} %param.21) | copy-start | bytes 1540
  28.9 65.1 %all-to-all-start.4 = ((bf16[64,2,8192]{2,1,0:T(2,128)(2,1)}), bf16[64,2,8192]{2,1,0:T(2,128)(2,1)}, u32[]{:S(2)}, u32[]{:S(2)}) async-start(bf16[64,2,8192]{2,1,0:T(2,128)(2,1)} %all_to_all.38), calls=%async_computation.4 | async-start | bytes 4194304 | tf_op jit(solution)/shard_map/all_to_all | solution.py:104
  94.0 15.6 %all-to-all-start = ((s32[64,2,2]{1,2,0:T(2,128)}), s32[64,2,2]{1,2,0:T(2,128)S(1)}, u32[]{:S(2)}, u32[]{:S(2)}) async-start(s32[64,2,2]{1,2,0:T(2,128)} %copy.31), calls=%async_computation | async-start | bytes 131072 | tf_op jit(solution)/shard_map/all_to_all | solution.py:106
  110.2 17.5 %all-to-all-start.1 = ((f32[64,1,16]{2,1,0:T(1,128)}), f32[64,1,16]{2,1,0:T(1,128)S(1)}, u32[]{:S(2)}, u32[]{:S(2)}) async-start(f32[64,1,16]{2,1,0:T(1,128)} %broadcast_in_dim.106), calls=%async_computation.1 | async-start | bytes 65536 | tf_op jit(solution)/shard_map/all_to_all | solution.py:21
  128.9 23.0 %all-to-all-start.5 = ((f32[4,1024,64]{1,2,0:T(8,128)}), f32[4,1024,64]{1,2,0:T(8,128)}, u32[]{:S(2)}, u32[]{:S(2)}) async-start(f32[4,1024,64]{1,2,0:T(8,128)} %broadcast_in_dim.110), calls=%async_computation.5 | async-start | bytes 2097152 | tf_op jit(solution)/shard_map/all_to_all | solution.py:21
  151.9 56.9 %all-to-all-start.3 = ((bf16[64,2,8192]{2,1,0:T(2,128)(2,1)}), bf16[64,2,8192]{2,1,0:T(2,128)(2,1)}, u32[]{:S(2)}, u32[]{:S(2)}) async-start(bf16[64,2,8192]{2,1,0:T(2,128)(2,1)} %all_to_all.36), calls=%async_computation.3 | async-start | bytes 4194304 | tf_op jit(solution)/shard_map/all_to_all | solution.py:105
  213.4 5.4 %copy-start.1 = (bf16[1,64,1024]{2,1,0:T(8,128)(2,1)S(1)}, bf16[1,64,1024]{2,1,0:T(8,128)(2,1)}, u32[]{:S(2)}) copy-start(bf16[1,64,1024]{2,1,0:T(8,128)(2,1)} %param.18) | copy-start | bytes 393220
  228.2 47.0 %all-to-all-start.6 = ((f32[4,1024,64]{1,2,0:T(8,128)}), f32[4,1024,64]{1,2,0:T(8,128)S(1)}, u32[]{:S(2)}, u32[]{:S(2)}) async-start(f32[4,1024,64]{1,2,0:T(8,128)} %broadcast_in_dim.111), calls=%async_computation.6 | async-start | bytes 2097152 | tf_op jit(solution)/shard_map/all_to_all | solution.py:21
Sparse Core Ops, SparseCore 0:
  20.5 53.1 all-gather.1
where the time goes:
time: 287 us; the launch traced here: 286 us
  waiting for transfers between devices  108 us (38%)
  blocking collectives  45.6 us (16%)
  starting transfers between devices  42.4 us (15%)
  local copies, waits for them, and re-layouts  34.5 us (12%)
  matrix products  31.2 us (11%)
  between operations  17.5 us (6%)
  other arithmetic  7.19 us (3%)
    all_to_all x1, waiting for transfers between devices, on_device(): lax.all_to_all(send_normed, DP, split_axis=0, concat_axis=0, tiled=True)  49.9 us
    all_to_all x1, waiting for transfers between devices, on_device(): lax.all_to_all(send_gap, DP, split_axis=0, concat_axis=0, tiled=True)  49 us
    psum x4, blocking collectives, over_axes(): return functools.reduce(lax.psum, axes, value)  36.6 us
    all_to_all x3, starting transfers between devices, sent_to_all(): lax.all_to_all(jnp.broadcast_to(value[None], (peers, *value.shape)), axis...  17 us
    all_to_all x1, starting transfers between devices, on_device(): lax.all_to_all(send_normed, DP, split_axis=0, concat_axis=0, tiled=True)  13.9 us
    dot_general x1, matrix products, frozen_gap(): jnp.dot(lax.all_gather(normed, 'mp', axis=1, tiled=True), frozen, preferr...  10.4 us
    convert_element_type x2, local copies, waits for them, and re-layouts, on_device(): base_gap.astype(jnp.float32)  10.1 us
    all_to_all x1, blocking collectives, sent_to_all(): lax.all_to_all(jnp.broadcast_to(value[None], (peers, *value.shape)), axis...  8.98 us
  transfers between devices with their start and end apart: 7, of which 4 were waited for; matrix products, arithmetic and copies ran while one was open for 13% of the time, Pallas kernels for 0%

commit v1 on v0

v1 whole, which is shorter than its diff:
```python
import jax
import jax.numpy as jnp
from jax import lax
from jax.experimental import pallas as pl
from jax.experimental.pallas import tpu as pltpu
from jax.sharding import Mesh
from jax.sharding import PartitionSpec as P

NB = 16
DP = ("dp_0", "dp_1", "dp_2")
DP_MP = ("dp_0", "dp_1", "dp_2", "mp")

RMS_EPSILON = 1e-05
SHARPNESS = 12.0
ADAPTER_SCALING = 2.0
PER_PAIR = 2
VMEM_BYTES = 48 * 1024 * 1024
CONTRACT_LAST = (((1,), (1,)), ((), ()))
CONTRACT_FIRST = (((0,), (0,)), ((), ()))


def of_everyone(value, axis):
    peers = lax.axis_size(axis)
    everything = lax.all_to_all(
        jnp.broadcast_to(value[None], (peers, *value.shape)), axis, 0, 0, tiled=True
    )
    return jnp.sum(everything, axis=0)


def route_kernel(
    ids, dest, buckets, lengths, pool, send, own, info, counts, slot_of, arrived, source, sem
):
    sampled = ids.shape[0]
    slots = send.shape[0]

    def clear(k, carry):
        arrived[k] = 0
        for s in range(PER_PAIR):
            source[k * PER_PAIR + s] = ids[0]
            info[k, s] = 0
            info[k, PER_PAIR + s] = 0
        return carry

    def clear_counts(b, carry):
        counts[b] = 0
        return carry

    lax.fori_loop(0, slots // PER_PAIR, clear, 0)
    lax.fori_loop(0, NB, clear_counts, 0)

    def place(j, carry):
        block = ids[j]
        trainer = dest[j]
        pltpu.make_async_copy(pool.at[block], own.at[j], sem.at[0]).start()
        order = arrived[trainer]
        arrived[trainer] = order + 1
        slot = trainer * PER_PAIR + order
        slot_of[j] = slot
        source[slot] = block
        bucket = buckets[block]
        length = lengths[block]
        info[trainer, order] = bucket
        info[trainer, PER_PAIR + order] = length
        counts[bucket] = counts[bucket] + length
        return carry

    lax.fori_loop(0, sampled, place, 0)

    def copy(s, carry):
        pltpu.make_async_copy(pool.at[source[s]], send.at[s], sem.at[1]).start()
        return carry

    lax.fori_loop(0, slots, copy, 0)

    def list_free(k, found):
        for s in range(PER_PAIR):
            free = arrived[k] <= s

            @pl.when(free)
            def _():
                slot_of[sampled + found] = k * PER_PAIR + s

            found = found + jnp.where(free, 1, 0)
        return found

    lax.fori_loop(0, slots // PER_PAIR, list_free, 0)
    pltpu.make_async_copy(pool.at[pl.ds(0, sampled)], own, sem.at[0]).wait()
    pltpu.make_async_copy(send, send, sem.at[1]).wait()


def route(ids, dest, buckets, lengths, pool, trainers):
    sampled = ids.shape[0]
    slots = trainers * PER_PAIR
    block = pool.shape[1:]
    smem = pl.BlockSpec(memory_space=pltpu.SMEM)
    hbm = pl.BlockSpec(memory_space=pl.ANY)
    return pl.pallas_call(
        route_kernel,
        out_shape=(
            jax.ShapeDtypeStruct((slots, *block), pool.dtype),
            jax.ShapeDtypeStruct((sampled, *block), pool.dtype),
            jax.ShapeDtypeStruct((trainers, 2 * PER_PAIR), jnp.int32),
            jax.ShapeDtypeStruct((NB,), jnp.int32),
            jax.ShapeDtypeStruct((slots,), jnp.int32),
        ),
        in_specs=[smem, smem, smem, smem, hbm],
        out_specs=(hbm, hbm, smem, smem, smem),
        scratch_shapes=[
            pltpu.SMEM((trainers,), jnp.int32),
            pltpu.SMEM((slots,), jnp.int32),
            pltpu.SemaphoreType.DMA((2,)),
        ],
        cost_estimate=pl.CostEstimate(flops=0, bytes_accessed=6 << 20, transcendentals=0),
        name="route",
    )(ids, dest, buckets, lengths, pool)


def gap_kernel(
    ids, slot_of, gathered, own, gain, frozen, targets, send, normed, target_rows, gap, sem
):
    step = pl.program_id(0)
    parts, rows, part = gathered.shape
    sampled, block_len, columns = gap.shape
    width = frozen.shape[1]
    slots = send.shape[0]

    @pl.when(step == 0)
    def _():
        def fetch(j, carry):
            pltpu.make_async_copy(targets.at[ids[j]], target_rows.at[j], sem.at[0]).start()
            return carry

        lax.fori_loop(0, sampled, fetch, 0)
        chunk = 128

        def normalize(i, carry):
            at = pl.ds(pl.multiple_of(i * chunk, chunk), chunk)
            total = jnp.zeros((chunk, 1), jnp.float32)
            for p in range(parts):
                x = gathered[p, at, :].astype(jnp.float32)
                total = total + jnp.sum(x * x, axis=1, keepdims=True)
            inverse = lax.rsqrt(total / (parts * part) + RMS_EPSILON)
            for p in range(parts):
                x = gathered[p, at, :].astype(jnp.float32)
                normed[p, at, :] = (x * inverse * gain[p : p + 1, :]).astype(jnp.bfloat16)
            return carry

        lax.fori_loop(0, rows // chunk, normalize, 0)
        pltpu.make_async_copy(targets.at[pl.ds(0, sampled)], target_rows, sem.at[0]).wait()

    def multiply(p, total):
        weights = frozen[pl.ds(pl.multiple_of(p * part, part), part), :]
        return total + jnp.dot(normed[p], weights, preferred_element_type=jnp.float32)

    projected = lax.fori_loop(0, parts, multiply, jnp.zeros((rows, width), jnp.float32))
    at = pl.ds(pl.multiple_of(step * width, width), width)
    x = own[:, :, at].astype(jnp.float32)
    t = target_rows[:, :, at].astype(jnp.float32)
    gap[:, :, at] = (x + projected.reshape(sampled, block_len, width) - t).astype(jnp.bfloat16)

    @pl.when(step == pl.num_programs(0) - 1)
    def _():
        def place(j, carry):
            pltpu.make_async_copy(gap.at[j], send.at[slot_of[j]], sem.at[1]).start()
            return carry

        lax.fori_loop(0, sampled, place, 0)

        def fill(s, carry):
            pltpu.make_async_copy(gap.at[0], send.at[slot_of[sampled + s]], sem.at[1]).start()
            return carry

        lax.fori_loop(0, slots - sampled, fill, 0)
        pltpu.make_async_copy(send, send, sem.at[1]).wait()


def base_gap_slots(ids, slot_of, gathered, own, gain, frozen, targets):
    parts, rows, part = gathered.shape
    width, columns = frozen.shape
    slots = slot_of.shape[0]
    tile = 256
    smem = pl.BlockSpec(memory_space=pltpu.SMEM)
    hbm = pl.BlockSpec(memory_space=pl.ANY)
    return pl.pallas_call(
        gap_kernel,
        grid=(columns // tile,),
        out_shape=jax.ShapeDtypeStruct((slots, *own.shape[1:]), jnp.bfloat16),
        in_specs=[
            smem,
            smem,
            pl.BlockSpec(gathered.shape, lambda n: (0, 0, 0)),
            pl.BlockSpec(own.shape, lambda n: (0, 0, 0)),
            pl.BlockSpec(gain.shape, lambda n: (0, 0)),
            pl.BlockSpec((width, tile), lambda n: (0, n)),
            hbm,
        ],
        out_specs=hbm,
        scratch_shapes=[
            pltpu.VMEM(gathered.shape, jnp.bfloat16),
            pltpu.VMEM(own.shape, jnp.bfloat16),
            pltpu.VMEM(own.shape, jnp.bfloat16),
            pltpu.SemaphoreType.DMA((2,)),
        ],
        compiler_params=pltpu.CompilerParams(vmem_limit_bytes=VMEM_BYTES),
        cost_estimate=pl.CostEstimate(
            flops=2 * rows * width * columns, bytes_accessed=18 << 20, transcendentals=rows
        ),
        name="base_gap",
    )(ids, slot_of, gathered, own, gain, frozen, targets)


def trainer_kernel(gap, lowered, up, facts, grad_up, back, loss):
    step = pl.program_id(0)
    low = lowered[...]
    up_map = up[...]
    facts_now = facts[...]
    distance = gap[...].astype(jnp.float32) + lax.dot_general(
        low, up_map, CONTRACT_FIRST, preferred_element_type=jnp.float32
    )
    output_grad = (facts_now[:, NB : NB + 1] * distance).astype(jnp.bfloat16)
    squares = jnp.sum(distance * distance, axis=1, keepdims=True)
    part = jnp.sum(facts_now * squares, axis=0, keepdims=True)
    back[...] = lax.dot_general(
        up_map, output_grad, CONTRACT_LAST, preferred_element_type=jnp.float32
    )
    own = jnp.dot(low, output_grad, preferred_element_type=jnp.float32)

    @pl.when(step == 0)
    def _():
        grad_up[...] = own
        loss[...] = part

    @pl.when(step > 0)
    def _():
        grad_up[...] += own
        loss[...] += part


def trainer_step(gap, lowered, up, facts):
    rows, columns = gap.shape
    rank = up.shape[0]
    lanes = facts.shape[1]
    chunk = 256
    return pl.pallas_call(
        trainer_kernel,
        grid=(rows // chunk,),
        out_shape=(
            jax.ShapeDtypeStruct((rank, columns), jnp.float32),
            jax.ShapeDtypeStruct((rank, rows), jnp.float32),
            jax.ShapeDtypeStruct((1, lanes), jnp.float32),
        ),
        in_specs=[
            pl.BlockSpec((chunk, columns), lambda i: (i, 0)),
            pl.BlockSpec((rank, chunk), lambda i: (0, i)),
            pl.BlockSpec((rank, columns), lambda i: (0, 0)),
            pl.BlockSpec((chunk, lanes), lambda i: (i, 0)),
        ],
        out_specs=(
            pl.BlockSpec((rank, columns), lambda i: (0, 0)),
            pl.BlockSpec((rank, chunk), lambda i: (0, i)),
            pl.BlockSpec((1, lanes), lambda i: (0, 0)),
        ),
        compiler_params=pltpu.CompilerParams(vmem_limit_bytes=VMEM_BYTES),
        cost_estimate=pl.CostEstimate(
            flops=6 * rows * rank * columns, bytes_accessed=4 << 20, transcendentals=0
        ),
        name="trainer_step",
    )(gap, lowered, up, facts)


def on_device(
    pool_inputs,
    pool_targets,
    frozen,
    gain,
    adapter_down,
    adapter_up,
    sample_ids,
    buckets,
    lengths,
    destinations,
    competence,
):
    trainers = lax.axis_size(DP)
    parts = lax.axis_size("mp")
    sampled = sample_ids.shape[0]
    _, block_len, part = pool_inputs.shape
    width = frozen.shape[0]
    slots = trainers * PER_PAIR
    rows = slots * block_len
    per_peer = PER_PAIR * block_len
    down_map = adapter_down[0]
    up_map = adapter_up[0]
    bucket_range = jnp.arange(NB, dtype=jnp.int32)

    send_x, own_x, info, counts, slot_of = route(
        sample_ids, destinations[:, 0], buckets, lengths, pool_inputs, trainers
    )
    got_x = lax.all_to_all(
        send_x.reshape(trainers, per_peer, part), DP, 0, 0, tiled=True
    )
    whole_gain = lax.all_gather(gain, "mp")
    gathered = lax.all_gather(own_x.reshape(sampled * block_len, part), "mp")
    message = jnp.concatenate(
        [info, jnp.broadcast_to(counts[None, :], (trainers, NB))], axis=1
    )
    got_info = lax.all_to_all(message[:, None, :], DP, 0, 0, tiled=True)[:, 0, :]

    send_gap = base_gap_slots(
        sample_ids,
        slot_of,
        gathered,
        own_x,
        whole_gain,
        frozen,
        pool_targets,
    )
    got_gap = lax.all_to_all(
        send_gap.reshape(trainers, per_peer, part), DP, 0, 0, tiled=True
    )

    floor_counts = jnp.maximum(
        jnp.sum(got_info[:, 2 * PER_PAIR :], axis=0).astype(jnp.float32), 1.0
    )
    weights = jax.nn.sigmoid(
        SHARPNESS * (competence[0] - (bucket_range.astype(jnp.float32) + 0.5) / NB)
    )
    row_bucket = jnp.repeat(got_info[:, :PER_PAIR].reshape(slots), block_len)
    row_length = jnp.repeat(got_info[:, PER_PAIR : 2 * PER_PAIR].reshape(slots), block_len)
    live = (jnp.arange(rows, dtype=jnp.int32) % block_len < row_length).astype(jnp.float32)
    onehot = (row_bucket[:, None] == bucket_range[None, :]).astype(jnp.float32) * live[:, None]
    coefficient = 2.0 * jnp.sum(onehot * (weights / floor_counts)[None, :], axis=1)
    facts = jnp.concatenate(
        [onehot, coefficient[:, None], jnp.zeros((rows, 128 - NB - 1), jnp.float32)], axis=1
    )

    values = got_x.reshape(rows, part).astype(jnp.float32)
    square_total = of_everyone(jnp.sum(values * values, axis=1), "mp")
    inverse_rms = lax.rsqrt(square_total / width + RMS_EPSILON)
    normed = (values * inverse_rms[:, None] * gain[None, :]).astype(jnp.bfloat16)
    latent_part = lax.dot_general(
        down_map, normed, CONTRACT_LAST, preferred_element_type=jnp.float32
    )
    lowered = (ADAPTER_SCALING * of_everyone(latent_part, "mp")).astype(jnp.bfloat16)

    grad_up, back_part, loss_part = trainer_step(
        got_gap.reshape(rows, part), lowered, up_map, facts
    )
    loss_sum = lax.psum(loss_part[0, :NB], DP_MP)
    lowered_gradient = (ADAPTER_SCALING * of_everyone(back_part, "mp")).astype(jnp.bfloat16)
    grad_down = jnp.dot(lowered_gradient, normed, preferred_element_type=jnp.float32)
    bucket_loss = loss_sum / (floor_counts * width)
    progress = jnp.sum(weights * bucket_loss) / jnp.sum(bucket_loss)
    competence_next = competence + 0.5 * (1.0 - competence) * progress
    return (grad_down[None], grad_up[None], bucket_loss, competence_next)


def solution(mesh):
    split = Mesh(mesh.devices.reshape(4, 8, 2, mesh.shape["mp"]), DP_MP)
    placed = (
        P(DP, None, "mp"),
        P(DP, None, "mp"),
        P(None, "mp"),
        P("mp"),
        P(DP, None, "mp"),
        P(DP, None, "mp"),
        P(DP),
        P(DP),
        P(DP),
        P(DP, None),
        P(),
    )
    return jax.shard_map(
        on_device,
        mesh=split,
        in_specs=placed,
        out_specs=(P(DP, None, "mp"), P(DP, None, "mp"), P(), P()),
        check_vma=False,
    )
```

time: 287 us -> 402 us (1.40)
  Pallas kernels: 0 us -> 121 us
  blocking collectives: 45.6 us -> 96.6 us
  matrix products: 31.2 us -> 3.53 us
  local copies, waits for them, and re-layouts: 34.5 us -> 8.07 us
    pallas_call x0 -> x3, Pallas kernels: none -> 121 us  [the longest x1 99 us: route(): pl.pallas_call(route_kernel, out_shape=(jax.ShapeDtypeStruct((slots, *blo...]
    psum x4 -> x1, blocking collectives: 36.6 us -> 78.6 us  [on_device(): loss_sum = lax.psum(loss_part[0, :NB], DP_MP)]
    dot_general x8 -> x2, matrix products: 31.2 us -> 3.53 us  [the longest x1 2.78 us: on_device(): jnp.dot(lowered_gradient, normed, preferred_element_type=jnp.float32)]
    all_gather x0 -> x1, blocking collectives: none -> 18 us  [on_device(): whole_gain = lax.all_gather(gain, 'mp')]
    convert_element_type x2 -> x0, local copies, waits for them, and re-layouts: 10.1 us -> none  [on_device(): base_gap.astype(jnp.float32)]
    all_to_all x1 -> x0, blocking collectives: 8.98 us -> none  [sent_to_all(): lax.all_to_all(jnp.broadcast_to(value[None], (peers, *value.shape)), axis...]
    all_to_all x4 -> x0, local copies, waits for them, and re-layouts: 8.94 us -> none  [the longest x1 4.4 us: on_device(): lax.all_to_all(send_gap, DP, split_axis=0, concat_axis=0, tiled=True)]
    reshape x1 -> x3, local copies, waits for them, and re-layouts: 4.48 us -> 0.38 us  [the longest x1 0.14 us: on_device(): got_info[:, PER_PAIR:2 * PER_PAIR].reshape(slots)]
  transfers between devices with their start and end apart: 7 -> 7, of which waited for: 4 -> 4; matrix products, arithmetic and copies ran while one was open for 13% -> 4% of each run, Pallas kernels for 0% -> 5%
where the time goes in v1:
time: 402 us; the launch traced here: 401 us
  Pallas kernels  121 us (30%)
  waiting for transfers between devices  106 us (26%)
  blocking collectives  96.6 us (24%)
  starting transfers between devices  39.6 us (10%)
  between operations  17.5 us (4%)
  other arithmetic  8.21 us (2%)
  local copies, waits for them, and re-layouts  8.07 us (2%)
    pallas_call x1, Pallas kernels, route(): pl.pallas_call(route_kernel, out_shape=(jax.ShapeDtypeStruct((slots, *blo...  99 us
    psum x1, blocking collectives, on_device(): loss_sum = lax.psum(loss_part[0, :NB], DP_MP)  78.6 us
    all_to_all x1, waiting for transfers between devices, on_device(): lax.all_to_all(send_x.reshape(trainers, per_peer, part), DP, 0, 0, tiled=...  51.1 us
    all_to_all x1, waiting for transfers between devices, on_device(): lax.all_to_all(send_gap.reshape(trainers, per_peer, part), DP, 0, 0, tile...  44.1 us
    pallas_call x1, Pallas kernels, base_gap_slots(): pl.pallas_call(gap_kernel, grid=(columns // tile,), out_shape=jax.ShapeDt...  18.9 us
    all_gather x1, blocking collectives, on_device(): whole_gain = lax.all_gather(gain, 'mp')  18 us
    all_to_all x1, starting transfers between devices, on_device(): lax.all_to_all(send_x.reshape(trainers, per_peer, part), DP, 0, 0, tiled=...  13 us
    all_to_all x3, starting transfers between devices, of_everyone(): lax.all_to_all(jnp.broadcast_to(value[None], (peers, *value.shape)), axis...  11.9 us
  transfers between devices with their start and end apart: 7, of which 4 were waited for; matrix products, arithmetic and copies ran while one was open for 4% of the time, Pallas kernels for 5%

profile of v1, /device:TPU:1, one launch (start us, length us, event | category | flops | bytes accessed | tf_op | source)
XLA Modules:
  0.0 400.9 jit_solution(3781633592658233687)
XLA Ops:
  7.2 99.0 %route.1 = (bf16[128,8,1024]{2,1,0:T(8,128)(2,1)}, bf16[64,8,1024]{2,1,0:T(8,128)(2,1)}, s32[64,4]{1,0:T(8,128)}, s32[16]{0:T(128)}, s32[128]{0:T(128)}) custom-call(s32[64]{0:T(128)} %ids.3, s32[64]{0:T(128)} %bitcast.39, s32[128]{0:T(128)} %buckets.1, s32[128]{0:T(128)} %lengths.1, bf16[128,8,1024]{2,1,0:T(8,128)(2,1)} %pool.1), custom_call_target="tpu_custom_call" | custom-call | bytes 6291456 | tf_op jit(solution)/shard_map/route/pallas_call | solution.py:97
  106.3 13.0 %all-to-all-start.1 = ((bf16[64,16,1024]{2,1,0:T(8,128)(2,1)}), bf16[64,16,1024]{2,1,0:T(8,128)(2,1)S(1)}, u32[]{:S(2)}, u32[]{:S(2)}) async-start(bf16[64,16,1024]{2,1,0:T(8,128)(2,1)} %bitcast.37), calls=%async_computation.1 | async-start | bytes 4194304 | tf_op jit(solution)/shard_map/all_to_all | solution.py:299
  119.5 51.1 %all-to-all-done.1 = bf16[64,16,1024]{2,1,0:T(8,128)(2,1)S(1)} async-done(((bf16[64,16,1024]{2,1,0:T(8,128)(2,1)}), bf16[64,16,1024]{2,1,0:T(8,128)(2,1)S(1)}, u32[]{:S(2)}, u32[]{:S(2)}) %all-to-all-start.1) | async-done | bytes 2097184 | tf_op jit(solution)/shard_map/all_to_all | solution.py:299
  170.5 0.5 multiply_reduce_fusion
  171.1 0.7 broadcast_in_dim.23
  171.8 4.2 %all-to-all-start.2 = ((f32[4,1,1024]{2,1,0:T(1,128)}), f32[4,1,1024]{2,1,0:T(1,128)S(1)}, u32[]{:S(2)}, u32[]{:S(2)}) async-start(f32[4,1,1024]{2,1,0:T(1,128)} %broadcast_in_dim.23), calls=%async_computation.2 | async-start | bytes 32768 | tf_op jit(solution)/shard_map/all_to_all | solution.py:24
  176.1 0.7 copy.24
  176.8 3.4 all-to-all-done.2
  180.2 7.4 %all-to-all-start.4 = ((s32[64,1,20]{2,1,0:T(1,128)}), s32[64,1,20]{2,1,0:T(1,128)}, u32[]{:S(2)}, u32[]{:S(2)}) async-start(s32[64,1,20]{2,1,0:T(1,128)} %bitcast.9), calls=%async_computation.4 | async-start | bytes 65536 | tf_op jit(solution)/shard_map/all_to_all | solution.py:307
  187.8 0.5 multiply_convert_fusion
  188.4 0.8 convolution_bitcast_fusion.1
  189.2 7.7 %all-to-all-done.4 = s32[64,1,20]{2,1,0:T(1,128)} async-done(((s32[64,1,20]{2,1,0:T(1,128)}), s32[64,1,20]{2,1,0:T(1,128)}, u32[]{:S(2)}, u32[]{:S(2)}) %all-to-all-start.4) | async-done | bytes 5152 | tf_op jit(solution)/shard_map/all_to_all | solution.py:307
  196.8 1.2 broadcast_in_dim.24
  198.0 4.2 %all-to-all-start.3 = ((f32[4,64,1024]{2,1,0:T(8,128)}), f32[4,64,1024]{2,1,0:T(8,128)}, u32[]{:S(2)}, u32[]{:S(2)}) async-start(f32[4,64,1024]{2,1,0:T(8,128)} %broadcast_in_dim.24), calls=%async_computation.3 | async-start | bytes 2097152 | tf_op jit(solution)/shard_map/all_to_all | solution.py:24
  202.2 18.0 %all-gather = f32[4096]{0:T(1024)S(1)} all-gather(f32[1024]{0:T(1024)S(1)} %copy-done.9), channel_id=2, replica_groups=mesh['dp_0'=4,'dp_1'=8,'dp_2'=2,'mp'=4] {'mp'}, dimensions={0}, use_global_device_ids=true | all-gather | bytes 20480 | tf_op jit(solution)/shard_map/all_gather | solution.py:302
  220.3 18.9 %base_gap.1 = bf16[128,8,1024]{2,1,0:T(8,128)(2,1)S(1)} custom-call(s32[64]{0:T(128)S(1)} %copy-done.5, s32[128]{0:T(128)S(1)} %copy-done.6, bf16[4,512,1024]{2,1,0:T(8,128)(2,1)} %all-gather.3.cloned.1.call-done.gathered, bf16[64,8,1024]{2,1,0:T(8,128)(2,1)S(1)} %copy-done.2, f32[4,1024]{1,0:T(4,128)S(1)} %reshape.114.gain, bf16[4096,1024]{1,0:T(8,128)(2,1)} %frozen.1, ...), custom_call_target="tpu_custom_call" | custom-call | flops 4294967296 | bytes 18874368 | tf_op jit(solution)/shard_map/base_gap/pallas_call | solution.py:184
  239.1 1.3 copy-done.1
  240.5 7.2 %all-to-all-start = ((bf16[64,16,1024]{2,1,0:T(8,128)(2,1)}), bf16[64,16,1024]{2,1,0:T(8,128)(2,1)S(1)}, u32[]{:S(2)}, u32[]{:S(2)}) async-start(bf16[64,16,1024]{2,1,0:T(8,128)(2,1)} %bitcast.33), calls=%async_computation | async-start | bytes 4194304 | tf_op jit(solution)/shard_map/all_to_all | solution.py:318
  248.4 0.9 fusion.13
  250.0 0.8 slice_reduce_fusion
  250.9 0.5 fusion.2
  251.4 1.0 copy.25
  252.4 1.2 maximum_maximum_fusion.facts
  253.6 1.3 reduce_sum.74
  255.0 44.1 %all-to-all-done = bf16[64,16,1024]{2,1,0:T(8,128)(2,1)S(1)} async-done(((bf16[64,16,1024]{2,1,0:T(8,128)(2,1)}), bf16[64,16,1024]{2,1,0:T(8,128)(2,1)S(1)}, u32[]{:S(2)}, u32[]{:S(2)}) %all-to-all-start) | async-done | bytes 2097184 | tf_op jit(solution)/shard_map/all_to_all | solution.py:318
  299.0 3.2 trainer_step.1
  302.3 1.1 broadcast_in_dim.58
  303.4 3.5 all-to-all-start.5
  306.9 1.9 fusion.1
  308.8 78.6 %psum.7 = f32[16]{0:T(128)S(1)} all-reduce(f32[16]{0:T(128)S(1)} %slice_bitcast_fusion), channel_id=1, replica_groups=mesh['dp_0'=4,'dp_1'=8,'dp_2'=2,'mp'=4] {'dp_0','dp_1','dp_2','mp'}, use_global_device_ids=true, to_apply=%region_6.7 | all-reduce | flops 16 | bytes 128 | tf_op jit(solution)/shard_map/psum | solution.py:349
  387.5 1.2 fusion.12
  390.1 2.8 convolution_bitcast_fusion
  (50 shorter events, 1.4 us)
Async XLA Ops:
  7.2 181.2 %copy-start = (bf16[1,64,1024]{2,1,0:T(8,128)(2,1)S(1)}, bf16[1,64,1024]{2,1,0:T(8,128)(2,1)}, u32[]{:S(2)}) copy-start(bf16[1,64,1024]{2,1,0:T(8,128)(2,1)} %param.15) | copy-start | bytes 393220
  7.2 213.0 %all-gather.3.cloned.1.call-start = ((), (), s32[]{:S(2)}) async-start(), calls=%async_computation.6 | async-start | bytes 5242880 | tf_op jit(solution)/shard_map/all_gather | solution.py:303
  106.3 13.0 %copy-start.10 = (s32[64,4]{1,0:T(8,128)S(1)}, s32[64,4]{1,0:T(8,128)}, u32[]{:S(2)}) copy-start(s32[64,4]{1,0:T(8,128)} %get-tuple-element.15) | copy-start | bytes 3076
  106.3 13.1 %copy-start.11 = (s32[16]{0:T(128)S(1)}, s32[16]{0:T(128)}, u32[]{:S(2)}) copy-start(s32[16]{0:T(128)} %get-tuple-element.16) | copy-start | bytes 196
  106.3 64.3 %all-to-all-start.1 = ((bf16[64,16,1024]{2,1,0:T(8,128)(2,1)}), bf16[64,16,1024]{2,1,0:T(8,128)(2,1)S(1)}, u32[]{:S(2)}, u32[]{:S(2)}) async-start(bf16[64,16,1024]{2,1,0:T(8,128)(2,1)} %bitcast.37), calls=%async_computation.1 | async-start | bytes 4194304 | tf_op jit(solution)/shard_map/all_to_all | solution.py:299
  119.3 68.5 %copy-start.9 = (f32[1024]{0:T(1024)S(1)}, f32[1024]{0:T(1024)}, u32[]{:S(2)}) copy-start(f32[1024]{0:T(1024)} %param.14) | copy-start | bytes 12292
  170.5 17.8 %copy-start.7 = (bf16[64,16,1024]{2,1,0:T(8,128)(2,1)}, bf16[64,16,1024]{2,1,0:T(8,128)(2,1)S(1)}, u32[]{:S(2)}) copy-start(bf16[64,16,1024]{2,1,0:T(8,128)(2,1)S(1)} %all-to-all-done.1) | copy-start | bytes 6291460
  171.8 8.4 %all-to-all-start.2 = ((f32[4,1,1024]{2,1,0:T(1,128)}), f32[4,1,1024]{2,1,0:T(1,128)S(1)}, u32[]{:S(2)}, u32[]{:S(2)}) async-start(f32[4,1,1024]{2,1,0:T(1,128)} %broadcast_in_dim.23), calls=%async_computation.2 | async-start | bytes 32768 | tf_op jit(solution)/shard_map/all_to_all | solution.py:24
  180.2 16.6 %all-to-all-start.4 = ((s32[64,1,20]{2,1,0:T(1,128)}), s32[64,1,20]{2,1,0:T(1,128)}, u32[]{:S(2)}, u32[]{:S(2)}) async-start(s32[64,1,20]{2,1,0:T(1,128)} %bitcast.9), calls=%async_computation.4 | async-start | bytes 65536 | tf_op jit(solution)/shard_map/all_to_all | solution.py:307
  189.1 31.1 %copy-start.2 = (bf16[64,8,1024]{2,1,0:T(8,128)(2,1)S(1)}, bf16[64,8,1024]{2,1,0:T(8,128)(2,1)}, u32[]{:S(2)}) copy-start(bf16[64,8,1024]{2,1,0:T(8,128)(2,1)} %get-tuple-element.13.own) | copy-start | bytes 3145732
  189.1 31.1 %copy-start.3 = (bf16[128,8,1024]{2,1,0:T(8,128)(2,1)S(1)}, bf16[128,8,1024]{2,1,0:T(8,128)(2,1)}, u32[]{:S(2)}) copy-start(bf16[128,8,1024]{2,1,0:T(8,128)(2,1)} %targets.1) | copy-start | bytes 6291460
  189.1 31.1 %copy-start.5 = (s32[64]{0:T(128)S(1)}, s32[64]{0:T(128)}, u32[]{:S(2)}) copy-start(s32[64]{0:T(128)} %ids.3) | copy-start | bytes 772
  189.2 31.1 %copy-start.6 = (s32[128]{0:T(128)S(1)}, s32[128]{0:T(128)}, u32[]{:S(2)}) copy-start(s32[128]{0:T(128)} %get-tuple-element.12.slot_of) | copy-start | bytes 1540
  198.0 42.5 %all-to-all-start.3 = ((f32[4,64,1024]{2,1,0:T(8,128)}), f32[4,64,1024]{2,1,0:T(8,128)}, u32[]{:S(2)}, u32[]{:S(2)}) async-start(f32[4,64,1024]{2,1,0:T(8,128)} %broadcast_in_dim.24), calls=%async_computation.3 | async-start | bytes 2097152 | tf_op jit(solution)/shard_map/all_to_all | solution.py:24
  239.1 1.3 copy-start.1
  240.5 58.6 %all-to-all-start = ((bf16[64,16,1024]{2,1,0:T(8,128)(2,1)}), bf16[64,16,1024]{2,1,0:T(8,128)(2,1)S(1)}, u32[]{:S(2)}, u32[]{:S(2)}) async-start(bf16[64,16,1024]{2,1,0:T(8,128)(2,1)} %bitcast.33), calls=%async_computation | async-start | bytes 4194304 | tf_op jit(solution)/shard_map/all_to_all | solution.py:318
  250.8 48.2 %copy-start.4 = (bf16[1,64,1024]{2,1,0:T(8,128)(2,1)S(1)}, bf16[1,64,1024]{2,1,0:T(8,128)(2,1)}, u32[]{:S(2)}) copy-start(bf16[1,64,1024]{2,1,0:T(8,128)(2,1)} %param.16) | copy-start | bytes 393220
  302.3 4.7 %copy-start.8 = (bf16[64,16,1024]{2,1,0:T(8,128)(2,1)S(1)}, bf16[64,16,1024]{2,1,0:T(8,128)(2,1)}, u32[]{:S(2)}) copy-start(bf16[64,16,1024]{2,1,0:T(8,128)(2,1)} %copy-done.7) | copy-start | bytes 6291460
  303.4 86.6 %all-to-all-start.5 = ((f32[4,64,1024]{2,1,0:T(8,128)}), f32[4,64,1024]{2,1,0:T(8,128)S(1)}, u32[]{:S(2)}, u32[]{:S(2)}) async-start(f32[4,64,1024]{2,1,0:T(8,128)} %broadcast_in_dim.58), calls=%async_computation.5 | async-start | bytes 2097152 | tf_op jit(solution)/shard_map/all_to_all | solution.py:24
Sparse Core Ops, SparseCore 0:
  106.4 54.6 all-gather.2

commit v2 on v1

--- a/solution.py
+++ b/solution.py
@@ -28,7 +28,7 @@
 
 
 def route_kernel(
-    ids, dest, buckets, lengths, pool, send, own, info, counts, slot_of, arrived, source, sem
+    ids, dest, buckets, lengths, pool, gain, send, own, info, counts, slot_of, arrived
 ):
     sampled = ids.shape[0]
     slots = send.shape[0]
@@ -36,7 +36,6 @@
     def clear(k, carry):
         arrived[k] = 0
         for s in range(PER_PAIR):
-            source[k * PER_PAIR + s] = ids[0]
             info[k, s] = 0
             info[k, PER_PAIR + s] = 0
         return carry
@@ -51,12 +50,13 @@
     def place(j, carry):
         block = ids[j]
         trainer = dest[j]
-        pltpu.make_async_copy(pool.at[block], own.at[j], sem.at[0]).start()
+        values = pool[block]
+        own[j] = values
         order = arrived[trainer]
         arrived[trainer] = order + 1
         slot = trainer * PER_PAIR + order
+        send[slot] = values
         slot_of[j] = slot
-        source[slot] = block
         bucket = buckets[block]
         length = lengths[block]
         info[trainer, order] = bucket
@@ -66,71 +66,64 @@
 
     lax.fori_loop(0, sampled, place, 0)
 
-    def copy(s, carry):
-        pltpu.make_async_copy(pool.at[source[s]], send.at[s], sem.at[1]).start()
-        return carry
-
-    lax.fori_loop(0, slots, copy, 0)
-
     def list_free(k, found):
         for s in range(PER_PAIR):
             free = arrived[k] <= s
 
             @pl.when(free)
             def _():
-                slot_of[sampled + found] = k * PER_PAIR + s
+                slot = k * PER_PAIR + s
+                slot_of[sampled + found] = slot
+                send[slot] = jnp.zeros(send.shape[1:], send.dtype)
 
             found = found + jnp.where(free, 1, 0)
         return found
 
     lax.fori_loop(0, slots // PER_PAIR, list_free, 0)
-    pltpu.make_async_copy(pool.at[pl.ds(0, sampled)], own, sem.at[0]).wait()
-    pltpu.make_async_copy(send, send, sem.at[1]).wait()
-
-
-def route(ids, dest, buckets, lengths, pool, trainers):
+    whole = gain[...]
+    high = whole.astype(jnp.bfloat16).astype(jnp.float32)
+    middle = (whole - high).astype(jnp.bfloat16).astype(jnp.float32)
+    low = whole - high - middle
+    zeros = jnp.zeros((own.shape[1] - 3, whole.shape[1]), jnp.float32)
+    own[sampled] = jnp.concatenate([high, middle, low, zeros], axis=0).astype(jnp.bfloat16)
+    own[sampled + 1] = jnp.zeros(own.shape[1:], own.dtype)
+
+
+def route(ids, dest, buckets, lengths, pool, gain, trainers):
     sampled = ids.shape[0]
     slots = trainers * PER_PAIR
     block = pool.shape[1:]
     smem = pl.BlockSpec(memory_space=pltpu.SMEM)
-    hbm = pl.BlockSpec(memory_space=pl.ANY)
+    vmem = pl.BlockSpec(memory_space=pltpu.VMEM)
     return pl.pallas_call(
         route_kernel,
         out_shape=(
             jax.ShapeDtypeStruct((slots, *block), pool.dtype),
-            jax.ShapeDtypeStruct((sampled, *block), pool.dtype),
+            jax.ShapeDtypeStruct((sampled + 2, *block), pool.dtype),
             jax.ShapeDtypeStruct((trainers, 2 * PER_PAIR), jnp.int32),
             jax.ShapeDtypeStruct((NB,), jnp.int32),
             jax.ShapeDtypeStruct((slots,), jnp.int32),
         ),
-        in_specs=[smem, smem, smem, smem, hbm],
-        out_specs=(hbm, hbm, smem, smem, smem),
-        scratch_shapes=[
-            pltpu.SMEM((trainers,), jnp.int32),
-            pltpu.SMEM((slots,), jnp.int32),
-            pltpu.SemaphoreType.DMA((2,)),
-        ],
-        cost_estimate=pl.CostEstimate(flops=0, bytes_accessed=6 << 20, transcendentals=0),
+        in_specs=[smem, smem, smem, smem, vmem, vmem],
+        out_specs=(vmem, vmem, smem, smem, smem),
+        scratch_shapes=[pltpu.SMEM((trainers,), jnp.int32)],
+        compiler_params=pltpu.CompilerParams(vmem_limit_bytes=VMEM_BYTES),
+        cost_estimate=pl.CostEstimate(flops=0, bytes_accessed=5 << 20, transcendentals=0),
         name="route",
-    )(ids, dest, buckets, lengths, pool)
-
-
-def gap_kernel(
-    ids, slot_of, gathered, own, gain, frozen, targets, send, normed, target_rows, gap, sem
-):
+    )(ids, dest, buckets, lengths, pool, gain[None, :])
+
+
+def gap_kernel(ids, slot_of, gathered, own, frozen, targets, send, done, normed, gap):
     step = pl.program_id(0)
-    parts, rows, part = gathered.shape
+    parts, _, part = gathered.shape
     sampled, block_len, columns = gap.shape
+    rows = sampled * block_len
     width = frozen.shape[1]
     slots = send.shape[0]
 
     @pl.when(step == 0)
     def _():
-        def fetch(j, carry):
-            pltpu.make_async_copy(targets.at[ids[j]], target_rows.at[j], sem.at[0]).start()
-            return carry
-
-        lax.fori_loop(0, sampled, fetch, 0)
+        done[0] = 0
         chunk = 128
 
         def normalize(i, carry):
@@ -142,71 +135,69 @@
             inverse = lax.rsqrt(total / (parts * part) + RMS_EPSILON)
             for p in range(parts):
                 x = gathered[p, at, :].astype(jnp.float32)
-                normed[p, at, :] = (x * inverse * gain[p : p + 1, :]).astype(jnp.bfloat16)
+                pieces = gathered[p, rows : rows + 16, :].astype(jnp.float32)
+                gain = pieces[0:1] + pieces[1:2] + pieces[2:3]
+                normed[at, p * part : (p + 1) * part] = (x * inverse * gain).astype(jnp.bfloat16)
             return carry
 
         lax.fori_loop(0, rows // chunk, normalize, 0)
-        pltpu.make_async_copy(targets.at[pl.ds(0, sampled)], target_rows, sem.at[0]).wait()
-
-    def multiply(p, total):
-        weights = frozen[pl.ds(pl.multiple_of(p * part, part), part), :]
-        return total + jnp.dot(normed[p], weights, preferred_element_type=jnp.float32)
-
-    projected = lax.fori_loop(0, parts, multiply, jnp.zeros((rows, width), jnp.float32))
+
+    projected = jnp.dot(normed[...], frozen[...], preferred_element_type=jnp.float32)
+    projected = projected.reshape(sampled, block_len, width)
     at = pl.ds(pl.multiple_of(step * width, width), width)
-    x = own[:, :, at].astype(jnp.float32)
-    t = target_rows[:, :, at].astype(jnp.float32)
-    gap[:, :, at] = (x + projected.reshape(sampled, block_len, width) - t).astype(jnp.bfloat16)
+    gap[:, :, at] = own[:sampled, :, at].astype(jnp.float32) + projected
 
     @pl.when(step == pl.num_programs(0) - 1)
     def _():
         def place(j, carry):
-            pltpu.make_async_copy(gap.at[j], send.at[slot_of[j]], sem.at[1]).start()
+            target = targets[ids[j]].astype(jnp.float32)
+            send[slot_of[j]] = (gap[j] - target).astype(jnp.bfloat16)
             return carry
 
         lax.fori_loop(0, sampled, place, 0)
 
         def fill(s, carry):
-            pltpu.make_async_copy(gap.at[0], send.at[slot_of[sampled + s]], sem.at[1]).start()
+            send[slot_of[sampled + s]] = jnp.zeros((block_len, columns), jnp.bfloat16)
             return carry
 
         lax.fori_loop(0, slots - sampled, fill, 0)
-        pltpu.make_async_copy(send, send, sem.at[1]).wait()
-
-
-def base_gap_slots(ids, slot_of, gathered, own, gain, frozen, targets):
-    parts, rows, part = gathered.shape
+
+
+def base_gap_slots(ids, slot_of, gathered, own, frozen, targets):
+    parts, _, part = gathered.shape
     width, columns = frozen.shape
     slots = slot_of.shape[0]
+    sampled = ids.shape[0]
+    block_len = own.shape[1]
+    rows = sampled * block_len
     tile = 256
     smem = pl.BlockSpec(memory_space=pltpu.SMEM)
-    hbm = pl.BlockSpec(memory_space=pl.ANY)
     return pl.pallas_call(
         gap_kernel,
         grid=(columns // tile,),
-        out_shape=jax.ShapeDtypeStruct((slots, *own.shape[1:]), jnp.bfloat16),
+        out_shape=(
+            jax.ShapeDtypeStruct((slots, *own.shape[1:]), jnp.bfloat16),
+            jax.ShapeDtypeStruct((1,), jnp.int32),
+        ),
         in_specs=[
             smem,
             smem,
             pl.BlockSpec(gathered.shape, lambda n: (0, 0, 0)),
             pl.BlockSpec(own.shape, lambda n: (0, 0, 0)),
-            pl.BlockSpec(gain.shape, lambda n: (0, 0)),
             pl.BlockSpec((width, tile), lambda n: (0, n)),
-            hbm,
+            pl.BlockSpec(targets.shape, lambda n: (0, 0, 0)),
         ],
-        out_specs=hbm,
+        out_specs=(pl.BlockSpec((slots, *own.shape[1:]), lambda n: (0, 0, 0)), smem),
         scratch_shapes=[
-            pltpu.VMEM(gathered.shape, jnp.bfloat16),
-            pltpu.VMEM(own.shape, jnp.bfloat16),
-            pltpu.VMEM(own.shape, jnp.bfloat16),
-            pltpu.SemaphoreType.DMA((2,)),
+            pltpu.VMEM((rows, width), jnp.bfloat16),
+            pltpu.VMEM((sampled, block_len, columns), jnp.float32),
         ],
         compiler_params=pltpu.CompilerParams(vmem_limit_bytes=VMEM_BYTES),
         cost_estimate=pl.CostEstimate(
             flops=2 * rows * width * columns, bytes_accessed=18 << 20, transcendentals=rows
         ),
         name="base_gap",
-    )(ids, slot_of, gathered, own, gain, frozen, targets)
+    )(ids, slot_of, gathered, own, frozen, targets)
 
 
 def trainer_kernel(gap, lowered, up, facts, grad_up, back, loss):
@@ -294,27 +285,18 @@
     bucket_range = jnp.arange(NB, dtype=jnp.int32)
 
     send_x, own_x, info, counts, slot_of = route(
-        sample_ids, destinations[:, 0], buckets, lengths, pool_inputs, trainers
+        sample_ids, destinations[:, 0], buckets, lengths, pool_inputs, gain, trainers
     )
     got_x = lax.all_to_all(
         send_x.reshape(trainers, per_peer, part), DP, 0, 0, tiled=True
     )
-    whole_gain = lax.all_gather(gain, "mp")
-    gathered = lax.all_gather(own_x.reshape(sampled * block_len, part), "mp")
+    gathered = lax.all_gather(own_x.reshape(-1, part), "mp")
     message = jnp.concatenate(
         [info, jnp.broadcast_to(counts[None, :], (trainers, NB))], axis=1
     )
     got_info = lax.all_to_all(message[:, None, :], DP, 0, 0, tiled=True)[:, 0, :]
 
-    send_gap = base_gap_slots(
-        sample_ids,
-        slot_of,
-        gathered,
-        own_x,
-        whole_gain,
-        frozen,
-        pool_targets,
-    )
+    send_gap, done = base_gap_slots(sample_ids, slot_of, gathered, own_x, frozen, pool_targets)
     got_gap = lax.all_to_all(
         send_gap.reshape(trainers, per_peer, part), DP, 0, 0, tiled=True
     )
@@ -334,6 +316,7 @@
         [onehot, coefficient[:, None], jnp.zeros((rows, 128 - NB - 1), jnp.float32)], axis=1
     )
 
+    got_x, done = lax.optimization_barrier((got_x, done))
     values = got_x.reshape(rows, part).astype(jnp.float32)
     square_total = of_everyone(jnp.sum(values * values, axis=1), "mp")
     inverse_rms = lax.rsqrt(square_total / width + RMS_EPSILON)
@@ -346,7 +329,7 @@
     grad_up, back_part, loss_part = trainer_step(
         got_gap.reshape(rows, part), lowered, up_map, facts
     )
-    loss_sum = lax.psum(loss_part[0, :NB], DP_MP)
+    loss_sum = of_everyone(loss_part[:, :NB], DP_MP)[0]
     lowered_gradient = (ADAPTER_SCALING * of_everyone(back_part, "mp")).astype(jnp.bfloat16)
     grad_down = jnp.dot(lowered_gradient, normed, preferred_element_type=jnp.float32)
     bucket_loss = loss_sum / (floor_counts * width)

time: 402 us -> 239 us (0.59)
  Pallas kernels: 121 us -> 21 us
  blocking collectives: 96.6 us -> 19.6 us
  waiting for transfers between devices: 106 us -> 116 us
  local copies, waits for them, and re-layouts: 8.07 us -> 13 us
    pallas_call x1, Pallas kernels: 99 us -> 5.58 us  [route(): pl.pallas_call(route_kernel, out_shape=(jax.ShapeDtypeStruct((slots, *blo...]
    psum x1 -> x0, blocking collectives: 78.6 us -> none  [on_device(): loss_sum = lax.psum(loss_part[0, :NB], DP_MP)]
    all_to_all x0 -> x1, blocking collectives: none -> 19.6 us  [of_everyone(): lax.all_to_all(jnp.broadcast_to(value[None], (peers, *value.shape)), axis...]
    all_gather x1 -> x0, blocking collectives: 18 us -> none  [on_device(): whole_gain = lax.all_gather(gain, 'mp')]
    all_to_all x3, waiting for transfers between devices: 3.44 us -> 13.6 us  [of_everyone(): lax.all_to_all(jnp.broadcast_to(value[None], (peers, *value.shape)), axis...]
    pallas_call x1, Pallas kernels: 18.9 us -> 12.2 us  [base_gap_slots(): pl.pallas_call(gap_kernel, grid=(columns // tile,), out_shape=(jax.ShapeD...]
    unnamed x24 -> x26, local copies, waits for them, and re-layouts: 1.4 us -> 7.28 us
  transfers between devices with their start and end apart: 7 -> 7, of which waited for: 4 -> 6; matrix products, arithmetic and copies ran while one was open for 4% -> 7% of each run, Pallas kernels for 5% -> 5%
where the time goes in v2:
time: 239 us; the launch traced here: 238 us
  waiting for transfers between devices  116 us (49%)
  starting transfers between devices  37.3 us (16%)
  Pallas kernels  21 us (9%)
  blocking collectives  19.6 us (8%)
  between operations  17.4 us (7%)
  local copies, waits for them, and re-layouts  13 us (5%)
  other arithmetic  11.2 us (5%)
    all_to_all x1, waiting for transfers between devices, on_device(): lax.all_to_all(send_x.reshape(trainers, per_peer, part), DP, 0, 0, tiled=...  51 us
    all_to_all x1, waiting for transfers between devices, on_device(): lax.all_to_all(send_gap.reshape(trainers, per_peer, part), DP, 0, 0, tile...  45.6 us
    all_to_all x1, blocking collectives, of_everyone(): lax.all_to_all(jnp.broadcast_to(value[None], (peers, *value.shape)), axis...  19.6 us
    all_to_all x3, waiting for transfers between devices, of_everyone(): lax.all_to_all(jnp.broadcast_to(value[None], (peers, *value.shape)), axis...  13.6 us
    all_to_all x1, starting transfers between devices, on_device(): lax.all_to_all(send_x.reshape(trainers, per_peer, part), DP, 0, 0, tiled=...  13.2 us
    pallas_call x1, Pallas kernels, base_gap_slots(): pl.pallas_call(gap_kernel, grid=(columns // tile,), out_shape=(jax.ShapeD...  12.2 us
    all_to_all x3, starting transfers between devices, of_everyone(): lax.all_to_all(jnp.broadcast_to(value[None], (peers, *value.shape)), axis...  11.2 us
    unnamed x26, local copies, waits for them, and re-layouts  7.28 us
  transfers between devices with their start and end apart: 7, of which 6 were waited for; matrix products, arithmetic and copies ran while one was open for 7% of the time, Pallas kernels for 5%

profile of v2, /device:TPU:1, one launch (start us, length us, event | category | flops | bytes accessed | tf_op | source)
XLA Modules:
  0.0 237.8 jit_solution(14855213477100155058)
XLA Ops:
  7.2 1.6 copy-done.1
  8.9 0.7 copy-done.4
  12.2 5.6 %route.1 = (bf16[128,8,1024]{2,1,0:T(8,128)(2,1)}, bf16[66,8,1024]{2,1,0:T(8,128)(2,1)}, s32[64,4]{1,0:T(8,128)S(1)}, s32[16]{0:T(128)S(1)}, s32[128]{0:T(128)S(1)}) custom-call(s32[64]{0:T(128)S(1)} %copy-done.9, s32[64]{0:T(128)S(1)} %bitcast.37, s32[128]{0:T(128)S(1)} %copy-done.7, s32[128]{0:T(128)S(1)} %copy-done.8, ...), custom_call_target="tpu_custom_call" | custom-call | bytes 5242880 | tf_op jit(solution)/shard_map/route/pallas_call | solution.py:98
  17.8 13.2 %all-to-all-start.1 = ((bf16[64,16,1024]{2,1,0:T(8,128)(2,1)}), bf16[64,16,1024]{2,1,0:T(8,128)(2,1)}, u32[]{:S(2)}, u32[]{:S(2)}) async-start(bf16[64,16,1024]{2,1,0:T(8,128)(2,1)} %bitcast.5), calls=%async_computation.1 | async-start | bytes 4194304 | tf_op jit(solution)/shard_map/all_to_all | solution.py:290
  31.1 51.0 %all-to-all-done.1 = bf16[64,16,1024]{2,1,0:T(8,128)(2,1)} async-done(((bf16[64,16,1024]{2,1,0:T(8,128)(2,1)}), bf16[64,16,1024]{2,1,0:T(8,128)(2,1)}, u32[]{:S(2)}, u32[]{:S(2)}) %all-to-all-start.1) | async-done | bytes 2097184 | tf_op jit(solution)/shard_map/all_to_all | solution.py:290
  82.1 2.1 multiply_reduce_fusion
  84.9 4.2 %all-to-all-start.2 = ((f32[4,1,1024]{2,1,0:T(1,128)}), f32[4,1,1024]{2,1,0:T(1,128)S(1)}, u32[]{:S(2)}, u32[]{:S(2)}) async-start(f32[4,1,1024]{2,1,0:T(1,128)} %broadcast_in_dim.30), calls=%async_computation.2 | async-start | bytes 32768 | tf_op jit(solution)/shard_map/all_to_all | solution.py:24
  89.1 0.7 copy.24
  89.9 3.4 %all-to-all-done.2 = f32[4,1,1024]{2,1,0:T(1,128)S(1)} async-done(((f32[4,1,1024]{2,1,0:T(1,128)}), f32[4,1,1024]{2,1,0:T(1,128)S(1)}, u32[]{:S(2)}, u32[]{:S(2)}) %all-to-all-start.2) | async-done | bytes 16416 | tf_op jit(solution)/shard_map/all_to_all | solution.py:24
  93.3 7.2 %all-to-all-start.4 = ((s32[64,1,20]{2,1,0:T(1,128)}), s32[64,1,20]{2,1,0:T(1,128)S(1)}, u32[]{:S(2)}, u32[]{:S(2)}) async-start(s32[64,1,20]{2,1,0:T(1,128)} %bitcast.10), calls=%async_computation.4 | async-start | bytes 65536 | tf_op jit(solution)/shard_map/all_to_all | solution.py:297
  100.7 2.1 multiply_convert_fusion
  102.8 0.8 convolution_bitcast_fusion.1
  103.6 6.2 %all-to-all-done.4 = s32[64,1,20]{2,1,0:T(1,128)S(1)} async-done(((s32[64,1,20]{2,1,0:T(1,128)}), s32[64,1,20]{2,1,0:T(1,128)S(1)}, u32[]{:S(2)}, u32[]{:S(2)}) %all-to-all-start.4) | async-done | bytes 5152 | tf_op jit(solution)/shard_map/all_to_all | solution.py:297
  109.8 1.1 broadcast_in_dim.31
  110.9 3.5 %all-to-all-start.3 = ((f32[4,64,1024]{2,1,0:T(8,128)}), f32[4,64,1024]{2,1,0:T(8,128)S(1)}, u32[]{:S(2)}, u32[]{:S(2)}) async-start(f32[4,64,1024]{2,1,0:T(8,128)} %broadcast_in_dim.31), calls=%async_computation.3 | async-start | bytes 2097152 | tf_op jit(solution)/shard_map/all_to_all | solution.py:24
  114.5 12.2 %base_gap.1 = (bf16[128,8,1024]{2,1,0:T(8,128)(2,1)S(1)}, s32[1]{0:T(128)}) custom-call(s32[64]{0:T(128)S(1)} %copy-done.10, s32[128]{0:T(128)S(1)} %get-tuple-element.13.slot_of, bf16[4,528,1024]{2,1,0:T(8,128)(2,1)} %all-gather.2.cloned.1.call-done.gathered, bf16[66,8,1024]{2,1,0:T(8,128)(2,1)} %get-tuple-element.14.own, bf16[4096,1024]{1,0:T(8,128)(2,1)} %frozen.1, ...), custom_call_target="tpu_custom_call" | custom-call | flops 4294967296 | bytes 18874368 | tf_op jit(solution)/shard_map/base_gap/pallas_call | solution.py:175
  126.6 1.3 copy-done.2
  128.0 0.9 all-to-all-done.3
  128.9 1.0 copy-done.12
  129.9 5.7 %all-to-all-start = ((bf16[64,16,1024]{2,1,0:T(8,128)(2,1)}), bf16[64,16,1024]{2,1,0:T(8,128)(2,1)S(1)}, u32[]{:S(2)}, u32[]{:S(2)}) async-start(bf16[64,16,1024]{2,1,0:T(8,128)(2,1)} %bitcast.34), calls=%async_computation | async-start | bytes 4194304 | tf_op jit(solution)/shard_map/all_to_all | solution.py:300
  137.6 1.0 copy.25
  138.7 1.2 maximum_maximum_fusion.facts
  139.9 1.3 reduce_sum.83
  141.2 45.6 %all-to-all-done = bf16[64,16,1024]{2,1,0:T(8,128)(2,1)S(1)} async-done(((bf16[64,16,1024]{2,1,0:T(8,128)(2,1)}), bf16[64,16,1024]{2,1,0:T(8,128)(2,1)S(1)}, u32[]{:S(2)}, u32[]{:S(2)}) %all-to-all-start) | async-done | bytes 2097184 | tf_op jit(solution)/shard_map/all_to_all | solution.py:300
  186.9 3.3 %trainer_step.1 = (f32[64,1024]{1,0:T(8,128)}, f32[64,1024]{1,0:T(8,128)S(1)}, f32[1,128]{1,0:T(1,128)S(1)}) custom-call(bf16[1024,1024]{1,0:T(8,128)(2,1)S(1)} %bitcast.33, bf16[64,1024]{1,0:T(8,128)(2,1)S(1)} %multiply_convert_fusion.2.lowered, bf16[64,1024]{1,0:T(8,128)(2,1)S(1)} %bitcast.35, f32[1024,128]{1,0:T(8,128)S(1)} %maximum_maximum_fusion.facts), custom_call_target="tpu_custom_call" | custom-call | flops 402653184 | bytes 4194304 | tf_op jit(solution)/shard_map/trainer_step/pallas_call | solution.py:235
  190.3 19.6 %all_to_all.36 = f32[256,1,16]{2,1,0:T(1,128)S(1)} all-to-all(f32[256,1,16]{2,1,0:T(1,128)S(1)} %broadcast_in_dim.74), channel_id=1, replica_groups=mesh['dp_0'=4,'dp_1'=8,'dp_2'=2,'mp'=4] {'dp_0','dp_1','dp_2','mp'}, dimensions={0} | all-to-all | bytes 32768 | tf_op jit(solution)/shard_map/all_to_all | solution.py:24
  209.8 1.1 broadcast_in_dim.70
  210.9 3.5 %all-to-all-start.5 = ((f32[4,64,1024]{2,1,0:T(8,128)}), f32[4,64,1024]{2,1,0:T(8,128)S(1)}, u32[]{:S(2)}, u32[]{:S(2)}) async-start(f32[4,64,1024]{2,1,0:T(8,128)} %broadcast_in_dim.70), calls=%async_computation.5 | async-start | bytes 2097152 | tf_op jit(solution)/shard_map/all_to_all | solution.py:24
  214.5 2.1 fusion.1
  216.9 1.2 fusion.12
  219.4 9.2 %all-to-all-done.5 = f32[4,64,1024]{2,1,0:T(8,128)S(1)} async-done(((f32[4,64,1024]{2,1,0:T(8,128)}), f32[4,64,1024]{2,1,0:T(8,128)S(1)}, u32[]{:S(2)}, u32[]{:S(2)}) %all-to-all-start.5) | async-done | bytes 1048608 | tf_op jit(solution)/shard_map/all_to_all | solution.py:24
  228.7 1.2 convolution_bitcast_fusion
  (52 shorter events, 5.6 us)
Async XLA Ops:
  7.2 95.6 %copy-start = (bf16[1,64,1024]{2,1,0:T(8,128)(2,1)S(1)}, bf16[1,64,1024]{2,1,0:T(8,128)(2,1)}, u32[]{:S(2)}) copy-start(bf16[1,64,1024]{2,1,0:T(8,128)(2,1)} %param.15) | copy-start | bytes 393220
  7.2 107.2 %all-gather.2.cloned.1.call-start = ((), (), s32[]{:S(2)}) async-start(), calls=%async_computation.7 | async-start | bytes 5406720 | tf_op jit(solution)/shard_map/all_gather | solution.py:293
  7.2 1.6 copy-start.1
  8.8 0.7 copy-start.4
  9.5 0.7 copy-start.6
  10.2 0.7 copy-start.7
  10.8 0.7 copy-start.8
  11.5 0.7 copy-start.9
  17.8 64.4 %all-to-all-start.1 = ((bf16[64,16,1024]{2,1,0:T(8,128)(2,1)}), bf16[64,16,1024]{2,1,0:T(8,128)(2,1)}, u32[]{:S(2)}, u32[]{:S(2)}) async-start(bf16[64,16,1024]{2,1,0:T(8,128)(2,1)} %bitcast.5), calls=%async_computation.1 | async-start | bytes 4194304 | tf_op jit(solution)/shard_map/all_to_all | solution.py:290
  31.0 69.7 %copy-start.5 = (f32[1024]{0:T(1024)S(1)}, f32[1024]{0:T(1024)}, u32[]{:S(2)}) copy-start(f32[1024]{0:T(1024)} %param.14) | copy-start | bytes 12292
  84.9 8.4 %all-to-all-start.2 = ((f32[4,1,1024]{2,1,0:T(1,128)}), f32[4,1,1024]{2,1,0:T(1,128)S(1)}, u32[]{:S(2)}, u32[]{:S(2)}) async-start(f32[4,1,1024]{2,1,0:T(1,128)} %broadcast_in_dim.30), calls=%async_computation.2 | async-start | bytes 32768 | tf_op jit(solution)/shard_map/all_to_all | solution.py:24
  93.3 16.5 %all-to-all-start.4 = ((s32[64,1,20]{2,1,0:T(1,128)}), s32[64,1,20]{2,1,0:T(1,128)S(1)}, u32[]{:S(2)}, u32[]{:S(2)}) async-start(s32[64,1,20]{2,1,0:T(1,128)} %bitcast.10), calls=%async_computation.4 | async-start | bytes 65536 | tf_op jit(solution)/shard_map/all_to_all | solution.py:297
  103.6 10.9 %copy-start.10 = (s32[64]{0:T(128)S(1)}, s32[64]{0:T(128)}, u32[]{:S(2)}) copy-start(s32[64]{0:T(128)} %ids.3) | copy-start | bytes 772
  103.6 10.9 %copy-start.11 = (bf16[128,8,1024]{2,1,0:T(8,128)(2,1)S(1)}, bf16[128,8,1024]{2,1,0:T(8,128)(2,1)}, u32[]{:S(2)}) copy-start(bf16[128,8,1024]{2,1,0:T(8,128)(2,1)} %targets.1) | copy-start | bytes 6291460
  110.9 18.0 %all-to-all-start.3 = ((f32[4,64,1024]{2,1,0:T(8,128)}), f32[4,64,1024]{2,1,0:T(8,128)S(1)}, u32[]{:S(2)}, u32[]{:S(2)}) async-start(f32[4,64,1024]{2,1,0:T(8,128)} %broadcast_in_dim.31), calls=%async_computation.3 | async-start | bytes 2097152 | tf_op jit(solution)/shard_map/all_to_all | solution.py:24
  126.6 1.3 copy-start.2
  128.9 1.0 copy-start.12
  129.9 57.0 %all-to-all-start = ((bf16[64,16,1024]{2,1,0:T(8,128)(2,1)}), bf16[64,16,1024]{2,1,0:T(8,128)(2,1)S(1)}, u32[]{:S(2)}, u32[]{:S(2)}) async-start(bf16[64,16,1024]{2,1,0:T(8,128)(2,1)} %bitcast.34), calls=%async_computation | async-start | bytes 4194304 | tf_op jit(solution)/shard_map/all_to_all | solution.py:300
  137.1 49.8 %copy-start.3 = (bf16[1,64,1024]{2,1,0:T(8,128)(2,1)S(1)}, bf16[1,64,1024]{2,1,0:T(8,128)(2,1)}, u32[]{:S(2)}) copy-start(bf16[1,64,1024]{2,1,0:T(8,128)(2,1)} %param.16) | copy-start | bytes 393220
  210.9 17.7 %all-to-all-start.5 = ((f32[4,64,1024]{2,1,0:T(8,128)}), f32[4,64,1024]{2,1,0:T(8,128)S(1)}, u32[]{:S(2)}, u32[]{:S(2)}) async-start(f32[4,64,1024]{2,1,0:T(8,128)} %broadcast_in_dim.70), calls=%async_computation.5 | async-start | bytes 2097152 | tf_op jit(solution)/shard_map/all_to_all | solution.py:24
Sparse Core Ops, SparseCore 0:
  17.9 55.7 all-gather.1

commit v3 on v2

--- a/solution.py
+++ b/solution.py
@@ -28,8 +28,24 @@
 
 
 def route_kernel(
-    ids, dest, buckets, lengths, pool, gain, send, own, info, counts, slot_of, arrived
+    ids_in, dest_in, buckets_in, lengths_in, pool_in, gain_in,
+    send_out, own_out, info, counts, slot_of,
+    ids, dest, buckets, lengths, pool, gain, send, own, arrived, sem,
 ):
+    pairs = (
+        (pool_in, pool),
+        (ids_in, ids),
+        (dest_in, dest),
+        (buckets_in, buckets),
+        (lengths_in, lengths),
+        (gain_in, gain),
+    )
+    copies = [
+        pltpu.make_async_copy(source, target, sem.at[i])
+        for i, (source, target) in enumerate(pairs)
+    ]
+    for copy in copies:
+        copy.start()
     sampled = ids.shape[0]
     slots = send.shape[0]
 
@@ -46,6 +62,8 @@
 
     lax.fori_loop(0, slots // PER_PAIR, clear, 0)
     lax.fori_loop(0, NB, clear_counts, 0)
+    for copy in copies:
+        copy.wait()
 
     def place(j, carry):
         block = ids[j]
@@ -80,6 +98,8 @@
         return found
 
     lax.fori_loop(0, slots // PER_PAIR, list_free, 0)
+    send_copy = pltpu.make_async_copy(send, send_out, sem.at[0])
+    send_copy.start()
     whole = gain[...]
     high = whole.astype(jnp.bfloat16).astype(jnp.float32)
     middle = (whole - high).astype(jnp.bfloat16).astype(jnp.float32)
@@ -87,6 +107,10 @@
     zeros = jnp.zeros((own.shape[1] - 3, whole.shape[1]), jnp.float32)
     own[sampled] = jnp.concatenate([high, middle, low, zeros], axis=0).astype(jnp.bfloat16)
     own[sampled + 1] = jnp.zeros(own.shape[1:], own.dtype)
+    own_copy = pltpu.make_async_copy(own, own_out, sem.at[1])
+    own_copy.start()
+    own_copy.wait()
+    send_copy.wait()
 
 
 def route(ids, dest, buckets, lengths, pool, gain, trainers):
@@ -94,7 +118,7 @@
     slots = trainers * PER_PAIR
     block = pool.shape[1:]
     smem = pl.BlockSpec(memory_space=pltpu.SMEM)
-    vmem = pl.BlockSpec(memory_space=pltpu.VMEM)
+    hbm = pl.BlockSpec(memory_space=pltpu.HBM)
     return pl.pallas_call(
         route_kernel,
         out_shape=(
@@ -104,16 +128,27 @@
             jax.ShapeDtypeStruct((NB,), jnp.int32),
             jax.ShapeDtypeStruct((slots,), jnp.int32),
         ),
-        in_specs=[smem, smem, smem, smem, vmem, vmem],
-        out_specs=(vmem, vmem, smem, smem, smem),
-        scratch_shapes=[pltpu.SMEM((trainers,), jnp.int32)],
+        in_specs=[hbm] * 6,
+        out_specs=(hbm, hbm, smem, smem, smem),
+        scratch_shapes=[
+            pltpu.SMEM(ids.shape, jnp.int32),
+            pltpu.SMEM(dest.shape, jnp.int32),
+            pltpu.SMEM(buckets.shape, jnp.int32),
+            pltpu.SMEM(lengths.shape, jnp.int32),
+            pltpu.VMEM(pool.shape, pool.dtype),
+            pltpu.VMEM((1, gain.shape[0]), jnp.float32),
+            pltpu.VMEM((slots, *block), pool.dtype),
+            pltpu.VMEM((sampled + 2, *block), pool.dtype),
+            pltpu.SMEM((trainers,), jnp.int32),
+            pltpu.SemaphoreType.DMA((6,)),
+        ],
         compiler_params=pltpu.CompilerParams(vmem_limit_bytes=VMEM_BYTES),
         cost_estimate=pl.CostEstimate(flops=0, bytes_accessed=5 << 20, transcendentals=0),
         name="route",
     )(ids, dest, buckets, lengths, pool, gain[None, :])
 
 
-def gap_kernel(ids, slot_of, gathered, own, frozen, targets, send, done, normed, gap):
+def gap_kernel(ids, slot_of, gathered, own, frozen, targets, send_out, done, send, normed, gap, sem):
     step = pl.program_id(0)
     parts, _, part = gathered.shape
     sampled, block_len, columns = gap.shape
@@ -123,7 +158,7 @@
 
     @pl.when(step == 0)
     def _():
-        done[0] = 0
+        done[0] = 0.0
         chunk = 128
 
         def normalize(i, carry):
@@ -161,6 +196,9 @@
             return carry
 
         lax.fori_loop(0, slots - sampled, fill, 0)
+        copy = pltpu.make_async_copy(send, send_out, sem.at[0])
+        copy.start()
+        copy.wait()
 
 
 def base_gap_slots(ids, slot_of, gathered, own, frozen, targets):
@@ -177,7 +215,7 @@
         grid=(columns // tile,),
         out_shape=(
             jax.ShapeDtypeStruct((slots, *own.shape[1:]), jnp.bfloat16),
-            jax.ShapeDtypeStruct((1,), jnp.int32),
+            jax.ShapeDtypeStruct((1,), jnp.float32),
         ),
         in_specs=[
             smem,
@@ -187,10 +225,12 @@
             pl.BlockSpec((width, tile), lambda n: (0, n)),
             pl.BlockSpec(targets.shape, lambda n: (0, 0, 0)),
         ],
-        out_specs=(pl.BlockSpec((slots, *own.shape[1:]), lambda n: (0, 0, 0)), smem),
+        out_specs=(pl.BlockSpec(memory_space=pltpu.HBM), smem),
         scratch_shapes=[
+            pltpu.VMEM((slots, *own.shape[1:]), jnp.bfloat16),
             pltpu.VMEM((rows, width), jnp.bfloat16),
             pltpu.VMEM((sampled, block_len, columns), jnp.float32),
+            pltpu.SemaphoreType.DMA((1,)),
         ],
         compiler_params=pltpu.CompilerParams(vmem_limit_bytes=VMEM_BYTES),
         cost_estimate=pl.CostEstimate(
@@ -200,8 +240,9 @@
     )(ids, slot_of, gathered, own, frozen, targets)
 
 
-def trainer_kernel(gap, lowered, up, facts, grad_up, back, loss):
+def trainer_kernel(gap, lowered, up, facts, grad_up, back_out, loss_out, back, loss, sem):
     step = pl.program_id(0)
+    chunk = gap.shape[0]
     low = lowered[...]
     up_map = up[...]
     facts_now = facts[...]
@@ -211,34 +252,49 @@
     output_grad = (facts_now[:, NB : NB + 1] * distance).astype(jnp.bfloat16)
     squares = jnp.sum(distance * distance, axis=1, keepdims=True)
     part = jnp.sum(facts_now * squares, axis=0, keepdims=True)
-    back[...] = lax.dot_general(
+    back_now = lax.dot_general(
         up_map, output_grad, CONTRACT_LAST, preferred_element_type=jnp.float32
     )
+    at = pl.ds(pl.multiple_of(step * chunk, chunk), chunk)
+    for p in range(back.shape[0]):
+        back[p, :, at] = back_now
     own = jnp.dot(low, output_grad, preferred_element_type=jnp.float32)
 
     @pl.when(step == 0)
     def _():
         grad_up[...] = own
-        loss[...] = part
+        loss[...] = jnp.broadcast_to(part[None], loss.shape)
 
     @pl.when(step > 0)
     def _():
         grad_up[...] += own
-        loss[...] += part
-
-
-def trainer_step(gap, lowered, up, facts):
+        loss[...] += part[None]
+
+    @pl.when(step == pl.num_programs(0) - 1)
+    def _():
+        copies = (
+            pltpu.make_async_copy(loss, loss_out, sem.at[0]),
+            pltpu.make_async_copy(back, back_out, sem.at[1]),
+        )
+        for copy in copies:
+            copy.start()
+        for copy in copies:
+            copy.wait()
+
+
+def trainer_step(gap, lowered, up, facts, trainers, parts):
     rows, columns = gap.shape
     rank = up.shape[0]
     lanes = facts.shape[1]
     chunk = 256
+    hbm = pl.BlockSpec(memory_space=pltpu.HBM)
     return pl.pallas_call(
         trainer_kernel,
         grid=(rows // chunk,),
         out_shape=(
             jax.ShapeDtypeStruct((rank, columns), jnp.float32),
-            jax.ShapeDtypeStruct((rank, rows), jnp.float32),
-            jax.ShapeDtypeStruct((1, lanes), jnp.float32),
+            jax.ShapeDtypeStruct((parts, rank, rows), jnp.float32),
+            jax.ShapeDtypeStruct((trainers, 1, lanes), jnp.float32),
         ),
         in_specs=[
             pl.BlockSpec((chunk, columns), lambda i: (i, 0)),
@@ -246,11 +302,12 @@
             pl.BlockSpec((rank, columns), lambda i: (0, 0)),
             pl.BlockSpec((chunk, lanes), lambda i: (i, 0)),
         ],
-        out_specs=(
-            pl.BlockSpec((rank, columns), lambda i: (0, 0)),
-            pl.BlockSpec((rank, chunk), lambda i: (0, i)),
-            pl.BlockSpec((1, lanes), lambda i: (0, 0)),
-        ),
+        out_specs=(pl.BlockSpec((rank, columns), lambda i: (0, 0)), hbm, hbm),
+        scratch_shapes=[
+            pltpu.VMEM((parts, rank, rows), jnp.float32),
+            pltpu.VMEM((trainers, 1, lanes), jnp.float32),
+            pltpu.SemaphoreType.DMA((2,)),
+        ],
         compiler_params=pltpu.CompilerParams(vmem_limit_bytes=VMEM_BYTES),
         cost_estimate=pl.CostEstimate(
             flops=6 * rows * rank * columns, bytes_accessed=4 << 20, transcendentals=0
@@ -316,9 +373,8 @@
         [onehot, coefficient[:, None], jnp.zeros((rows, 128 - NB - 1), jnp.float32)], axis=1
     )
 
-    got_x, done = lax.optimization_barrier((got_x, done))
     values = got_x.reshape(rows, part).astype(jnp.float32)
-    square_total = of_everyone(jnp.sum(values * values, axis=1), "mp")
+    square_total = of_everyone(jnp.sum(values * values, axis=1) + done, "mp")
     inverse_rms = lax.rsqrt(square_total / width + RMS_EPSILON)
     normed = (values * inverse_rms[:, None] * gain[None, :]).astype(jnp.bfloat16)
     latent_part = lax.dot_general(
@@ -327,10 +383,12 @@
     lowered = (ADAPTER_SCALING * of_everyone(latent_part, "mp")).astype(jnp.bfloat16)
 
     grad_up, back_part, loss_part = trainer_step(
-        got_gap.reshape(rows, part), lowered, up_map, facts
-    )
-    loss_sum = of_everyone(loss_part[:, :NB], DP_MP)[0]
-    lowered_gradient = (ADAPTER_SCALING * of_everyone(back_part, "mp")).astype(jnp.bfloat16)
+        got_gap.reshape(rows, part), lowered, up_map, facts, trainers, parts
+    )
+    loss_over_dp = jnp.sum(lax.all_to_all(loss_part, DP, 0, 0, tiled=True), axis=0)
+    back = jnp.sum(lax.all_to_all(back_part, "mp", 0, 0, tiled=True), axis=0)
+    loss_sum = of_everyone(loss_over_dp, "mp")[0, :NB]
+    lowered_gradient = (ADAPTER_SCALING * back).astype(jnp.bfloat16)
     grad_down = jnp.dot(lowered_gradient, normed, preferred_element_type=jnp.float32)
     bucket_loss = loss_sum / (floor_counts * width)
     progress = jnp.sum(weights * bucket_loss) / jnp.sum(bucket_loss)

time: 239 us -> 253 us (1.059)
  blocking collectives: 19.6 us -> 38.7 us
  starting transfers between devices: 37.3 us -> 34.1 us
    all_to_all x0 -> x1, blocking collectives: none -> 14.9 us  [on_device(): lax.all_to_all(loss_part, DP, 0, 0, tiled=True)]
    all_to_all x3 -> x1, waiting for transfers between devices: 13.6 us -> 3.43 us  [of_everyone(): lax.all_to_all(jnp.broadcast_to(value[None], (peers, *value.shape)), axis...]
    all_to_all x0 -> x1, waiting for transfers between devices: none -> 8.59 us  [on_device(): back = jnp.sum(lax.all_to_all(back_part, 'mp', 0, 0, tiled=True), axis=0)]
    all_to_all x3 -> x1, starting transfers between devices: 11.2 us -> 4.18 us  [of_everyone(): lax.all_to_all(jnp.broadcast_to(value[None], (peers, *value.shape)), axis...]
    all_to_all x1 -> x2, blocking collectives: 19.6 us -> 23.8 us  [of_everyone(): lax.all_to_all(jnp.broadcast_to(value[None], (peers, *value.shape)), axis...]
    all_to_all x0 -> x1, starting transfers between devices: none -> 3.52 us  [on_device(): back = jnp.sum(lax.all_to_all(back_part, 'mp', 0, 0, tiled=True), axis=0)]
  transfers between devices with their start and end apart: 7 -> 6, of which waited for: 6 -> 5; matrix products, arithmetic and copies ran while one was open for 7% -> 6% of each run, Pallas kernels for 5% -> 0%
where the time goes in v3:
time: 253 us; the launch traced here: 252 us
  waiting for transfers between devices  115 us (45%)
  blocking collectives  38.7 us (15%)
  starting transfers between devices  34.1 us (13%)
  Pallas kernels  22.1 us (9%)
  between operations  17.4 us (7%)
  other arithmetic  11.6 us (5%)
  local copies, waits for them, and re-layouts  10.8 us (4%)
    all_to_all x1, waiting for transfers between devices, on_device(): lax.all_to_all(send_x.reshape(trainers, per_peer, part), DP, 0, 0, tiled=...  51 us
    all_to_all x1, waiting for transfers between devices, on_device(): lax.all_to_all(send_gap.reshape(trainers, per_peer, part), DP, 0, 0, tile...  45.6 us
    all_to_all x2, blocking collectives, of_everyone(): lax.all_to_all(jnp.broadcast_to(value[None], (peers, *value.shape)), axis...  23.8 us
    all_to_all x1, blocking collectives, on_device(): lax.all_to_all(loss_part, DP, 0, 0, tiled=True)  14.9 us
    all_to_all x1, starting transfers between devices, on_device(): lax.all_to_all(send_x.reshape(trainers, per_peer, part), DP, 0, 0, tiled=...  13.2 us
    pallas_call x1, Pallas kernels, base_gap_slots(): pl.pallas_call(gap_kernel, grid=(columns // tile,), out_shape=(jax.ShapeD...  12.4 us
    all_to_all x1, waiting for transfers between devices, on_device(): back = jnp.sum(lax.all_to_all(back_part, 'mp', 0, 0, tiled=True), axis=0)  8.59 us
    unnamed x26, local copies, waits for them, and re-layouts  7.25 us
  transfers between devices with their start and end apart: 6, of which 5 were waited for; matrix products, arithmetic and copies ran while one was open for 6% of the time, Pallas kernels for 0%

profile of v3, /device:TPU:1, one launch (start us, length us, event | category | flops | bytes accessed | tf_op | source)
XLA Modules:
  0.0 251.6 jit_solution(6474488188336494702)
XLA Ops:
  7.2 1.6 copy-done.1
  8.9 0.7 copy-done.5
  9.5 0.7 copy-done.7
  10.2 0.7 copy-done.8
  12.2 6.2 %route.1 = (bf16[128,8,1024]{2,1,0:T(8,128)(2,1)}, bf16[66,8,1024]{2,1,0:T(8,128)(2,1)}, s32[64,4]{1,0:T(8,128)S(1)}, s32[16]{0:T(128)S(1)}, s32[128]{0:T(128)S(1)}) custom-call(s32[64]{0:T(128)S(1)} %copy-done.10, s32[64]{0:T(128)S(1)} %bitcast.41, s32[128]{0:T(128)S(1)} %copy-done.8, s32[128]{0:T(128)S(1)} %copy-done.9, ...), custom_call_target="tpu_custom_call" | custom-call | bytes 5242880 | tf_op jit(solution)/shard_map/route/pallas_call | solution.py:122
  18.4 13.2 %all-to-all-start.1 = ((bf16[64,16,1024]{2,1,0:T(8,128)(2,1)}), bf16[64,16,1024]{2,1,0:T(8,128)(2,1)}, u32[]{:S(2)}, u32[]{:S(2)}) async-start(bf16[64,16,1024]{2,1,0:T(8,128)(2,1)} %bitcast.5), calls=%async_computation.1 | async-start | bytes 4194304 | tf_op jit(solution)/shard_map/all_to_all | solution.py:347
  31.8 51.0 %all-to-all-done.1 = bf16[64,16,1024]{2,1,0:T(8,128)(2,1)} async-done(((bf16[64,16,1024]{2,1,0:T(8,128)(2,1)}), bf16[64,16,1024]{2,1,0:T(8,128)(2,1)}, u32[]{:S(2)}, u32[]{:S(2)}) %all-to-all-start.1) | async-done | bytes 2097184 | tf_op jit(solution)/shard_map/all_to_all | solution.py:347
  82.8 2.1 multiply_reduce_fusion
  84.9 12.4 %base_gap.1 = (bf16[128,8,1024]{2,1,0:T(8,128)(2,1)S(1)}, f32[1]{0:T(128)}) custom-call(s32[64]{0:T(128)S(1)} %copy-done.11, s32[128]{0:T(128)S(1)} %get-tuple-element.14.slot_of, bf16[4,528,1024]{2,1,0:T(8,128)(2,1)} %all-gather.2.cloned.1.call-done.gathered, bf16[66,8,1024]{2,1,0:T(8,128)(2,1)} %get-tuple-element.15.own, bf16[4096,1024]{1,0:T(8,128)(2,1)} %frozen.1, ...), custom_call_target="tpu_custom_call" | custom-call | flops 4294967296 | bytes 18874368 | tf_op jit(solution)/shard_map/base_gap/pallas_call | solution.py:213
  97.3 1.3 copy-done.2
  100.0 4.2 %all-to-all-start.2 = ((f32[4,1,1024]{2,1,0:T(1,128)}), f32[4,1,1024]{2,1,0:T(1,128)S(1)}, u32[]{:S(2)}, u32[]{:S(2)}) async-start(f32[4,1,1024]{2,1,0:T(1,128)} %broadcast_in_dim.23), calls=%async_computation.2 | async-start | bytes 32768 | tf_op jit(solution)/shard_map/all_to_all | solution.py:24
  104.3 0.7 copy.24
  105.0 3.4 %all-to-all-done.2 = f32[4,1,1024]{2,1,0:T(1,128)S(1)} async-done(((f32[4,1,1024]{2,1,0:T(1,128)}), f32[4,1,1024]{2,1,0:T(1,128)S(1)}, u32[]{:S(2)}, u32[]{:S(2)}) %all-to-all-start.2) | async-done | bytes 16416 | tf_op jit(solution)/shard_map/all_to_all | solution.py:24
  108.4 7.2 %all-to-all-start.4 = ((s32[64,1,20]{2,1,0:T(1,128)}), s32[64,1,20]{2,1,0:T(1,128)S(1)}, u32[]{:S(2)}, u32[]{:S(2)}) async-start(s32[64,1,20]{2,1,0:T(1,128)} %bitcast.11), calls=%async_computation.4 | async-start | bytes 65536 | tf_op jit(solution)/shard_map/all_to_all | solution.py:354
  115.8 2.1 multiply_convert_fusion
  117.9 0.8 convolution_bitcast_fusion.1
  118.7 6.2 %all-to-all-done.4 = s32[64,1,20]{2,1,0:T(1,128)S(1)} async-done(((s32[64,1,20]{2,1,0:T(1,128)}), s32[64,1,20]{2,1,0:T(1,128)S(1)}, u32[]{:S(2)}, u32[]{:S(2)}) %all-to-all-start.4) | async-done | bytes 5152 | tf_op jit(solution)/shard_map/all_to_all | solution.py:354
  125.0 17.4 %all_to_all.41 = f32[4,64,1024]{2,1,0:T(8,128)} all-to-all(f32[4,64,1024]{2,1,0:T(8,128)S(1)} %broadcast_in_dim.24), channel_id=1, replica_groups=mesh['dp_0'=4,'dp_1'=8,'dp_2'=2,'mp'=4] {'mp'}, dimensions={0} | all-to-all | bytes 2097152 | tf_op jit(solution)/shard_map/all_to_all | solution.py:24
  142.4 6.0 %all-to-all-start = ((bf16[64,16,1024]{2,1,0:T(8,128)(2,1)}), bf16[64,16,1024]{2,1,0:T(8,128)(2,1)S(1)}, u32[]{:S(2)}, u32[]{:S(2)}) async-start(bf16[64,16,1024]{2,1,0:T(8,128)(2,1)} %bitcast.38), calls=%async_computation | async-start | bytes 4194304 | tf_op jit(solution)/shard_map/all_to_all | solution.py:357
  150.4 1.0 copy.25
  151.5 1.2 maximum_maximum_fusion.facts
  152.7 1.3 reduce_sum.94
  154.1 45.6 %all-to-all-done = bf16[64,16,1024]{2,1,0:T(8,128)(2,1)S(1)} async-done(((bf16[64,16,1024]{2,1,0:T(8,128)(2,1)}), bf16[64,16,1024]{2,1,0:T(8,128)(2,1)S(1)}, u32[]{:S(2)}, u32[]{:S(2)}) %all-to-all-start) | async-done | bytes 2097184 | tf_op jit(solution)/shard_map/all_to_all | solution.py:357
  199.7 3.5 %trainer_step.1 = (f32[64,1024]{1,0:T(8,128)}, f32[4,64,1024]{2,1,0:T(8,128)S(1)}, f32[64,1,128]{2,1,0:T(1,128)S(1)}) custom-call(bf16[1024,1024]{1,0:T(8,128)(2,1)S(1)} %bitcast.37, bf16[64,1024]{1,0:T(8,128)(2,1)S(1)} %multiply_convert_fusion.2.lowered, bf16[64,1024]{1,0:T(8,128)(2,1)S(1)} %bitcast.39, f32[1024,128]{1,0:T(8,128)S(1)} %maximum_maximum_fusion.facts), custom_call_target="tpu_custom_call" | custom-call | flops 402653184 | bytes 4194304 | tf_op jit(solution)/shard_map/trainer_step/pallas_call | solution.py:291
  203.2 1.0 copy-done.3
  204.2 14.9 %all_to_all.42 = f32[64,1,128]{2,1,0:T(1,128)S(1)} all-to-all(f32[64,1,128]{2,1,0:T(1,128)S(1)} %get-tuple-element.23), channel_id=1, replica_groups=mesh['dp_0'=4,'dp_1'=8,'dp_2'=2,'mp'=4] {'dp_0','dp_1','dp_2'}, dimensions={0} | all-to-all | bytes 65536 | tf_op jit(solution)/shard_map/all_to_all | solution.py:388
  219.2 6.4 %all_to_all.43 = f32[4,1,128]{2,1,0:T(1,128)S(1)} all-to-all(f32[4,1,128]{2,1,0:T(1,128)S(1)} %broadcast_in_dim.61), channel_id=1, replica_groups=mesh['dp_0'=4,'dp_1'=8,'dp_2'=2,'mp'=4] {'mp'}, dimensions={0} | all-to-all | bytes 4096 | tf_op jit(solution)/shard_map/all_to_all | solution.py:24
  225.6 3.5 %all-to-all-start.5 = ((f32[4,64,1024]{2,1,0:T(8,128)}), f32[4,64,1024]{2,1,0:T(8,128)S(1)}, u32[]{:S(2)}, u32[]{:S(2)}) async-start(f32[4,64,1024]{2,1,0:T(8,128)} %copy-done.3), calls=%async_computation.5 | async-start | bytes 2097152 | tf_op jit(solution)/shard_map/all_to_all | solution.py:389
  229.1 2.1 fusion.1
  231.3 1.2 fusion.12
  233.8 8.6 %all-to-all-done.5 = f32[4,64,1024]{2,1,0:T(8,128)S(1)} async-done(((f32[4,64,1024]{2,1,0:T(8,128)}), f32[4,64,1024]{2,1,0:T(8,128)S(1)}, u32[]{:S(2)}, u32[]{:S(2)}) %all-to-all-start.5) | async-done | bytes 1048608 | tf_op jit(solution)/shard_map/all_to_all | solution.py:389
  242.5 1.2 convolution_bitcast_fusion
  (52 shorter events, 4.8 us)
Async XLA Ops:
  7.2 110.8 %copy-start = (bf16[1,64,1024]{2,1,0:T(8,128)(2,1)S(1)}, bf16[1,64,1024]{2,1,0:T(8,128)(2,1)}, u32[]{:S(2)}) copy-start(bf16[1,64,1024]{2,1,0:T(8,128)(2,1)} %param.15) | copy-start | bytes 393220
  7.2 77.7 %all-gather.2.cloned.1.call-start = ((), (), s32[]{:S(2)}) async-start(), calls=%async_computation.8 | async-start | bytes 5406720 | tf_op jit(solution)/shard_map/all_gather | solution.py:350
  7.2 1.6 copy-start.1
  8.8 0.7 copy-start.5
  9.5 0.7 copy-start.7
  10.2 0.7 copy-start.8
  10.8 0.7 copy-start.9
  11.5 0.7 copy-start.10
  18.4 64.4 %all-to-all-start.1 = ((bf16[64,16,1024]{2,1,0:T(8,128)(2,1)}), bf16[64,16,1024]{2,1,0:T(8,128)(2,1)}, u32[]{:S(2)}, u32[]{:S(2)}) async-start(bf16[64,16,1024]{2,1,0:T(8,128)(2,1)} %bitcast.5), calls=%async_computation.1 | async-start | bytes 4194304 | tf_op jit(solution)/shard_map/all_to_all | solution.py:347
  31.6 53.3 %copy-start.11 = (s32[64]{0:T(128)S(1)}, s32[64]{0:T(128)}, u32[]{:S(2)}) copy-start(s32[64]{0:T(128)} %ids.1) | copy-start | bytes 772
  31.6 53.3 %copy-start.12 = (bf16[128,8,1024]{2,1,0:T(8,128)(2,1)S(1)}, bf16[128,8,1024]{2,1,0:T(8,128)(2,1)}, u32[]{:S(2)}) copy-start(bf16[128,8,1024]{2,1,0:T(8,128)(2,1)} %targets.1) | copy-start | bytes 6291460
  84.9 30.9 %copy-start.6 = (f32[1024]{0:T(1024)S(1)}, f32[1024]{0:T(1024)}, u32[]{:S(2)}) copy-start(f32[1024]{0:T(1024)} %param.14) | copy-start | bytes 12292
  97.3 1.3 copy-start.2
  100.0 8.4 %all-to-all-start.2 = ((f32[4,1,1024]{2,1,0:T(1,128)}), f32[4,1,1024]{2,1,0:T(1,128)S(1)}, u32[]{:S(2)}, u32[]{:S(2)}) async-start(f32[4,1,1024]{2,1,0:T(1,128)} %broadcast_in_dim.23), calls=%async_computation.2 | async-start | bytes 32768 | tf_op jit(solution)/shard_map/all_to_all | solution.py:24
  108.4 16.5 %all-to-all-start.4 = ((s32[64,1,20]{2,1,0:T(1,128)}), s32[64,1,20]{2,1,0:T(1,128)S(1)}, u32[]{:S(2)}, u32[]{:S(2)}) async-start(s32[64,1,20]{2,1,0:T(1,128)} %bitcast.11), calls=%async_computation.4 | async-start | bytes 65536 | tf_op jit(solution)/shard_map/all_to_all | solution.py:354
  142.4 57.3 %all-to-all-start = ((bf16[64,16,1024]{2,1,0:T(8,128)(2,1)}), bf16[64,16,1024]{2,1,0:T(8,128)(2,1)S(1)}, u32[]{:S(2)}, u32[]{:S(2)}) async-start(bf16[64,16,1024]{2,1,0:T(8,128)(2,1)} %bitcast.38), calls=%async_computation | async-start | bytes 4194304 | tf_op jit(solution)/shard_map/all_to_all | solution.py:357
  149.9 49.8 %copy-start.4 = (bf16[1,64,1024]{2,1,0:T(8,128)(2,1)S(1)}, bf16[1,64,1024]{2,1,0:T(8,128)(2,1)}, u32[]{:S(2)}) copy-start(bf16[1,64,1024]{2,1,0:T(8,128)(2,1)} %param.16) | copy-start | bytes 393220
  203.2 1.0 copy-start.3
  225.6 16.8 %all-to-all-start.5 = ((f32[4,64,1024]{2,1,0:T(8,128)}), f32[4,64,1024]{2,1,0:T(8,128)S(1)}, u32[]{:S(2)}, u32[]{:S(2)}) async-start(f32[4,64,1024]{2,1,0:T(8,128)} %copy-done.3), calls=%async_computation.5 | async-start | bytes 2097152 | tf_op jit(solution)/shard_map/all_to_all | solution.py:389
Sparse Core Ops, SparseCore 0:
  18.6 55.7 all-gather.1

commit v4 on v3

--- a/solution.py
+++ b/solution.py
@@ -14,17 +14,47 @@
 SHARPNESS = 12.0
 ADAPTER_SCALING = 2.0
 PER_PAIR = 2
-VMEM_BYTES = 48 * 1024 * 1024
+VMEM_BYTES = 62 * 1024 * 1024
 CONTRACT_LAST = (((1,), (1,)), ((), ()))
 CONTRACT_FIRST = (((0,), (0,)), ((), ()))
 
 
-def of_everyone(value, axis):
+def over_parts(value, axis):
     peers = lax.axis_size(axis)
-    everything = lax.all_to_all(
-        jnp.broadcast_to(value[None], (peers, *value.shape)), axis, 0, 0, tiled=True
-    )
-    return jnp.sum(everything, axis=0)
+    others = [
+        lax.ppermute(value, axis, [(i, i ^ distance) for i in range(peers)])
+        for distance in range(1, peers)
+    ]
+    return (value + others[0]) + (others[1] + others[2])
+
+
+def square_kernel(values, done, total):
+    lanes = 128
+    sums = jnp.zeros((values.shape[0], lanes), jnp.float32)
+    for g in range(values.shape[1] // lanes):
+        x = values[:, g * lanes : (g + 1) * lanes].astype(jnp.float32)
+        sums = sums + x * x
+    total[...] = jnp.sum(sums.T, axis=0, keepdims=True) + done[0]
+
+
+def row_squares(values, done):
+    rows, columns = values.shape
+    chunk = 256
+    return pl.pallas_call(
+        square_kernel,
+        grid=(rows // chunk,),
+        out_shape=jax.ShapeDtypeStruct((1, rows), jnp.float32),
+        in_specs=[
+            pl.BlockSpec((chunk, columns), lambda i: (i, 0)),
+            pl.BlockSpec(memory_space=pltpu.SMEM),
+        ],
+        out_specs=pl.BlockSpec((1, chunk), lambda i: (0, i)),
+        compiler_params=pltpu.CompilerParams(vmem_limit_bytes=VMEM_BYTES),
+        cost_estimate=pl.CostEstimate(
+            flops=2 * rows * columns, bytes_accessed=2 << 20, transcendentals=0
+        ),
+        name="row_squares",
+    )(values, done)
 
 
 def route_kernel(
@@ -240,9 +270,8 @@
     )(ids, slot_of, gathered, own, frozen, targets)
 
 
-def trainer_kernel(gap, lowered, up, facts, grad_up, back_out, loss_out, back, loss, sem):
+def trainer_kernel(gap, lowered, up, facts, grad_up, back, loss_out, loss, sem):
     step = pl.program_id(0)
-    chunk = gap.shape[0]
     low = lowered[...]
     up_map = up[...]
     facts_now = facts[...]
@@ -252,12 +281,9 @@
     output_grad = (facts_now[:, NB : NB + 1] * distance).astype(jnp.bfloat16)
     squares = jnp.sum(distance * distance, axis=1, keepdims=True)
     part = jnp.sum(facts_now * squares, axis=0, keepdims=True)
-    back_now = lax.dot_general(
+    back[...] = lax.dot_general(
         up_map, output_grad, CONTRACT_LAST, preferred_element_type=jnp.float32
     )
-    at = pl.ds(pl.multiple_of(step * chunk, chunk), chunk)
-    for p in range(back.shape[0]):
-        back[p, :, at] = back_now
     own = jnp.dot(low, output_grad, preferred_element_type=jnp.float32)
 
     @pl.when(step == 0)
@@ -272,28 +298,22 @@
 
     @pl.when(step == pl.num_programs(0) - 1)
     def _():
-        copies = (
-            pltpu.make_async_copy(loss, loss_out, sem.at[0]),
-            pltpu.make_async_copy(back, back_out, sem.at[1]),
-        )
-        for copy in copies:
-            copy.start()
-        for copy in copies:
-            copy.wait()
-
-
-def trainer_step(gap, lowered, up, facts, trainers, parts):
+        copy = pltpu.make_async_copy(loss, loss_out, sem.at[0])
+        copy.start()
+        copy.wait()
+
+
+def trainer_step(gap, lowered, up, facts, trainers):
     rows, columns = gap.shape
     rank = up.shape[0]
     lanes = facts.shape[1]
     chunk = 256
-    hbm = pl.BlockSpec(memory_space=pltpu.HBM)
     return pl.pallas_call(
         trainer_kernel,
         grid=(rows // chunk,),
         out_shape=(
             jax.ShapeDtypeStruct((rank, columns), jnp.float32),
-            jax.ShapeDtypeStruct((parts, rank, rows), jnp.float32),
+            jax.ShapeDtypeStruct((rank, rows), jnp.float32),
             jax.ShapeDtypeStruct((trainers, 1, lanes), jnp.float32),
         ),
         in_specs=[
@@ -302,11 +322,14 @@
             pl.BlockSpec((rank, columns), lambda i: (0, 0)),
             pl.BlockSpec((chunk, lanes), lambda i: (i, 0)),
         ],
-        out_specs=(pl.BlockSpec((rank, columns), lambda i: (0, 0)), hbm, hbm),
+        out_specs=(
+            pl.BlockSpec((rank, columns), lambda i: (0, 0)),
+            pl.BlockSpec((rank, chunk), lambda i: (0, i)),
+            pl.BlockSpec(memory_space=pltpu.HBM),
+        ),
         scratch_shapes=[
-            pltpu.VMEM((parts, rank, rows), jnp.float32),
             pltpu.VMEM((trainers, 1, lanes), jnp.float32),
-            pltpu.SemaphoreType.DMA((2,)),
+            pltpu.SemaphoreType.DMA((1,)),
         ],
         compiler_params=pltpu.CompilerParams(vmem_limit_bytes=VMEM_BYTES),
         cost_estimate=pl.CostEstimate(
@@ -373,21 +396,22 @@
         [onehot, coefficient[:, None], jnp.zeros((rows, 128 - NB - 1), jnp.float32)], axis=1
     )
 
-    values = got_x.reshape(rows, part).astype(jnp.float32)
-    square_total = of_everyone(jnp.sum(values * values, axis=1) + done, "mp")
+    rows_x = got_x.reshape(rows, part)
+    values = rows_x.astype(jnp.float32)
+    square_total = over_parts(row_squares(rows_x, done), "mp")[0]
     inverse_rms = lax.rsqrt(square_total / width + RMS_EPSILON)
     normed = (values * inverse_rms[:, None] * gain[None, :]).astype(jnp.bfloat16)
     latent_part = lax.dot_general(
         down_map, normed, CONTRACT_LAST, preferred_element_type=jnp.float32
     )
-    lowered = (ADAPTER_SCALING * of_everyone(latent_part, "mp")).astype(jnp.bfloat16)
+    lowered = (ADAPTER_SCALING * over_parts(latent_part, "mp")).astype(jnp.bfloat16)
 
     grad_up, back_part, loss_part = trainer_step(
-        got_gap.reshape(rows, part), lowered, up_map, facts, trainers, parts
+        got_gap.reshape(rows, part), lowered, up_map, facts, trainers
     )
     loss_over_dp = jnp.sum(lax.all_to_all(loss_part, DP, 0, 0, tiled=True), axis=0)
-    back = jnp.sum(lax.all_to_all(back_part, "mp", 0, 0, tiled=True), axis=0)
-    loss_sum = of_everyone(loss_over_dp, "mp")[0, :NB]
+    back = over_parts(back_part, "mp")
+    loss_sum = over_parts(loss_over_dp, "mp")[0, :NB]
     lowered_gradient = (ADAPTER_SCALING * back).astype(jnp.bfloat16)
     grad_down = jnp.dot(lowered_gradient, normed, preferred_element_type=jnp.float32)
     bucket_loss = loss_sum / (floor_counts * width)

time: 253 us -> 205 us (0.81)
  waiting for transfers between devices: 115 us -> 77.5 us
  Pallas kernels: 22.1 us -> 31.1 us
  local copies, waits for them, and re-layouts: 10.8 us -> 3.27 us
  starting transfers between devices: 34.1 us -> 27.1 us
  other arithmetic: 11.6 us -> 7.13 us
    all_to_all x1, waiting for transfers between devices: 51 us -> 10.5 us  [on_device(): lax.all_to_all(send_x.reshape(trainers, per_peer, part), DP, 0, 0, tiled=...]
    all_to_all x1, waiting for transfers between devices: 45.6 us -> 16.7 us  [on_device(): lax.all_to_all(send_gap.reshape(trainers, per_peer, part), DP, 0, 0, tile...]
    all_gather x1, waiting for transfers between devices: 0.02 us -> 26.5 us  [on_device(): gathered = lax.all_gather(own_x.reshape(-1, part), 'mp')]
    ppermute x0 -> x12, waiting for transfers between devices: none -> 23.7 us  [over_parts(): lax.ppermute(value, axis, [(i, i ^ distance) for i in range(peers)])]
    all_to_all x3 -> x0, waiting for transfers between devices: 18.2 us -> none  [the longest x1 8.59 us: on_device(): back = jnp.sum(lax.all_to_all(back_part, 'mp', 0, 0, tiled=True), axis=0)]
    ppermute x0 -> x12, starting transfers between devices: none -> 15.5 us  [over_parts(): lax.ppermute(value, axis, [(i, i ^ distance) for i in range(peers)])]
    all_to_all x3 -> x0, starting transfers between devices: 14.9 us -> none  [the longest x1 7.25 us: on_device(): lax.all_to_all(message[:, None, :], DP, 0, 0, tiled=True)[:, 0, :]]
    all_to_all x1, starting transfers between devices: 13.2 us -> 5.59 us  [on_device(): lax.all_to_all(send_x.reshape(trainers, per_peer, part), DP, 0, 0, tiled=...]
  transfers between devices with their start and end apart: 6 -> 15, of which waited for: 5 -> 11; matrix products, arithmetic and copies ran while one was open for 6% -> 5% of each run, Pallas kernels for 0% -> 9%
where the time goes in v4:
time: 205 us
  waiting for transfers between devices  77.5 us (38%)
  blocking collectives  37.2 us (18%)
  Pallas kernels  31.1 us (15%)
  starting transfers between devices  27.1 us (13%)
  between operations  17.3 us (8%)
  other arithmetic  7.13 us (3%)
  matrix products  3.94 us (2%)
  local copies, waits for them, and re-layouts  3.27 us (2%)
    all_gather x1, waiting for transfers between devices, on_device(): gathered = lax.all_gather(own_x.reshape(-1, part), 'mp')  26.5 us
    ppermute x12, waiting for transfers between devices, over_parts(): lax.ppermute(value, axis, [(i, i ^ distance) for i in range(peers)])  23.7 us
    all_to_all x1, blocking collectives, on_device(): lax.all_to_all(message[:, None, :], DP, 0, 0, tiled=True)[:, 0, :]  22.1 us
    all_to_all x1, waiting for transfers between devices, on_device(): lax.all_to_all(send_gap.reshape(trainers, per_peer, part), DP, 0, 0, tile...  16.7 us
    ppermute x12, starting transfers between devices, over_parts(): lax.ppermute(value, axis, [(i, i ^ distance) for i in range(peers)])  15.5 us
    all_to_all x1, blocking collectives, on_device(): lax.all_to_all(loss_part, DP, 0, 0, tiled=True)  15.1 us
    pallas_call x1, Pallas kernels, base_gap_slots(): pl.pallas_call(gap_kernel, grid=(columns // tile,), out_shape=(jax.ShapeD...  14.2 us
    all_to_all x1, waiting for transfers between devices, on_device(): lax.all_to_all(send_x.reshape(trainers, per_peer, part), DP, 0, 0, tiled=...  10.5 us
  transfers between devices with their start and end apart: 15, of which 11 were waited for; matrix products, arithmetic and copies ran while one was open for 5% of the time, Pallas kernels for 9%

profile of v4, /device:TPU:1, one launch (start us, length us, event | category | flops | bytes accessed | tf_op | source)
XLA Modules:
  0.0 204.6 jit_solution(10206219649323275507)
XLA Ops:
  7.2 7.0 %route.1 = (bf16[128,8,1024]{2,1,0:T(8,128)(2,1)}, bf16[66,8,1024]{2,1,0:T(8,128)(2,1)}, s32[64,4]{1,0:T(8,128)}, s32[16]{0:T(128)}, s32[128]{0:T(128)}) custom-call(s32[64]{0:T(128)} %ids.1, s32[64]{0:T(128)} %bitcast.45, s32[128]{0:T(128)} %buckets_in.1, s32[128]{0:T(128)} %lengths_in.1, bf16[128,8,1024]{2,1,0:T(8,128)(2,1)} %pool_in.1, f32[1,1024]{1,0:T(1,128)} %bitcast.39), custom_call_target="tpu_custom_call" | custom-call | bytes 5242880 | tf_op jit(solution)/shard_map/route/pallas_call | solution.py:152
  14.3 0.8 copy.16
  16.0 22.1 %all_to_all.20 = s32[64,1,20]{2,1,0:T(1,128)S(1)} all-to-all(s32[64,1,20]{2,1,0:T(1,128)S(1)} %bitcast.38), channel_id=1, replica_groups=mesh['dp_0'=4,'dp_1'=8,'dp_2'=2,'mp'=4] {'dp_0','dp_1','dp_2'}, dimensions={0} | all-to-all | bytes 10240 | tf_op jit(solution)/shard_map/all_to_all | solution.py:377
  38.1 5.6 %all-to-all-start.1 = ((bf16[64,16,1024]{2,1,0:T(8,128)(2,1)}), bf16[64,16,1024]{2,1,0:T(8,128)(2,1)}, u32[]{:S(2)}, u32[]{:S(2)}) async-start(bf16[64,16,1024]{2,1,0:T(8,128)(2,1)} %bitcast.33), calls=%async_computation.1 | async-start | bytes 4194304 | tf_op jit(solution)/shard_map/all_to_all | solution.py:370
  43.7 26.5 %all-gather.2.cloned.1.call-done.gathered = bf16[4,528,1024]{2,1,0:T(8,128)(2,1)} async-done(((bf16[1,528,1024]{2,1,0:T(8,128)(2,1)}), bf16[4,528,1024]{2,1,0:T(8,128)(2,1)}) %all-gather.2.cloned.1.call-update) | async-done | bytes 4325392 | tf_op jit(solution)/shard_map/all_gather | solution.py:373
  70.2 14.2 %base_gap.1 = (bf16[128,8,1024]{2,1,0:T(8,128)(2,1)}, f32[1]{0:T(128)}) custom-call(s32[64]{0:T(128)} %ids.1, s32[128]{0:T(128)} %get-tuple-element.14.slot_of, bf16[4,528,1024]{2,1,0:T(8,128)(2,1)} %all-gather.2.cloned.1.call-done.gathered, bf16[66,8,1024]{2,1,0:T(8,128)(2,1)} %get-tuple-element.15.own, bf16[4096,1024]{1,0:T(8,128)(2,1)} %frozen.1, ...), custom_call_target="tpu_custom_call" | custom-call | flops 4294967296 | bytes 18874368 | tf_op jit(solution)/shard_map/base_gap/pallas_call | solution.py:243
  84.4 10.5 %all-to-all-done.1 = bf16[64,16,1024]{2,1,0:T(8,128)(2,1)} async-done(((bf16[64,16,1024]{2,1,0:T(8,128)(2,1)}), bf16[64,16,1024]{2,1,0:T(8,128)(2,1)}, u32[]{:S(2)}, u32[]{:S(2)}) %all-to-all-start.1) | async-done | bytes 2097184 | tf_op jit(solution)/shard_map/all_to_all | solution.py:370
  95.0 6.0 %all-to-all-start = ((bf16[64,16,1024]{2,1,0:T(8,128)(2,1)}), bf16[64,16,1024]{2,1,0:T(8,128)(2,1)}, u32[]{:S(2)}, u32[]{:S(2)}) async-start(bf16[64,16,1024]{2,1,0:T(8,128)(2,1)} %bitcast.32), calls=%async_computation | async-start | bytes 4194304 | tf_op jit(solution)/shard_map/all_to_all | solution.py:380
  102.6 4.3 %row_squares.1 = f32[1,1024]{1,0:T(1,128)} custom-call(bf16[1024,1024]{1,0:T(8,128)(2,1)} %bitcast.6.values, f32[1]{0:T(128)} %get-tuple-element.18.done), custom_call_target="tpu_custom_call" | custom-call | flops 2097152 | bytes 2097152 | tf_op jit(solution)/shard_map/row_squares/pallas_call | solution.py:43
  106.8 1.3 collective-permute-start
  108.1 2.6 %collective-permute-start.1 = (f32[1,1024]{1,0:T(1,128)}, f32[1,1024]{1,0:T(1,128)S(1)}, u32[]{:S(2)}, u32[]{:S(2)}) collective-permute-start(f32[1,1024]{1,0:T(1,128)} %row_squares.1), channel_id=1, source_target_pairs={{0,2},{1,3},{2,0},{3,1},{4,6},{5,7},{6,4},{7,5},{8,10},{9,11},{10,... | collective-permute-start | bytes 12296 | tf_op jit(solution)/shard_map/ppermute | solution.py:25
  111.3 1.4 collective-permute-done.1
  112.7 2.3 %collective-permute-done.2 = f32[1,1024]{1,0:T(1,128)S(1)} collective-permute-done((f32[1,1024]{1,0:T(1,128)}, f32[1,1024]{1,0:T(1,128)S(1)}, u32[]{:S(2)}, u32[]{:S(2)}) %collective-permute-start.2) | collective-permute-done | bytes 4128 | tf_op jit(solution)/shard_map/ppermute | solution.py:25
  115.6 1.4 fusion.15
  117.0 2.1 %multiply_convert_fusion.1 = bf16[64,16,1024]{2,1,0:T(8,128)(2,1)S(1)} fusion(bf16[64,16,1024]{2,1,0:T(8,128)(2,1)} %all-to-all-done.1, f32[1024]{0:T(1024)S(1)} %copy-done.1, f32[64,16]{1,0:T(8,128)S(1)} %rsqrt.15), kind=kLoop, calls=%fused_computation.1 | loop fusion | flops 4194304 | bytes 4202496 | tf_op jit(solution)/shard_map/convert_element_type | solution.py:403
  120.0 1.2 collective-permute-start.4
  121.2 2.6 %collective-permute-start.5 = (f32[64,1024]{1,0:T(8,128)S(1)}, f32[64,1024]{1,0:T(8,128)S(1)}, u32[]{:S(2)}, u32[]{:S(2)}) collective-permute-start(f32[64,1024]{1,0:T(8,128)S(1)} %convolution_bitcast_fusion), channel_id=1, source_target_pairs={{0,3},{1,2},{2,1},{3,0},{4,7},{5,6},{6,5},{7,4},{8,11},{9,10},{10,... | collective-permute-start | bytes 786440 | tf_op jit(solution)/shard_map/ppermute | solution.py:25
  124.1 1.0 maximum_maximum_fusion.facts
  125.1 1.0 collective-permute-done.3
  126.1 5.5 %collective-permute-done.4 = f32[64,1024]{1,0:T(8,128)S(1)} collective-permute-done((f32[64,1024]{1,0:T(8,128)S(1)}, f32[64,1024]{1,0:T(8,128)S(1)}, u32[]{:S(2)}, u32[]{:S(2)}) %collective-permute-start.4) | collective-permute-done | bytes 262176 | tf_op jit(solution)/shard_map/ppermute | solution.py:25
  131.6 3.1 %collective-permute-done.5 = f32[64,1024]{1,0:T(8,128)S(1)} collective-permute-done((f32[64,1024]{1,0:T(8,128)S(1)}, f32[64,1024]{1,0:T(8,128)S(1)}, u32[]{:S(2)}, u32[]{:S(2)}) %collective-permute-start.5) | collective-permute-done | bytes 262176 | tf_op jit(solution)/shard_map/ppermute | solution.py:25
  135.4 16.7 %all-to-all-done = bf16[64,16,1024]{2,1,0:T(8,128)(2,1)} async-done(((bf16[64,16,1024]{2,1,0:T(8,128)(2,1)}), bf16[64,16,1024]{2,1,0:T(8,128)(2,1)}, u32[]{:S(2)}, u32[]{:S(2)}) %all-to-all-start) | async-done | bytes 2097184 | tf_op jit(solution)/shard_map/all_to_all | solution.py:380
  152.1 5.6 %trainer_step.1 = (f32[64,1024]{1,0:T(8,128)}, f32[64,1024]{1,0:T(8,128)}, f32[64,1,128]{2,1,0:T(1,128)}) custom-call(bf16[1024,1024]{1,0:T(8,128)(2,1)} %bitcast.4.gap, bf16[64,1024]{1,0:T(8,128)(2,1)} %multiply_convert_fusion.6.lowered, bf16[64,1024]{1,0:T(8,128)(2,1)} %bitcast.37, f32[1024,128]{1,0:T(8,128)} %maximum_maximum_fusion.facts), custom_call_target="tpu_custom_call" | custom-call | flops 402653184 | bytes 4194304 | tf_op jit(solution)/shard_map/trainer_step/pallas_call | solution.py:311
  157.7 15.1 %all_to_all.21 = f32[64,1,128]{2,1,0:T(1,128)S(1)} all-to-all(f32[64,1,128]{2,1,0:T(1,128)} %get-tuple-element.23), channel_id=1, replica_groups=mesh['dp_0'=4,'dp_1'=8,'dp_2'=2,'mp'=4] {'dp_0','dp_1','dp_2'}, dimensions={0} | all-to-all | bytes 65536 | tf_op jit(solution)/shard_map/all_to_all | solution.py:412
  172.9 3.0 %collective-permute-start.10 = (f32[1,128]{1,0:T(1,128)S(1)}, f32[1,128]{1,0:T(1,128)S(1)}, u32[]{:S(2)}, u32[]{:S(2)}) collective-permute-start(f32[1,128]{1,0:T(1,128)S(1)} %bitcast.42), channel_id=1, source_target_pairs={{0,2},{1,3},{2,0},{3,1},{4,6},{5,7},{6,4},{7,5},{8,10},{9,11},{10,... | collective-permute-start | bytes 1544 | tf_op jit(solution)/shard_map/ppermute | solution.py:25
  176.7 1.5 collective-permute-start.6
  178.2 1.7 collective-permute-start.7
  179.8 0.8 collective-permute-start.8
  180.6 1.1 fusion.14
  183.5 7.2 %collective-permute-done.7 = f32[64,1024]{1,0:T(8,128)S(1)} collective-permute-done((f32[64,1024]{1,0:T(8,128)}, f32[64,1024]{1,0:T(8,128)S(1)}, u32[]{:S(2)}, u32[]{:S(2)}) %collective-permute-start.7) | collective-permute-done | bytes 262176 | tf_op jit(solution)/shard_map/ppermute | solution.py:25
  190.8 2.6 %collective-permute-done.8 = f32[64,1024]{1,0:T(8,128)S(1)} collective-permute-done((f32[64,1024]{1,0:T(8,128)}, f32[64,1024]{1,0:T(8,128)S(1)}, u32[]{:S(2)}, u32[]{:S(2)}) %collective-permute-start.8) | collective-permute-done | bytes 262176 | tf_op jit(solution)/shard_map/ppermute | solution.py:25
  193.4 3.2 %fusion.3 = f32[1,64,1024]{2,1,0:T(8,128)} fusion(bf16[1024,1024]{1,0:T(8,128)(2,1)} %bitcast.6.values, f32[1024]{0:T(1024)S(1)} %copy-done.1, f32[1024]{0:T(1024)S(1)} %bitcast.41, f32[64,1024]{1,0:T(8,128)S(1)} %collective-permute-done.7, f32[64,1024]{1,0:T(8,128)S(1)} %collective-permute-done.8, f32[64,1024]{1,0:T(8,128)} %get-tuple-element.21, ...), kind=kOutput, calls=%fused_computation.5 | convolution fusion | flops 138739712 | bytes 3416064 | tf_op jit(solution)/shard_map/dot_general | solution.py:416
  (39 shorter events, 6.1 us)
Async XLA Ops:
  7.2 112.0 %copy-start = (bf16[1,64,1024]{2,1,0:T(8,128)(2,1)S(1)}, bf16[1,64,1024]{2,1,0:T(8,128)(2,1)}, u32[]{:S(2)}) copy-start(bf16[1,64,1024]{2,1,0:T(8,128)(2,1)} %param.15) | copy-start | bytes 393220
  7.2 63.0 %all-gather.2.cloned.1.call-start = ((), (), s32[]{:S(2)}) async-start(), calls=%async_computation.4 | async-start | bytes 5406720 | tf_op jit(solution)/shard_map/all_gather | solution.py:373
  38.1 56.9 %all-to-all-start.1 = ((bf16[64,16,1024]{2,1,0:T(8,128)(2,1)}), bf16[64,16,1024]{2,1,0:T(8,128)(2,1)}, u32[]{:S(2)}, u32[]{:S(2)}) async-start(bf16[64,16,1024]{2,1,0:T(8,128)(2,1)} %bitcast.33), calls=%async_computation.1 | async-start | bytes 4194304 | tf_op jit(solution)/shard_map/all_to_all | solution.py:370
  95.0 57.2 %all-to-all-start = ((bf16[64,16,1024]{2,1,0:T(8,128)(2,1)}), bf16[64,16,1024]{2,1,0:T(8,128)(2,1)}, u32[]{:S(2)}, u32[]{:S(2)}) async-start(bf16[64,16,1024]{2,1,0:T(8,128)(2,1)} %bitcast.32), calls=%async_computation | async-start | bytes 4194304 | tf_op jit(solution)/shard_map/all_to_all | solution.py:380
  101.0 16.0 %copy-start.1 = (f32[1024]{0:T(1024)S(1)}, f32[1024]{0:T(1024)}, u32[]{:S(2)}) copy-start(f32[1024]{0:T(1024)} %param.14) | copy-start | bytes 12292
  106.8 4.4 %collective-permute-start = (f32[1,1024]{1,0:T(1,128)}, f32[1,1024]{1,0:T(1,128)S(1)}, u32[]{:S(2)}, u32[]{:S(2)}) collective-permute-start(f32[1,1024]{1,0:T(1,128)} %row_squares.1), channel_id=1, source_target_pairs={{0,1},{1,0},{2,3},{3,2},{4,5},{5,4},{6,7},{7,6},{8,9},{9,8},{10,11... | collective-permute-start | bytes 12296 | tf_op jit(solution)/shard_map/ppermute | solution.py:25
  108.1 4.6 %collective-permute-start.1 = (f32[1,1024]{1,0:T(1,128)}, f32[1,1024]{1,0:T(1,128)S(1)}, u32[]{:S(2)}, u32[]{:S(2)}) collective-permute-start(f32[1,1024]{1,0:T(1,128)} %row_squares.1), channel_id=1, source_target_pairs={{0,2},{1,3},{2,0},{3,1},{4,6},{5,7},{6,4},{7,5},{8,10},{9,11},{10,... | collective-permute-start | bytes 12296 | tf_op jit(solution)/shard_map/ppermute | solution.py:25
  110.8 4.3 %collective-permute-start.2 = (f32[1,1024]{1,0:T(1,128)}, f32[1,1024]{1,0:T(1,128)S(1)}, u32[]{:S(2)}, u32[]{:S(2)}) collective-permute-start(f32[1,1024]{1,0:T(1,128)} %row_squares.1), channel_id=1, source_target_pairs={{0,3},{1,2},{2,1},{3,0},{4,7},{5,6},{6,5},{7,4},{8,11},{9,10},{10,... | collective-permute-start | bytes 12296 | tf_op jit(solution)/shard_map/ppermute | solution.py:25
  119.9 6.2 %collective-permute-start.3 = (f32[64,1024]{1,0:T(8,128)S(1)}, f32[64,1024]{1,0:T(8,128)S(1)}, u32[]{:S(2)}, u32[]{:S(2)}) collective-permute-start(f32[64,1024]{1,0:T(8,128)S(1)} %convolution_bitcast_fusion), channel_id=1, source_target_pairs={{0,1},{1,0},{2,3},{3,2},{4,5},{5,4},{6,7},{7,6},{8,9},{9,8},{10,11... | collective-permute-start | bytes 786440 | tf_op jit(solution)/shard_map/ppermute | solution.py:25
  120.0 11.6 %collective-permute-start.4 = (f32[64,1024]{1,0:T(8,128)S(1)}, f32[64,1024]{1,0:T(8,128)S(1)}, u32[]{:S(2)}, u32[]{:S(2)}) collective-permute-start(f32[64,1024]{1,0:T(8,128)S(1)} %convolution_bitcast_fusion), channel_id=1, source_target_pairs={{0,2},{1,3},{2,0},{3,1},{4,6},{5,7},{6,4},{7,5},{8,10},{9,11},{10,... | collective-permute-start | bytes 786440 | tf_op jit(solution)/shard_map/ppermute | solution.py:25
  121.2 13.5 %collective-permute-start.5 = (f32[64,1024]{1,0:T(8,128)S(1)}, f32[64,1024]{1,0:T(8,128)S(1)}, u32[]{:S(2)}, u32[]{:S(2)}) collective-permute-start(f32[64,1024]{1,0:T(8,128)S(1)} %convolution_bitcast_fusion), channel_id=1, source_target_pairs={{0,3},{1,2},{2,1},{3,0},{4,7},{5,6},{6,5},{7,4},{8,11},{9,10},{10,... | collective-permute-start | bytes 786440 | tf_op jit(solution)/shard_map/ppermute | solution.py:25
  172.9 6.9 %collective-permute-start.10 = (f32[1,128]{1,0:T(1,128)S(1)}, f32[1,128]{1,0:T(1,128)S(1)}, u32[]{:S(2)}, u32[]{:S(2)}) collective-permute-start(f32[1,128]{1,0:T(1,128)S(1)} %bitcast.42), channel_id=1, source_target_pairs={{0,2},{1,3},{2,0},{3,1},{4,6},{5,7},{6,4},{7,5},{8,10},{9,11},{10,... | collective-permute-start | bytes 1544 | tf_op jit(solution)/shard_map/ppermute | solution.py:25
  175.9 4.7 %collective-permute-start.11 = (f32[1,128]{1,0:T(1,128)S(1)}, f32[1,128]{1,0:T(1,128)S(1)}, u32[]{:S(2)}, u32[]{:S(2)}) collective-permute-start(f32[1,128]{1,0:T(1,128)S(1)} %bitcast.43), channel_id=1, source_target_pairs={{0,3},{1,2},{2,1},{3,0},{4,7},{5,6},{6,5},{7,4},{8,11},{9,10},{10,... | collective-permute-start | bytes 1544 | tf_op jit(solution)/shard_map/ppermute | solution.py:25
  176.7 3.9 %collective-permute-start.9 = (f32[1,128]{1,0:T(1,128)S(1)}, f32[1,128]{1,0:T(1,128)S(1)}, u32[]{:S(2)}, u32[]{:S(2)}) collective-permute-start(f32[1,128]{1,0:T(1,128)S(1)} %bitcast.44), channel_id=1, source_target_pairs={{0,1},{1,0},{2,3},{3,2},{4,5},{5,4},{6,7},{7,6},{8,9},{9,8},{10,11... | collective-permute-start | bytes 1544 | tf_op jit(solution)/shard_map/ppermute | solution.py:25
  176.7 6.8 %collective-permute-start.6 = (f32[64,1024]{1,0:T(8,128)}, f32[64,1024]{1,0:T(8,128)S(1)}, u32[]{:S(2)}, u32[]{:S(2)}) collective-permute-start(f32[64,1024]{1,0:T(8,128)} %get-tuple-element.21), channel_id=1, source_target_pairs={{0,1},{1,0},{2,3},{3,2},{4,5},{5,4},{6,7},{7,6},{8,9},{9,8},{10,11... | collective-permute-start | bytes 786440 | tf_op jit(solution)/shard_map/ppermute | solution.py:25
  178.2 12.6 %collective-permute-start.7 = (f32[64,1024]{1,0:T(8,128)}, f32[64,1024]{1,0:T(8,128)S(1)}, u32[]{:S(2)}, u32[]{:S(2)}) collective-permute-start(f32[64,1024]{1,0:T(8,128)} %get-tuple-element.21), channel_id=1, source_target_pairs={{0,2},{1,3},{2,0},{3,1},{4,6},{5,7},{6,4},{7,5},{8,10},{9,11},{10,... | collective-permute-start | bytes 786440 | tf_op jit(solution)/shard_map/ppermute | solution.py:25
  179.8 13.6 %collective-permute-start.8 = (f32[64,1024]{1,0:T(8,128)}, f32[64,1024]{1,0:T(8,128)S(1)}, u32[]{:S(2)}, u32[]{:S(2)}) collective-permute-start(f32[64,1024]{1,0:T(8,128)} %get-tuple-element.21), channel_id=1, source_target_pairs={{0,3},{1,2},{2,1},{3,0},{4,7},{5,6},{6,5},{7,4},{8,11},{9,10},{10,... | collective-permute-start | bytes 786440 | tf_op jit(solution)/shard_map/ppermute | solution.py:25
Sparse Core Ops, SparseCore 0:
  14.4 55.7 all-gather.1

commit v5 on v4

v5 whole, which is shorter than its diff:
```python
import jax
import jax.numpy as jnp
from jax import lax
from jax.experimental import pallas as pl
from jax.experimental.pallas import tpu as pltpu
from jax.sharding import Mesh
from jax.sharding import PartitionSpec as P

NB = 16
DP = ("dp_0", "dp_1", "dp_2")
DP_MP = ("dp_0", "dp_1", "dp_2", "mp")

RMS_EPSILON = 1e-05
SHARPNESS = 12.0
ADAPTER_SCALING = 2.0
PER_PAIR = 2
VMEM_BYTES = 62 * 1024 * 1024
CONTRACT_LAST = (((1,), (1,)), ((), ()))
CONTRACT_FIRST = (((0,), (0,)), ((), ()))


def over_parts(value, axis):
    peers = lax.axis_size(axis)
    others = [
        lax.ppermute(value, axis, [(i, i ^ distance) for i in range(peers)])
        for distance in range(1, peers)
    ]
    return (value + others[0]) + (others[1] + others[2])


def lane_group(packed, group, groups):
    slots = [packed[:, s * groups + group][:, None] for s in range(PER_PAIR)]
    whole = jnp.concatenate(slots, axis=1).astype(jnp.float32)
    return whole.reshape(-1, packed.shape[-1])


def square_kernel(packed, done, total):
    groups = (packed.shape[1] - 1) // PER_PAIR
    sums = None
    for g in range(groups):
        x = lane_group(packed, g, groups)
        sums = x * x if sums is None else sums + x * x
    total[...] = jnp.sum(sums.T, axis=0, keepdims=True) + done[0]


def row_squares(packed, done):
    peers, pieces, block_len, lanes = packed.shape
    rows = peers * PER_PAIR * block_len
    chunk = 16
    return pl.pallas_call(
        square_kernel,
        grid=(peers // chunk,),
        out_shape=jax.ShapeDtypeStruct((1, rows), jnp.float32),
        in_specs=[
            pl.BlockSpec((chunk, pieces, block_len, lanes), lambda i: (i, 0, 0, 0)),
            pl.BlockSpec(memory_space=pltpu.SMEM),
        ],
        out_specs=pl.BlockSpec((1, rows * chunk // peers), lambda i: (0, i)),
        compiler_params=pltpu.CompilerParams(vmem_limit_bytes=VMEM_BYTES),
        cost_estimate=pl.CostEstimate(flops=4 << 20, bytes_accessed=2 << 20, transcendentals=0),
        name="row_squares",
    )(packed, done)


def latent_kernel(packed, squares, gain, down, normed, latent):
    lanes = packed.shape[-1]
    groups = (packed.shape[1] - 1) // PER_PAIR
    inverse = lax.rsqrt(squares[...] + RMS_EPSILON)
    inverse = jnp.broadcast_to(inverse, (lanes, inverse.shape[1])).T
    for g in range(groups):
        at = slice(g * lanes, (g + 1) * lanes)
        x = lane_group(packed, g, groups)
        normed[:, at] = (x * inverse * gain[:, at]).astype(jnp.bfloat16)
    latent[...] = lax.dot_general(
        down[...], normed[...], CONTRACT_LAST, preferred_element_type=jnp.float32
    )


def latents(packed, mean_squares, gain, down):
    peers, pieces, block_len, lanes = packed.shape
    rows = peers * PER_PAIR * block_len
    rank, columns = down.shape
    chunk = 16
    part = rows * chunk // peers
    return pl.pallas_call(
        latent_kernel,
        grid=(peers // chunk,),
        out_shape=(
            jax.ShapeDtypeStruct((rows, columns), jnp.bfloat16),
            jax.ShapeDtypeStruct((rank, rows), jnp.float32),
        ),
        in_specs=[
            pl.BlockSpec((chunk, pieces, block_len, lanes), lambda i: (i, 0, 0, 0)),
            pl.BlockSpec((1, part), lambda i: (0, i)),
            pl.BlockSpec((1, columns), lambda i: (0, 0)),
            pl.BlockSpec((rank, columns), lambda i: (0, 0)),
        ],
        out_specs=(
            pl.BlockSpec((part, columns), lambda i: (i, 0)),
            pl.BlockSpec((rank, part), lambda i: (0, i)),
        ),
        compiler_params=pltpu.CompilerParams(vmem_limit_bytes=VMEM_BYTES),
        cost_estimate=pl.CostEstimate(
            flops=2 * rows * rank * columns, bytes_accessed=4 << 20, transcendentals=rows
        ),
        name="latents",
    )(packed, mean_squares, gain[None, :], down)


def route_kernel(
    ids_in, dest_in, buckets_in, lengths_in, pool_in, gain_in,
    send_out, own_out, slot_of,
    ids, dest, buckets, lengths, pool, gain, send, own, arrived, info, counts, sem,
):
    pairs = (
        (pool_in, pool),
        (ids_in, ids),
        (dest_in, dest),
        (buckets_in, buckets),
        (lengths_in, lengths),
        (gain_in, gain),
    )
    copies = [
        pltpu.make_async_copy(source, target, sem.at[i])
        for i, (source, target) in enumerate(pairs)
    ]
    for copy in copies:
        copy.start()
    sampled = ids.shape[0]
    trainers, pieces, block_len, lanes = send.shape
    groups = (pieces - 1) // PER_PAIR

    def clear(k, carry):
        arrived[k] = 0
        for s in range(PER_PAIR):
            info[s, k] = 0
            info[PER_PAIR + s, k] = 0
        return carry

    def clear_counts(b, carry):
        counts[b] = 0
        return carry

    lax.fori_loop(0, trainers, clear, 0)
    lax.fori_loop(0, NB, clear_counts, 0)
    for copy in copies:
        copy.wait()

    def place(j, carry):
        block = ids[j]
        trainer = dest[j]
        values = pool[block]
        own[j] = values
        order = arrived[trainer]
        arrived[trainer] = order + 1
        slot = trainer * PER_PAIR + order
        for g in range(groups):
            send[trainer, order * groups + g] = values[:, g * lanes : (g + 1) * lanes]
        slot_of[j] = slot
        bucket = buckets[block]
        length = lengths[block]
        info[order, trainer] = bucket
        info[PER_PAIR + order, trainer] = length
        counts[bucket] = counts[bucket] + length
        return carry

    lax.fori_loop(0, sampled, place, 0)

    row = lax.broadcasted_iota(jnp.int32, (block_len, lanes), 0)
    lane = lax.broadcasted_iota(jnp.int32, (block_len, lanes), 1)
    holder = jnp.zeros((block_len, lanes), jnp.int32)
    for b in range(NB):
        count = counts[b]
        holder = jnp.where((row == 1) & (lane == b), count // 16, holder)
        holder = jnp.where((row == 2) & (lane == b), count % 16, holder)

    def finish(k, found):
        for s in range(PER_PAIR):
            free = arrived[k] <= s

            @pl.when(free)
            def _():
                slot_of[sampled + found] = k * PER_PAIR + s
                for g in range(groups):
                    send[k, s * groups + g] = jnp.zeros((block_len, lanes), send.dtype)

            found = found + jnp.where(free, 1, 0)
        facts = holder
        for i in range(2 * PER_PAIR):
            facts = jnp.where((row == 0) & (lane == i), info[i, k], facts)
        send[k, pieces - 1] = facts.astype(jnp.float32).astype(send.dtype)
        return found

    lax.fori_loop(0, trainers, finish, 0)
    send_copy = pltpu.make_async_copy(send, send_out, sem.at[0])
    send_copy.start()
    whole = gain[...]
    high = whole.astype(jnp.bfloat16).astype(jnp.float32)
    middle = (whole - high).astype(jnp.bfloat16).astype(jnp.float32)
    low = whole - high - middle
    zeros = jnp.zeros((own.shape[1] - 3, whole.shape[1]), jnp.float32)
    own[sampled] = jnp.concatenate([high, middle, low, zeros], axis=0).astype(jnp.bfloat16)
    own[sampled + 1] = jnp.zeros(own.shape[1:], own.dtype)
    own_copy = pltpu.make_async_copy(own, own_out, sem.at[1])
    own_copy.start()
    own_copy.wait()
    send_copy.wait()


def route(ids, dest, buckets, lengths, pool, gain, trainers):
    sampled = ids.shape[0]
    slots = trainers * PER_PAIR
    block = pool.shape[1:]
    lanes = 128
    message = (trainers, PER_PAIR * (block[1] // lanes) + 1, block[0], lanes)
    smem = pl.BlockSpec(memory_space=pltpu.SMEM)
    hbm = pl.BlockSpec(memory_space=pltpu.HBM)
    return pl.pallas_call(
        route_kernel,
        out_shape=(
            jax.ShapeDtypeStruct(message, pool.dtype),
            jax.ShapeDtypeStruct((sampled + 2, *block), pool.dtype),
            jax.ShapeDtypeStruct((slots,), jnp.int32),
        ),
        in_specs=[hbm] * 6,
        out_specs=(hbm, hbm, smem),
        scratch_shapes=[
            pltpu.SMEM(ids.shape, jnp.int32),
            pltpu.SMEM(dest.shape, jnp.int32),
            pltpu.SMEM(buckets.shape, jnp.int32),
            pltpu.SMEM(lengths.shape, jnp.int32),
            pltpu.VMEM(pool.shape, pool.dtype),
            pltpu.VMEM((1, gain.shape[0]), jnp.float32),
            pltpu.VMEM(message, pool.dtype),
            pltpu.VMEM((sampled + 2, *block), pool.dtype),
            pltpu.SMEM((trainers,), jnp.int32),
            pltpu.SMEM((2 * PER_PAIR, trainers), jnp.int32),
            pltpu.SMEM((NB,), jnp.int32),
            pltpu.SemaphoreType.DMA((6,)),
        ],
        compiler_params=pltpu.CompilerParams(vmem_limit_bytes=VMEM_BYTES),
        cost_estimate=pl.CostEstimate(flops=0, bytes_accessed=5 << 20, transcendentals=0),
        name="route",
    )(ids, dest, buckets, lengths, pool, gain[None, :])


def gap_kernel(
    ids, slot_of, gathered, pieces, frozen, own_in, targets_in,
    send_out, done, own, targets, send, normed, gap, sem,
):
    step = pl.program_id(0)
    parts, chunk, part = gathered.shape
    sampled, block_len, columns = gap.shape
    chunks = sampled * block_len // chunk
    width = frozen.shape[1]
    slots = send.shape[0]
    own_copy = pltpu.make_async_copy(own_in.at[pl.ds(0, sampled)], own, sem.at[0])
    target_copy = pltpu.make_async_copy(targets_in, targets, sem.at[1])

    @pl.when(step == 0)
    def _():
        own_copy.start()
        target_copy.start()
        done[0] = 0.0

        def fill(s, carry):
            send[slot_of[sampled + s]] = jnp.zeros((block_len, columns), jnp.bfloat16)
            return carry

        lax.fori_loop(0, slots - sampled, fill, 0)

    @pl.when(step < chunks)
    def _():
        total = jnp.zeros((chunk, 1), jnp.float32)
        for p in range(parts):
            x = gathered[p].astype(jnp.float32)
            total = total + jnp.sum(x * x, axis=1, keepdims=True)
        inverse = lax.rsqrt(total / (parts * part) + RMS_EPSILON)
        at = pl.ds(pl.multiple_of(step * chunk, chunk), chunk)
        for p in range(parts):
            three = pieces[p].astype(jnp.float32)
            gain = three[0:1] + three[1:2] + three[2:3]
            x = gathered[p].astype(jnp.float32)
            normed[at, p * part : (p + 1) * part] = (x * inverse * gain).astype(jnp.bfloat16)

    @pl.when(step == chunks)
    def _():
        own_copy.wait()
        target_copy.wait()

    @pl.when(step >= chunks)
    def _():
        projected = jnp.dot(normed[...], frozen[...], preferred_element_type=jnp.float32)
        at = pl.ds(pl.multiple_of((step - chunks) * width, width), width)
        x = own[:, :, at].astype(jnp.float32)
        gap[:, :, at] = x + projected.reshape(sampled, block_len, width)

    @pl.when(step == pl.num_programs(0) - 1)
    def _():
        def place(j, carry):
            target = targets[ids[j]].astype(jnp.float32)
            send[slot_of[j]] = (gap[j] - target).astype(jnp.bfloat16)
            return carry

        lax.fori_loop(0, sampled, place, 0, unroll=4)
        copy = pltpu.make_async_copy(send, send_out, sem.at[0])
        copy.start()
        copy.wait()


def base_gap_slots(ids, slot_of, gathered, own, frozen, targets):
    parts, _, part = gathered.shape
    width, columns = frozen.shape
    slots = slot_of.shape[0]
    sampled = ids.shape[0]
    block = own.shape[1:]
    rows = sampled * block[0]
    tile = 256
    chunk = 128
    chunks = rows // chunk
    smem = pl.BlockSpec(memory_space=pltpu.SMEM)
    hbm = pl.BlockSpec(memory_space=pltpu.HBM)
    return pl.pallas_call(
        gap_kernel,
        grid=(chunks + columns // tile,),
        out_shape=(
            jax.ShapeDtypeStruct((slots, *block), jnp.bfloat16),
            jax.ShapeDtypeStruct((1,), jnp.float32),
        ),
        in_specs=[
            smem,
            smem,
            pl.BlockSpec((parts, chunk, part), lambda n: (0, jnp.minimum(n, chunks - 1), 0)),
            pl.BlockSpec((parts, 16, part), lambda n: (0, rows // 16, 0)),
            pl.BlockSpec((width, tile), lambda n: (0, jnp.maximum(n - chunks, 0))),
            hbm,
            hbm,
        ],
        out_specs=(hbm, smem),
        scratch_shapes=[
            pltpu.VMEM((sampled, *block), jnp.bfloat16),
            pltpu.VMEM(targets.shape, jnp.bfloat16),
            pltpu.VMEM((slots, *block), jnp.bfloat16),
            pltpu.VMEM((rows, width), jnp.bfloat16),
            pltpu.VMEM((sampled, *block), jnp.float32),
            pltpu.SemaphoreType.DMA((2,)),
        ],
        compiler_params=pltpu.CompilerParams(vmem_limit_bytes=VMEM_BYTES),
        cost_estimate=pl.CostEstimate(
            flops=2 * rows * width * columns, bytes_accessed=18 << 20, transcendentals=rows
        ),
        name="base_gap",
    )(ids, slot_of, gathered, gathered, frozen, own, targets)


def trainer_kernel(gap, lowered, up, facts, grad_up, back, loss):
    step = pl.program_id(0)
    rank, columns = up.shape
    lanes = facts.shape[1]
    low = lowered[...]
    up_map = up[...]
    facts_now = facts[...]
    distance = gap[...].astype(jnp.float32) + lax.dot_general(
        low, up_map, CONTRACT_FIRST, preferred_element_type=jnp.float32
    )
    output_grad = (facts_now[:, NB : NB + 1] * distance).astype(jnp.bfloat16)
    squares = jnp.sum(distance * distance, axis=1, keepdims=True)
    loss[...] = jnp.zeros(loss.shape, jnp.float32)
    loss[0:1, 0:lanes] = jnp.sum(facts_now * squares, axis=0, keepdims=True)
    back[0:rank] = lax.dot_general(
        up_map, output_grad, CONTRACT_LAST, preferred_element_type=jnp.float32
    )
    back[rank:] = loss[...]
    own = jnp.dot(low, output_grad, preferred_element_type=jnp.float32)

    @pl.when(step == 0)
    def _():
        grad_up[...] = own

    @pl.when(step > 0)
    def _():
        grad_up[...] += own


def trainer_step(gap, lowered, up, facts):
    rows, columns = gap.shape
    rank = up.shape[0]
    lanes = facts.shape[1]
    chunk = 256
    return pl.pallas_call(
        trainer_kernel,
        grid=(rows // chunk,),
        out_shape=(
            jax.ShapeDtypeStruct((rank, columns), jnp.float32),
            jax.ShapeDtypeStruct((rank + 8, rows), jnp.float32),
        ),
        in_specs=[
            pl.BlockSpec((chunk, columns), lambda i: (i, 0)),
            pl.BlockSpec((rank, chunk), lambda i: (0, i)),
            pl.BlockSpec((rank, columns), lambda i: (0, 0)),
            pl.BlockSpec((chunk, lanes), lambda i: (i, 0)),
        ],
        out_specs=(
            pl.BlockSpec((rank, columns), lambda i: (0, 0)),
            pl.BlockSpec((rank + 8, chunk), lambda i: (0, i)),
        ),
        scratch_shapes=[pltpu.VMEM((8, chunk), jnp.float32)],
        compiler_params=pltpu.CompilerParams(vmem_limit_bytes=VMEM_BYTES),
        cost_estimate=pl.CostEstimate(
            flops=6 * rows * rank * columns, bytes_accessed=4 << 20, transcendentals=0
        ),
        name="trainer_step",
    )(gap, lowered, up, facts)


def on_device(
    pool_inputs,
    pool_targets,
    frozen,
    gain,
    adapter_down,
    adapter_up,
    sample_ids,
    buckets,
    lengths,
    destinations,
    competence,
):
    trainers = lax.axis_size(DP)
    parts = lax.axis_size("mp")
    sampled = sample_ids.shape[0]
    _, block_len, part = pool_inputs.shape
    width = frozen.shape[0]
    slots = trainers * PER_PAIR
    rows = slots * block_len
    per_peer = PER_PAIR * block_len
    down_map = adapter_down[0]
    up_map = adapter_up[0]
    bucket_range = jnp.arange(NB, dtype=jnp.int32)

    send_x, own_x, slot_of = route(
        sample_ids, destinations[:, 0], buckets, lengths, pool_inputs, gain, trainers
    )
    got_x = lax.all_to_all(send_x, DP, 0, 0, tiled=True)
    gathered = lax.all_gather(own_x.reshape(-1, part), "mp")
    send_gap, done = base_gap_slots(sample_ids, slot_of, gathered, own_x, frozen, pool_targets)
    got_gap = lax.all_to_all(
        send_gap.reshape(trainers, per_peer, part), DP, 0, 0, tiled=True
    )

    got_info = got_x[:, -1, 0, : 2 * PER_PAIR].astype(jnp.float32).astype(jnp.int32)
    got_counts = got_x[:, -1, 1:3, :NB].astype(jnp.float32)
    counts = jnp.sum(16.0 * got_counts[:, 0] + got_counts[:, 1], axis=0)
    floor_counts = jnp.maximum(counts, 1.0)
    weights = jax.nn.sigmoid(
        SHARPNESS * (competence[0] - (bucket_range.astype(jnp.float32) + 0.5) / NB)
    )
    row_bucket = jnp.repeat(got_info[:, :PER_PAIR].reshape(slots), block_len)
    row_length = jnp.repeat(got_info[:, PER_PAIR:].reshape(slots), block_len)
    live = (jnp.arange(rows, dtype=jnp.int32) % block_len < row_length).astype(jnp.float32)
    onehot = (row_bucket[:, None] == bucket_range[None, :]).astype(jnp.float32) * live[:, None]
    coefficient = 2.0 * jnp.sum(onehot * (weights / floor_counts)[None, :], axis=1)
    facts = jnp.concatenate(
        [onehot, coefficient[:, None], jnp.zeros((rows, 128 - NB - 1), jnp.float32)], axis=1
    )

    mean_squares = over_parts(row_squares(got_x, done), "mp") / width
    normed, latent_part = latents(got_x, mean_squares, gain, down_map)
    lowered = (ADAPTER_SCALING * over_parts(latent_part, "mp")).astype(jnp.bfloat16)

    grad_up, back_part = trainer_step(got_gap.reshape(rows, part), lowered, up_map, facts)
    back = over_parts(back_part, "mp")
    rank = up_map.shape[0]
    own_loss = jnp.sum(back[rank].reshape(-1, 256)[:, :NB], axis=0)
    loss_sum = jnp.sum(
        lax.all_to_all(jnp.broadcast_to(own_loss, (trainers, 1, NB)), DP, 0, 0, tiled=True),
        axis=(0, 1),
    )
    lowered_gradient = (ADAPTER_SCALING * back[:rank]).astype(jnp.bfloat16)
    grad_down = jnp.dot(lowered_gradient, normed, preferred_element_type=jnp.float32)
    bucket_loss = loss_sum / (floor_counts * width)
    progress = jnp.sum(weights * bucket_loss) / jnp.sum(bucket_loss)
    competence_next = competence + 0.5 * (1.0 - competence) * progress
    return (grad_down[None], grad_up[None], bucket_loss, competence_next)


def solution(mesh):
    split = Mesh(mesh.devices.reshape(4, 8, 2, mesh.shape["mp"]), DP_MP)
    placed = (
        P(DP, None, "mp"),
        P(DP, None, "mp"),
        P(None, "mp"),
        P("mp"),
        P(DP, None, "mp"),
        P(DP, None, "mp"),
        P(DP),
        P(DP),
        P(DP),
        P(DP, None),
        P(),
    )
    return jax.shard_map(
        on_device,
        mesh=split,
        in_specs=placed,
        out_specs=(P(DP, None, "mp"), P(DP, None, "mp"), P(), P()),
        check_vma=False,
    )
```

time: 205 us -> 196 us (0.956)
  blocking collectives: 37.2 us -> 0 us
  waiting for transfers between devices: 77.5 us -> 92.9 us
  starting transfers between devices: 27.1 us -> 38.4 us
  Pallas kernels: 31.1 us -> 34 us
    all_to_all x2 -> x0, blocking collectives: 37.2 us -> none  [the longest x1 22.1 us: on_device(): lax.all_to_all(message[:, None, :], DP, 0, 0, tiled=True)[:, 0, :]]
    all_gather x1, waiting for transfers between devices: 26.5 us -> 42.7 us  [on_device(): gathered = lax.all_gather(own_x.reshape(-1, part), 'mp')]
    all_to_all x1 -> x2, starting transfers between devices: 5.59 us -> 18.9 us  [the longest x1 13.2 us: on_device(): got_x = lax.all_to_all(send_x, DP, 0, 0, tiled=True)]
    ppermute x12 -> x9, starting transfers between devices: 15.5 us -> 8.66 us  [over_parts(): lax.ppermute(value, axis, [(i, i ^ distance) for i in range(peers)])]
    all_to_all x1, starting transfers between devices: 6.01 us -> 10.9 us  [on_device(): lax.all_to_all(send_gap.reshape(trainers, per_peer, part), DP, 0, 0, tile...]
    ppermute x12 -> x9, waiting for transfers between devices: 23.7 us -> 28.4 us  [over_parts(): lax.ppermute(value, axis, [(i, i ^ distance) for i in range(peers)])]
    all_to_all x1 -> x2, waiting for transfers between devices: 10.5 us -> 6.51 us  [the longest x1 6.51 us: on_device(): lax.all_to_all(jnp.broadcast_to(own_loss, (trainers, 1, NB)), DP, 0, 0, t...]
    pallas_call x3 -> x4, Pallas kernels: 25.5 us -> 29.1 us  [the longest x1 13.5 us: base_gap_slots(): pl.pallas_call(gap_kernel, grid=(chunks + columns // tile,), out_shape=(j...]
  transfers between devices with their start and end apart: 15 -> 13, of which waited for: 11 -> 9; matrix products, arithmetic and copies ran while one was open for 5% -> 5% of each run, Pallas kernels for 9% -> 11%
where the time goes in v5:
time: 196 us; the launch traced here: 195 us
  waiting for transfers between devices  92.9 us (47%)
  starting transfers between devices  38.4 us (20%)
  Pallas kernels  34 us (17%)
  between operations  17.2 us (9%)
  other arithmetic  7.75 us (4%)
  matrix products  2.78 us (1%)
    all_gather x1, waiting for transfers between devices, on_device(): gathered = lax.all_gather(own_x.reshape(-1, part), 'mp')  42.7 us
    ppermute x9, waiting for transfers between devices, over_parts(): lax.ppermute(value, axis, [(i, i ^ distance) for i in range(peers)])  28.4 us
    all_to_all x1, waiting for transfers between devices, on_device(): lax.all_to_all(send_gap.reshape(trainers, per_peer, part), DP, 0, 0, tile...  15.2 us
    pallas_call x1, Pallas kernels, base_gap_slots(): pl.pallas_call(gap_kernel, grid=(chunks + columns // tile,), out_shape=(j...  13.5 us
    all_to_all x1, starting transfers between devices, on_device(): got_x = lax.all_to_all(send_x, DP, 0, 0, tiled=True)  13.2 us
    all_to_all x1, starting transfers between devices, on_device(): lax.all_to_all(send_gap.reshape(trainers, per_peer, part), DP, 0, 0, tile...  10.9 us
    ppermute x9, starting transfers between devices, over_parts(): lax.ppermute(value, axis, [(i, i ^ distance) for i in range(peers)])  8.66 us
    pallas_call x1, Pallas kernels, route(): pl.pallas_call(route_kernel, out_shape=(jax.ShapeDtypeStruct(message, poo...  6.94 us
  transfers between devices with their start and end apart: 13, of which 9 were waited for; matrix products, arithmetic and copies ran while one was open for 5% of the time, Pallas kernels for 11%

profile of v5, /device:TPU:1, one launch (start us, length us, event | category | flops | bytes accessed | tf_op | source)
XLA Modules:
  0.0 194.7 jit_solution(8397206345195911247)
XLA Ops:
  7.2 6.9 %route.1 = (bf16[64,17,8,128]{3,2,1,0:T(8,128)(2,1)}, bf16[66,8,1024]{2,1,0:T(8,128)(2,1)}, s32[128]{0:T(128)}) custom-call(s32[64]{0:T(128)} %ids.1, s32[64]{0:T(128)} %bitcast.30, s32[128]{0:T(128)} %buckets_in.1, s32[128]{0:T(128)} %lengths_in.1, bf16[128,8,1024]{2,1,0:T(8,128)(2,1)} %pool_in.1, f32[1,1024]{1,0:T(1,128)} %bitcast.27), custom_call_target="tpu_custom_call" | custom-call | bytes 5242880 | tf_op jit(solution)/shard_map/route/pallas_call | solution.py:218
  14.2 13.2 %all-to-all-start.1 = ((bf16[64,17,8,128]{3,2,1,0:T(8,128)(2,1)}), bf16[64,17,8,128]{3,2,1,0:T(8,128)(2,1)}, u32[]{:S(2)}, u32[]{:S(2)}) async-start(bf16[64,17,8,128]{3,2,1,0:T(8,128)(2,1)} %get-tuple-element.16), calls=%async_computation.1 | async-start | bytes 4456448 | tf_op jit(solution)/shard_map/all_to_all | solution.py:444
  27.4 42.7 %all-gather.2.cloned.1.call-done.gathered.pieces = bf16[4,528,1024]{2,1,0:T(8,128)(2,1)} async-done(((bf16[1,528,1024]{2,1,0:T(8,128)(2,1)}), bf16[4,528,1024]{2,1,0:T(8,128)(2,1)}) %all-gather.2.cloned.1.call-update) | async-done | bytes 4325392 | tf_op jit(solution)/shard_map/all_gather | solution.py:445
  70.1 13.5 %base_gap.1 = (bf16[128,8,1024]{2,1,0:T(8,128)(2,1)}, f32[1]{0:T(128)}) custom-call(s32[64]{0:T(128)} %ids.1, s32[128]{0:T(128)} %get-tuple-element.13.slot_of, bf16[4,528,1024]{2,1,0:T(8,128)(2,1)} %all-gather.2.cloned.1.call-done.gathered.pieces, bf16[4,528,1024]{2,1,0:T(8,128)(2,1)} %all-gather.2.cloned.1.call-done.gathered.pieces, ...), custom_call_target="tpu_custom_call" | custom-call | flops 4294967296 | bytes 18874368 | tf_op jit(solution)/shard_map/base_gap/pallas_call | solution.py:323
  83.6 10.9 %all-to-all-start = ((bf16[64,16,1024]{2,1,0:T(8,128)(2,1)}), bf16[64,16,1024]{2,1,0:T(8,128)(2,1)}, u32[]{:S(2)}, u32[]{:S(2)}) async-start(bf16[64,16,1024]{2,1,0:T(8,128)(2,1)} %bitcast.23), calls=%async_computation | async-start | bytes 4194304 | tf_op jit(solution)/shard_map/all_to_all | solution.py:447
  95.2 0.9 fusion.5
  96.8 0.9 fusion.4
  97.9 4.3 %row_squares.1 = f32[1,1024]{1,0:T(1,128)} custom-call(bf16[64,17,8,128]{3,2,1,0:T(8,128)(2,1)} %all-to-all-done.1.packed, f32[1]{0:T(128)} %get-tuple-element.17.done), custom_call_target="tpu_custom_call" | custom-call | flops 4194304 | bytes 2097152 | tf_op jit(solution)/shard_map/row_squares/pallas_call | solution.py:50
  102.2 1.8 collective-permute-start.1
  104.0 1.2 collective-permute-start.2
  105.7 1.1 collective-permute-done.1
  106.8 1.5 collective-permute-done.2
  108.3 1.3 add_multiply_fusion.squares
  109.6 4.4 %latents.1 = (bf16[1024,1024]{1,0:T(8,128)(2,1)}, f32[64,1024]{1,0:T(8,128)}) custom-call(bf16[64,17,8,128]{3,2,1,0:T(8,128)(2,1)} %all-to-all-done.1.packed, f32[1,1024]{1,0:T(1,128)} %add_multiply_fusion.squares, f32[1,1024]{1,0:T(1,128)} %bitcast.28, bf16[64,1024]{1,0:T(8,128)(2,1)} %bitcast.25), custom_call_target="tpu_custom_call" | custom-call | flops 134217728 | bytes 4194304 | tf_op jit(solution)/shard_map/latents/pallas_call | solution.py:85
  113.9 1.3 collective-permute-start.4
  115.2 1.2 collective-permute-start.5
  116.9 1.0 maximum_maximum_fusion.facts
  117.9 4.0 %collective-permute-done.4 = f32[64,1024]{1,0:T(8,128)S(1)} collective-permute-done((f32[64,1024]{1,0:T(8,128)}, f32[64,1024]{1,0:T(8,128)S(1)}, u32[]{:S(2)}, u32[]{:S(2)}) %collective-permute-start.4) | collective-permute-done | bytes 262176 | tf_op jit(solution)/shard_map/ppermute | solution.py:25
  121.9 7.8 %collective-permute-done.5 = f32[64,1024]{1,0:T(8,128)S(1)} collective-permute-done((f32[64,1024]{1,0:T(8,128)}, f32[64,1024]{1,0:T(8,128)S(1)}, u32[]{:S(2)}, u32[]{:S(2)}) %collective-permute-start.5) | collective-permute-done | bytes 262176 | tf_op jit(solution)/shard_map/ppermute | solution.py:25
  129.7 0.7 multiply_convert_fusion.lowered
  130.4 15.2 %all-to-all-done = bf16[64,16,1024]{2,1,0:T(8,128)(2,1)} async-done(((bf16[64,16,1024]{2,1,0:T(8,128)(2,1)}), bf16[64,16,1024]{2,1,0:T(8,128)(2,1)}, u32[]{:S(2)}, u32[]{:S(2)}) %all-to-all-start) | async-done | bytes 2097184 | tf_op jit(solution)/shard_map/all_to_all | solution.py:447
  145.6 4.9 %trainer_step.1 = (f32[64,1024]{1,0:T(8,128)}, f32[72,1024]{1,0:T(8,128)}) custom-call(bf16[1024,1024]{1,0:T(8,128)(2,1)} %bitcast.4.gap, bf16[64,1024]{1,0:T(8,128)(2,1)} %multiply_convert_fusion.lowered, bf16[64,1024]{1,0:T(8,128)(2,1)} %bitcast.26, f32[1024,128]{1,0:T(8,128)} %maximum_maximum_fusion.facts), custom_call_target="tpu_custom_call" | custom-call | flops 402653184 | bytes 4194304 | tf_op jit(solution)/shard_map/trainer_step/pallas_call | solution.py:390
  150.5 1.8 collective-permute-start.7
  152.3 1.2 collective-permute-start.8
  153.5 7.0 %collective-permute-done.7 = f32[72,1024]{1,0:T(8,128)S(1)} collective-permute-done((f32[72,1024]{1,0:T(8,128)}, f32[72,1024]{1,0:T(8,128)S(1)}, u32[]{:S(2)}, u32[]{:S(2)}) %collective-permute-start.7) | collective-permute-done | bytes 294944 | tf_op jit(solution)/shard_map/ppermute | solution.py:25
  160.5 7.0 %collective-permute-done.8 = f32[72,1024]{1,0:T(8,128)S(1)} collective-permute-done((f32[72,1024]{1,0:T(8,128)}, f32[72,1024]{1,0:T(8,128)S(1)}, u32[]{:S(2)}, u32[]{:S(2)}) %collective-permute-start.8) | collective-permute-done | bytes 294944 | tf_op jit(solution)/shard_map/ppermute | solution.py:25
  167.5 1.0 add_add_fusion
  168.6 0.6 broadcast_in_dim.32
  169.2 5.7 %all-to-all-start.2 = ((f32[64,1,16]{2,1,0:T(1,128)}), f32[64,1,16]{2,1,0:T(1,128)S(1)}, u32[]{:S(2)}, u32[]{:S(2)}) async-start(f32[64,1,16]{2,1,0:T(1,128)} %broadcast_in_dim.32), calls=%async_computation.2 | async-start | bytes 65536 | tf_op jit(solution)/shard_map/all_to_all | solution.py:476
  175.0 2.8 %convolution_bitcast_fusion = f32[1,64,1024]{2,1,0:T(8,128)} fusion(bf16[1024,1024]{1,0:T(8,128)(2,1)} %get-tuple-element.20, f32[72,1024]{1,0:T(8,128)S(1)} %add_add_fusion), kind=kOutput, calls=%fused_computation | convolution fusion | flops 134348800 | bytes 2621440 | tf_op jit(solution)/shard_map/dot_general | solution.py:480
  177.7 6.5 %all-to-all-done.2 = f32[64,1,16]{2,1,0:T(1,128)S(1)} async-done(((f32[64,1,16]{2,1,0:T(1,128)}), f32[64,1,16]{2,1,0:T(1,128)S(1)}, u32[]{:S(2)}, u32[]{:S(2)}) %all-to-all-start.2) | async-done | bytes 4128 | tf_op jit(solution)/shard_map/all_to_all | solution.py:476
  184.3 1.1 fusion.14
  (30 shorter events, 2.1 us)
Async XLA Ops:
  7.2 62.9 %all-gather.2.cloned.1.call-start = ((), (), s32[]{:S(2)}) async-start(), calls=%async_computation.3 | async-start | bytes 5406720 | tf_op jit(solution)/shard_map/all_gather | solution.py:445
  14.2 69.4 %all-to-all-start.1 = ((bf16[64,17,8,128]{3,2,1,0:T(8,128)(2,1)}), bf16[64,17,8,128]{3,2,1,0:T(8,128)(2,1)}, u32[]{:S(2)}, u32[]{:S(2)}) async-start(bf16[64,17,8,128]{3,2,1,0:T(8,128)(2,1)} %get-tuple-element.16), calls=%async_computation.1 | async-start | bytes 4456448 | tf_op jit(solution)/shard_map/all_to_all | solution.py:444
  83.6 62.0 %all-to-all-start = ((bf16[64,16,1024]{2,1,0:T(8,128)(2,1)}), bf16[64,16,1024]{2,1,0:T(8,128)(2,1)}, u32[]{:S(2)}, u32[]{:S(2)}) async-start(bf16[64,16,1024]{2,1,0:T(8,128)(2,1)} %bitcast.23), calls=%async_computation | async-start | bytes 4194304 | tf_op jit(solution)/shard_map/all_to_all | solution.py:447
  102.2 4.6 %collective-permute-start.1 = (f32[1,1024]{1,0:T(1,128)}, f32[1,1024]{1,0:T(1,128)S(1)}, u32[]{:S(2)}, u32[]{:S(2)}) collective-permute-start(f32[1,1024]{1,0:T(1,128)} %row_squares.1), channel_id=1, source_target_pairs={{0,2},{1,3},{2,0},{3,1},{4,6},{5,7},{6,4},{7,5},{8,10},{9,11},{10,... | collective-permute-start | bytes 12296 | tf_op jit(solution)/shard_map/ppermute | solution.py:25
  104.0 4.3 %collective-permute-start.2 = (f32[1,1024]{1,0:T(1,128)}, f32[1,1024]{1,0:T(1,128)S(1)}, u32[]{:S(2)}, u32[]{:S(2)}) collective-permute-start(f32[1,1024]{1,0:T(1,128)} %row_squares.1), channel_id=1, source_target_pairs={{0,3},{1,2},{2,1},{3,0},{4,7},{5,6},{6,5},{7,4},{8,11},{9,10},{10,... | collective-permute-start | bytes 12296 | tf_op jit(solution)/shard_map/ppermute | solution.py:25
  105.2 3.1 %collective-permute-start = (f32[1,1024]{1,0:T(1,128)}, f32[1,1024]{1,0:T(1,128)S(1)}, u32[]{:S(2)}, u32[]{:S(2)}) collective-permute-start(f32[1,1024]{1,0:T(1,128)} %row_squares.1), channel_id=1, source_target_pairs={{0,1},{1,0},{2,3},{3,2},{4,5},{5,4},{6,7},{7,6},{8,9},{9,8},{10,11... | collective-permute-start | bytes 12296 | tf_op jit(solution)/shard_map/ppermute | solution.py:25
  113.9 15.8 %copy-start = (f32[64,1024]{1,0:T(8,128)S(1)}, f32[64,1024]{1,0:T(8,128)}, u32[]{:S(2)}) copy-start(f32[64,1024]{1,0:T(8,128)} %get-tuple-element.18) | copy-start | bytes 786436
  113.9 8.0 %collective-permute-start.4 = (f32[64,1024]{1,0:T(8,128)}, f32[64,1024]{1,0:T(8,128)S(1)}, u32[]{:S(2)}, u32[]{:S(2)}) collective-permute-start(f32[64,1024]{1,0:T(8,128)} %get-tuple-element.18), channel_id=1, source_target_pairs={{0,2},{1,3},{2,0},{3,1},{4,6},{5,7},{6,4},{7,5},{8,10},{9,11},{10,... | collective-permute-start | bytes 786440 | tf_op jit(solution)/shard_map/ppermute | solution.py:25
  115.2 14.4 %collective-permute-start.5 = (f32[64,1024]{1,0:T(8,128)}, f32[64,1024]{1,0:T(8,128)S(1)}, u32[]{:S(2)}, u32[]{:S(2)}) collective-permute-start(f32[64,1024]{1,0:T(8,128)} %get-tuple-element.18), channel_id=1, source_target_pairs={{0,3},{1,2},{2,1},{3,0},{4,7},{5,6},{6,5},{7,4},{8,11},{9,10},{10,... | collective-permute-start | bytes 786440 | tf_op jit(solution)/shard_map/ppermute | solution.py:25
  116.4 13.3 %collective-permute-start.3 = (f32[64,1024]{1,0:T(8,128)}, f32[64,1024]{1,0:T(8,128)S(1)}, u32[]{:S(2)}, u32[]{:S(2)}) collective-permute-start(f32[64,1024]{1,0:T(8,128)} %get-tuple-element.18), channel_id=1, source_target_pairs={{0,1},{1,0},{2,3},{3,2},{4,5},{5,4},{6,7},{7,6},{8,9},{9,8},{10,11... | collective-permute-start | bytes 786440 | tf_op jit(solution)/shard_map/ppermute | solution.py:25
  150.5 10.0 %collective-permute-start.7 = (f32[72,1024]{1,0:T(8,128)}, f32[72,1024]{1,0:T(8,128)S(1)}, u32[]{:S(2)}, u32[]{:S(2)}) collective-permute-start(f32[72,1024]{1,0:T(8,128)} %get-tuple-element.19), channel_id=1, source_target_pairs={{0,2},{1,3},{2,0},{3,1},{4,6},{5,7},{6,4},{7,5},{8,10},{9,11},{10,... | collective-permute-start | bytes 884744 | tf_op jit(solution)/shard_map/ppermute | solution.py:25
  152.3 15.2 %collective-permute-start.8 = (f32[72,1024]{1,0:T(8,128)}, f32[72,1024]{1,0:T(8,128)S(1)}, u32[]{:S(2)}, u32[]{:S(2)}) collective-permute-start(f32[72,1024]{1,0:T(8,128)} %get-tuple-element.19), channel_id=1, source_target_pairs={{0,3},{1,2},{2,1},{3,0},{4,7},{5,6},{6,5},{7,4},{8,11},{9,10},{10,... | collective-permute-start | bytes 884744 | tf_op jit(solution)/shard_map/ppermute | solution.py:25
  153.5 14.0 %collective-permute-start.6 = (f32[72,1024]{1,0:T(8,128)}, f32[72,1024]{1,0:T(8,128)S(1)}, u32[]{:S(2)}, u32[]{:S(2)}) collective-permute-start(f32[72,1024]{1,0:T(8,128)} %get-tuple-element.19), channel_id=1, source_target_pairs={{0,1},{1,0},{2,3},{3,2},{4,5},{5,4},{6,7},{7,6},{8,9},{9,8},{10,11... | collective-permute-start | bytes 884744 | tf_op jit(solution)/shard_map/ppermute | solution.py:25
  169.2 15.0 %all-to-all-start.2 = ((f32[64,1,16]{2,1,0:T(1,128)}), f32[64,1,16]{2,1,0:T(1,128)S(1)}, u32[]{:S(2)}, u32[]{:S(2)}) async-start(f32[64,1,16]{2,1,0:T(1,128)} %broadcast_in_dim.32), calls=%async_computation.2 | async-start | bytes 65536 | tf_op jit(solution)/shard_map/all_to_all | solution.py:476
Sparse Core Ops, SparseCore 0:
  14.3 55.7 all-gather.1

commit v6 on v5

--- a/solution.py
+++ b/solution.py
@@ -19,13 +19,20 @@
 CONTRACT_FIRST = (((0,), (0,)), ((), ()))
 
 
+def swap(value, axis, distance):
+    peers = lax.axis_size(axis)
+    return lax.ppermute(value, axis, [(i, i ^ distance) for i in range(peers)])
+
+
 def over_parts(value, axis):
-    peers = lax.axis_size(axis)
-    others = [
-        lax.ppermute(value, axis, [(i, i ^ distance) for i in range(peers)])
-        for distance in range(1, peers)
-    ]
-    return (value + others[0]) + (others[1] + others[2])
+    pair = value + swap(value, axis, 1)
+    return pair + swap(pair, axis, 3)
+
+
+def from_parts(value, axis, cut):
+    near = swap(value, axis, 1)
+    other = swap(value, axis, 3)
+    return near, other, swap(other[:cut], axis, 1), swap(near[cut:], axis, 3)
 
 
 def lane_group(packed, group, groups):
@@ -245,14 +252,16 @@
 
 
 def gap_kernel(
-    ids, slot_of, gathered, pieces, frozen, own_in, targets_in,
+    ids, slot_of, order, mine, near, other, far_first, far_last,
+    mine_gain, near_gain, other_gain, far_gain, frozen, own_in, targets_in,
     send_out, done, own, targets, send, normed, gap, sem,
 ):
     step = pl.program_id(0)
-    parts, chunk, part = gathered.shape
+    chunk, part = mine.shape
     sampled, block_len, columns = gap.shape
     chunks = sampled * block_len // chunk
-    width = frozen.shape[1]
+    width, tile = frozen.shape
+    far_first_chunks = chunks // 2
     slots = send.shape[0]
     own_copy = pltpu.make_async_copy(own_in.at[pl.ds(0, sampled)], own, sem.at[0])
     target_copy = pltpu.make_async_copy(targets_in, targets, sem.at[1])
@@ -271,17 +280,26 @@
 
     @pl.when(step < chunks)
     def _():
-        total = jnp.zeros((chunk, 1), jnp.float32)
-        for p in range(parts):
-            x = gathered[p].astype(jnp.float32)
-            total = total + jnp.sum(x * x, axis=1, keepdims=True)
-        inverse = lax.rsqrt(total / (parts * part) + RMS_EPSILON)
+        first = step < far_first_chunks
+        rows_of = (
+            lambda: mine[...].astype(jnp.float32),
+            lambda: near[...].astype(jnp.float32),
+            lambda: jnp.where(first, far_first[...], far_last[...]).astype(jnp.float32),
+            lambda: other[...].astype(jnp.float32),
+        )
+        gains = (mine_gain, near_gain, far_gain, other_gain)
+        squares = jnp.zeros((chunk, part), jnp.float32)
+        for get in rows_of:
+            x = get()
+            squares = squares + x * x
+        total = jnp.sum(squares, axis=1, keepdims=True)
+        inverse = lax.rsqrt(total / width + RMS_EPSILON)
         at = pl.ds(pl.multiple_of(step * chunk, chunk), chunk)
-        for p in range(parts):
-            three = pieces[p].astype(jnp.float32)
+        for p, (get, pieces) in enumerate(zip(rows_of, gains)):
+            three = pieces[...].astype(jnp.float32)
             gain = three[0:1] + three[1:2] + three[2:3]
-            x = gathered[p].astype(jnp.float32)
-            normed[at, p * part : (p + 1) * part] = (x * inverse * gain).astype(jnp.bfloat16)
+            to = pl.ds(pl.multiple_of(order[p] * part, part), part)
+            normed[at, to] = (get() * inverse * gain).astype(jnp.bfloat16)
 
     @pl.when(step == chunks)
     def _():
@@ -291,9 +309,9 @@
     @pl.when(step >= chunks)
     def _():
         projected = jnp.dot(normed[...], frozen[...], preferred_element_type=jnp.float32)
-        at = pl.ds(pl.multiple_of((step - chunks) * width, width), width)
+        at = pl.ds(pl.multiple_of((step - chunks) * tile, tile), tile)
         x = own[:, :, at].astype(jnp.float32)
-        gap[:, :, at] = x + projected.reshape(sampled, block_len, width)
+        gap[:, :, at] = x + projected.reshape(sampled, block_len, tile)
 
     @pl.when(step == pl.num_programs(0) - 1)
     def _():
@@ -308,8 +326,9 @@
         copy.wait()
 
 
-def base_gap_slots(ids, slot_of, gathered, own, frozen, targets):
-    parts, _, part = gathered.shape
+def base_gap_slots(ids, slot_of, order, own, received, frozen, targets):
+    near, other, far_first, far_last = received
+    part = near.shape[1]
     width, columns = frozen.shape
     slots = slot_of.shape[0]
     sampled = ids.shape[0]
@@ -318,6 +337,10 @@
     tile = 256
     chunk = 128
     chunks = rows // chunk
+    half = chunks // 2
+    all_rows = pl.BlockSpec((chunk, part), lambda n: (jnp.minimum(n, chunks - 1), 0))
+    all_gain = pl.BlockSpec((16, part), lambda n: (rows // 16, 0))
+    mine = own.reshape(-1, part)
     smem = pl.BlockSpec(memory_space=pltpu.SMEM)
     hbm = pl.BlockSpec(memory_space=pltpu.HBM)
     return pl.pallas_call(
@@ -330,8 +353,16 @@
         in_specs=[
             smem,
             smem,
-            pl.BlockSpec((parts, chunk, part), lambda n: (0, jnp.minimum(n, chunks - 1), 0)),
-            pl.BlockSpec((parts, 16, part), lambda n: (0, rows // 16, 0)),
+            smem,
+            all_rows,
+            all_rows,
+            all_rows,
+            pl.BlockSpec((chunk, part), lambda n: (jnp.minimum(n, half - 1), 0)),
+            pl.BlockSpec((chunk, part), lambda n: (jnp.clip(n - half, 0, half - 1), 0)),
+            all_gain,
+            all_gain,
+            all_gain,
+            pl.BlockSpec((16, part), lambda n: (rows // 32, 0)),
             pl.BlockSpec((width, tile), lambda n: (0, jnp.maximum(n - chunks, 0))),
             hbm,
             hbm,
@@ -350,13 +381,14 @@
             flops=2 * rows * width * columns, bytes_accessed=18 << 20, transcendentals=rows
         ),
         name="base_gap",
-    )(ids, slot_of, gathered, gathered, frozen, own, targets)
+    )(
+        ids, slot_of, order, mine, near, other, far_first, far_last,
+        mine, near, other, far_last, frozen, own, targets,
+    )
 
 
 def trainer_kernel(gap, lowered, up, facts, grad_up, back, loss):
     step = pl.program_id(0)
-    rank, columns = up.shape
-    lanes = facts.shape[1]
     low = lowered[...]
     up_map = up[...]
     facts_now = facts[...]
@@ -365,21 +397,21 @@
     )
     output_grad = (facts_now[:, NB : NB + 1] * distance).astype(jnp.bfloat16)
     squares = jnp.sum(distance * distance, axis=1, keepdims=True)
-    loss[...] = jnp.zeros(loss.shape, jnp.float32)
-    loss[0:1, 0:lanes] = jnp.sum(facts_now * squares, axis=0, keepdims=True)
-    back[0:rank] = lax.dot_general(
+    part = jnp.sum(facts_now * squares, axis=0, keepdims=True)
+    back[...] = lax.dot_general(
         up_map, output_grad, CONTRACT_LAST, preferred_element_type=jnp.float32
     )
-    back[rank:] = loss[...]
     own = jnp.dot(low, output_grad, preferred_element_type=jnp.float32)
 
     @pl.when(step == 0)
     def _():
         grad_up[...] = own
+        loss[...] = part
 
     @pl.when(step > 0)
     def _():
         grad_up[...] += own
+        loss[...] += part
 
 
 def trainer_step(gap, lowered, up, facts):
@@ -392,7 +424,8 @@
         grid=(rows // chunk,),
         out_shape=(
             jax.ShapeDtypeStruct((rank, columns), jnp.float32),
-            jax.ShapeDtypeStruct((rank + 8, rows), jnp.float32),
+            jax.ShapeDtypeStruct((rank, rows), jnp.float32),
+            jax.ShapeDtypeStruct((1, lanes), jnp.float32),
         ),
         in_specs=[
             pl.BlockSpec((chunk, columns), lambda i: (i, 0)),
@@ -402,9 +435,9 @@
         ],
         out_specs=(
             pl.BlockSpec((rank, columns), lambda i: (0, 0)),
-            pl.BlockSpec((rank + 8, chunk), lambda i: (0, i)),
-        ),
-        scratch_shapes=[pltpu.VMEM((8, chunk), jnp.float32)],
+            pl.BlockSpec((rank, chunk), lambda i: (0, i)),
+            pl.BlockSpec((1, lanes), lambda i: (0, 0)),
+        ),
         compiler_params=pltpu.CompilerParams(vmem_limit_bytes=VMEM_BYTES),
         cost_estimate=pl.CostEstimate(
             flops=6 * rows * rank * columns, bytes_accessed=4 << 20, transcendentals=0
@@ -427,7 +460,6 @@
     competence,
 ):
     trainers = lax.axis_size(DP)
-    parts = lax.axis_size("mp")
     sampled = sample_ids.shape[0]
     _, block_len, part = pool_inputs.shape
     width = frozen.shape[0]
@@ -442,8 +474,12 @@
         sample_ids, destinations[:, 0], buckets, lengths, pool_inputs, gain, trainers
     )
     got_x = lax.all_to_all(send_x, DP, 0, 0, tiled=True)
-    gathered = lax.all_gather(own_x.reshape(-1, part), "mp")
-    send_gap, done = base_gap_slots(sample_ids, slot_of, gathered, own_x, frozen, pool_targets)
+    cut = sampled * block_len // 2
+    received = from_parts(own_x.reshape(-1, part), "mp", cut)
+    order = lax.axis_index("mp") ^ jnp.arange(lax.axis_size("mp"), dtype=jnp.int32)
+    send_gap, done = base_gap_slots(
+        sample_ids, slot_of, order, own_x, received, frozen, pool_targets
+    )
     got_gap = lax.all_to_all(
         send_gap.reshape(trainers, per_peer, part), DP, 0, 0, tiled=True
     )
@@ -468,15 +504,16 @@
     normed, latent_part = latents(got_x, mean_squares, gain, down_map)
     lowered = (ADAPTER_SCALING * over_parts(latent_part, "mp")).astype(jnp.bfloat16)
 
-    grad_up, back_part = trainer_step(got_gap.reshape(rows, part), lowered, up_map, facts)
-    back = over_parts(back_part, "mp")
-    rank = up_map.shape[0]
-    own_loss = jnp.sum(back[rank].reshape(-1, 256)[:, :NB], axis=0)
+    grad_up, back_part, loss_part = trainer_step(
+        got_gap.reshape(rows, part), lowered, up_map, facts
+    )
+    own_loss = over_parts(loss_part, "mp")[:, :NB]
     loss_sum = jnp.sum(
         lax.all_to_all(jnp.broadcast_to(own_loss, (trainers, 1, NB)), DP, 0, 0, tiled=True),
         axis=(0, 1),
     )
-    lowered_gradient = (ADAPTER_SCALING * back[:rank]).astype(jnp.bfloat16)
+    back = over_parts(back_part, "mp")
+    lowered_gradient = (ADAPTER_SCALING * back).astype(jnp.bfloat16)
     grad_down = jnp.dot(lowered_gradient, normed, preferred_element_type=jnp.float32)
     bucket_loss = loss_sum / (floor_counts * width)
     progress = jnp.sum(weights * bucket_loss) / jnp.sum(bucket_loss)

time: 196 us -> 185 us (0.944)
  between operations: 17.2 us -> 3.92 us
  waiting for transfers between devices: 92.9 us -> 83.3 us
  starting transfers between devices: 38.4 us -> 46.1 us
  local copies, waits for them, and re-layouts: 1.66 us -> 3.73 us
  other arithmetic: 7.75 us -> 9.8 us
    all_gather x1 -> x0, waiting for transfers between devices: 42.7 us -> none  [on_device(): gathered = lax.all_gather(own_x.reshape(-1, part), 'mp')]
    ppermute x9 -> x12, waiting for transfers between devices: 28.4 us -> 55.4 us  [swap(): return lax.ppermute(value, axis, [(i, i ^ distance) for i in range(peers)])]
    ppermute x9 -> x12, starting transfers between devices: 8.66 us -> 12.2 us  [swap(): return lax.ppermute(value, axis, [(i, i ^ distance) for i in range(peers)])]
    all_to_all x1, waiting for transfers between devices: 15.2 us -> 18.7 us  [on_device(): lax.all_to_all(send_gap.reshape(trainers, per_peer, part), DP, 0, 0, tile...]
    all_to_all x1, waiting for transfers between devices: 6.51 us -> 9.21 us  [on_device(): lax.all_to_all(jnp.broadcast_to(own_loss, (trainers, 1, NB)), DP, 0, 0, t...]
    add x1 -> x5, other arithmetic: 1.05 us -> 3.32 us  [the longest x4 3.32 us: over_parts(): pair = value + swap(value, axis, 1)]
    all_to_all x1, starting transfers between devices: 5.72 us -> 7.91 us  [on_device(): lax.all_to_all(jnp.broadcast_to(own_loss, (trainers, 1, NB)), DP, 0, 0, t...]
    unnamed x2 -> x10, local copies, waits for them, and re-layouts: 0.01 us -> 2 us
  transfers between devices with their start and end apart: 13 -> 15, of which waited for: 9 -> 10; matrix products, arithmetic and copies ran while one was open for 5% -> 6% of each run, Pallas kernels for 11% -> 12%
where the time goes in v6:
time: 185 us; the launch traced here: 184 us
  waiting for transfers between devices  83.3 us (45%)
  starting transfers between devices  46.1 us (25%)
  Pallas kernels  34.5 us (19%)
  other arithmetic  9.8 us (5%)
  between operations  3.92 us (2%)
  local copies, waits for them, and re-layouts  3.73 us (2%)
  matrix products  2.78 us (2%)
    ppermute x12, waiting for transfers between devices, swap(): return lax.ppermute(value, axis, [(i, i ^ distance) for i in range(peers)])  55.4 us
    all_to_all x1, waiting for transfers between devices, on_device(): lax.all_to_all(send_gap.reshape(trainers, per_peer, part), DP, 0, 0, tile...  18.7 us
    pallas_call x1, Pallas kernels, base_gap_slots(): pl.pallas_call(gap_kernel, grid=(chunks + columns // tile,), out_shape=(j...  14.1 us
    all_to_all x1, starting transfers between devices, on_device(): got_x = lax.all_to_all(send_x, DP, 0, 0, tiled=True)  13.3 us
    all_to_all x1, starting transfers between devices, on_device(): lax.all_to_all(send_gap.reshape(trainers, per_peer, part), DP, 0, 0, tile...  12.7 us
    ppermute x12, starting transfers between devices, swap(): return lax.ppermute(value, axis, [(i, i ^ distance) for i in range(peers)])  12.2 us
    all_to_all x1, waiting for transfers between devices, on_device(): lax.all_to_all(jnp.broadcast_to(own_loss, (trainers, 1, NB)), DP, 0, 0, t...  9.21 us
    all_to_all x1, starting transfers between devices, on_device(): lax.all_to_all(jnp.broadcast_to(own_loss, (trainers, 1, NB)), DP, 0, 0, t...  7.91 us
  transfers between devices with their start and end apart: 15, of which 10 were waited for; matrix products, arithmetic and copies ran while one was open for 6% of the time, Pallas kernels for 12%

profile of v6, /device:TPU:1, one launch (start us, length us, event | category | flops | bytes accessed | tf_op | source)
XLA Modules:
  0.0 184.1 jit_solution(12789953698843178774)
XLA Ops:
  0.6 6.9 %route.1 = (bf16[64,17,8,128]{3,2,1,0:T(8,128)(2,1)}, bf16[66,8,1024]{2,1,0:T(8,128)(2,1)}, s32[128]{0:T(128)}) custom-call(s32[64]{0:T(128)} %ids.1, s32[64]{0:T(128)} %bitcast.35, s32[128]{0:T(128)} %buckets_in.1, s32[128]{0:T(128)} %lengths_in.1, bf16[128,8,1024]{2,1,0:T(8,128)(2,1)} %pool_in.1, f32[1,1024]{1,0:T(1,128)} %bitcast.32), custom_call_target="tpu_custom_call" | custom-call | bytes 5242880 | tf_op jit(solution)/shard_map/route/pallas_call | solution.py:225
  7.5 13.3 %all-to-all-start.1 = ((bf16[64,17,8,128]{3,2,1,0:T(8,128)(2,1)}), bf16[64,17,8,128]{3,2,1,0:T(8,128)(2,1)}, u32[]{:S(2)}, u32[]{:S(2)}) async-start(bf16[64,17,8,128]{3,2,1,0:T(8,128)(2,1)} %get-tuple-element.17), calls=%async_computation.1 | async-start | bytes 4456448 | tf_op jit(solution)/shard_map/all_to_all | solution.py:476
  20.8 1.4 collective-permute-start
  22.2 1.9 %collective-permute-start.1 = (bf16[528,1024]{1,0:T(8,128)(2,1)S(1)}, bf16[528,1024]{1,0:T(8,128)(2,1)S(1)}, u32[]{:S(2)}, u32[]{:S(2)}) collective-permute-start(bf16[528,1024]{1,0:T(8,128)(2,1)S(1)} %bitcast.27), channel_id=1, source_target_pairs={{0,3},{1,2},{2,1},{3,0},{4,7},{5,6},{6,5},{7,4},{8,11},{9,10},{10,... | collective-permute-start | bytes 3244040 | tf_op jit(solution)/shard_map/ppermute | solution.py:24
  24.1 21.8 %collective-permute-done.near.near_gain = bf16[528,1024]{1,0:T(8,128)(2,1)S(1)} collective-permute-done((bf16[528,1024]{1,0:T(8,128)(2,1)S(1)}, bf16[528,1024]{1,0:T(8,128)(2,1)S(1)}, u32[]{:S(2)}, u32[]{:S(2)}) %collective-permute-start) | collective-permute-done | bytes 1081376 | tf_op jit(solution)/shard_map/ppermute | solution.py:24
  46.0 2.8 %collective-permute-start.3 = (bf16[272,1024]{1,0:T(8,128)(2,1)S(1)}, bf16[272,1024]{1,0:T(8,128)(2,1)S(1)}, u32[]{:S(2)}, u32[]{:S(2)}) collective-permute-start(bf16[272,1024]{1,0:T(8,128)(2,1)S(1)} %slice.40), channel_id=1, source_target_pairs={{0,3},{1,2},{2,1},{3,0},{4,7},{5,6},{6,5},{7,4},{8,11},{9,10},{10,... | collective-permute-start | bytes 1671176 | tf_op jit(solution)/shard_map/ppermute | solution.py:24
  48.8 1.0 copy-done.2
  50.3 11.5 %collective-permute-done.2.far_first = bf16[256,1024]{1,0:T(8,128)(2,1)S(1)} collective-permute-done((bf16[256,1024]{1,0:T(8,128)(2,1)S(1)}, bf16[256,1024]{1,0:T(8,128)(2,1)S(1)}, u32[]{:S(2)}, u32[]{:S(2)}) %collective-permute-start.2) | collective-permute-done | bytes 524320 | tf_op jit(solution)/shard_map/ppermute | solution.py:24
  62.8 14.1 %base_gap.1 = (bf16[128,8,1024]{2,1,0:T(8,128)(2,1)}, f32[1]{0:T(128)}) custom-call(s32[64]{0:T(128)} %ids.1, s32[128]{0:T(128)} %get-tuple-element.14.slot_of, s32[4]{0:T(128)} %iota_xor_fusion.order, bf16[528,1024]{1,0:T(8,128)(2,1)} %bitcast.24, bf16[528,1024]{1,0:T(8,128)(2,1)} %copy-done.1, bf16[528,1024]{1,0:T(8,128)(2,1)} %copy-done.2, ...), custom_call_target="tpu_custom_call" | custom-call | flops 4294967296 | bytes 18874368 | tf_op jit(solution)/shard_map/base_gap/pallas_call | solution.py:346
  77.0 12.7 %all-to-all-start = ((bf16[64,16,1024]{2,1,0:T(8,128)(2,1)}), bf16[64,16,1024]{2,1,0:T(8,128)(2,1)}, u32[]{:S(2)}, u32[]{:S(2)}) async-start(bf16[64,16,1024]{2,1,0:T(8,128)(2,1)} %bitcast.28), calls=%async_computation | async-start | bytes 4194304 | tf_op jit(solution)/shard_map/all_to_all | solution.py:483
  90.4 4.3 %row_squares.1 = f32[1,1024]{1,0:T(1,128)} custom-call(bf16[64,17,8,128]{3,2,1,0:T(8,128)(2,1)} %all-to-all-done.1.packed, f32[1]{0:T(128)} %get-tuple-element.18.done), custom_call_target="tpu_custom_call" | custom-call | flops 4194304 | bytes 2097152 | tf_op jit(solution)/shard_map/row_squares/pallas_call | solution.py:57
  96.0 0.9 fusion.2
  98.5 1.1 collective-permute-start.5
  99.7 2.9 %collective-permute-done.5 = f32[1,1024]{1,0:T(1,128)S(1)} collective-permute-done((f32[1,1024]{1,0:T(1,128)S(1)}, f32[1,1024]{1,0:T(1,128)S(1)}, u32[]{:S(2)}, u32[]{:S(2)}) %collective-permute-start.5) | collective-permute-done | bytes 4128 | tf_op jit(solution)/shard_map/ppermute | solution.py:24
  103.1 4.4 %latents.1 = (bf16[1024,1024]{1,0:T(8,128)(2,1)}, f32[64,1024]{1,0:T(8,128)}) custom-call(bf16[64,17,8,128]{3,2,1,0:T(8,128)(2,1)} %all-to-all-done.1.packed, f32[1,1024]{1,0:T(1,128)} %add_multiply_fusion.squares, f32[1,1024]{1,0:T(1,128)} %bitcast.33, bf16[64,1024]{1,0:T(8,128)(2,1)} %bitcast.30), custom_call_target="tpu_custom_call" | custom-call | flops 134217728 | bytes 4194304 | tf_op jit(solution)/shard_map/latents/pallas_call | solution.py:92
  108.3 5.2 %collective-permute-done.6 = f32[64,1024]{1,0:T(8,128)S(1)} collective-permute-done((f32[64,1024]{1,0:T(8,128)}, f32[64,1024]{1,0:T(8,128)S(1)}, u32[]{:S(2)}, u32[]{:S(2)}) %collective-permute-start.6) | collective-permute-done | bytes 262176 | tf_op jit(solution)/shard_map/ppermute | solution.py:24
  113.6 1.0 add.57
  114.5 1.2 collective-permute-start.7
  116.0 1.0 maximum_maximum_fusion.facts
  117.0 4.5 %collective-permute-done.7 = f32[64,1024]{1,0:T(8,128)S(1)} collective-permute-done((f32[64,1024]{1,0:T(8,128)S(1)}, f32[64,1024]{1,0:T(8,128)S(1)}, u32[]{:S(2)}, u32[]{:S(2)}) %collective-permute-start.7) | collective-permute-done | bytes 262176 | tf_op jit(solution)/shard_map/ppermute | solution.py:24
  122.1 18.7 %all-to-all-done = bf16[64,16,1024]{2,1,0:T(8,128)(2,1)} async-done(((bf16[64,16,1024]{2,1,0:T(8,128)(2,1)}), bf16[64,16,1024]{2,1,0:T(8,128)(2,1)}, u32[]{:S(2)}, u32[]{:S(2)}) %all-to-all-start) | async-done | bytes 2097184 | tf_op jit(solution)/shard_map/all_to_all | solution.py:483
  140.8 4.9 %trainer_step.1 = (f32[64,1024]{1,0:T(8,128)}, f32[64,1024]{1,0:T(8,128)}, f32[1,128]{1,0:T(1,128)}) custom-call(bf16[1024,1024]{1,0:T(8,128)(2,1)} %bitcast.4.gap, bf16[64,1024]{1,0:T(8,128)(2,1)} %multiply_convert_fusion.1.lowered, bf16[64,1024]{1,0:T(8,128)(2,1)} %bitcast.31, f32[1024,128]{1,0:T(8,128)} %maximum_maximum_fusion.facts), custom_call_target="tpu_custom_call" | custom-call | flops 402653184 | bytes 4194304 | tf_op jit(solution)/shard_map/trainer_step/pallas_call | solution.py:422
  145.7 1.5 collective-permute-start.10
  147.2 6.2 %collective-permute-done.10 = f32[1,128]{1,0:T(1,128)S(1)} collective-permute-done((f32[1,128]{1,0:T(1,128)}, f32[1,128]{1,0:T(1,128)S(1)}, u32[]{:S(2)}, u32[]{:S(2)}) %collective-permute-start.10) | collective-permute-done | bytes 544 | tf_op jit(solution)/shard_map/ppermute | solution.py:24
  154.1 1.1 collective-permute-start.11
  155.2 2.5 %collective-permute-done.11 = f32[1,128]{1,0:T(1,128)S(1)} collective-permute-done((f32[1,128]{1,0:T(1,128)S(1)}, f32[1,128]{1,0:T(1,128)S(1)}, u32[]{:S(2)}, u32[]{:S(2)}) %collective-permute-start.11) | collective-permute-done | bytes 544 | tf_op jit(solution)/shard_map/ppermute | solution.py:24
  157.7 1.0 add.63
  158.7 1.2 collective-permute-start.9
  160.5 7.9 %all-to-all-start.2 = ((f32[64,1,16]{2,1,0:T(1,128)}), f32[64,1,16]{2,1,0:T(1,128)S(1)}, u32[]{:S(2)}, u32[]{:S(2)}) async-start(f32[64,1,16]{2,1,0:T(1,128)} %broadcast_in_dim.32), calls=%async_computation.2 | async-start | bytes 65536 | tf_op jit(solution)/shard_map/all_to_all | solution.py:512
  168.5 9.2 %all-to-all-done.2 = f32[64,1,16]{2,1,0:T(1,128)S(1)} async-done(((f32[64,1,16]{2,1,0:T(1,128)}), f32[64,1,16]{2,1,0:T(1,128)S(1)}, u32[]{:S(2)}, u32[]{:S(2)}) %all-to-all-start.2) | async-done | bytes 4128 | tf_op jit(solution)/shard_map/all_to_all | solution.py:512
  177.7 1.1 fusion.12
  180.2 2.8 %convolution_bitcast_fusion = f32[1,64,1024]{2,1,0:T(8,128)} fusion(bf16[1024,1024]{1,0:T(8,128)(2,1)} %get-tuple-element.21, f32[64,1024]{1,0:T(8,128)S(1)} %add.63, f32[64,1024]{1,0:T(8,128)S(1)} %collective-permute-done.9), kind=kOutput, calls=%fused_computation | convolution fusion | flops 134414336 | bytes 2883584 | tf_op jit(solution)/shard_map/dot_general | solution.py:517
  (46 shorter events, 8.3 us)
Async XLA Ops:
  7.5 13.3 %copy-start = (bf16[66,8,1024]{2,1,0:T(8,128)(2,1)S(1)}, bf16[66,8,1024]{2,1,0:T(8,128)(2,1)}, u32[]{:S(2)}) copy-start(bf16[66,8,1024]{2,1,0:T(8,128)(2,1)} %get-tuple-element.15.own_in) | copy-start | bytes 3244036
  7.5 69.4 %all-to-all-start.1 = ((bf16[64,17,8,128]{3,2,1,0:T(8,128)(2,1)}), bf16[64,17,8,128]{3,2,1,0:T(8,128)(2,1)}, u32[]{:S(2)}, u32[]{:S(2)}) async-start(bf16[64,17,8,128]{3,2,1,0:T(8,128)(2,1)} %get-tuple-element.17), calls=%async_computation.1 | async-start | bytes 4456448 | tf_op jit(solution)/shard_map/all_to_all | solution.py:476
  20.8 25.1 %collective-permute-start = (bf16[528,1024]{1,0:T(8,128)(2,1)S(1)}, bf16[528,1024]{1,0:T(8,128)(2,1)S(1)}, u32[]{:S(2)}, u32[]{:S(2)}) collective-permute-start(bf16[528,1024]{1,0:T(8,128)(2,1)S(1)} %bitcast.26), channel_id=1, source_target_pairs={{0,1},{1,0},{2,3},{3,2},{4,5},{5,4},{6,7},{7,6},{8,9},{9,8},{10,11... | collective-permute-start | bytes 3244040 | tf_op jit(solution)/shard_map/ppermute | solution.py:24
  22.2 26.6 %collective-permute-start.1 = (bf16[528,1024]{1,0:T(8,128)(2,1)S(1)}, bf16[528,1024]{1,0:T(8,128)(2,1)S(1)}, u32[]{:S(2)}, u32[]{:S(2)}) collective-permute-start(bf16[528,1024]{1,0:T(8,128)(2,1)S(1)} %bitcast.27), channel_id=1, source_target_pairs={{0,3},{1,2},{2,1},{3,0},{4,7},{5,6},{6,5},{7,4},{8,11},{9,10},{10,... | collective-permute-start | bytes 3244040 | tf_op jit(solution)/shard_map/ppermute | solution.py:24
  45.9 2.9 %copy-start.1 = (bf16[528,1024]{1,0:T(8,128)(2,1)}, bf16[528,1024]{1,0:T(8,128)(2,1)S(1)}, u32[]{:S(2)}) copy-start(bf16[528,1024]{1,0:T(8,128)(2,1)S(1)} %collective-permute-done.near.near_gain) | copy-start | bytes 3244036
  46.0 15.8 %collective-permute-start.3 = (bf16[272,1024]{1,0:T(8,128)(2,1)S(1)}, bf16[272,1024]{1,0:T(8,128)(2,1)S(1)}, u32[]{:S(2)}, u32[]{:S(2)}) collective-permute-start(bf16[272,1024]{1,0:T(8,128)(2,1)S(1)} %slice.40), channel_id=1, source_target_pairs={{0,3},{1,2},{2,1},{3,0},{4,7},{5,6},{6,5},{7,4},{8,11},{9,10},{10,... | collective-permute-start | bytes 1671176 | tf_op jit(solution)/shard_map/ppermute | solution.py:24
  48.8 1.0 copy-start.2
  49.8 12.0 %collective-permute-start.2 = (bf16[256,1024]{1,0:T(8,128)(2,1)S(1)}, bf16[256,1024]{1,0:T(8,128)(2,1)S(1)}, u32[]{:S(2)}, u32[]{:S(2)}) collective-permute-start(bf16[256,1024]{1,0:T(8,128)(2,1)S(1)} %slice.39), channel_id=1, source_target_pairs={{0,1},{1,0},{2,3},{3,2},{4,5},{5,4},{6,7},{7,6},{8,9},{9,8},{10,11... | collective-permute-start | bytes 1572872 | tf_op jit(solution)/shard_map/ppermute | solution.py:24
  61.8 0.8 copy-start.4
  61.8 1.0 copy-start.3
  77.0 63.9 %all-to-all-start = ((bf16[64,16,1024]{2,1,0:T(8,128)(2,1)}), bf16[64,16,1024]{2,1,0:T(8,128)(2,1)}, u32[]{:S(2)}, u32[]{:S(2)}) async-start(bf16[64,16,1024]{2,1,0:T(8,128)(2,1)} %bitcast.28), calls=%async_computation | async-start | bytes 4194304 | tf_op jit(solution)/shard_map/all_to_all | solution.py:483
  94.7 3.1 %collective-permute-start.4 = (f32[1,1024]{1,0:T(1,128)}, f32[1,1024]{1,0:T(1,128)S(1)}, u32[]{:S(2)}, u32[]{:S(2)}) collective-permute-start(f32[1,1024]{1,0:T(1,128)} %row_squares.1), channel_id=1, source_target_pairs={{0,1},{1,0},{2,3},{3,2},{4,5},{5,4},{6,7},{7,6},{8,9},{9,8},{10,11... | collective-permute-start | bytes 12296 | tf_op jit(solution)/shard_map/ppermute | solution.py:24
  98.5 4.1 %collective-permute-start.5 = (f32[1,1024]{1,0:T(1,128)S(1)}, f32[1,1024]{1,0:T(1,128)S(1)}, u32[]{:S(2)}, u32[]{:S(2)}) collective-permute-start(f32[1,1024]{1,0:T(1,128)S(1)} %add.55), channel_id=1, source_target_pairs={{0,3},{1,2},{2,1},{3,0},{4,7},{5,6},{6,5},{7,4},{8,11},{9,10},{10,... | collective-permute-start | bytes 12296 | tf_op jit(solution)/shard_map/ppermute | solution.py:24
  107.5 6.1 %collective-permute-start.6 = (f32[64,1024]{1,0:T(8,128)}, f32[64,1024]{1,0:T(8,128)S(1)}, u32[]{:S(2)}, u32[]{:S(2)}) collective-permute-start(f32[64,1024]{1,0:T(8,128)} %get-tuple-element.19), channel_id=1, source_target_pairs={{0,1},{1,0},{2,3},{3,2},{4,5},{5,4},{6,7},{7,6},{8,9},{9,8},{10,11... | collective-permute-start | bytes 786440 | tf_op jit(solution)/shard_map/ppermute | solution.py:24
  114.5 6.9 %collective-permute-start.7 = (f32[64,1024]{1,0:T(8,128)S(1)}, f32[64,1024]{1,0:T(8,128)S(1)}, u32[]{:S(2)}, u32[]{:S(2)}) collective-permute-start(f32[64,1024]{1,0:T(8,128)S(1)} %add.57), channel_id=1, source_target_pairs={{0,3},{1,2},{2,1},{3,0},{4,7},{5,6},{6,5},{7,4},{8,11},{9,10},{10,... | collective-permute-start | bytes 786440 | tf_op jit(solution)/shard_map/ppermute | solution.py:24
  145.7 12.0 %collective-permute-start.8 = (f32[64,1024]{1,0:T(8,128)}, f32[64,1024]{1,0:T(8,128)S(1)}, u32[]{:S(2)}, u32[]{:S(2)}) collective-permute-start(f32[64,1024]{1,0:T(8,128)} %get-tuple-element.20), channel_id=1, source_target_pairs={{0,1},{1,0},{2,3},{3,2},{4,5},{5,4},{6,7},{7,6},{8,9},{9,8},{10,11... | collective-permute-start | bytes 786440 | tf_op jit(solution)/shard_map/ppermute | solution.py:24
  145.7 7.7 %collective-permute-start.10 = (f32[1,128]{1,0:T(1,128)}, f32[1,128]{1,0:T(1,128)S(1)}, u32[]{:S(2)}, u32[]{:S(2)}) collective-permute-start(f32[1,128]{1,0:T(1,128)} %get-tuple-element.23), channel_id=1, source_target_pairs={{0,1},{1,0},{2,3},{3,2},{4,5},{5,4},{6,7},{7,6},{8,9},{9,8},{10,11... | collective-permute-start | bytes 1544 | tf_op jit(solution)/shard_map/ppermute | solution.py:24
  154.1 3.6 %collective-permute-start.11 = (f32[1,128]{1,0:T(1,128)S(1)}, f32[1,128]{1,0:T(1,128)S(1)}, u32[]{:S(2)}, u32[]{:S(2)}) collective-permute-start(f32[1,128]{1,0:T(1,128)S(1)} %add.65), channel_id=1, source_target_pairs={{0,3},{1,2},{2,1},{3,0},{4,7},{5,6},{6,5},{7,4},{8,11},{9,10},{10,... | collective-permute-start | bytes 1544 | tf_op jit(solution)/shard_map/ppermute | solution.py:24
  158.7 21.5 %collective-permute-start.9 = (f32[64,1024]{1,0:T(8,128)S(1)}, f32[64,1024]{1,0:T(8,128)S(1)}, u32[]{:S(2)}, u32[]{:S(2)}) collective-permute-start(f32[64,1024]{1,0:T(8,128)S(1)} %add.63), channel_id=1, source_target_pairs={{0,3},{1,2},{2,1},{3,0},{4,7},{5,6},{6,5},{7,4},{8,11},{9,10},{10,... | collective-permute-start | bytes 786440 | tf_op jit(solution)/shard_map/ppermute | solution.py:24
  160.5 17.1 %all-to-all-start.2 = ((f32[64,1,16]{2,1,0:T(1,128)}), f32[64,1,16]{2,1,0:T(1,128)S(1)}, u32[]{:S(2)}, u32[]{:S(2)}) async-start(f32[64,1,16]{2,1,0:T(1,128)} %broadcast_in_dim.32), calls=%async_computation.2 | async-start | bytes 65536 | tf_op jit(solution)/shard_map/all_to_all | solution.py:512

commit v7 on v6

--- a/solution.py
+++ b/solution.py
@@ -251,130 +251,182 @@
     )(ids, dest, buckets, lengths, pool, gain[None, :])
 
 
+def early_kernel(ids, own, near, other, targets, apart, squares):
+    step = pl.program_id(0)
+    chunk, part = near.shape
+    lanes = squares.shape[1]
+    blocks, block_len, _ = own.shape
+    sums = jnp.zeros(squares.shape, jnp.float32)
+    for g in range(part // lanes):
+        at = slice(g * lanes, (g + 1) * lanes)
+        for piece in (own[:, :, at].reshape(chunk, lanes), near[:, at], other[:, at]):
+            x = piece.astype(jnp.float32)
+            sums = sums + x * x
+    squares[...] = sums
+
+    def subtract(j, carry):
+        target = targets[ids[step * blocks + j]].astype(jnp.float32)
+        apart[j] = own[j].astype(jnp.float32) - target
+        return carry
+
+    lax.fori_loop(0, blocks, subtract, 0)
+
+
+def early_part(ids, own, near, other, targets):
+    part = near.shape[1]
+    block = own.shape[1:]
+    sampled = ids.shape[0]
+    rows = sampled * block[0]
+    chunk = 128
+    blocks = chunk // block[0]
+    lanes = 128
+    return pl.pallas_call(
+        early_kernel,
+        grid=(rows // chunk,),
+        out_shape=(
+            jax.ShapeDtypeStruct((sampled, *block), jnp.float32),
+            jax.ShapeDtypeStruct((rows, lanes), jnp.float32),
+        ),
+        in_specs=[
+            pl.BlockSpec(memory_space=pltpu.SMEM),
+            pl.BlockSpec((blocks, *block), lambda n: (n, 0, 0)),
+            pl.BlockSpec((chunk, part), lambda n: (n, 0)),
+            pl.BlockSpec((chunk, part), lambda n: (n, 0)),
+            pl.BlockSpec(targets.shape, lambda n: (0, 0, 0)),
+        ],
+        out_specs=(
+            pl.BlockSpec((blocks, *block), lambda n: (n, 0, 0)),
+            pl.BlockSpec((chunk, lanes), lambda n: (n, 0)),
+        ),
+        compiler_params=pltpu.CompilerParams(vmem_limit_bytes=VMEM_BYTES),
+        cost_estimate=pl.CostEstimate(flops=6 << 20, bytes_accessed=8 << 20, transcendentals=0),
+        name="early_part",
+    )(ids, own, near, other, targets)
+
+
 def gap_kernel(
-    ids, slot_of, order, mine, near, other, far_first, far_last,
-    mine_gain, near_gain, other_gain, far_gain, frozen, own_in, targets_in,
-    send_out, done, own, targets, send, normed, gap, sem,
+    slot_of, order, mine, near, other, far_first, far_last,
+    mine_gain, near_gain, other_gain, far_gain, squares, apart_in, frozen_in,
+    send_out, done, apart, frozen, send, normed, gap, sem,
 ):
     step = pl.program_id(0)
     chunk, part = mine.shape
     sampled, block_len, columns = gap.shape
     chunks = sampled * block_len // chunk
-    width, tile = frozen.shape
-    far_first_chunks = chunks // 2
+    tiles, width, tile = frozen.shape
     slots = send.shape[0]
-    own_copy = pltpu.make_async_copy(own_in.at[pl.ds(0, sampled)], own, sem.at[0])
-    target_copy = pltpu.make_async_copy(targets_in, targets, sem.at[1])
+    apart_copy = pltpu.make_async_copy(apart_in, apart, sem.at[0])
+    frozen_copies = [
+        pltpu.make_async_copy(
+            frozen_in.at[:, pl.ds(t * tile, tile)], frozen.at[t], sem.at[1 + t]
+        )
+        for t in range(tiles)
+    ]
 
     @pl.when(step == 0)
     def _():
-        own_copy.start()
-        target_copy.start()
+        frozen_copies[0].start()
+        apart_copy.start()
+        for copy in frozen_copies[1:]:
+            copy.start()
         done[0] = 0.0
 
         def fill(s, carry):
             send[slot_of[sampled + s]] = jnp.zeros((block_len, columns), jnp.bfloat16)
             return carry
 
-        lax.fori_loop(0, slots - sampled, fill, 0)
-
-    @pl.when(step < chunks)
-    def _():
-        first = step < far_first_chunks
-        rows_of = (
-            lambda: mine[...].astype(jnp.float32),
-            lambda: near[...].astype(jnp.float32),
-            lambda: jnp.where(first, far_first[...], far_last[...]).astype(jnp.float32),
-            lambda: other[...].astype(jnp.float32),
-        )
-        gains = (mine_gain, near_gain, far_gain, other_gain)
-        squares = jnp.zeros((chunk, part), jnp.float32)
-        for get in rows_of:
-            x = get()
-            squares = squares + x * x
-        total = jnp.sum(squares, axis=1, keepdims=True)
+        lax.fori_loop(0, slots - sampled, fill, 0, unroll=4)
+
+    def normalize(far):
+        x = far[...].astype(jnp.float32)
+        total = jnp.sum(squares[...], axis=1, keepdims=True)
+        total = total + jnp.sum(x * x, axis=1, keepdims=True)
         inverse = lax.rsqrt(total / width + RMS_EPSILON)
         at = pl.ds(pl.multiple_of(step * chunk, chunk), chunk)
-        for p, (get, pieces) in enumerate(zip(rows_of, gains)):
-            three = pieces[...].astype(jnp.float32)
+        pieces = ((mine, mine_gain), (near, near_gain), (far, far_gain), (other, other_gain))
+        for p, (piece, gains) in enumerate(pieces):
+            three = gains[...].astype(jnp.float32)
             gain = three[0:1] + three[1:2] + three[2:3]
             to = pl.ds(pl.multiple_of(order[p] * part, part), part)
-            normed[at, to] = (get() * inverse * gain).astype(jnp.bfloat16)
-
-    @pl.when(step == chunks)
+            x = piece[...].astype(jnp.float32)
+            normed[at, to] = (x * inverse * gain).astype(jnp.bfloat16)
+
+    @pl.when(step < chunks // 2)
     def _():
-        own_copy.wait()
-        target_copy.wait()
-
-    @pl.when(step >= chunks)
+        normalize(far_first)
+
+    @pl.when(step >= chunks // 2)
     def _():
-        projected = jnp.dot(normed[...], frozen[...], preferred_element_type=jnp.float32)
-        at = pl.ds(pl.multiple_of((step - chunks) * tile, tile), tile)
-        x = own[:, :, at].astype(jnp.float32)
-        gap[:, :, at] = x + projected.reshape(sampled, block_len, tile)
-
-    @pl.when(step == pl.num_programs(0) - 1)
+        normalize(far_last)
+
+    @pl.when(step == chunks - 1)
     def _():
+        apart_copy.wait()
+        for t in range(tiles):
+            frozen_copies[t].wait()
+            projected = jnp.dot(normed[...], frozen[t], preferred_element_type=jnp.float32)
+            at = slice(t * tile, (t + 1) * tile)
+            whole = apart[:, :, at] + projected.reshape(sampled, block_len, tile)
+            gap[:, :, at] = whole.astype(jnp.bfloat16)
+
         def place(j, carry):
-            target = targets[ids[j]].astype(jnp.float32)
-            send[slot_of[j]] = (gap[j] - target).astype(jnp.bfloat16)
+            send[slot_of[j]] = gap[j]
             return carry
 
-        lax.fori_loop(0, sampled, place, 0, unroll=4)
+        lax.fori_loop(0, sampled, place, 0, unroll=8)
         copy = pltpu.make_async_copy(send, send_out, sem.at[0])
         copy.start()
         copy.wait()
 
 
-def base_gap_slots(ids, slot_of, order, own, received, frozen, targets):
+def base_gap_slots(slot_of, order, own, received, apart, squares, frozen):
     near, other, far_first, far_last = received
     part = near.shape[1]
     width, columns = frozen.shape
     slots = slot_of.shape[0]
-    sampled = ids.shape[0]
-    block = own.shape[1:]
+    sampled, *block = apart.shape
     rows = sampled * block[0]
     tile = 256
+    tiles = columns // tile
     chunk = 128
     chunks = rows // chunk
     half = chunks // 2
-    all_rows = pl.BlockSpec((chunk, part), lambda n: (jnp.minimum(n, chunks - 1), 0))
+    all_rows = pl.BlockSpec((chunk, part), lambda n: (n, 0))
     all_gain = pl.BlockSpec((16, part), lambda n: (rows // 16, 0))
     mine = own.reshape(-1, part)
     smem = pl.BlockSpec(memory_space=pltpu.SMEM)
     hbm = pl.BlockSpec(memory_space=pltpu.HBM)
     return pl.pallas_call(
         gap_kernel,
-        grid=(chunks + columns // tile,),
+        grid=(chunks,),
         out_shape=(
             jax.ShapeDtypeStruct((slots, *block), jnp.bfloat16),
             jax.ShapeDtypeStruct((1,), jnp.float32),
         ),
         in_specs=[
-            smem,
             smem,
             smem,
             all_rows,
             all_rows,
             all_rows,
             pl.BlockSpec((chunk, part), lambda n: (jnp.minimum(n, half - 1), 0)),
-            pl.BlockSpec((chunk, part), lambda n: (jnp.clip(n - half, 0, half - 1), 0)),
+            pl.BlockSpec((chunk, part), lambda n: (jnp.maximum(n - half, 0), 0)),
             all_gain,
             all_gain,
             all_gain,
             pl.BlockSpec((16, part), lambda n: (rows // 32, 0)),
-            pl.BlockSpec((width, tile), lambda n: (0, jnp.maximum(n - chunks, 0))),
+            pl.BlockSpec((chunk, squares.shape[1]), lambda n: (n, 0)),
             hbm,
             hbm,
         ],
         out_specs=(hbm, smem),
         scratch_shapes=[
-            pltpu.VMEM((sampled, *block), jnp.bfloat16),
-            pltpu.VMEM(targets.shape, jnp.bfloat16),
+            pltpu.VMEM((sampled, *block), jnp.float32),
+            pltpu.VMEM((tiles, width, tile), jnp.bfloat16),
             pltpu.VMEM((slots, *block), jnp.bfloat16),
             pltpu.VMEM((rows, width), jnp.bfloat16),
-            pltpu.VMEM((sampled, *block), jnp.float32),
-            pltpu.SemaphoreType.DMA((2,)),
+            pltpu.VMEM((sampled, *block), jnp.bfloat16),
+            pltpu.SemaphoreType.DMA((1 + tiles,)),
         ],
         compiler_params=pltpu.CompilerParams(vmem_limit_bytes=VMEM_BYTES),
         cost_estimate=pl.CostEstimate(
@@ -382,8 +434,8 @@
         ),
         name="base_gap",
     )(
-        ids, slot_of, order, mine, near, other, far_first, far_last,
-        mine, near, other, far_last, frozen, own, targets,
+        slot_of, order, mine, near, other, far_first, far_last,
+        mine, near, other, far_last, squares, apart, frozen,
     )
 
 
@@ -477,8 +529,11 @@
     cut = sampled * block_len // 2
     received = from_parts(own_x.reshape(-1, part), "mp", cut)
     order = lax.axis_index("mp") ^ jnp.arange(lax.axis_size("mp"), dtype=jnp.int32)
+    apart, near_squares = early_part(
+        sample_ids, own_x, received[0], received[1], pool_targets
+    )
     send_gap, done = base_gap_slots(
-        sample_ids, slot_of, order, own_x, received, frozen, pool_targets
+        slot_of, order, own_x, received, apart, near_squares, frozen
     )
     got_gap = lax.all_to_all(
         send_gap.reshape(trainers, per_peer, part), DP, 0, 0, tiled=True
@@ -507,9 +562,11 @@
     grad_up, back_part, loss_part = trainer_step(
         got_gap.reshape(rows, part), lowered, up_map, facts
     )
-    own_loss = over_parts(loss_part, "mp")[:, :NB]
+    everyone = trainers * lax.axis_size("mp")
     loss_sum = jnp.sum(
-        lax.all_to_all(jnp.broadcast_to(own_loss, (trainers, 1, NB)), DP, 0, 0, tiled=True),
+        lax.all_to_all(
+            jnp.broadcast_to(loss_part[:, :NB], (everyone, 1, NB)), DP_MP, 0, 0, tiled=True
+        ),
         axis=(0, 1),
     )
     back = over_parts(back_part, "mp")

time: 185 us -> 191 us (1.032)
  Pallas kernels: 34.5 us -> 43.8 us
  starting transfers between devices: 46.1 us -> 42.1 us
  local copies, waits for them, and re-layouts: 3.73 us -> 5.93 us
    pallas_call x1 -> x2, Pallas kernels: 14.1 us -> 23.3 us  [the longest x1 17.9 us: base_gap_slots(): pl.pallas_call(gap_kernel, grid=(chunks,), out_shape=(jax.ShapeDtypeStruc...]
    ppermute x12 -> x10, starting transfers between devices: 12.2 us -> 7.19 us  [swap(): return lax.ppermute(value, axis, [(i, i ^ distance) for i in range(peers)])]
    ppermute x12 -> x10, waiting for transfers between devices: 55.4 us -> 50.7 us  [swap(): return lax.ppermute(value, axis, [(i, i ^ distance) for i in range(peers)])]
    all_to_all x1, waiting for transfers between devices: 9.21 us -> 12.7 us  [on_device(): lax.all_to_all(jnp.broadcast_to(loss_part[:, :NB], (everyone, 1, NB)), DP...]
  transfers between devices with their start and end apart: 15 -> 13, of which waited for: 10 -> 9; matrix products, arithmetic and copies ran while one was open for 6% -> 7% of each run, Pallas kernels for 12% -> 17%
where the time goes in v7:
time: 191 us; the launch traced here: 190 us
  waiting for transfers between devices  82.1 us (43%)
  Pallas kernels  43.8 us (23%)
  starting transfers between devices  42.1 us (22%)
  other arithmetic  9.34 us (5%)
  local copies, waits for them, and re-layouts  5.93 us (3%)
  between operations  3.91 us (2%)
  matrix products  2.78 us (1%)
    ppermute x10, waiting for transfers between devices, swap(): return lax.ppermute(value, axis, [(i, i ^ distance) for i in range(peers)])  50.7 us
    all_to_all x1, waiting for transfers between devices, on_device(): lax.all_to_all(send_gap.reshape(trainers, per_peer, part), DP, 0, 0, tile...  18.7 us
    pallas_call x1, Pallas kernels, base_gap_slots(): pl.pallas_call(gap_kernel, grid=(chunks,), out_shape=(jax.ShapeDtypeStruc...  17.9 us
    all_to_all x1, starting transfers between devices, on_device(): got_x = lax.all_to_all(send_x, DP, 0, 0, tiled=True)  13.3 us
    all_to_all x1, starting transfers between devices, on_device(): lax.all_to_all(send_gap.reshape(trainers, per_peer, part), DP, 0, 0, tile...  12.8 us
    all_to_all x1, waiting for transfers between devices, on_device(): lax.all_to_all(jnp.broadcast_to(loss_part[:, :NB], (everyone, 1, NB)), DP...  12.7 us
    all_to_all x1, starting transfers between devices, on_device(): lax.all_to_all(jnp.broadcast_to(loss_part[:, :NB], (everyone, 1, NB)), DP...  8.84 us
    ppermute x10, starting transfers between devices, swap(): return lax.ppermute(value, axis, [(i, i ^ distance) for i in range(peers)])  7.19 us
  transfers between devices with their start and end apart: 13, of which 9 were waited for; matrix products, arithmetic and copies ran while one was open for 7% of the time, Pallas kernels for 17%

profile of v7, /device:TPU:1, one launch (start us, length us, event | category | flops | bytes accessed | tf_op | source)
XLA Modules:
  0.0 190.1 jit_solution(666651493535889405)
XLA Ops:
  0.6 7.0 %route.1 = (bf16[64,17,8,128]{3,2,1,0:T(8,128)(2,1)}, bf16[66,8,1024]{2,1,0:T(8,128)(2,1)}, s32[128]{0:T(128)}) custom-call(s32[64]{0:T(128)} %ids.1, s32[64]{0:T(128)} %bitcast.35, s32[128]{0:T(128)} %buckets_in.1, s32[128]{0:T(128)} %lengths_in.1, bf16[128,8,1024]{2,1,0:T(8,128)(2,1)} %pool_in.1, f32[1,1024]{1,0:T(1,128)} %bitcast.32), custom_call_target="tpu_custom_call" | custom-call | bytes 5242880 | tf_op jit(solution)/shard_map/route/pallas_call | solution.py:225
  7.6 13.3 %all-to-all-start.1 = ((bf16[64,17,8,128]{3,2,1,0:T(8,128)(2,1)}), bf16[64,17,8,128]{3,2,1,0:T(8,128)(2,1)}, u32[]{:S(2)}, u32[]{:S(2)}) async-start(bf16[64,17,8,128]{3,2,1,0:T(8,128)(2,1)} %get-tuple-element.21), calls=%async_computation.1 | async-start | bytes 4456448 | tf_op jit(solution)/shard_map/all_to_all | solution.py:528
  21.0 1.4 collective-permute-start
  22.3 1.9 %collective-permute-start.1 = (bf16[528,1024]{1,0:T(8,128)(2,1)S(1)}, bf16[528,1024]{1,0:T(8,128)(2,1)S(1)}, u32[]{:S(2)}, u32[]{:S(2)}) collective-permute-start(bf16[528,1024]{1,0:T(8,128)(2,1)S(1)} %bitcast.27), channel_id=1, source_target_pairs={{0,3},{1,2},{2,1},{3,0},{4,7},{5,6},{6,5},{7,4},{8,11},{9,10},{10,... | collective-permute-start | bytes 3244040 | tf_op jit(solution)/shard_map/ppermute | solution.py:24
  24.2 21.8 %collective-permute-done.near.near_gain = bf16[528,1024]{1,0:T(8,128)(2,1)S(1)} collective-permute-done((bf16[528,1024]{1,0:T(8,128)(2,1)S(1)}, bf16[528,1024]{1,0:T(8,128)(2,1)S(1)}, u32[]{:S(2)}, u32[]{:S(2)}) %collective-permute-start) | collective-permute-done | bytes 1081376 | tf_op jit(solution)/shard_map/ppermute | solution.py:24
  46.1 0.9 slice.40
  47.0 2.7 %collective-permute-start.3 = (bf16[272,1024]{1,0:T(8,128)(2,1)}, bf16[272,1024]{1,0:T(8,128)(2,1)S(1)}, u32[]{:S(2)}, u32[]{:S(2)}) collective-permute-start(bf16[272,1024]{1,0:T(8,128)(2,1)} %slice.40), channel_id=1, source_target_pairs={{0,3},{1,2},{2,1},{3,0},{4,7},{5,6},{6,5},{7,4},{8,11},{9,10},{10,... | collective-permute-start | bytes 1671176 | tf_op jit(solution)/shard_map/ppermute | solution.py:24
  49.7 1.0 copy-done.1
  50.7 0.8 slice.39
  52.0 5.4 %early_part.1 = (f32[64,8,1024]{2,1,0:T(8,128)}, f32[512,128]{1,0:T(8,128)}) custom-call(s32[64]{0:T(128)} %ids.1, bf16[66,8,1024]{2,1,0:T(8,128)(2,1)} %get-tuple-element.17.own, bf16[528,1024]{1,0:T(8,128)(2,1)} %copy-done, bf16[528,1024]{1,0:T(8,128)(2,1)} %copy-done.1, bf16[128,8,1024]{2,1,0:T(8,128)(2,1)} %targets.1), custom_call_target="tpu_custom_call" | custom-call | flops 6291456 | bytes 8388608 | tf_op jit(solution)/shard_map/early_part/pallas_call | solution.py:283
  57.4 6.3 %collective-permute-done.2.far_first = bf16[256,1024]{1,0:T(8,128)(2,1)} collective-permute-done((bf16[256,1024]{1,0:T(8,128)(2,1)}, bf16[256,1024]{1,0:T(8,128)(2,1)}, u32[]{:S(2)}, u32[]{:S(2)}) %collective-permute-start.2) | collective-permute-done | bytes 524320 | tf_op jit(solution)/shard_map/ppermute | solution.py:24
  63.7 0.8 copy-done.3
  64.5 17.9 %base_gap.1 = (bf16[128,8,1024]{2,1,0:T(8,128)(2,1)}, f32[1]{0:T(128)}) custom-call(s32[128]{0:T(128)} %get-tuple-element.16.slot_of, s32[4]{0:T(128)} %iota_xor_fusion.order, bf16[528,1024]{1,0:T(8,128)(2,1)} %bitcast.24, bf16[528,1024]{1,0:T(8,128)(2,1)} %copy-done, bf16[528,1024]{1,0:T(8,128)(2,1)} %copy-done.1, ...), custom_call_target="tpu_custom_call" | custom-call | flops 4294967296 | bytes 18874368 | tf_op jit(solution)/shard_map/base_gap/pallas_call | solution.py:399
  82.5 12.8 %all-to-all-start = ((bf16[64,16,1024]{2,1,0:T(8,128)(2,1)}), bf16[64,16,1024]{2,1,0:T(8,128)(2,1)}, u32[]{:S(2)}, u32[]{:S(2)}) async-start(bf16[64,16,1024]{2,1,0:T(8,128)(2,1)} %bitcast.28), calls=%async_computation | async-start | bytes 4194304 | tf_op jit(solution)/shard_map/all_to_all | solution.py:538
  96.0 4.3 %row_squares.1 = f32[1,1024]{1,0:T(1,128)} custom-call(bf16[64,17,8,128]{3,2,1,0:T(8,128)(2,1)} %all-to-all-done.1.packed, f32[1]{0:T(128)} %get-tuple-element.22.done), custom_call_target="tpu_custom_call" | custom-call | flops 4194304 | bytes 2097152 | tf_op jit(solution)/shard_map/row_squares/pallas_call | solution.py:57
  100.3 0.9 fusion.3
  101.6 0.9 fusion.2
  102.6 0.8 collective-permute-done.4
  104.5 3.6 %collective-permute-done.5 = f32[1,1024]{1,0:T(1,128)S(1)} collective-permute-done((f32[1,1024]{1,0:T(1,128)S(1)}, f32[1,1024]{1,0:T(1,128)S(1)}, u32[]{:S(2)}, u32[]{:S(2)}) %collective-permute-start.5) | collective-permute-done | bytes 4128 | tf_op jit(solution)/shard_map/ppermute | solution.py:24
  108.7 4.4 %latents.1 = (bf16[1024,1024]{1,0:T(8,128)(2,1)}, f32[64,1024]{1,0:T(8,128)}) custom-call(bf16[64,17,8,128]{3,2,1,0:T(8,128)(2,1)} %all-to-all-done.1.packed, f32[1,1024]{1,0:T(1,128)} %add_multiply_fusion.squares, f32[1,1024]{1,0:T(1,128)} %bitcast.33, bf16[64,1024]{1,0:T(8,128)(2,1)} %bitcast.30), custom_call_target="tpu_custom_call" | custom-call | flops 134217728 | bytes 4194304 | tf_op jit(solution)/shard_map/latents/pallas_call | solution.py:92
  113.9 5.2 %collective-permute-done.6 = f32[64,1024]{1,0:T(8,128)S(1)} collective-permute-done((f32[64,1024]{1,0:T(8,128)}, f32[64,1024]{1,0:T(8,128)S(1)}, u32[]{:S(2)}, u32[]{:S(2)}) %collective-permute-start.6) | collective-permute-done | bytes 262176 | tf_op jit(solution)/shard_map/ppermute | solution.py:24
  119.2 1.0 add.51
  120.8 1.0 maximum_maximum_fusion.facts
  121.8 5.3 %collective-permute-done.7 = f32[64,1024]{1,0:T(8,128)S(1)} collective-permute-done((f32[64,1024]{1,0:T(8,128)S(1)}, f32[64,1024]{1,0:T(8,128)S(1)}, u32[]{:S(2)}, u32[]{:S(2)}) %collective-permute-start.7) | collective-permute-done | bytes 262176 | tf_op jit(solution)/shard_map/ppermute | solution.py:24
  127.8 18.7 %all-to-all-done = bf16[64,16,1024]{2,1,0:T(8,128)(2,1)} async-done(((bf16[64,16,1024]{2,1,0:T(8,128)(2,1)}), bf16[64,16,1024]{2,1,0:T(8,128)(2,1)}, u32[]{:S(2)}, u32[]{:S(2)}) %all-to-all-start) | async-done | bytes 2097184 | tf_op jit(solution)/shard_map/all_to_all | solution.py:538
  146.4 4.9 %trainer_step.1 = (f32[64,1024]{1,0:T(8,128)}, f32[64,1024]{1,0:T(8,128)}, f32[1,128]{1,0:T(1,128)}) custom-call(bf16[1024,1024]{1,0:T(8,128)(2,1)} %bitcast.4.gap, bf16[64,1024]{1,0:T(8,128)(2,1)} %multiply_convert_fusion.1.lowered, bf16[64,1024]{1,0:T(8,128)(2,1)} %bitcast.31, f32[1024,128]{1,0:T(8,128)} %maximum_maximum_fusion.facts), custom_call_target="tpu_custom_call" | custom-call | flops 402653184 | bytes 4194304 | tf_op jit(solution)/shard_map/trainer_step/pallas_call | solution.py:474
  151.3 7.7 %collective-permute-done.8 = f32[64,1024]{1,0:T(8,128)S(1)} collective-permute-done((f32[64,1024]{1,0:T(8,128)}, f32[64,1024]{1,0:T(8,128)S(1)}, u32[]{:S(2)}, u32[]{:S(2)}) %collective-permute-start.8) | collective-permute-done | bytes 262176 | tf_op jit(solution)/shard_map/ppermute | solution.py:24
  159.0 1.0 add.57
  161.8 8.8 %all-to-all-start.2 = ((f32[256,1,16]{2,1,0:T(1,128)}), f32[256,1,16]{2,1,0:T(1,128)S(1)}, u32[]{:S(2)}, u32[]{:S(2)}) async-start(f32[256,1,16]{2,1,0:T(1,128)} %broadcast_in_dim.32), calls=%async_computation.2 | async-start | bytes 262144 | tf_op jit(solution)/shard_map/all_to_all | solution.py:567
  170.7 12.7 %all-to-all-done.2 = f32[256,1,16]{2,1,0:T(1,128)S(1)} async-done(((f32[256,1,16]{2,1,0:T(1,128)}), f32[256,1,16]{2,1,0:T(1,128)S(1)}, u32[]{:S(2)}, u32[]{:S(2)}) %all-to-all-start.2) | async-done | bytes 16416 | tf_op jit(solution)/shard_map/all_to_all | solution.py:567
  183.7 1.1 fusion.12
  186.2 2.8 %convolution_bitcast_fusion = f32[1,64,1024]{2,1,0:T(8,128)} fusion(bf16[1024,1024]{1,0:T(8,128)(2,1)} %get-tuple-element.25, f32[64,1024]{1,0:T(8,128)S(1)} %add.57, f32[64,1024]{1,0:T(8,128)S(1)} %collective-permute-done.9), kind=kOutput, calls=%fused_computation | convolution fusion | flops 134414336 | bytes 2883584 | tf_op jit(solution)/shard_map/dot_general | solution.py:574
  (39 shorter events, 7.0 us)
Async XLA Ops:
  7.6 13.3 %copy-start.2 = (bf16[66,8,1024]{2,1,0:T(8,128)(2,1)S(1)}, bf16[66,8,1024]{2,1,0:T(8,128)(2,1)}, u32[]{:S(2)}) copy-start(bf16[66,8,1024]{2,1,0:T(8,128)(2,1)} %get-tuple-element.17.own) | copy-start | bytes 3244036
  7.6 74.8 %all-to-all-start.1 = ((bf16[64,17,8,128]{3,2,1,0:T(8,128)(2,1)}), bf16[64,17,8,128]{3,2,1,0:T(8,128)(2,1)}, u32[]{:S(2)}, u32[]{:S(2)}) async-start(bf16[64,17,8,128]{3,2,1,0:T(8,128)(2,1)} %get-tuple-element.21), calls=%async_computation.1 | async-start | bytes 4456448 | tf_op jit(solution)/shard_map/all_to_all | solution.py:528
  21.0 25.1 %collective-permute-start = (bf16[528,1024]{1,0:T(8,128)(2,1)S(1)}, bf16[528,1024]{1,0:T(8,128)(2,1)S(1)}, u32[]{:S(2)}, u32[]{:S(2)}) collective-permute-start(bf16[528,1024]{1,0:T(8,128)(2,1)S(1)} %bitcast.26), channel_id=1, source_target_pairs={{0,1},{1,0},{2,3},{3,2},{4,5},{5,4},{6,7},{7,6},{8,9},{9,8},{10,11... | collective-permute-start | bytes 3244040 | tf_op jit(solution)/shard_map/ppermute | solution.py:24
  22.3 27.4 %collective-permute-start.1 = (bf16[528,1024]{1,0:T(8,128)(2,1)S(1)}, bf16[528,1024]{1,0:T(8,128)(2,1)S(1)}, u32[]{:S(2)}, u32[]{:S(2)}) collective-permute-start(bf16[528,1024]{1,0:T(8,128)(2,1)S(1)} %bitcast.27), channel_id=1, source_target_pairs={{0,3},{1,2},{2,1},{3,0},{4,7},{5,6},{6,5},{7,4},{8,11},{9,10},{10,... | collective-permute-start | bytes 3244040 | tf_op jit(solution)/shard_map/ppermute | solution.py:24
  46.1 6.0 %copy-start = (bf16[528,1024]{1,0:T(8,128)(2,1)}, bf16[528,1024]{1,0:T(8,128)(2,1)S(1)}, u32[]{:S(2)}) copy-start(bf16[528,1024]{1,0:T(8,128)(2,1)S(1)} %collective-permute-done.near.near_gain) | copy-start | bytes 3244036
  47.0 16.7 %collective-permute-start.3 = (bf16[272,1024]{1,0:T(8,128)(2,1)}, bf16[272,1024]{1,0:T(8,128)(2,1)S(1)}, u32[]{:S(2)}, u32[]{:S(2)}) collective-permute-start(bf16[272,1024]{1,0:T(8,128)(2,1)} %slice.40), channel_id=1, source_target_pairs={{0,3},{1,2},{2,1},{3,0},{4,7},{5,6},{6,5},{7,4},{8,11},{9,10},{10,... | collective-permute-start | bytes 1671176 | tf_op jit(solution)/shard_map/ppermute | solution.py:24
  49.7 1.0 copy-start.1
  51.5 12.2 %collective-permute-start.2 = (bf16[256,1024]{1,0:T(8,128)(2,1)}, bf16[256,1024]{1,0:T(8,128)(2,1)}, u32[]{:S(2)}, u32[]{:S(2)}) collective-permute-start(bf16[256,1024]{1,0:T(8,128)(2,1)} %slice.39), channel_id=1, source_target_pairs={{0,1},{1,0},{2,3},{3,2},{4,5},{5,4},{6,7},{7,6},{8,9},{9,8},{10,11... | collective-permute-start | bytes 1572872 | tf_op jit(solution)/shard_map/ppermute | solution.py:24
  63.7 0.8 copy-start.3
  82.5 64.0 %all-to-all-start = ((bf16[64,16,1024]{2,1,0:T(8,128)(2,1)}), bf16[64,16,1024]{2,1,0:T(8,128)(2,1)}, u32[]{:S(2)}, u32[]{:S(2)}) async-start(bf16[64,16,1024]{2,1,0:T(8,128)(2,1)} %bitcast.28), calls=%async_computation | async-start | bytes 4194304 | tf_op jit(solution)/shard_map/all_to_all | solution.py:538
  100.3 3.1 %collective-permute-start.4 = (f32[1,1024]{1,0:T(1,128)}, f32[1,1024]{1,0:T(1,128)S(1)}, u32[]{:S(2)}, u32[]{:S(2)}) collective-permute-start(f32[1,1024]{1,0:T(1,128)} %row_squares.1), channel_id=1, source_target_pairs={{0,1},{1,0},{2,3},{3,2},{4,5},{5,4},{6,7},{7,6},{8,9},{9,8},{10,11... | collective-permute-start | bytes 12296 | tf_op jit(solution)/shard_map/ppermute | solution.py:24
  104.1 4.1 %collective-permute-start.5 = (f32[1,1024]{1,0:T(1,128)S(1)}, f32[1,1024]{1,0:T(1,128)S(1)}, u32[]{:S(2)}, u32[]{:S(2)}) collective-permute-start(f32[1,1024]{1,0:T(1,128)S(1)} %add.49), channel_id=1, source_target_pairs={{0,3},{1,2},{2,1},{3,0},{4,7},{5,6},{6,5},{7,4},{8,11},{9,10},{10,... | collective-permute-start | bytes 12296 | tf_op jit(solution)/shard_map/ppermute | solution.py:24
  113.1 6.1 %collective-permute-start.6 = (f32[64,1024]{1,0:T(8,128)}, f32[64,1024]{1,0:T(8,128)S(1)}, u32[]{:S(2)}, u32[]{:S(2)}) collective-permute-start(f32[64,1024]{1,0:T(8,128)} %get-tuple-element.23), channel_id=1, source_target_pairs={{0,1},{1,0},{2,3},{3,2},{4,5},{5,4},{6,7},{7,6},{8,9},{9,8},{10,11... | collective-permute-start | bytes 786440 | tf_op jit(solution)/shard_map/ppermute | solution.py:24
  120.2 6.9 %collective-permute-start.7 = (f32[64,1024]{1,0:T(8,128)S(1)}, f32[64,1024]{1,0:T(8,128)S(1)}, u32[]{:S(2)}, u32[]{:S(2)}) collective-permute-start(f32[64,1024]{1,0:T(8,128)S(1)} %add.51), channel_id=1, source_target_pairs={{0,3},{1,2},{2,1},{3,0},{4,7},{5,6},{6,5},{7,4},{8,11},{9,10},{10,... | collective-permute-start | bytes 786440 | tf_op jit(solution)/shard_map/ppermute | solution.py:24
  151.3 7.7 %collective-permute-start.8 = (f32[64,1024]{1,0:T(8,128)}, f32[64,1024]{1,0:T(8,128)S(1)}, u32[]{:S(2)}, u32[]{:S(2)}) collective-permute-start(f32[64,1024]{1,0:T(8,128)} %get-tuple-element.24), channel_id=1, source_target_pairs={{0,1},{1,0},{2,3},{3,2},{4,5},{5,4},{6,7},{7,6},{8,9},{9,8},{10,11... | collective-permute-start | bytes 786440 | tf_op jit(solution)/shard_map/ppermute | solution.py:24
  160.0 26.1 %collective-permute-start.9 = (f32[64,1024]{1,0:T(8,128)S(1)}, f32[64,1024]{1,0:T(8,128)S(1)}, u32[]{:S(2)}, u32[]{:S(2)}) collective-permute-start(f32[64,1024]{1,0:T(8,128)S(1)} %add.57), channel_id=1, source_target_pairs={{0,3},{1,2},{2,1},{3,0},{4,7},{5,6},{6,5},{7,4},{8,11},{9,10},{10,... | collective-permute-start | bytes 786440 | tf_op jit(solution)/shard_map/ppermute | solution.py:24
  161.8 21.6 %all-to-all-start.2 = ((f32[256,1,16]{2,1,0:T(1,128)}), f32[256,1,16]{2,1,0:T(1,128)S(1)}, u32[]{:S(2)}, u32[]{:S(2)}) async-start(f32[256,1,16]{2,1,0:T(1,128)} %broadcast_in_dim.32), calls=%async_computation.2 | async-start | bytes 262144 | tf_op jit(solution)/shard_map/all_to_all | solution.py:567

commit v8 on v7

--- a/solution.py
+++ b/solution.py
@@ -14,6 +14,7 @@
 SHARPNESS = 12.0
 ADAPTER_SCALING = 2.0
 PER_PAIR = 2
+TILES = 1
 VMEM_BYTES = 62 * 1024 * 1024
 CONTRACT_LAST = (((1,), (1,)), ((), ()))
 CONTRACT_FIRST = (((0,), (0,)), ((), ()))
@@ -251,11 +252,11 @@
     )(ids, dest, buckets, lengths, pool, gain[None, :])
 
 
-def early_kernel(ids, own, near, other, targets, apart, squares):
+def early_kernel(ids, own, near, other, targets, taken, squares):
     step = pl.program_id(0)
     chunk, part = near.shape
     lanes = squares.shape[1]
-    blocks, block_len, _ = own.shape
+    blocks = own.shape[0]
     sums = jnp.zeros(squares.shape, jnp.float32)
     for g in range(part // lanes):
         at = slice(g * lanes, (g + 1) * lanes)
@@ -264,12 +265,11 @@
             sums = sums + x * x
     squares[...] = sums
 
-    def subtract(j, carry):
-        target = targets[ids[step * blocks + j]].astype(jnp.float32)
-        apart[j] = own[j].astype(jnp.float32) - target
+    def take(j, carry):
+        taken[j] = targets[ids[step * blocks + j]]
         return carry
 
-    lax.fori_loop(0, blocks, subtract, 0)
+    lax.fori_loop(0, blocks, take, 0, unroll=4)
 
 
 def early_part(ids, own, near, other, targets):
@@ -284,7 +284,7 @@
         early_kernel,
         grid=(rows // chunk,),
         out_shape=(
-            jax.ShapeDtypeStruct((sampled, *block), jnp.float32),
+            jax.ShapeDtypeStruct((sampled, *block), jnp.bfloat16),
             jax.ShapeDtypeStruct((rows, lanes), jnp.float32),
         ),
         in_specs=[
@@ -299,134 +299,141 @@
             pl.BlockSpec((chunk, lanes), lambda n: (n, 0)),
         ),
         compiler_params=pltpu.CompilerParams(vmem_limit_bytes=VMEM_BYTES),
-        cost_estimate=pl.CostEstimate(flops=6 << 20, bytes_accessed=8 << 20, transcendentals=0),
+        cost_estimate=pl.CostEstimate(flops=6 << 20, bytes_accessed=7 << 20, transcendentals=0),
         name="early_part",
     )(ids, own, near, other, targets)
 
 
 def gap_kernel(
-    slot_of, order, mine, near, other, far_first, far_last,
-    mine_gain, near_gain, other_gain, far_gain, squares, apart_in, frozen_in,
-    send_out, done, apart, frozen, send, normed, gap, sem,
+    slot_of, order, far_first_in, far_last_in, mine_in, near_in, other_in, squares_in,
+    frozen_in, taken_in,
+    send_out, done, pieces, squares, frozen, taken, send, normed, total, gap, sem,
 ):
-    step = pl.program_id(0)
-    chunk, part = mine.shape
+    parts, _, part = pieces.shape
     sampled, block_len, columns = gap.shape
-    chunks = sampled * block_len // chunk
-    tiles, width, tile = frozen.shape
+    rows = sampled * block_len
+    cut = far_first_in.shape[0]
     slots = send.shape[0]
-    apart_copy = pltpu.make_async_copy(apart_in, apart, sem.at[0])
-    frozen_copies = [
+    places = (2, 0, 1, 3)
+    copies = [
         pltpu.make_async_copy(
-            frozen_in.at[:, pl.ds(t * tile, tile)], frozen.at[t], sem.at[1 + t]
+            far_first_in, pieces.at[0, pl.ds(0, cut)], sem.at[0]
+        ),
+        pltpu.make_async_copy(
+            far_last_in, pieces.at[0, pl.ds(cut, far_last_in.shape[0])], sem.at[1]
+        ),
+        pltpu.make_async_copy(squares_in, squares, sem.at[2]),
+        pltpu.make_async_copy(mine_in, pieces.at[1], sem.at[3]),
+        pltpu.make_async_copy(near_in, pieces.at[2], sem.at[4]),
+        pltpu.make_async_copy(other_in, pieces.at[3], sem.at[5]),
+        pltpu.make_async_copy(taken_in, taken, sem.at[6]),
+    ]
+    weights = [
+        pltpu.make_async_copy(
+            frozen_in.at[pl.ds(pl.multiple_of(order[places[i]] * part, part), part)],
+            frozen.at[i],
+            sem.at[7 + i],
         )
-        for t in range(tiles)
+        for i in range(parts)
     ]
-
-    @pl.when(step == 0)
-    def _():
-        frozen_copies[0].start()
-        apart_copy.start()
-        for copy in frozen_copies[1:]:
-            copy.start()
-        done[0] = 0.0
-
-        def fill(s, carry):
-            send[slot_of[sampled + s]] = jnp.zeros((block_len, columns), jnp.bfloat16)
-            return carry
-
-        lax.fori_loop(0, slots - sampled, fill, 0, unroll=4)
-
-    def normalize(far):
-        x = far[...].astype(jnp.float32)
-        total = jnp.sum(squares[...], axis=1, keepdims=True)
-        total = total + jnp.sum(x * x, axis=1, keepdims=True)
-        inverse = lax.rsqrt(total / width + RMS_EPSILON)
-        at = pl.ds(pl.multiple_of(step * chunk, chunk), chunk)
-        pieces = ((mine, mine_gain), (near, near_gain), (far, far_gain), (other, other_gain))
-        for p, (piece, gains) in enumerate(pieces):
-            three = gains[...].astype(jnp.float32)
-            gain = three[0:1] + three[1:2] + three[2:3]
-            to = pl.ds(pl.multiple_of(order[p] * part, part), part)
-            x = piece[...].astype(jnp.float32)
-            normed[at, to] = (x * inverse * gain).astype(jnp.bfloat16)
-
-    @pl.when(step < chunks // 2)
-    def _():
-        normalize(far_first)
-
-    @pl.when(step >= chunks // 2)
-    def _():
-        normalize(far_last)
-
-    @pl.when(step == chunks - 1)
-    def _():
-        apart_copy.wait()
-        for t in range(tiles):
-            frozen_copies[t].wait()
-            projected = jnp.dot(normed[...], frozen[t], preferred_element_type=jnp.float32)
-            at = slice(t * tile, (t + 1) * tile)
-            whole = apart[:, :, at] + projected.reshape(sampled, block_len, tile)
-            gap[:, :, at] = whole.astype(jnp.bfloat16)
-
-        def place(j, carry):
-            send[slot_of[j]] = gap[j]
-            return carry
-
-        lax.fori_loop(0, sampled, place, 0, unroll=8)
-        copy = pltpu.make_async_copy(send, send_out, sem.at[0])
+    started = copies[:3] + weights[:1]
+    for i in range(1, parts):
+        started += [copies[2 + i], weights[i]]
+    for copy in started + copies[6:]:
         copy.start()
+    done[0] = 0.0
+
+    def fill(s, carry):
+        send[slot_of[sampled + s]] = jnp.zeros((block_len, columns), jnp.bfloat16)
+        return carry
+
+    lax.fori_loop(0, slots - sampled, fill, 0, unroll=8)
+    for copy in copies[:3]:
         copy.wait()
-
-
-def base_gap_slots(slot_of, order, own, received, apart, squares, frozen):
+    chunk = 128
+
+    def invert(r):
+        at = slice(r * chunk, (r + 1) * chunk)
+        x = pieces[0, at].astype(jnp.float32)
+        sums = squares[at]
+        lanes = sums.shape[1]
+        for g in range(part // lanes):
+            sums = sums + x[:, g * lanes : (g + 1) * lanes] * x[:, g * lanes : (g + 1) * lanes]
+        mean = jnp.sum(sums, axis=1, keepdims=True) / (parts * part)
+        squares[at] = jnp.broadcast_to(lax.rsqrt(mean + RMS_EPSILON), sums.shape)
+
+    def normalize(i, r):
+        at = slice(r * chunk, (r + 1) * chunk)
+        three = pieces[i, rows : rows + 16].astype(jnp.float32)
+        gain = three[0:1] + three[1:2] + three[2:3]
+        x = pieces[i, at].astype(jnp.float32)
+        normed[i, at] = (x * squares[at, 0:1] * gain).astype(jnp.bfloat16)
+
+    chunks = rows // chunk
+    for r in range(chunks):
+        invert(r)
+        normalize(0, r)
+    tile = columns // TILES
+    for i in range(parts):
+        weights[i].wait()
+        if i + 1 < parts:
+            copies[3 + i].wait()
+        else:
+            copies[6].wait()
+        for n in range(TILES):
+            at = slice(n * tile, (n + 1) * tile)
+            product = jnp.dot(
+                normed[i], frozen[i, :, at], preferred_element_type=jnp.float32
+            )
+            if i > 0:
+                product = total[:, at] + product
+            if i + 1 < parts:
+                total[:, at] = product
+                for r in range(n * chunks // TILES, (n + 1) * chunks // TILES):
+                    normalize(i + 1, r)
+            else:
+                x = pieces[1, :rows, at].astype(jnp.float32)
+                whole = (x + product).reshape(sampled, block_len, tile)
+                gap[:, :, at] = (whole - taken[:, :, at].astype(jnp.float32)).astype(jnp.bfloat16)
+
+    def place(j, carry):
+        send[slot_of[j]] = gap[j]
+        return carry
+
+    lax.fori_loop(0, sampled, place, 0, unroll=8)
+    copy = pltpu.make_async_copy(send, send_out, sem.at[0])
+    copy.start()
+    copy.wait()
+
+
+def base_gap_slots(slot_of, order, own, received, taken, squares, frozen):
     near, other, far_first, far_last = received
-    part = near.shape[1]
+    height, part = near.shape
     width, columns = frozen.shape
     slots = slot_of.shape[0]
-    sampled, *block = apart.shape
+    sampled, *block = taken.shape
     rows = sampled * block[0]
-    tile = 256
-    tiles = columns // tile
-    chunk = 128
-    chunks = rows // chunk
-    half = chunks // 2
-    all_rows = pl.BlockSpec((chunk, part), lambda n: (n, 0))
-    all_gain = pl.BlockSpec((16, part), lambda n: (rows // 16, 0))
-    mine = own.reshape(-1, part)
+    parts = width // part
     smem = pl.BlockSpec(memory_space=pltpu.SMEM)
     hbm = pl.BlockSpec(memory_space=pltpu.HBM)
     return pl.pallas_call(
         gap_kernel,
-        grid=(chunks,),
         out_shape=(
             jax.ShapeDtypeStruct((slots, *block), jnp.bfloat16),
             jax.ShapeDtypeStruct((1,), jnp.float32),
         ),
-        in_specs=[
-            smem,
-            smem,
-            all_rows,
-            all_rows,
-            all_rows,
-            pl.BlockSpec((chunk, part), lambda n: (jnp.minimum(n, half - 1), 0)),
-            pl.BlockSpec((chunk, part), lambda n: (jnp.maximum(n - half, 0), 0)),
-            all_gain,
-            all_gain,
-            all_gain,
-            pl.BlockSpec((16, part), lambda n: (rows // 32, 0)),
-            pl.BlockSpec((chunk, squares.shape[1]), lambda n: (n, 0)),
-            hbm,
-            hbm,
-        ],
+        in_specs=[smem, smem] + [hbm] * 8,
         out_specs=(hbm, smem),
         scratch_shapes=[
-            pltpu.VMEM((sampled, *block), jnp.float32),
-            pltpu.VMEM((tiles, width, tile), jnp.bfloat16),
+            pltpu.VMEM((parts, height, part), jnp.bfloat16),
+            pltpu.VMEM(squares.shape, jnp.float32),
+            pltpu.VMEM((parts, part, columns), jnp.bfloat16),
+            pltpu.VMEM((sampled, *block), jnp.bfloat16),
             pltpu.VMEM((slots, *block), jnp.bfloat16),
-            pltpu.VMEM((rows, width), jnp.bfloat16),
+            pltpu.VMEM((parts, rows, part), jnp.bfloat16),
+            pltpu.VMEM((rows, columns), jnp.float32),
             pltpu.VMEM((sampled, *block), jnp.bfloat16),
-            pltpu.SemaphoreType.DMA((1 + tiles,)),
+            pltpu.SemaphoreType.DMA((7 + parts,)),
         ],
         compiler_params=pltpu.CompilerParams(vmem_limit_bytes=VMEM_BYTES),
         cost_estimate=pl.CostEstimate(
@@ -434,13 +441,15 @@
         ),
         name="base_gap",
     )(
-        slot_of, order, mine, near, other, far_first, far_last,
-        mine, near, other, far_last, squares, apart, frozen,
+        slot_of, order, far_first, far_last, own.reshape(-1, part), near, other, squares,
+        frozen, taken,
     )
 
 
 def trainer_kernel(gap, lowered, up, facts, grad_up, back, loss):
     step = pl.program_id(0)
+    rank, columns = up.shape
+    lanes = facts.shape[1]
     low = lowered[...]
     up_map = up[...]
     facts_now = facts[...]
@@ -449,21 +458,21 @@
     )
     output_grad = (facts_now[:, NB : NB + 1] * distance).astype(jnp.bfloat16)
     squares = jnp.sum(distance * distance, axis=1, keepdims=True)
-    part = jnp.sum(facts_now * squares, axis=0, keepdims=True)
-    back[...] = lax.dot_general(
+    loss[...] = jnp.zeros(loss.shape, jnp.float32)
+    loss[0:1, 0:lanes] = jnp.sum(facts_now * squares, axis=0, keepdims=True)
+    back[0:rank] = lax.dot_general(
         up_map, output_grad, CONTRACT_LAST, preferred_element_type=jnp.float32
     )
+    back[rank:] = loss[...]
     own = jnp.dot(low, output_grad, preferred_element_type=jnp.float32)
 
     @pl.when(step == 0)
     def _():
         grad_up[...] = own
-        loss[...] = part
 
     @pl.when(step > 0)
     def _():
         grad_up[...] += own
-        loss[...] += part
 
 
 def trainer_step(gap, lowered, up, facts):
@@ -476,8 +485,7 @@
         grid=(rows // chunk,),
         out_shape=(
             jax.ShapeDtypeStruct((rank, columns), jnp.float32),
-            jax.ShapeDtypeStruct((rank, rows), jnp.float32),
-            jax.ShapeDtypeStruct((1, lanes), jnp.float32),
+            jax.ShapeDtypeStruct((rank + 8, rows), jnp.float32),
         ),
         in_specs=[
             pl.BlockSpec((chunk, columns), lambda i: (i, 0)),
@@ -487,9 +495,9 @@
         ],
         out_specs=(
             pl.BlockSpec((rank, columns), lambda i: (0, 0)),
-            pl.BlockSpec((rank, chunk), lambda i: (0, i)),
-            pl.BlockSpec((1, lanes), lambda i: (0, 0)),
-        ),
+            pl.BlockSpec((rank + 8, chunk), lambda i: (0, i)),
+        ),
+        scratch_shapes=[pltpu.VMEM((8, chunk), jnp.float32)],
         compiler_params=pltpu.CompilerParams(vmem_limit_bytes=VMEM_BYTES),
         cost_estimate=pl.CostEstimate(
             flops=6 * rows * rank * columns, bytes_accessed=4 << 20, transcendentals=0
@@ -529,11 +537,11 @@
     cut = sampled * block_len // 2
     received = from_parts(own_x.reshape(-1, part), "mp", cut)
     order = lax.axis_index("mp") ^ jnp.arange(lax.axis_size("mp"), dtype=jnp.int32)
-    apart, near_squares = early_part(
+    taken, near_squares = early_part(
         sample_ids, own_x, received[0], received[1], pool_targets
     )
     send_gap, done = base_gap_slots(
-        slot_of, order, own_x, received, apart, near_squares, frozen
+        slot_of, order, own_x, received, taken, near_squares, frozen
     )
     got_gap = lax.all_to_all(
         send_gap.reshape(trainers, per_peer, part), DP, 0, 0, tiled=True
@@ -559,18 +567,15 @@
     normed, latent_part = latents(got_x, mean_squares, gain, down_map)
     lowered = (ADAPTER_SCALING * over_parts(latent_part, "mp")).astype(jnp.bfloat16)
 
-    grad_up, back_part, loss_part = trainer_step(
-        got_gap.reshape(rows, part), lowered, up_map, facts
-    )
-    everyone = trainers * lax.axis_size("mp")
+    grad_up, back_part = trainer_step(got_gap.reshape(rows, part), lowered, up_map, facts)
+    back = over_parts(back_part, "mp")
+    rank = up_map.shape[0]
+    own_loss = jnp.sum(back[rank].reshape(-1, 256)[:, :NB], axis=0)
     loss_sum = jnp.sum(
-        lax.all_to_all(
-            jnp.broadcast_to(loss_part[:, :NB], (everyone, 1, NB)), DP_MP, 0, 0, tiled=True
-        ),
+        lax.all_to_all(jnp.broadcast_to(own_loss, (trainers, 1, NB)), DP, 0, 0, tiled=True),
         axis=(0, 1),
     )
-    back = over_parts(back_part, "mp")
-    lowered_gradient = (ADAPTER_SCALING * back).astype(jnp.bfloat16)
+    lowered_gradient = (ADAPTER_SCALING * back[:rank]).astype(jnp.bfloat16)
     grad_down = jnp.dot(lowered_gradient, normed, preferred_element_type=jnp.float32)
     bucket_loss = loss_sum / (floor_counts * width)
     progress = jnp.sum(weights * bucket_loss) / jnp.sum(bucket_loss)

time: 191 us -> 182 us (0.953)
  Pallas kernels: 43.8 us -> 35.1 us
  waiting for transfers between devices: 82.1 us -> 84.8 us
  local copies, waits for them, and re-layouts: 5.93 us -> 3.63 us
    pallas_call x1, Pallas kernels: 17.9 us -> 9.85 us  [base_gap_slots(): pl.pallas_call(gap_kernel, out_shape=(jax.ShapeDtypeStruct((slots, *block...]
    ppermute x10, waiting for transfers between devices: 50.7 us -> 57.7 us  [swap(): return lax.ppermute(value, axis, [(i, i ^ distance) for i in range(peers)])]
    all_to_all x1, waiting for transfers between devices: 12.7 us -> 6.51 us  [on_device(): lax.all_to_all(jnp.broadcast_to(own_loss, (trainers, 1, NB)), DP, 0, 0, t...]
    ppermute x10, starting transfers between devices: 7.19 us -> 9.6 us  [swap(): return lax.ppermute(value, axis, [(i, i ^ distance) for i in range(peers)])]
  transfers between devices with their start and end apart: 13 -> 13, of which waited for: 9 -> 11; matrix products, arithmetic and copies ran while one was open for 7% -> 6% of each run, Pallas kernels for 17% -> 13%
where the time goes in v8:
time: 182 us
  waiting for transfers between devices  84.8 us (47%)
  starting transfers between devices  42.1 us (23%)
  Pallas kernels  35.1 us (19%)
  other arithmetic  9.29 us (5%)
  between operations  3.95 us (2%)
  local copies, waits for them, and re-layouts  3.63 us (2%)
  matrix products  2.78 us (2%)
    ppermute x10, waiting for transfers between devices, swap(): return lax.ppermute(value, axis, [(i, i ^ distance) for i in range(peers)])  57.7 us
    all_to_all x1, waiting for transfers between devices, on_device(): lax.all_to_all(send_gap.reshape(trainers, per_peer, part), DP, 0, 0, tile...  18.7 us
    all_to_all x1, starting transfers between devices, on_device(): got_x = lax.all_to_all(send_x, DP, 0, 0, tiled=True)  13.3 us
    all_to_all x1, starting transfers between devices, on_device(): lax.all_to_all(send_gap.reshape(trainers, per_peer, part), DP, 0, 0, tile...  11 us
    pallas_call x1, Pallas kernels, base_gap_slots(): pl.pallas_call(gap_kernel, out_shape=(jax.ShapeDtypeStruct((slots, *block...  9.85 us
    ppermute x10, starting transfers between devices, swap(): return lax.ppermute(value, axis, [(i, i ^ distance) for i in range(peers)])  9.6 us
    all_to_all x1, starting transfers between devices, on_device(): lax.all_to_all(jnp.broadcast_to(own_loss, (trainers, 1, NB)), DP, 0, 0, t...  8.2 us
    pallas_call x1, Pallas kernels, route(): pl.pallas_call(route_kernel, out_shape=(jax.ShapeDtypeStruct(message, poo...  6.84 us
  transfers between devices with their start and end apart: 13, of which 11 were waited for; matrix products, arithmetic and copies ran while one was open for 6% of the time, Pallas kernels for 13%

profile of v8, /device:TPU:1, one launch (start us, length us, event | category | flops | bytes accessed | tf_op | source)
XLA Modules:
  0.0 181.6 jit_solution(3421164160167808)
XLA Ops:
  0.6 6.8 %route.1 = (bf16[64,17,8,128]{3,2,1,0:T(8,128)(2,1)}, bf16[66,8,1024]{2,1,0:T(8,128)(2,1)}, s32[128]{0:T(128)}) custom-call(s32[64]{0:T(128)} %ids.1, s32[64]{0:T(128)} %bitcast.32, s32[128]{0:T(128)} %buckets_in.1, s32[128]{0:T(128)} %lengths_in.1, bf16[128,8,1024]{2,1,0:T(8,128)(2,1)} %pool_in.1, f32[1,1024]{1,0:T(1,128)} %bitcast.29), custom_call_target="tpu_custom_call" | custom-call | bytes 5242880 | tf_op jit(solution)/shard_map/route/pallas_call | solution.py:226
  7.5 13.3 %all-to-all-start.1 = ((bf16[64,17,8,128]{3,2,1,0:T(8,128)(2,1)}), bf16[64,17,8,128]{3,2,1,0:T(8,128)(2,1)}, u32[]{:S(2)}, u32[]{:S(2)}) async-start(bf16[64,17,8,128]{3,2,1,0:T(8,128)(2,1)} %get-tuple-element.20), calls=%async_computation.1 | async-start | bytes 4456448 | tf_op jit(solution)/shard_map/all_to_all | solution.py:536
  20.8 1.4 collective-permute-start.2
  22.2 1.9 %collective-permute-start = (bf16[528,1024]{1,0:T(8,128)(2,1)S(1)}, bf16[528,1024]{1,0:T(8,128)(2,1)S(1)}, u32[]{:S(2)}, u32[]{:S(2)}) collective-permute-start(bf16[528,1024]{1,0:T(8,128)(2,1)S(1)} %bitcast.25), channel_id=1, source_target_pairs={{0,3},{1,2},{2,1},{3,0},{4,7},{5,6},{6,5},{7,4},{8,11},{9,10},{10,... | collective-permute-start | bytes 3244040 | tf_op jit(solution)/shard_map/ppermute | solution.py:25
  24.1 21.8 %collective-permute-done.2.near.near_in = bf16[528,1024]{1,0:T(8,128)(2,1)S(1)} collective-permute-done((bf16[528,1024]{1,0:T(8,128)(2,1)S(1)}, bf16[528,1024]{1,0:T(8,128)(2,1)S(1)}, u32[]{:S(2)}, u32[]{:S(2)}) %collective-permute-start.2) | collective-permute-done | bytes 1081376 | tf_op jit(solution)/shard_map/ppermute | solution.py:25
  45.9 2.8 %collective-permute-start.3 = (bf16[272,1024]{1,0:T(8,128)(2,1)S(1)}, bf16[272,1024]{1,0:T(8,128)(2,1)}, u32[]{:S(2)}, u32[]{:S(2)}) collective-permute-start(bf16[272,1024]{1,0:T(8,128)(2,1)S(1)} %slice.45), channel_id=1, source_target_pairs={{0,3},{1,2},{2,1},{3,0},{4,7},{5,6},{6,5},{7,4},{8,11},{9,10},{10,... | collective-permute-start | bytes 1671176 | tf_op jit(solution)/shard_map/ppermute | solution.py:25
  48.8 1.1 copy-done.1
  51.2 4.9 %early_part.1 = (bf16[64,8,1024]{2,1,0:T(8,128)(2,1)}, f32[512,128]{1,0:T(8,128)}) custom-call(s32[64]{0:T(128)} %ids.1, bf16[66,8,1024]{2,1,0:T(8,128)(2,1)} %get-tuple-element.16.own, bf16[528,1024]{1,0:T(8,128)(2,1)} %copy-done, bf16[528,1024]{1,0:T(8,128)(2,1)} %copy-done.1, bf16[128,8,1024]{2,1,0:T(8,128)(2,1)} %targets.1), custom_call_target="tpu_custom_call" | custom-call | flops 6291456 | bytes 7340032 | tf_op jit(solution)/shard_map/early_part/pallas_call | solution.py:283
  56.1 6.8 %collective-permute-done.1.far_first_in = bf16[256,1024]{1,0:T(8,128)(2,1)} collective-permute-done((bf16[256,1024]{1,0:T(8,128)(2,1)}, bf16[256,1024]{1,0:T(8,128)(2,1)}, u32[]{:S(2)}, u32[]{:S(2)}) %collective-permute-start.1) | collective-permute-done | bytes 524320 | tf_op jit(solution)/shard_map/ppermute | solution.py:25
  62.9 9.9 %base_gap.1 = (bf16[128,8,1024]{2,1,0:T(8,128)(2,1)}, f32[1]{0:T(128)}) custom-call(s32[128]{0:T(128)} %get-tuple-element.15.slot_of, s32[4]{0:T(128)} %iota_xor_fusion.order, bf16[256,1024]{1,0:T(8,128)(2,1)} %collective-permute-done.1.far_first_in, bf16[272,1024]{1,0:T(8,128)(2,1)} %collective-permute-done.3.far_last_in, bf16[528,1024]{1,0:T(8,128)(2,1)} %bitcast.23, ...), custom_call_target="tpu_custom_call" | custom-call | flops 4294967296 | bytes 18874368 | tf_op jit(solution)/shard_map/base_gap/pallas_call | solution.py:419
  72.7 1.8 %all-to-all-done.1.packed = bf16[64,17,8,128]{3,2,1,0:T(8,128)(2,1)} async-done(((bf16[64,17,8,128]{3,2,1,0:T(8,128)(2,1)}), bf16[64,17,8,128]{3,2,1,0:T(8,128)(2,1)}, u32[]{:S(2)}, u32[]{:S(2)}) %all-to-all-start.1) | async-done | bytes 2228256 | tf_op jit(solution)/shard_map/all_to_all | solution.py:536
  74.6 11.0 %all-to-all-start = ((bf16[64,16,1024]{2,1,0:T(8,128)(2,1)}), bf16[64,16,1024]{2,1,0:T(8,128)(2,1)}, u32[]{:S(2)}, u32[]{:S(2)}) async-start(bf16[64,16,1024]{2,1,0:T(8,128)(2,1)} %bitcast.22), calls=%async_computation | async-start | bytes 4194304 | tf_op jit(solution)/shard_map/all_to_all | solution.py:546
  86.3 4.3 %row_squares.1 = f32[1,1024]{1,0:T(1,128)} custom-call(bf16[64,17,8,128]{3,2,1,0:T(8,128)(2,1)} %all-to-all-done.1.packed, f32[1]{0:T(128)} %get-tuple-element.21.done), custom_call_target="tpu_custom_call" | custom-call | flops 4194304 | bytes 2097152 | tf_op jit(solution)/shard_map/row_squares/pallas_call | solution.py:58
  91.9 0.9 fusion.4
  94.3 1.1 collective-permute-start.5
  95.5 2.9 %collective-permute-done.5 = f32[1,1024]{1,0:T(1,128)S(1)} collective-permute-done((f32[1,1024]{1,0:T(1,128)S(1)}, f32[1,1024]{1,0:T(1,128)S(1)}, u32[]{:S(2)}, u32[]{:S(2)}) %collective-permute-start.5) | collective-permute-done | bytes 4128 | tf_op jit(solution)/shard_map/ppermute | solution.py:25
  99.0 4.4 %latents.1 = (bf16[1024,1024]{1,0:T(8,128)(2,1)}, f32[64,1024]{1,0:T(8,128)}) custom-call(bf16[64,17,8,128]{3,2,1,0:T(8,128)(2,1)} %all-to-all-done.1.packed, f32[1,1024]{1,0:T(1,128)} %add_multiply_fusion.squares, f32[1,1024]{1,0:T(1,128)} %bitcast.30, bf16[64,1024]{1,0:T(8,128)(2,1)} %bitcast.27), custom_call_target="tpu_custom_call" | custom-call | flops 134217728 | bytes 4194304 | tf_op jit(solution)/shard_map/latents/pallas_call | solution.py:93
  104.2 5.2 %collective-permute-done.6 = f32[64,1024]{1,0:T(8,128)S(1)} collective-permute-done((f32[64,1024]{1,0:T(8,128)}, f32[64,1024]{1,0:T(8,128)S(1)}, u32[]{:S(2)}, u32[]{:S(2)}) %collective-permute-start.6) | collective-permute-done | bytes 262176 | tf_op jit(solution)/shard_map/ppermute | solution.py:25
  109.5 1.0 add.51
  110.4 1.2 collective-permute-start.7
  111.9 1.0 maximum_maximum_fusion.facts
  112.9 4.5 %collective-permute-done.7 = f32[64,1024]{1,0:T(8,128)S(1)} collective-permute-done((f32[64,1024]{1,0:T(8,128)S(1)}, f32[64,1024]{1,0:T(8,128)S(1)}, u32[]{:S(2)}, u32[]{:S(2)}) %collective-permute-start.7) | collective-permute-done | bytes 262176 | tf_op jit(solution)/shard_map/ppermute | solution.py:25
  118.0 18.7 %all-to-all-done = bf16[64,16,1024]{2,1,0:T(8,128)(2,1)} async-done(((bf16[64,16,1024]{2,1,0:T(8,128)(2,1)}), bf16[64,16,1024]{2,1,0:T(8,128)(2,1)}, u32[]{:S(2)}, u32[]{:S(2)}) %all-to-all-start) | async-done | bytes 2097184 | tf_op jit(solution)/shard_map/all_to_all | solution.py:546
  136.7 4.9 %trainer_step.1 = (f32[64,1024]{1,0:T(8,128)}, f32[72,1024]{1,0:T(8,128)}) custom-call(bf16[1024,1024]{1,0:T(8,128)(2,1)} %bitcast.4.gap, bf16[64,1024]{1,0:T(8,128)(2,1)} %multiply_convert_fusion.lowered, bf16[64,1024]{1,0:T(8,128)(2,1)} %bitcast.28, f32[1024,128]{1,0:T(8,128)} %maximum_maximum_fusion.facts), custom_call_target="tpu_custom_call" | custom-call | flops 402653184 | bytes 4194304 | tf_op jit(solution)/shard_map/trainer_step/pallas_call | solution.py:483
  141.6 8.4 %collective-permute-done.8 = f32[72,1024]{1,0:T(8,128)S(1)} collective-permute-done((f32[72,1024]{1,0:T(8,128)}, f32[72,1024]{1,0:T(8,128)S(1)}, u32[]{:S(2)}, u32[]{:S(2)}) %collective-permute-start.8) | collective-permute-done | bytes 294944 | tf_op jit(solution)/shard_map/ppermute | solution.py:25
  150.0 1.0 add.57
  151.0 1.2 collective-permute-start.9
  152.2 7.4 %collective-permute-done.9 = f32[72,1024]{1,0:T(8,128)S(1)} collective-permute-done((f32[72,1024]{1,0:T(8,128)S(1)}, f32[72,1024]{1,0:T(8,128)S(1)}, u32[]{:S(2)}, u32[]{:S(2)}) %collective-permute-start.9) | collective-permute-done | bytes 294944 | tf_op jit(solution)/shard_map/ppermute | solution.py:25
  160.3 8.2 %all-to-all-start.2 = ((f32[64,1,16]{2,1,0:T(1,128)}), f32[64,1,16]{2,1,0:T(1,128)S(1)}, u32[]{:S(2)}, u32[]{:S(2)}) async-start(f32[64,1,16]{2,1,0:T(1,128)} %broadcast_in_dim.32), calls=%async_computation.2 | async-start | bytes 65536 | tf_op jit(solution)/shard_map/all_to_all | solution.py:575
  168.5 2.8 %convolution_bitcast_fusion = f32[1,64,1024]{2,1,0:T(8,128)} fusion(bf16[1024,1024]{1,0:T(8,128)(2,1)} %get-tuple-element.24, f32[72,1024]{1,0:T(8,128)S(1)} %add.58), kind=kOutput, calls=%fused_computation | convolution fusion | flops 134348800 | bytes 2621440 | tf_op jit(solution)/shard_map/dot_general | solution.py:579
  171.3 6.5 %all-to-all-done.2 = f32[64,1,16]{2,1,0:T(1,128)S(1)} async-done(((f32[64,1,16]{2,1,0:T(1,128)}), f32[64,1,16]{2,1,0:T(1,128)S(1)}, u32[]{:S(2)}, u32[]{:S(2)}) %all-to-all-start.2) | async-done | bytes 4128 | tf_op jit(solution)/shard_map/all_to_all | solution.py:575
  177.9 1.2 fusion.14
  (40 shorter events, 7.5 us)
Async XLA Ops:
  7.5 13.3 %copy-start.2 = (bf16[66,8,1024]{2,1,0:T(8,128)(2,1)S(1)}, bf16[66,8,1024]{2,1,0:T(8,128)(2,1)}, u32[]{:S(2)}) copy-start(bf16[66,8,1024]{2,1,0:T(8,128)(2,1)} %get-tuple-element.16.own) | copy-start | bytes 3244036
  7.5 67.1 %all-to-all-start.1 = ((bf16[64,17,8,128]{3,2,1,0:T(8,128)(2,1)}), bf16[64,17,8,128]{3,2,1,0:T(8,128)(2,1)}, u32[]{:S(2)}, u32[]{:S(2)}) async-start(bf16[64,17,8,128]{3,2,1,0:T(8,128)(2,1)} %get-tuple-element.20), calls=%async_computation.1 | async-start | bytes 4456448 | tf_op jit(solution)/shard_map/all_to_all | solution.py:536
  20.8 25.1 %collective-permute-start.2 = (bf16[528,1024]{1,0:T(8,128)(2,1)S(1)}, bf16[528,1024]{1,0:T(8,128)(2,1)S(1)}, u32[]{:S(2)}, u32[]{:S(2)}) collective-permute-start(bf16[528,1024]{1,0:T(8,128)(2,1)S(1)} %bitcast.24), channel_id=1, source_target_pairs={{0,1},{1,0},{2,3},{3,2},{4,5},{5,4},{6,7},{7,6},{8,9},{9,8},{10,11... | collective-permute-start | bytes 3244040 | tf_op jit(solution)/shard_map/ppermute | solution.py:25
  22.2 26.6 %collective-permute-start = (bf16[528,1024]{1,0:T(8,128)(2,1)S(1)}, bf16[528,1024]{1,0:T(8,128)(2,1)S(1)}, u32[]{:S(2)}, u32[]{:S(2)}) collective-permute-start(bf16[528,1024]{1,0:T(8,128)(2,1)S(1)} %bitcast.25), channel_id=1, source_target_pairs={{0,3},{1,2},{2,1},{3,0},{4,7},{5,6},{6,5},{7,4},{8,11},{9,10},{10,... | collective-permute-start | bytes 3244040 | tf_op jit(solution)/shard_map/ppermute | solution.py:25
  45.9 5.3 %copy-start = (bf16[528,1024]{1,0:T(8,128)(2,1)}, bf16[528,1024]{1,0:T(8,128)(2,1)S(1)}, u32[]{:S(2)}) copy-start(bf16[528,1024]{1,0:T(8,128)(2,1)S(1)} %collective-permute-done.2.near.near_in) | copy-start | bytes 3244036
  45.9 16.9 %collective-permute-start.3 = (bf16[272,1024]{1,0:T(8,128)(2,1)S(1)}, bf16[272,1024]{1,0:T(8,128)(2,1)}, u32[]{:S(2)}, u32[]{:S(2)}) collective-permute-start(bf16[272,1024]{1,0:T(8,128)(2,1)S(1)} %slice.45), channel_id=1, source_target_pairs={{0,3},{1,2},{2,1},{3,0},{4,7},{5,6},{6,5},{7,4},{8,11},{9,10},{10,... | collective-permute-start | bytes 1671176 | tf_op jit(solution)/shard_map/ppermute | solution.py:25
  48.8 1.1 copy-start.1
  50.7 12.2 %collective-permute-start.1 = (bf16[256,1024]{1,0:T(8,128)(2,1)}, bf16[256,1024]{1,0:T(8,128)(2,1)}, u32[]{:S(2)}, u32[]{:S(2)}) collective-permute-start(bf16[256,1024]{1,0:T(8,128)(2,1)} %slice.44), channel_id=1, source_target_pairs={{0,1},{1,0},{2,3},{3,2},{4,5},{5,4},{6,7},{7,6},{8,9},{9,8},{10,11... | collective-permute-start | bytes 1572872 | tf_op jit(solution)/shard_map/ppermute | solution.py:25
  74.6 62.2 %all-to-all-start = ((bf16[64,16,1024]{2,1,0:T(8,128)(2,1)}), bf16[64,16,1024]{2,1,0:T(8,128)(2,1)}, u32[]{:S(2)}, u32[]{:S(2)}) async-start(bf16[64,16,1024]{2,1,0:T(8,128)(2,1)} %bitcast.22), calls=%async_computation | async-start | bytes 4194304 | tf_op jit(solution)/shard_map/all_to_all | solution.py:546
  90.6 3.1 %collective-permute-start.4 = (f32[1,1024]{1,0:T(1,128)}, f32[1,1024]{1,0:T(1,128)S(1)}, u32[]{:S(2)}, u32[]{:S(2)}) collective-permute-start(f32[1,1024]{1,0:T(1,128)} %row_squares.1), channel_id=1, source_target_pairs={{0,1},{1,0},{2,3},{3,2},{4,5},{5,4},{6,7},{7,6},{8,9},{9,8},{10,11... | collective-permute-start | bytes 12296 | tf_op jit(solution)/shard_map/ppermute | solution.py:25
  94.3 4.1 %collective-permute-start.5 = (f32[1,1024]{1,0:T(1,128)S(1)}, f32[1,1024]{1,0:T(1,128)S(1)}, u32[]{:S(2)}, u32[]{:S(2)}) collective-permute-start(f32[1,1024]{1,0:T(1,128)S(1)} %add.49), channel_id=1, source_target_pairs={{0,3},{1,2},{2,1},{3,0},{4,7},{5,6},{6,5},{7,4},{8,11},{9,10},{10,... | collective-permute-start | bytes 12296 | tf_op jit(solution)/shard_map/ppermute | solution.py:25
  103.4 6.1 %collective-permute-start.6 = (f32[64,1024]{1,0:T(8,128)}, f32[64,1024]{1,0:T(8,128)S(1)}, u32[]{:S(2)}, u32[]{:S(2)}) collective-permute-start(f32[64,1024]{1,0:T(8,128)} %get-tuple-element.22), channel_id=1, source_target_pairs={{0,1},{1,0},{2,3},{3,2},{4,5},{5,4},{6,7},{7,6},{8,9},{9,8},{10,11... | collective-permute-start | bytes 786440 | tf_op jit(solution)/shard_map/ppermute | solution.py:25
  110.4 6.9 %collective-permute-start.7 = (f32[64,1024]{1,0:T(8,128)S(1)}, f32[64,1024]{1,0:T(8,128)S(1)}, u32[]{:S(2)}, u32[]{:S(2)}) collective-permute-start(f32[64,1024]{1,0:T(8,128)S(1)} %add.51), channel_id=1, source_target_pairs={{0,3},{1,2},{2,1},{3,0},{4,7},{5,6},{6,5},{7,4},{8,11},{9,10},{10,... | collective-permute-start | bytes 786440 | tf_op jit(solution)/shard_map/ppermute | solution.py:25
  141.6 8.4 %collective-permute-start.8 = (f32[72,1024]{1,0:T(8,128)}, f32[72,1024]{1,0:T(8,128)S(1)}, u32[]{:S(2)}, u32[]{:S(2)}) collective-permute-start(f32[72,1024]{1,0:T(8,128)} %get-tuple-element.23), channel_id=1, source_target_pairs={{0,1},{1,0},{2,3},{3,2},{4,5},{5,4},{6,7},{7,6},{8,9},{9,8},{10,11... | collective-permute-start | bytes 884744 | tf_op jit(solution)/shard_map/ppermute | solution.py:25
  151.0 8.6 %collective-permute-start.9 = (f32[72,1024]{1,0:T(8,128)S(1)}, f32[72,1024]{1,0:T(8,128)S(1)}, u32[]{:S(2)}, u32[]{:S(2)}) collective-permute-start(f32[72,1024]{1,0:T(8,128)S(1)} %add.57), channel_id=1, source_target_pairs={{0,3},{1,2},{2,1},{3,0},{4,7},{5,6},{6,5},{7,4},{8,11},{9,10},{10,... | collective-permute-start | bytes 884744 | tf_op jit(solution)/shard_map/ppermute | solution.py:25
  160.3 17.5 %all-to-all-start.2 = ((f32[64,1,16]{2,1,0:T(1,128)}), f32[64,1,16]{2,1,0:T(1,128)S(1)}, u32[]{:S(2)}, u32[]{:S(2)}) async-start(f32[64,1,16]{2,1,0:T(1,128)} %broadcast_in_dim.32), calls=%async_computation.2 | async-start | bytes 65536 | tf_op jit(solution)/shard_map/all_to_all | solution.py:575

commit v9 on v8

--- a/solution.py
+++ b/solution.py
@@ -15,6 +15,7 @@
 ADAPTER_SCALING = 2.0
 PER_PAIR = 2
 TILES = 1
+MODEL_PARTS = 4
 VMEM_BYTES = 62 * 1024 * 1024
 CONTRACT_LAST = (((1,), (1,)), ((), ()))
 CONTRACT_FIRST = (((0,), (0,)), ((), ()))
@@ -30,10 +31,18 @@
     return pair + swap(pair, axis, 3)
 
 
-def from_parts(value, axis, cut):
-    near = swap(value, axis, 1)
-    other = swap(value, axis, 3)
-    return near, other, swap(other[:cut], axis, 1), swap(near[cut:], axis, 3)
+def rounded_over_parts(value, sent, axis):
+    pair = value + swap(sent, axis, 1).astype(jnp.float32)
+    return pair + swap(pair.astype(sent.dtype), axis, 3).astype(jnp.float32)
+
+
+def from_parts(first, last, axis):
+    other_first = swap(first, axis, 3)
+    near_last = swap(last, axis, 1)
+    near_first = swap(first, axis, 1)
+    other_last = swap(last, axis, 3)
+    far = (swap(other_first, axis, 1), swap(near_last, axis, 3))
+    return (near_first, near_last), (other_first, other_last), far
 
 
 def lane_group(packed, group, groups):
@@ -117,7 +126,7 @@
 
 def route_kernel(
     ids_in, dest_in, buckets_in, lengths_in, pool_in, gain_in,
-    send_out, own_out, slot_of,
+    send_out, first_out, last_out, slot_of,
     ids, dest, buckets, lengths, pool, gain, send, own, arrived, info, counts, sem,
 ):
     pairs = (
@@ -209,9 +218,15 @@
     zeros = jnp.zeros((own.shape[1] - 3, whole.shape[1]), jnp.float32)
     own[sampled] = jnp.concatenate([high, middle, low, zeros], axis=0).astype(jnp.bfloat16)
     own[sampled + 1] = jnp.zeros(own.shape[1:], own.dtype)
-    own_copy = pltpu.make_async_copy(own, own_out, sem.at[1])
-    own_copy.start()
-    own_copy.wait()
+    cut = first_out.shape[0]
+    own_copies = (
+        pltpu.make_async_copy(own.at[pl.ds(0, cut)], first_out, sem.at[1]),
+        pltpu.make_async_copy(own.at[pl.ds(cut, last_out.shape[0])], last_out, sem.at[2]),
+    )
+    for copy in own_copies:
+        copy.start()
+    for copy in own_copies:
+        copy.wait()
     send_copy.wait()
 
 
@@ -227,11 +242,12 @@
         route_kernel,
         out_shape=(
             jax.ShapeDtypeStruct(message, pool.dtype),
-            jax.ShapeDtypeStruct((sampled + 2, *block), pool.dtype),
+            jax.ShapeDtypeStruct((sampled // 2, *block), pool.dtype),
+            jax.ShapeDtypeStruct((sampled - sampled // 2 + 2, *block), pool.dtype),
             jax.ShapeDtypeStruct((slots,), jnp.int32),
         ),
         in_specs=[hbm] * 6,
-        out_specs=(hbm, hbm, smem),
+        out_specs=(hbm, hbm, hbm, smem),
         scratch_shapes=[
             pltpu.SMEM(ids.shape, jnp.int32),
             pltpu.SMEM(dest.shape, jnp.int32),
@@ -252,18 +268,32 @@
     )(ids, dest, buckets, lengths, pool, gain[None, :])
 
 
-def early_kernel(ids, own, near, other, targets, taken, squares):
+def early_kernel(
+    ids, mine_first, mine_last, near_first, near_last, other_first, other_last, targets,
+    taken, squares,
+):
     step = pl.program_id(0)
-    chunk, part = near.shape
+    half = pl.num_programs(0) // 2
+    part = near_first.shape[1]
     lanes = squares.shape[1]
-    blocks = own.shape[0]
-    sums = jnp.zeros(squares.shape, jnp.float32)
-    for g in range(part // lanes):
-        at = slice(g * lanes, (g + 1) * lanes)
-        for piece in (own[:, :, at].reshape(chunk, lanes), near[:, at], other[:, at]):
-            x = piece.astype(jnp.float32)
-            sums = sums + x * x
-    squares[...] = sums
+    blocks = taken.shape[0]
+
+    def add_squares(pieces):
+        sums = jnp.zeros(squares.shape, jnp.float32)
+        for g in range(part // lanes):
+            at = slice(g * lanes, (g + 1) * lanes)
+            for piece in pieces:
+                x = piece[:, at].astype(jnp.float32)
+                sums = sums + x * x
+        squares[...] = sums
+
+    @pl.when(step < half)
+    def _():
+        add_squares((mine_first, near_first, other_first))
+
+    @pl.when(step >= half)
+    def _():
+        add_squares((mine_last, near_last, other_last))
 
     def take(j, carry):
         taken[j] = targets[ids[step * blocks + j]]
@@ -272,14 +302,17 @@
     lax.fori_loop(0, blocks, take, 0, unroll=4)
 
 
-def early_part(ids, own, near, other, targets):
-    part = near.shape[1]
-    block = own.shape[1:]
+def early_part(ids, mine, near, other, targets):
+    part = near[0].shape[1]
+    block = targets.shape[1:]
     sampled = ids.shape[0]
     rows = sampled * block[0]
     chunk = 128
     blocks = chunk // block[0]
+    half = rows // chunk // 2
     lanes = 128
+    first = pl.BlockSpec((chunk, part), lambda n: (jnp.minimum(n, half - 1), 0))
+    last = pl.BlockSpec((chunk, part), lambda n: (jnp.maximum(n - half, 0), 0))
     return pl.pallas_call(
         early_kernel,
         grid=(rows // chunk,),
@@ -287,13 +320,9 @@
             jax.ShapeDtypeStruct((sampled, *block), jnp.bfloat16),
             jax.ShapeDtypeStruct((rows, lanes), jnp.float32),
         ),
-        in_specs=[
-            pl.BlockSpec(memory_space=pltpu.SMEM),
-            pl.BlockSpec((blocks, *block), lambda n: (n, 0, 0)),
-            pl.BlockSpec((chunk, part), lambda n: (n, 0)),
-            pl.BlockSpec((chunk, part), lambda n: (n, 0)),
-            pl.BlockSpec(targets.shape, lambda n: (0, 0, 0)),
-        ],
+        in_specs=[pl.BlockSpec(memory_space=pltpu.SMEM)]
+        + [first, last] * 3
+        + [pl.BlockSpec(targets.shape, lambda n: (0, 0, 0))],
         out_specs=(
             pl.BlockSpec((blocks, *block), lambda n: (n, 0, 0)),
             pl.BlockSpec((chunk, lanes), lambda n: (n, 0)),
@@ -301,46 +330,51 @@
         compiler_params=pltpu.CompilerParams(vmem_limit_bytes=VMEM_BYTES),
         cost_estimate=pl.CostEstimate(flops=6 << 20, bytes_accessed=7 << 20, transcendentals=0),
         name="early_part",
-    )(ids, own, near, other, targets)
+    )(ids, *mine, *near, *other, targets)
 
 
 def gap_kernel(
-    slot_of, order, far_first_in, far_last_in, mine_in, near_in, other_in, squares_in,
-    frozen_in, taken_in,
+    slot_of, order, far_first, far_last, mine_first, mine_last, near_first, near_last,
+    other_first, other_last, squares_in, frozen_in, taken_in,
     send_out, done, pieces, squares, frozen, taken, send, normed, total, gap, sem,
 ):
     parts, _, part = pieces.shape
     sampled, block_len, columns = gap.shape
     rows = sampled * block_len
-    cut = far_first_in.shape[0]
+    cut = far_first.shape[0]
     slots = send.shape[0]
     places = (2, 0, 1, 3)
+    halves = (
+        (far_first, far_last),
+        (mine_first, mine_last),
+        (near_first, near_last),
+        (other_first, other_last),
+    )
     copies = [
-        pltpu.make_async_copy(
-            far_first_in, pieces.at[0, pl.ds(0, cut)], sem.at[0]
-        ),
-        pltpu.make_async_copy(
-            far_last_in, pieces.at[0, pl.ds(cut, far_last_in.shape[0])], sem.at[1]
-        ),
-        pltpu.make_async_copy(squares_in, squares, sem.at[2]),
-        pltpu.make_async_copy(mine_in, pieces.at[1], sem.at[3]),
-        pltpu.make_async_copy(near_in, pieces.at[2], sem.at[4]),
-        pltpu.make_async_copy(other_in, pieces.at[3], sem.at[5]),
-        pltpu.make_async_copy(taken_in, taken, sem.at[6]),
+        (
+            pltpu.make_async_copy(first, pieces.at[i, pl.ds(0, cut)], sem.at[2 * i]),
+            pltpu.make_async_copy(
+                last, pieces.at[i, pl.ds(cut, last.shape[0])], sem.at[2 * i + 1]
+            ),
+        )
+        for i, (first, last) in enumerate(halves)
     ]
+    squares_copy = pltpu.make_async_copy(squares_in, squares, sem.at[2 * parts])
+    taken_copy = pltpu.make_async_copy(taken_in, taken, sem.at[2 * parts + 1])
     weights = [
         pltpu.make_async_copy(
             frozen_in.at[pl.ds(pl.multiple_of(order[places[i]] * part, part), part)],
             frozen.at[i],
-            sem.at[7 + i],
+            sem.at[2 * parts + 2 + i],
         )
         for i in range(parts)
     ]
-    started = copies[:3] + weights[:1]
-    for i in range(1, parts):
-        started += [copies[2 + i], weights[i]]
-    for copy in started + copies[6:]:
-        copy.start()
+    squares_copy.start()
+    for i in range(parts):
+        for copy in copies[i]:
+            copy.start()
+        weights[i].start()
+    taken_copy.start()
     done[0] = 0.0
 
     def fill(s, carry):
@@ -348,7 +382,8 @@
         return carry
 
     lax.fori_loop(0, slots - sampled, fill, 0, unroll=8)
-    for copy in copies[:3]:
+    squares_copy.wait()
+    for copy in copies[0]:
         copy.wait()
     chunk = 128
 
@@ -377,9 +412,10 @@
     for i in range(parts):
         weights[i].wait()
         if i + 1 < parts:
-            copies[3 + i].wait()
+            for copy in copies[i + 1]:
+                copy.wait()
         else:
-            copies[6].wait()
+            taken_copy.wait()
         for n in range(TILES):
             at = slice(n * tile, (n + 1) * tile)
             product = jnp.dot(
@@ -406,9 +442,9 @@
     copy.wait()
 
 
-def base_gap_slots(slot_of, order, own, received, taken, squares, frozen):
-    near, other, far_first, far_last = received
-    height, part = near.shape
+def base_gap_slots(slot_of, order, mine, near, other, far, taken, squares, frozen):
+    part = mine[0].shape[1]
+    height = mine[0].shape[0] + mine[1].shape[0]
     width, columns = frozen.shape
     slots = slot_of.shape[0]
     sampled, *block = taken.shape
@@ -422,7 +458,7 @@
             jax.ShapeDtypeStruct((slots, *block), jnp.bfloat16),
             jax.ShapeDtypeStruct((1,), jnp.float32),
         ),
-        in_specs=[smem, smem] + [hbm] * 8,
+        in_specs=[smem, smem] + [hbm] * 11,
         out_specs=(hbm, smem),
         scratch_shapes=[
             pltpu.VMEM((parts, height, part), jnp.bfloat16),
@@ -433,7 +469,7 @@
             pltpu.VMEM((parts, rows, part), jnp.bfloat16),
             pltpu.VMEM((rows, columns), jnp.float32),
             pltpu.VMEM((sampled, *block), jnp.bfloat16),
-            pltpu.SemaphoreType.DMA((7 + parts,)),
+            pltpu.SemaphoreType.DMA((3 * parts + 2,)),
         ],
         compiler_params=pltpu.CompilerParams(vmem_limit_bytes=VMEM_BYTES),
         cost_estimate=pl.CostEstimate(
@@ -441,15 +477,12 @@
         ),
         name="base_gap",
     )(
-        slot_of, order, far_first, far_last, own.reshape(-1, part), near, other, squares,
-        frozen, taken,
-    )
-
-
-def trainer_kernel(gap, lowered, up, facts, grad_up, back, loss):
+        slot_of, order, *far, *mine, *near, *other, squares, frozen, taken,
+    )
+
+
+def trainer_kernel(gap, lowered, up, facts, grad_up, back, sent, loss):
     step = pl.program_id(0)
-    rank, columns = up.shape
-    lanes = facts.shape[1]
     low = lowered[...]
     up_map = up[...]
     facts_now = facts[...]
@@ -458,21 +491,23 @@
     )
     output_grad = (facts_now[:, NB : NB + 1] * distance).astype(jnp.bfloat16)
     squares = jnp.sum(distance * distance, axis=1, keepdims=True)
-    loss[...] = jnp.zeros(loss.shape, jnp.float32)
-    loss[0:1, 0:lanes] = jnp.sum(facts_now * squares, axis=0, keepdims=True)
-    back[0:rank] = lax.dot_general(
+    part = jnp.sum(facts_now * squares, axis=0, keepdims=True)
+    back_now = lax.dot_general(
         up_map, output_grad, CONTRACT_LAST, preferred_element_type=jnp.float32
     )
-    back[rank:] = loss[...]
+    back[...] = back_now
+    sent[...] = back_now.astype(jnp.bfloat16)
     own = jnp.dot(low, output_grad, preferred_element_type=jnp.float32)
 
     @pl.when(step == 0)
     def _():
         grad_up[...] = own
+        loss[...] = part
 
     @pl.when(step > 0)
     def _():
         grad_up[...] += own
+        loss[...] += part
 
 
 def trainer_step(gap, lowered, up, facts):
@@ -485,7 +520,9 @@
         grid=(rows // chunk,),
         out_shape=(
             jax.ShapeDtypeStruct((rank, columns), jnp.float32),
-            jax.ShapeDtypeStruct((rank + 8, rows), jnp.float32),
+            jax.ShapeDtypeStruct((rank, rows), jnp.float32),
+            jax.ShapeDtypeStruct((rank, rows), jnp.bfloat16),
+            jax.ShapeDtypeStruct((1, lanes), jnp.float32),
         ),
         in_specs=[
             pl.BlockSpec((chunk, columns), lambda i: (i, 0)),
@@ -495,15 +532,44 @@
         ],
         out_specs=(
             pl.BlockSpec((rank, columns), lambda i: (0, 0)),
-            pl.BlockSpec((rank + 8, chunk), lambda i: (0, i)),
-        ),
-        scratch_shapes=[pltpu.VMEM((8, chunk), jnp.float32)],
+            pl.BlockSpec((rank, chunk), lambda i: (0, i)),
+            pl.BlockSpec((rank, chunk), lambda i: (0, i)),
+            pl.BlockSpec((1, lanes), lambda i: (0, 0)),
+        ),
         compiler_params=pltpu.CompilerParams(vmem_limit_bytes=VMEM_BYTES),
         cost_estimate=pl.CostEstimate(
             flops=6 * rows * rank * columns, bytes_accessed=4 << 20, transcendentals=0
         ),
         name="trainer_step",
     )(gap, lowered, up, facts)
+
+
+def down_kernel(back, normed, floor_counts, grad_down, denominators):
+    lowered_gradient = (ADAPTER_SCALING * back[...]).astype(jnp.bfloat16)
+    grad_down[...] = jnp.dot(
+        lowered_gradient, normed[...], preferred_element_type=jnp.float32
+    )
+    denominators[...] = floor_counts[...] * MODEL_PARTS * normed.shape[1]
+
+
+def down_step(back, normed, floor_counts):
+    rank, rows = back.shape
+    columns = normed.shape[1]
+    vmem = pl.BlockSpec(memory_space=pltpu.VMEM)
+    return pl.pallas_call(
+        down_kernel,
+        out_shape=(
+            jax.ShapeDtypeStruct((rank, columns), jnp.float32),
+            jax.ShapeDtypeStruct((1, floor_counts.shape[0]), jnp.float32),
+        ),
+        in_specs=[vmem] * 3,
+        out_specs=(vmem, vmem),
+        compiler_params=pltpu.CompilerParams(vmem_limit_bytes=VMEM_BYTES),
+        cost_estimate=pl.CostEstimate(
+            flops=2 * rows * rank * columns, bytes_accessed=3 << 20, transcendentals=0
+        ),
+        name="down_step",
+    )(back, normed, floor_counts[None, :])
 
 
 def on_device(
@@ -530,18 +596,16 @@
     up_map = adapter_up[0]
     bucket_range = jnp.arange(NB, dtype=jnp.int32)
 
-    send_x, own_x, slot_of = route(
+    send_x, own_first, own_last, slot_of = route(
         sample_ids, destinations[:, 0], buckets, lengths, pool_inputs, gain, trainers
     )
     got_x = lax.all_to_all(send_x, DP, 0, 0, tiled=True)
-    cut = sampled * block_len // 2
-    received = from_parts(own_x.reshape(-1, part), "mp", cut)
+    mine = (own_first.reshape(-1, part), own_last.reshape(-1, part))
+    near, other, far = from_parts(*mine, "mp")
     order = lax.axis_index("mp") ^ jnp.arange(lax.axis_size("mp"), dtype=jnp.int32)
-    taken, near_squares = early_part(
-        sample_ids, own_x, received[0], received[1], pool_targets
-    )
+    taken, near_squares = early_part(sample_ids, mine, near, other, pool_targets)
     send_gap, done = base_gap_slots(
-        slot_of, order, own_x, received, taken, near_squares, frozen
+        slot_of, order, mine, near, other, far, taken, near_squares, frozen
     )
     got_gap = lax.all_to_all(
         send_gap.reshape(trainers, per_peer, part), DP, 0, 0, tiled=True
@@ -567,17 +631,17 @@
     normed, latent_part = latents(got_x, mean_squares, gain, down_map)
     lowered = (ADAPTER_SCALING * over_parts(latent_part, "mp")).astype(jnp.bfloat16)
 
-    grad_up, back_part = trainer_step(got_gap.reshape(rows, part), lowered, up_map, facts)
-    back = over_parts(back_part, "mp")
-    rank = up_map.shape[0]
-    own_loss = jnp.sum(back[rank].reshape(-1, 256)[:, :NB], axis=0)
+    grad_up, back_part, back_sent, loss_part = trainer_step(
+        got_gap.reshape(rows, part), lowered, up_map, facts
+    )
+    own_loss = over_parts(loss_part, "mp")[:, :NB]
     loss_sum = jnp.sum(
         lax.all_to_all(jnp.broadcast_to(own_loss, (trainers, 1, NB)), DP, 0, 0, tiled=True),
         axis=(0, 1),
     )
-    lowered_gradient = (ADAPTER_SCALING * back[:rank]).astype(jnp.bfloat16)
-    grad_down = jnp.dot(lowered_gradient, normed, preferred_element_type=jnp.float32)
-    bucket_loss = loss_sum / (floor_counts * width)
+    back = rounded_over_parts(back_part, back_sent, "mp")
+    grad_down, denominators = down_step(back, normed, floor_counts)
+    bucket_loss = loss_sum / denominators[0]
     progress = jnp.sum(weights * bucket_loss) / jnp.sum(bucket_loss)
     competence_next = competence + 0.5 * (1.0 - competence) * progress
     return (grad_down[None], grad_up[None], bucket_loss, competence_next)

time: 182 us -> 178 us (0.978)
  waiting for transfers between devices: 84.8 us -> 77.5 us
  other arithmetic: 9.29 us -> 12.6 us
  Pallas kernels: 35.1 us -> 38.2 us
  matrix products: 2.78 us -> 0 us
    ppermute x10 -> x14, waiting for transfers between devices: 57.7 us -> 45.5 us  [swap(): return lax.ppermute(value, axis, [(i, i ^ distance) for i in range(peers)])]
    pallas_call x0 -> x1, Pallas kernels: none -> 2.78 us  [down_step(): pl.pallas_call(down_kernel, out_shape=(jax.ShapeDtypeStruct((rank, column...]
    dot_general x1 -> x0, matrix products: 2.78 us -> none  [on_device(): jnp.dot(lowered_gradient, normed, preferred_element_type=jnp.float32)]
    all_to_all x1, waiting for transfers between devices: 6.51 us -> 9.28 us  [on_device(): lax.all_to_all(jnp.broadcast_to(own_loss, (trainers, 1, NB)), DP, 0, 0, t...]
    all_to_all x1, starting transfers between devices: 11 us -> 8.77 us  [on_device(): lax.all_to_all(send_gap.reshape(trainers, per_peer, part), DP, 0, 0, tile...]
    all_to_all x1, waiting for transfers between devices: 1.84 us -> 4.06 us  [on_device(): got_x = lax.all_to_all(send_x, DP, 0, 0, tiled=True)]
    ppermute x10 -> x14, starting transfers between devices: 9.6 us -> 11.3 us  [swap(): return lax.ppermute(value, axis, [(i, i ^ distance) for i in range(peers)])]
  transfers between devices with their start and end apart: 13 -> 17, of which waited for: 11 -> 12; matrix products, arithmetic and copies ran while one was open for 6% -> 6% of each run, Pallas kernels for 13% -> 13%
where the time goes in v9:
time: 178 us; the launch traced here: 177 us
  waiting for transfers between devices  77.5 us (44%)
  starting transfers between devices  41.3 us (23%)
  Pallas kernels  38.2 us (21%)
  other arithmetic  12.6 us (7%)
  between operations  3.83 us (2%)
  local copies, waits for them, and re-layouts  3.26 us (2%)
    ppermute x14, waiting for transfers between devices, swap(): return lax.ppermute(value, axis, [(i, i ^ distance) for i in range(peers)])  45.5 us
    all_to_all x1, waiting for transfers between devices, on_device(): lax.all_to_all(send_gap.reshape(trainers, per_peer, part), DP, 0, 0, tile...  18.7 us
    all_to_all x1, starting transfers between devices, on_device(): got_x = lax.all_to_all(send_x, DP, 0, 0, tiled=True)  13.3 us
    ppermute x14, starting transfers between devices, swap(): return lax.ppermute(value, axis, [(i, i ^ distance) for i in range(peers)])  11.3 us
    pallas_call x1, Pallas kernels, base_gap_slots(): pl.pallas_call(gap_kernel, out_shape=(jax.ShapeDtypeStruct((slots, *block...  9.89 us
    all_to_all x1, waiting for transfers between devices, on_device(): lax.all_to_all(jnp.broadcast_to(own_loss, (trainers, 1, NB)), DP, 0, 0, t...  9.28 us
    all_to_all x1, starting transfers between devices, on_device(): lax.all_to_all(send_gap.reshape(trainers, per_peer, part), DP, 0, 0, tile...  8.77 us
    all_to_all x1, starting transfers between devices, on_device(): lax.all_to_all(jnp.broadcast_to(own_loss, (trainers, 1, NB)), DP, 0, 0, t...  7.96 us
  transfers between devices with their start and end apart: 17, of which 12 were waited for; matrix products, arithmetic and copies ran while one was open for 6% of the time, Pallas kernels for 13%

profile of v9, /device:TPU:1, one launch (start us, length us, event | category | flops | bytes accessed | tf_op | source)
XLA Modules:
  0.0 176.7 jit_solution(12931929984433958124)
XLA Ops:
  0.6 6.9 %route.1 = (bf16[64,17,8,128]{3,2,1,0:T(8,128)(2,1)}, bf16[32,8,1024]{2,1,0:T(8,128)(2,1)}, bf16[34,8,1024]{2,1,0:T(8,128)(2,1)}, s32[128]{0:T(128)}) custom-call(s32[64]{0:T(128)} %ids.1, s32[64]{0:T(128)} %bitcast.43, s32[128]{0:T(128)} %buckets_in.1, s32[128]{0:T(128)} %lengths_in.1, bf16[128,8,1024]{2,1,0:T(8,128)(2,1)} %pool_in.1, f32[1,1024]{1,0:T(1,128)} %bitcast.40), custom_call_target="tpu_custom_call" | custom-call | bytes 5242880 | tf_op jit(solution)/shard_map/route/pallas_call | solution.py:241
  7.6 13.3 %all-to-all-start.1 = ((bf16[64,17,8,128]{3,2,1,0:T(8,128)(2,1)}), bf16[64,17,8,128]{3,2,1,0:T(8,128)(2,1)}, u32[]{:S(2)}, u32[]{:S(2)}) async-start(bf16[64,17,8,128]{3,2,1,0:T(8,128)(2,1)} %get-tuple-element.26), calls=%async_computation.1 | async-start | bytes 4456448 | tf_op jit(solution)/shard_map/all_to_all | solution.py:602
  20.9 1.4 collective-permute-start.2
  22.3 1.9 %collective-permute-start = (bf16[256,1024]{1,0:T(8,128)(2,1)S(1)}, bf16[256,1024]{1,0:T(8,128)(2,1)}, u32[]{:S(2)}, u32[]{:S(2)}) collective-permute-start(bf16[256,1024]{1,0:T(8,128)(2,1)S(1)} %bitcast.35), channel_id=1, source_target_pairs={{0,3},{1,2},{2,1},{3,0},{4,7},{5,6},{6,5},{7,4},{8,11},{9,10},{10,... | collective-permute-start | bytes 1572872 | tf_op jit(solution)/shard_map/ppermute | solution.py:26
  24.9 9.8 %collective-permute-done.2.near_last = bf16[272,1024]{1,0:T(8,128)(2,1)S(1)} collective-permute-done((bf16[272,1024]{1,0:T(8,128)(2,1)S(1)}, bf16[272,1024]{1,0:T(8,128)(2,1)S(1)}, u32[]{:S(2)}, u32[]{:S(2)}) %collective-permute-start.2) | collective-permute-done | bytes 557088 | tf_op jit(solution)/shard_map/ppermute | solution.py:26
  34.7 2.7 %collective-permute-start.3 = (bf16[272,1024]{1,0:T(8,128)(2,1)S(1)}, bf16[272,1024]{1,0:T(8,128)(2,1)}, u32[]{:S(2)}, u32[]{:S(2)}) collective-permute-start(bf16[272,1024]{1,0:T(8,128)(2,1)S(1)} %collective-permute-done.2.near_last), channel_id=1, source_target_pairs={{0,3},{1,2},{2,1},{3,0},{4,7},{5,6},{6,5},{7,4},{8,11},{9,10},{10,... | collective-permute-start | bytes 1671176 | tf_op jit(solution)/shard_map/ppermute | solution.py:26
  37.5 1.5 collective-permute-start.1
  39.5 10.0 %collective-permute-done.4.near_first = bf16[256,1024]{1,0:T(8,128)(2,1)S(1)} collective-permute-done((bf16[256,1024]{1,0:T(8,128)(2,1)S(1)}, bf16[256,1024]{1,0:T(8,128)(2,1)S(1)}, u32[]{:S(2)}, u32[]{:S(2)}) %collective-permute-start.4) | collective-permute-done | bytes 524320 | tf_op jit(solution)/shard_map/ppermute | solution.py:26
  51.1 5.1 %early_part.1 = (bf16[64,8,1024]{2,1,0:T(8,128)(2,1)}, f32[512,128]{1,0:T(8,128)}) custom-call(s32[64]{0:T(128)} %ids.1, bf16[256,1024]{1,0:T(8,128)(2,1)} %bitcast.33, bf16[272,1024]{1,0:T(8,128)(2,1)} %bitcast.29, bf16[256,1024]{1,0:T(8,128)(2,1)} %copy-done.4, bf16[272,1024]{1,0:T(8,128)(2,1)} %copy-done.1, ...), custom_call_target="tpu_custom_call" | custom-call | flops 6291456 | bytes 7340032 | tf_op jit(solution)/shard_map/early_part/pallas_call | solution.py:316
  56.1 4.5 %collective-permute-done.1.far_first = bf16[256,1024]{1,0:T(8,128)(2,1)} collective-permute-done((bf16[256,1024]{1,0:T(8,128)(2,1)}, bf16[256,1024]{1,0:T(8,128)(2,1)}, u32[]{:S(2)}, u32[]{:S(2)}) %collective-permute-start.1) | collective-permute-done | bytes 524320 | tf_op jit(solution)/shard_map/ppermute | solution.py:26
  60.7 9.9 %base_gap.1 = (bf16[128,8,1024]{2,1,0:T(8,128)(2,1)}, f32[1]{0:T(128)}) custom-call(s32[128]{0:T(128)} %get-tuple-element.20.slot_of, s32[4]{0:T(128)} %iota_xor_fusion.order, bf16[256,1024]{1,0:T(8,128)(2,1)} %collective-permute-done.1.far_first, bf16[272,1024]{1,0:T(8,128)(2,1)} %collective-permute-done.3.far_last, bf16[256,1024]{1,0:T(8,128)(2,1)} %bitcast.34, ...), custom_call_target="tpu_custom_call" | custom-call | flops 4294967296 | bytes 18874368 | tf_op jit(solution)/shard_map/base_gap/pallas_call | solution.py:455
  70.6 4.1 %all-to-all-done.1.packed = bf16[64,17,8,128]{3,2,1,0:T(8,128)(2,1)} async-done(((bf16[64,17,8,128]{3,2,1,0:T(8,128)(2,1)}), bf16[64,17,8,128]{3,2,1,0:T(8,128)(2,1)}, u32[]{:S(2)}, u32[]{:S(2)}) %all-to-all-start.1) | async-done | bytes 2228256 | tf_op jit(solution)/shard_map/all_to_all | solution.py:602
  74.6 8.8 %all-to-all-start = ((bf16[64,16,1024]{2,1,0:T(8,128)(2,1)}), bf16[64,16,1024]{2,1,0:T(8,128)(2,1)}, u32[]{:S(2)}, u32[]{:S(2)}) async-start(bf16[64,16,1024]{2,1,0:T(8,128)(2,1)} %bitcast.28), calls=%async_computation | async-start | bytes 4194304 | tf_op jit(solution)/shard_map/all_to_all | solution.py:610
  84.2 4.3 %row_squares.1 = f32[1,1024]{1,0:T(1,128)} custom-call(bf16[64,17,8,128]{3,2,1,0:T(8,128)(2,1)} %all-to-all-done.1.packed, f32[1]{0:T(128)} %get-tuple-element.27.done), custom_call_target="tpu_custom_call" | custom-call | flops 4194304 | bytes 2097152 | tf_op jit(solution)/shard_map/row_squares/pallas_call | solution.py:67
  89.8 0.9 fusion.2
  92.6 3.6 %collective-permute-done.7 = f32[1,1024]{1,0:T(1,128)S(1)} collective-permute-done((f32[1,1024]{1,0:T(1,128)S(1)}, f32[1,1024]{1,0:T(1,128)S(1)}, u32[]{:S(2)}, u32[]{:S(2)}) %collective-permute-start.7) | collective-permute-done | bytes 4128 | tf_op jit(solution)/shard_map/ppermute | solution.py:26
  96.9 4.4 %latents.1 = (bf16[1024,1024]{1,0:T(8,128)(2,1)}, f32[64,1024]{1,0:T(8,128)}) custom-call(bf16[64,17,8,128]{3,2,1,0:T(8,128)(2,1)} %all-to-all-done.1.packed, f32[1,1024]{1,0:T(1,128)} %add_multiply_fusion.squares, f32[1,1024]{1,0:T(1,128)} %bitcast.41, bf16[64,1024]{1,0:T(8,128)(2,1)} %bitcast.38), custom_call_target="tpu_custom_call" | custom-call | flops 134217728 | bytes 4194304 | tf_op jit(solution)/shard_map/latents/pallas_call | solution.py:102
  102.6 4.7 %collective-permute-done.8 = f32[64,1024]{1,0:T(8,128)S(1)} collective-permute-done((f32[64,1024]{1,0:T(8,128)}, f32[64,1024]{1,0:T(8,128)S(1)}, u32[]{:S(2)}, u32[]{:S(2)}) %collective-permute-start.8) | collective-permute-done | bytes 262176 | tf_op jit(solution)/shard_map/ppermute | solution.py:26
  107.3 1.0 add.57
  109.0 1.0 maximum_maximum_fusion.facts
  110.0 5.2 %collective-permute-done.9 = f32[64,1024]{1,0:T(8,128)S(1)} collective-permute-done((f32[64,1024]{1,0:T(8,128)S(1)}, f32[64,1024]{1,0:T(8,128)S(1)}, u32[]{:S(2)}, u32[]{:S(2)}) %collective-permute-start.9) | collective-permute-done | bytes 262176 | tf_op jit(solution)/shard_map/ppermute | solution.py:26
  115.9 18.7 %all-to-all-done = bf16[64,16,1024]{2,1,0:T(8,128)(2,1)} async-done(((bf16[64,16,1024]{2,1,0:T(8,128)(2,1)}), bf16[64,16,1024]{2,1,0:T(8,128)(2,1)}, u32[]{:S(2)}, u32[]{:S(2)}) %all-to-all-start) | async-done | bytes 2097184 | tf_op jit(solution)/shard_map/all_to_all | solution.py:610
  134.6 4.9 %trainer_step.1 = (f32[64,1024]{1,0:T(8,128)}, f32[64,1024]{1,0:T(8,128)}, bf16[64,1024]{1,0:T(8,128)(2,1)}, f32[1,128]{1,0:T(1,128)}) custom-call(bf16[1024,1024]{1,0:T(8,128)(2,1)} %bitcast.5.gap, bf16[64,1024]{1,0:T(8,128)(2,1)} %multiply_convert_fusion.lowered, bf16[64,1024]{1,0:T(8,128)(2,1)} %bitcast.39, f32[1024,128]{1,0:T(8,128)} %maximum_maximum_fusion.facts), custom_call_target="tpu_custom_call" | custom-call | flops 402653184 | bytes 4194304 | tf_op jit(solution)/shard_map/trainer_step/pallas_call | solution.py:518
  139.6 1.5 collective-permute-start.12
  141.1 3.4 %collective-permute-done.12 = f32[1,128]{1,0:T(1,128)S(1)} collective-permute-done((f32[1,128]{1,0:T(1,128)}, f32[1,128]{1,0:T(1,128)S(1)}, u32[]{:S(2)}, u32[]{:S(2)}) %collective-permute-start.12) | collective-permute-done | bytes 544 | tf_op jit(solution)/shard_map/ppermute | solution.py:26
  145.5 3.3 %collective-permute-done.13 = f32[1,128]{1,0:T(1,128)S(1)} collective-permute-done((f32[1,128]{1,0:T(1,128)S(1)}, f32[1,128]{1,0:T(1,128)S(1)}, u32[]{:S(2)}, u32[]{:S(2)}) %collective-permute-start.13) | collective-permute-done | bytes 544 | tf_op jit(solution)/shard_map/ppermute | solution.py:26
  148.7 1.0 fusion.1
  150.8 8.0 %all-to-all-start.2 = ((f32[64,1,16]{2,1,0:T(1,128)}), f32[64,1,16]{2,1,0:T(1,128)S(1)}, u32[]{:S(2)}, u32[]{:S(2)}) async-start(f32[64,1,16]{2,1,0:T(1,128)} %broadcast_in_dim.33), calls=%async_computation.2 | async-start | bytes 65536 | tf_op jit(solution)/shard_map/all_to_all | solution.py:639
  158.7 9.3 %all-to-all-done.2 = f32[64,1,16]{2,1,0:T(1,128)S(1)} async-done(((f32[64,1,16]{2,1,0:T(1,128)}), f32[64,1,16]{2,1,0:T(1,128)S(1)}, u32[]{:S(2)}, u32[]{:S(2)}) %all-to-all-start.2) | async-done | bytes 4128 | tf_op jit(solution)/shard_map/all_to_all | solution.py:639
  168.1 1.7 convert_add_fusion.back
  169.8 2.8 %down_step.1 = (f32[64,1024]{1,0:T(8,128)}, f32[1,16]{1,0:T(1,128)}) custom-call(f32[64,1024]{1,0:T(8,128)} %convert_add_fusion.back, bf16[1024,1024]{1,0:T(8,128)(2,1)} %get-tuple-element.31.normed, f32[1,16]{1,0:T(1,128)} %get-tuple-element.43.floor_counts), custom_call_target="tpu_custom_call" | custom-call | flops 134217728 | bytes 3145728 | tf_op jit(solution)/shard_map/down_step/pallas_call | solution.py:559
  172.6 1.8 %fusion.11 = (f32[]{:T(128)}, f32[]{:T(128)}, f32[16]{0:T(128)}) fusion(f32[]{:T(128)} %bitcast.27, f32[16]{0:T(128)S(1)} %reduce_sum.47, f32[1,16]{1,0:T(1,128)} %get-tuple-element.35), kind=kLoop, calls=%fused_computation.32 | loop fusion | flops 190 | bytes 204 | tf_op jit(solution)/shard_map/reduce_sum | solution.py:645
  (50 shorter events, 11.7 us)
Async XLA Ops:
  7.5 13.3 %copy-start = (bf16[34,8,1024]{2,1,0:T(8,128)(2,1)S(1)}, bf16[34,8,1024]{2,1,0:T(8,128)(2,1)}, u32[]{:S(2)}) copy-start(bf16[34,8,1024]{2,1,0:T(8,128)(2,1)} %get-tuple-element.22) | copy-start | bytes 1671172
  7.6 14.7 %copy-start.3 = (bf16[32,8,1024]{2,1,0:T(8,128)(2,1)S(1)}, bf16[32,8,1024]{2,1,0:T(8,128)(2,1)}, u32[]{:S(2)}) copy-start(bf16[32,8,1024]{2,1,0:T(8,128)(2,1)} %get-tuple-element.21) | copy-start | bytes 1572868
  7.6 67.1 %all-to-all-start.1 = ((bf16[64,17,8,128]{3,2,1,0:T(8,128)(2,1)}), bf16[64,17,8,128]{3,2,1,0:T(8,128)(2,1)}, u32[]{:S(2)}, u32[]{:S(2)}) async-start(bf16[64,17,8,128]{3,2,1,0:T(8,128)(2,1)} %get-tuple-element.26), calls=%async_computation.1 | async-start | bytes 4456448 | tf_op jit(solution)/shard_map/all_to_all | solution.py:602
  20.9 13.9 %collective-permute-start.2 = (bf16[272,1024]{1,0:T(8,128)(2,1)S(1)}, bf16[272,1024]{1,0:T(8,128)(2,1)S(1)}, u32[]{:S(2)}, u32[]{:S(2)}) collective-permute-start(bf16[272,1024]{1,0:T(8,128)(2,1)S(1)} %bitcast.31), channel_id=1, source_target_pairs={{0,1},{1,0},{2,3},{3,2},{4,5},{5,4},{6,7},{7,6},{8,9},{9,8},{10,11... | collective-permute-start | bytes 1671176 | tf_op jit(solution)/shard_map/ppermute | solution.py:26
  22.3 15.2 %collective-permute-start = (bf16[256,1024]{1,0:T(8,128)(2,1)S(1)}, bf16[256,1024]{1,0:T(8,128)(2,1)}, u32[]{:S(2)}, u32[]{:S(2)}) collective-permute-start(bf16[256,1024]{1,0:T(8,128)(2,1)S(1)} %bitcast.35), channel_id=1, source_target_pairs={{0,3},{1,2},{2,1},{3,0},{4,7},{5,6},{6,5},{7,4},{8,11},{9,10},{10,... | collective-permute-start | bytes 1572872 | tf_op jit(solution)/shard_map/ppermute | solution.py:26
  24.2 26.1 %collective-permute-start.5 = (bf16[272,1024]{1,0:T(8,128)(2,1)S(1)}, bf16[272,1024]{1,0:T(8,128)(2,1)S(1)}, u32[]{:S(2)}, u32[]{:S(2)}) collective-permute-start(bf16[272,1024]{1,0:T(8,128)(2,1)S(1)} %bitcast.32), channel_id=1, source_target_pairs={{0,3},{1,2},{2,1},{3,0},{4,7},{5,6},{6,5},{7,4},{8,11},{9,10},{10,... | collective-permute-start | bytes 1671176 | tf_op jit(solution)/shard_map/ppermute | solution.py:26
  34.7 15.5 %copy-start.1 = (bf16[272,1024]{1,0:T(8,128)(2,1)}, bf16[272,1024]{1,0:T(8,128)(2,1)S(1)}, u32[]{:S(2)}) copy-start(bf16[272,1024]{1,0:T(8,128)(2,1)S(1)} %collective-permute-done.2.near_last) | copy-start | bytes 1671172
  34.7 25.9 %collective-permute-start.3 = (bf16[272,1024]{1,0:T(8,128)(2,1)S(1)}, bf16[272,1024]{1,0:T(8,128)(2,1)}, u32[]{:S(2)}, u32[]{:S(2)}) collective-permute-start(bf16[272,1024]{1,0:T(8,128)(2,1)S(1)} %collective-permute-done.2.near_last), channel_id=1, source_target_pairs={{0,3},{1,2},{2,1},{3,0},{4,7},{5,6},{6,5},{7,4},{8,11},{9,10},{10,... | collective-permute-start | bytes 1671176 | tf_op jit(solution)/shard_map/ppermute | solution.py:26
  37.5 12.0 %collective-permute-start.4 = (bf16[256,1024]{1,0:T(8,128)(2,1)S(1)}, bf16[256,1024]{1,0:T(8,128)(2,1)S(1)}, u32[]{:S(2)}, u32[]{:S(2)}) collective-permute-start(bf16[256,1024]{1,0:T(8,128)(2,1)S(1)} %bitcast.36), channel_id=1, source_target_pairs={{0,1},{1,0},{2,3},{3,2},{4,5},{5,4},{6,7},{7,6},{8,9},{9,8},{10,11... | collective-permute-start | bytes 1572872 | tf_op jit(solution)/shard_map/ppermute | solution.py:26
  37.5 23.2 %collective-permute-start.1 = (bf16[256,1024]{1,0:T(8,128)(2,1)}, bf16[256,1024]{1,0:T(8,128)(2,1)}, u32[]{:S(2)}, u32[]{:S(2)}) collective-permute-start(bf16[256,1024]{1,0:T(8,128)(2,1)} %collective-permute-done.other_first), channel_id=1, source_target_pairs={{0,1},{1,0},{2,3},{3,2},{4,5},{5,4},{6,7},{7,6},{8,9},{9,8},{10,11... | collective-permute-start | bytes 1572872 | tf_op jit(solution)/shard_map/ppermute | solution.py:26
  49.5 0.8 copy-start.4
  50.3 0.8 copy-start.2
  74.6 59.9 %all-to-all-start = ((bf16[64,16,1024]{2,1,0:T(8,128)(2,1)}), bf16[64,16,1024]{2,1,0:T(8,128)(2,1)}, u32[]{:S(2)}, u32[]{:S(2)}) async-start(bf16[64,16,1024]{2,1,0:T(8,128)(2,1)} %bitcast.28), calls=%async_computation | async-start | bytes 4194304 | tf_op jit(solution)/shard_map/all_to_all | solution.py:610
  88.4 3.1 %collective-permute-start.6 = (f32[1,1024]{1,0:T(1,128)}, f32[1,1024]{1,0:T(1,128)S(1)}, u32[]{:S(2)}, u32[]{:S(2)}) collective-permute-start(f32[1,1024]{1,0:T(1,128)} %row_squares.1), channel_id=1, source_target_pairs={{0,1},{1,0},{2,3},{3,2},{4,5},{5,4},{6,7},{7,6},{8,9},{9,8},{10,11... | collective-permute-start | bytes 12296 | tf_op jit(solution)/shard_map/ppermute | solution.py:26
  92.2 4.1 %collective-permute-start.7 = (f32[1,1024]{1,0:T(1,128)S(1)}, f32[1,1024]{1,0:T(1,128)S(1)}, u32[]{:S(2)}, u32[]{:S(2)}) collective-permute-start(f32[1,1024]{1,0:T(1,128)S(1)} %add.55), channel_id=1, source_target_pairs={{0,3},{1,2},{2,1},{3,0},{4,7},{5,6},{6,5},{7,4},{8,11},{9,10},{10,... | collective-permute-start | bytes 12296 | tf_op jit(solution)/shard_map/ppermute | solution.py:26
  101.2 6.1 %collective-permute-start.8 = (f32[64,1024]{1,0:T(8,128)}, f32[64,1024]{1,0:T(8,128)S(1)}, u32[]{:S(2)}, u32[]{:S(2)}) collective-permute-start(f32[64,1024]{1,0:T(8,128)} %get-tuple-element.28), channel_id=1, source_target_pairs={{0,1},{1,0},{2,3},{3,2},{4,5},{5,4},{6,7},{7,6},{8,9},{9,8},{10,11... | collective-permute-start | bytes 786440 | tf_op jit(solution)/shard_map/ppermute | solution.py:26
  108.3 6.9 %collective-permute-start.9 = (f32[64,1024]{1,0:T(8,128)S(1)}, f32[64,1024]{1,0:T(8,128)S(1)}, u32[]{:S(2)}, u32[]{:S(2)}) collective-permute-start(f32[64,1024]{1,0:T(8,128)S(1)} %add.57), channel_id=1, source_target_pairs={{0,3},{1,2},{2,1},{3,0},{4,7},{5,6},{6,5},{7,4},{8,11},{9,10},{10,... | collective-permute-start | bytes 786440 | tf_op jit(solution)/shard_map/ppermute | solution.py:26
  139.5 9.2 %collective-permute-start.10 = (bf16[64,1024]{1,0:T(8,128)(2,1)}, bf16[64,1024]{1,0:T(8,128)(2,1)S(1)}, u32[]{:S(2)}, u32[]{:S(2)}) collective-permute-start(bf16[64,1024]{1,0:T(8,128)(2,1)} %get-tuple-element.30), channel_id=1, source_target_pairs={{0,1},{1,0},{2,3},{3,2},{4,5},{5,4},{6,7},{7,6},{8,9},{9,8},{10,11... | collective-permute-start | bytes 393224 | tf_op jit(solution)/shard_map/ppermute | solution.py:26
  139.6 4.9 %collective-permute-start.12 = (f32[1,128]{1,0:T(1,128)}, f32[1,128]{1,0:T(1,128)S(1)}, u32[]{:S(2)}, u32[]{:S(2)}) collective-permute-start(f32[1,128]{1,0:T(1,128)} %get-tuple-element.34), channel_id=1, source_target_pairs={{0,1},{1,0},{2,3},{3,2},{4,5},{5,4},{6,7},{7,6},{8,9},{9,8},{10,11... | collective-permute-start | bytes 1544 | tf_op jit(solution)/shard_map/ppermute | solution.py:26
  145.1 3.6 %collective-permute-start.13 = (f32[1,128]{1,0:T(1,128)S(1)}, f32[1,128]{1,0:T(1,128)S(1)}, u32[]{:S(2)}, u32[]{:S(2)}) collective-permute-start(f32[1,128]{1,0:T(1,128)S(1)} %add.65), channel_id=1, source_target_pairs={{0,3},{1,2},{2,1},{3,0},{4,7},{5,6},{6,5},{7,4},{8,11},{9,10},{10,... | collective-permute-start | bytes 1544 | tf_op jit(solution)/shard_map/ppermute | solution.py:26
  149.7 18.4 %collective-permute-start.11 = (bf16[64,1024]{1,0:T(8,128)(2,1)S(1)}, bf16[64,1024]{1,0:T(8,128)(2,1)S(1)}, u32[]{:S(2)}, u32[]{:S(2)}) collective-permute-start(bf16[64,1024]{1,0:T(8,128)(2,1)S(1)} %fusion.1), channel_id=1, source_target_pairs={{0,3},{1,2},{2,1},{3,0},{4,7},{5,6},{6,5},{7,4},{8,11},{9,10},{10,... | collective-permute-start | bytes 393224 | tf_op jit(solution)/shard_map/ppermute | solution.py:26
  150.8 17.3 %all-to-all-start.2 = ((f32[64,1,16]{2,1,0:T(1,128)}), f32[64,1,16]{2,1,0:T(1,128)S(1)}, u32[]{:S(2)}, u32[]{:S(2)}) async-start(f32[64,1,16]{2,1,0:T(1,128)} %broadcast_in_dim.33), calls=%async_computation.2 | async-start | bytes 65536 | tf_op jit(solution)/shard_map/all_to_all | solution.py:639

commit v10 on v9

--- a/solution.py
+++ b/solution.py
@@ -15,7 +15,7 @@
 ADAPTER_SCALING = 2.0
 PER_PAIR = 2
 TILES = 1
-MODEL_PARTS = 4
+LAST_CHUNK = 256
 VMEM_BYTES = 62 * 1024 * 1024
 CONTRACT_LAST = (((1,), (1,)), ((), ()))
 CONTRACT_FIRST = (((0,), (0,)), ((), ()))
@@ -31,9 +31,12 @@
     return pair + swap(pair, axis, 3)
 
 
-def rounded_over_parts(value, sent, axis):
-    pair = value + swap(sent, axis, 1).astype(jnp.float32)
-    return pair + swap(pair.astype(sent.dtype), axis, 3).astype(jnp.float32)
+def in_three(row, height):
+    high = row.astype(jnp.bfloat16).astype(jnp.float32)
+    middle = (row - high).astype(jnp.bfloat16).astype(jnp.float32)
+    low = row - high - middle
+    zeros = jnp.zeros((height - 3, row.shape[1]), jnp.float32)
+    return jnp.concatenate([high, middle, low, zeros], axis=0).astype(jnp.bfloat16)
 
 
 def from_parts(first, last, axis):
@@ -496,7 +499,10 @@
         up_map, output_grad, CONTRACT_LAST, preferred_element_type=jnp.float32
     )
     back[...] = back_now
-    sent[...] = back_now.astype(jnp.bfloat16)
+    rank = up_map.shape[0]
+    lanes = loss.shape[1]
+    sent[0:rank] = back_now.astype(jnp.bfloat16)
+    sent[rank:] = jnp.zeros((sent.shape[0] - rank, sent.shape[1]), jnp.bfloat16)
     own = jnp.dot(low, output_grad, preferred_element_type=jnp.float32)
 
     @pl.when(step == 0)
@@ -509,19 +515,23 @@
         grad_up[...] += own
         loss[...] += part
 
+    @pl.when(step == pl.num_programs(0) - 1)
+    def _():
+        sent[rank:, 0:lanes] = in_three(loss[...], sent.shape[0] - rank)
+
 
 def trainer_step(gap, lowered, up, facts):
     rows, columns = gap.shape
     rank = up.shape[0]
     lanes = facts.shape[1]
-    chunk = 256
+    chunk = LAST_CHUNK
     return pl.pallas_call(
         trainer_kernel,
         grid=(rows // chunk,),
         out_shape=(
             jax.ShapeDtypeStruct((rank, columns), jnp.float32),
             jax.ShapeDtypeStruct((rank, rows), jnp.float32),
-            jax.ShapeDtypeStruct((rank, rows), jnp.bfloat16),
+            jax.ShapeDtypeStruct((rank + 16, rows), jnp.bfloat16),
             jax.ShapeDtypeStruct((1, lanes), jnp.float32),
         ),
         in_specs=[
@@ -533,7 +543,7 @@
         out_specs=(
             pl.BlockSpec((rank, columns), lambda i: (0, 0)),
             pl.BlockSpec((rank, chunk), lambda i: (0, i)),
-            pl.BlockSpec((rank, chunk), lambda i: (0, i)),
+            pl.BlockSpec((rank + 16, chunk), lambda i: (0, i)),
             pl.BlockSpec((1, lanes), lambda i: (0, 0)),
         ),
         compiler_params=pltpu.CompilerParams(vmem_limit_bytes=VMEM_BYTES),
@@ -544,32 +554,62 @@
     )(gap, lowered, up, facts)
 
 
-def down_kernel(back, normed, floor_counts, grad_down, denominators):
-    lowered_gradient = (ADAPTER_SCALING * back[...]).astype(jnp.bfloat16)
+def pair_kernel(back, loss, got, pair, pair_loss, sent):
+    rank, rows = back.shape
+    lanes = loss.shape[1]
+    at = slice(rows - LAST_CHUNK, rows - LAST_CHUNK + lanes)
+    total = back[...] + got[0:rank].astype(jnp.float32)
+    pair[...] = total
+    sent[0:rank] = total.astype(jnp.bfloat16)
+    three = got[rank:, at].astype(jnp.float32)
+    whole = loss[...] + (three[0:1] + three[1:2] + three[2:3])
+    pair_loss[...] = whole
+    height = sent.shape[0] - rank
+    sent[rank:] = jnp.zeros((height, rows), jnp.bfloat16)
+    sent[rank:, at] = in_three(whole, height)
+
+
+def pair_step(back, loss, got):
+    vmem = pl.BlockSpec(memory_space=pltpu.VMEM)
+    return pl.pallas_call(
+        pair_kernel,
+        out_shape=(
+            jax.ShapeDtypeStruct(back.shape, jnp.float32),
+            jax.ShapeDtypeStruct(loss.shape, jnp.float32),
+            jax.ShapeDtypeStruct(got.shape, jnp.bfloat16),
+        ),
+        in_specs=[vmem] * 3,
+        out_specs=(vmem, vmem, vmem),
+        compiler_params=pltpu.CompilerParams(vmem_limit_bytes=VMEM_BYTES),
+        cost_estimate=pl.CostEstimate(flops=1 << 17, bytes_accessed=1 << 20, transcendentals=0),
+        name="pair_step",
+    )(back, loss, got)
+
+
+def down_kernel(pair, got, normed, grad_down):
+    rank = pair.shape[0]
+    back = pair[...] + got[0:rank].astype(jnp.float32)
+    lowered_gradient = (ADAPTER_SCALING * back).astype(jnp.bfloat16)
     grad_down[...] = jnp.dot(
         lowered_gradient, normed[...], preferred_element_type=jnp.float32
     )
-    denominators[...] = floor_counts[...] * MODEL_PARTS * normed.shape[1]
-
-
-def down_step(back, normed, floor_counts):
-    rank, rows = back.shape
+
+
+def down_step(pair, got, normed):
+    rank, rows = pair.shape
     columns = normed.shape[1]
     vmem = pl.BlockSpec(memory_space=pltpu.VMEM)
     return pl.pallas_call(
         down_kernel,
-        out_shape=(
-            jax.ShapeDtypeStruct((rank, columns), jnp.float32),
-            jax.ShapeDtypeStruct((1, floor_counts.shape[0]), jnp.float32),
-        ),
+        out_shape=jax.ShapeDtypeStruct((rank, columns), jnp.float32),
         in_specs=[vmem] * 3,
-        out_specs=(vmem, vmem),
+        out_specs=vmem,
         compiler_params=pltpu.CompilerParams(vmem_limit_bytes=VMEM_BYTES),
         cost_estimate=pl.CostEstimate(
             flops=2 * rows * rank * columns, bytes_accessed=3 << 20, transcendentals=0
         ),
         name="down_step",
-    )(back, normed, floor_counts[None, :])
+    )(pair, got, normed)
 
 
 def on_device(
@@ -634,14 +674,18 @@
     grad_up, back_part, back_sent, loss_part = trainer_step(
         got_gap.reshape(rows, part), lowered, up_map, facts
     )
-    own_loss = over_parts(loss_part, "mp")[:, :NB]
+    pair, pair_loss, pair_sent = pair_step(back_part, loss_part, swap(back_sent, "mp", 1))
+    got_pair = swap(pair_sent, "mp", 3)
+    rank = up_map.shape[0]
+    at = rows - LAST_CHUNK
+    three = got_pair[rank : rank + 3, at : at + NB].astype(jnp.float32)
+    own_loss = pair_loss[0, :NB] + (three[0] + three[1] + three[2])
     loss_sum = jnp.sum(
         lax.all_to_all(jnp.broadcast_to(own_loss, (trainers, 1, NB)), DP, 0, 0, tiled=True),
         axis=(0, 1),
     )
-    back = rounded_over_parts(back_part, back_sent, "mp")
-    grad_down, denominators = down_step(back, normed, floor_counts)
-    bucket_loss = loss_sum / denominators[0]
+    grad_down = down_step(pair, got_pair, normed)
+    bucket_loss = loss_sum / (floor_counts * width)
     progress = jnp.sum(weights * bucket_loss) / jnp.sum(bucket_loss)
     competence_next = competence + 0.5 * (1.0 - competence) * progress
     return (grad_down[None], grad_up[None], bucket_loss, competence_next)

time: 178 us -> 177 us (level)
  other arithmetic: 12.6 us -> 8.9 us
  Pallas kernels: 38.2 us -> 40.2 us
    ppermute x14 -> x12, waiting for transfers between devices: 45.5 us -> 50 us  [swap(): return lax.ppermute(value, axis, [(i, i ^ distance) for i in range(peers)])]
    all_to_all x1, waiting for transfers between devices: 9.28 us -> 6.33 us  [on_device(): lax.all_to_all(jnp.broadcast_to(own_loss, (trainers, 1, NB)), DP, 0, 0, t...]
    pallas_call x1 -> x2, Pallas kernels: 2.78 us -> 4.74 us  [the longest x1 2.95 us: down_step(): pl.pallas_call(down_kernel, out_shape=jax.ShapeDtypeStruct((rank, columns...]
    ppermute x14 -> x12, starting transfers between devices: 11.3 us -> 9.47 us  [swap(): return lax.ppermute(value, axis, [(i, i ^ distance) for i in range(peers)])]
  transfers between devices with their start and end apart: 17 -> 15, of which waited for: 12 -> 12; matrix products, arithmetic and copies ran while one was open for 6% -> 5% of each run, Pallas kernels for 13% -> 15%
where the time goes in v10:
time: 177 us; the launch traced here: 176 us
  waiting for transfers between devices  79.1 us (45%)
  Pallas kernels  40.2 us (23%)
  starting transfers between devices  40 us (23%)
  other arithmetic  8.9 us (5%)
  between operations  3.96 us (2%)
  local copies, waits for them, and re-layouts  3.92 us (2%)
    ppermute x12, waiting for transfers between devices, swap(): return lax.ppermute(value, axis, [(i, i ^ distance) for i in range(peers)])  50 us
    all_to_all x1, waiting for transfers between devices, on_device(): lax.all_to_all(send_gap.reshape(trainers, per_peer, part), DP, 0, 0, tile...  18.7 us
    all_to_all x1, starting transfers between devices, on_device(): got_x = lax.all_to_all(send_x, DP, 0, 0, tiled=True)  13.3 us
    pallas_call x1, Pallas kernels, base_gap_slots(): pl.pallas_call(gap_kernel, out_shape=(jax.ShapeDtypeStruct((slots, *block...  9.88 us
    ppermute x12, starting transfers between devices, swap(): return lax.ppermute(value, axis, [(i, i ^ distance) for i in range(peers)])  9.47 us
    all_to_all x1, starting transfers between devices, on_device(): lax.all_to_all(send_gap.reshape(trainers, per_peer, part), DP, 0, 0, tile...  8.76 us
    all_to_all x1, starting transfers between devices, on_device(): lax.all_to_all(jnp.broadcast_to(own_loss, (trainers, 1, NB)), DP, 0, 0, t...  8.5 us
    pallas_call x1, Pallas kernels, route(): pl.pallas_call(route_kernel, out_shape=(jax.ShapeDtypeStruct(message, poo...  6.91 us
  transfers between devices with their start and end apart: 15, of which 12 were waited for; matrix products, arithmetic and copies ran while one was open for 5% of the time, Pallas kernels for 15%

profile of v10, /device:TPU:1, one launch (start us, length us, event | category | flops | bytes accessed | tf_op | source)
XLA Modules:
  0.0 176.1 jit_solution(10404554273826445772)
XLA Ops:
  0.6 6.9 %route.1 = (bf16[64,17,8,128]{3,2,1,0:T(8,128)(2,1)}, bf16[32,8,1024]{2,1,0:T(8,128)(2,1)}, bf16[34,8,1024]{2,1,0:T(8,128)(2,1)}, s32[128]{0:T(128)}) custom-call(s32[64]{0:T(128)} %ids.1, s32[64]{0:T(128)} %bitcast.39, s32[128]{0:T(128)} %buckets_in.1, s32[128]{0:T(128)} %lengths_in.1, bf16[128,8,1024]{2,1,0:T(8,128)(2,1)} %pool_in.1, f32[1,1024]{1,0:T(1,128)} %bitcast.36), custom_call_target="tpu_custom_call" | custom-call | bytes 5242880 | tf_op jit(solution)/shard_map/route/pallas_call | solution.py:244
  7.6 13.3 %all-to-all-start.1 = ((bf16[64,17,8,128]{3,2,1,0:T(8,128)(2,1)}), bf16[64,17,8,128]{3,2,1,0:T(8,128)(2,1)}, u32[]{:S(2)}, u32[]{:S(2)}) async-start(bf16[64,17,8,128]{3,2,1,0:T(8,128)(2,1)} %get-tuple-element.27), calls=%async_computation.1 | async-start | bytes 4456448 | tf_op jit(solution)/shard_map/all_to_all | solution.py:642
  20.9 1.4 collective-permute-start.2
  22.3 1.9 %collective-permute-start = (bf16[256,1024]{1,0:T(8,128)(2,1)S(1)}, bf16[256,1024]{1,0:T(8,128)(2,1)}, u32[]{:S(2)}, u32[]{:S(2)}) collective-permute-start(bf16[256,1024]{1,0:T(8,128)(2,1)S(1)} %bitcast.30), channel_id=1, source_target_pairs={{0,3},{1,2},{2,1},{3,0},{4,7},{5,6},{6,5},{7,4},{8,11},{9,10},{10,... | collective-permute-start | bytes 1572872 | tf_op jit(solution)/shard_map/ppermute | solution.py:26
  24.9 9.8 %collective-permute-done.2.near_last = bf16[272,1024]{1,0:T(8,128)(2,1)S(1)} collective-permute-done((bf16[272,1024]{1,0:T(8,128)(2,1)S(1)}, bf16[272,1024]{1,0:T(8,128)(2,1)S(1)}, u32[]{:S(2)}, u32[]{:S(2)}) %collective-permute-start.2) | collective-permute-done | bytes 557088 | tf_op jit(solution)/shard_map/ppermute | solution.py:26
  34.7 2.7 %collective-permute-start.3 = (bf16[272,1024]{1,0:T(8,128)(2,1)S(1)}, bf16[272,1024]{1,0:T(8,128)(2,1)}, u32[]{:S(2)}, u32[]{:S(2)}) collective-permute-start(bf16[272,1024]{1,0:T(8,128)(2,1)S(1)} %collective-permute-done.2.near_last), channel_id=1, source_target_pairs={{0,3},{1,2},{2,1},{3,0},{4,7},{5,6},{6,5},{7,4},{8,11},{9,10},{10,... | collective-permute-start | bytes 1671176 | tf_op jit(solution)/shard_map/ppermute | solution.py:26
  37.5 1.5 collective-permute-start.1
  39.5 10.0 %collective-permute-done.4.near_first = bf16[256,1024]{1,0:T(8,128)(2,1)S(1)} collective-permute-done((bf16[256,1024]{1,0:T(8,128)(2,1)S(1)}, bf16[256,1024]{1,0:T(8,128)(2,1)S(1)}, u32[]{:S(2)}, u32[]{:S(2)}) %collective-permute-start.4) | collective-permute-done | bytes 524320 | tf_op jit(solution)/shard_map/ppermute | solution.py:26
  50.3 0.8 copy-done.2
  51.1 5.1 %early_part.1 = (bf16[64,8,1024]{2,1,0:T(8,128)(2,1)}, f32[512,128]{1,0:T(8,128)}) custom-call(s32[64]{0:T(128)} %ids.1, bf16[256,1024]{1,0:T(8,128)(2,1)} %bitcast.28, bf16[272,1024]{1,0:T(8,128)(2,1)} %bitcast.24, bf16[256,1024]{1,0:T(8,128)(2,1)} %copy-done.4, bf16[272,1024]{1,0:T(8,128)(2,1)} %copy-done.1, ...), custom_call_target="tpu_custom_call" | custom-call | flops 6291456 | bytes 7340032 | tf_op jit(solution)/shard_map/early_part/pallas_call | solution.py:319
  56.1 4.5 %collective-permute-done.1.far_first = bf16[256,1024]{1,0:T(8,128)(2,1)} collective-permute-done((bf16[256,1024]{1,0:T(8,128)(2,1)}, bf16[256,1024]{1,0:T(8,128)(2,1)}, u32[]{:S(2)}, u32[]{:S(2)}) %collective-permute-start.1) | collective-permute-done | bytes 524320 | tf_op jit(solution)/shard_map/ppermute | solution.py:26
  60.7 9.9 %base_gap.1 = (bf16[128,8,1024]{2,1,0:T(8,128)(2,1)}, f32[1]{0:T(128)}) custom-call(s32[128]{0:T(128)} %get-tuple-element.21.slot_of, s32[4]{0:T(128)} %iota_xor_fusion.order, bf16[256,1024]{1,0:T(8,128)(2,1)} %collective-permute-done.1.far_first, bf16[272,1024]{1,0:T(8,128)(2,1)} %collective-permute-done.3.far_last, bf16[256,1024]{1,0:T(8,128)(2,1)} %bitcast.29, ...), custom_call_target="tpu_custom_call" | custom-call | flops 4294967296 | bytes 18874368 | tf_op jit(solution)/shard_map/base_gap/pallas_call | solution.py:458
  70.6 4.1 %all-to-all-done.1.packed = bf16[64,17,8,128]{3,2,1,0:T(8,128)(2,1)} async-done(((bf16[64,17,8,128]{3,2,1,0:T(8,128)(2,1)}), bf16[64,17,8,128]{3,2,1,0:T(8,128)(2,1)}, u32[]{:S(2)}, u32[]{:S(2)}) %all-to-all-start.1) | async-done | bytes 2228256 | tf_op jit(solution)/shard_map/all_to_all | solution.py:642
  74.6 8.8 %all-to-all-start = ((bf16[64,16,1024]{2,1,0:T(8,128)(2,1)}), bf16[64,16,1024]{2,1,0:T(8,128)(2,1)}, u32[]{:S(2)}, u32[]{:S(2)}) async-start(bf16[64,16,1024]{2,1,0:T(8,128)(2,1)} %bitcast.23), calls=%async_computation | async-start | bytes 4194304 | tf_op jit(solution)/shard_map/all_to_all | solution.py:650
  84.1 4.3 %row_squares.1 = f32[1,1024]{1,0:T(1,128)} custom-call(bf16[64,17,8,128]{3,2,1,0:T(8,128)(2,1)} %all-to-all-done.1.packed, f32[1]{0:T(128)} %get-tuple-element.28.done), custom_call_target="tpu_custom_call" | custom-call | flops 4194304 | bytes 2097152 | tf_op jit(solution)/shard_map/row_squares/pallas_call | solution.py:70
  88.4 0.9 fusion.2
  89.8 0.9 fusion.1
  92.6 3.6 %collective-permute-done.7 = f32[1,1024]{1,0:T(1,128)S(1)} collective-permute-done((f32[1,1024]{1,0:T(1,128)S(1)}, f32[1,1024]{1,0:T(1,128)S(1)}, u32[]{:S(2)}, u32[]{:S(2)}) %collective-permute-start.7) | collective-permute-done | bytes 4128 | tf_op jit(solution)/shard_map/ppermute | solution.py:26
  96.9 4.4 %latents.1 = (bf16[1024,1024]{1,0:T(8,128)(2,1)}, f32[64,1024]{1,0:T(8,128)}) custom-call(bf16[64,17,8,128]{3,2,1,0:T(8,128)(2,1)} %all-to-all-done.1.packed, f32[1,1024]{1,0:T(1,128)} %add_multiply_fusion.squares, f32[1,1024]{1,0:T(1,128)} %bitcast.37, bf16[64,1024]{1,0:T(8,128)(2,1)} %bitcast.34), custom_call_target="tpu_custom_call" | custom-call | flops 134217728 | bytes 4194304 | tf_op jit(solution)/shard_map/latents/pallas_call | solution.py:105
  102.1 5.2 %collective-permute-done.8 = f32[64,1024]{1,0:T(8,128)S(1)} collective-permute-done((f32[64,1024]{1,0:T(8,128)}, f32[64,1024]{1,0:T(8,128)S(1)}, u32[]{:S(2)}, u32[]{:S(2)}) %collective-permute-start.8) | collective-permute-done | bytes 262176 | tf_op jit(solution)/shard_map/ppermute | solution.py:26
  107.3 1.0 add.59
  109.0 1.0 maximum_maximum_fusion.facts
  110.0 5.2 %collective-permute-done.9 = f32[64,1024]{1,0:T(8,128)S(1)} collective-permute-done((f32[64,1024]{1,0:T(8,128)S(1)}, f32[64,1024]{1,0:T(8,128)S(1)}, u32[]{:S(2)}, u32[]{:S(2)}) %collective-permute-start.9) | collective-permute-done | bytes 262176 | tf_op jit(solution)/shard_map/ppermute | solution.py:26
  115.9 18.7 %all-to-all-done = bf16[64,16,1024]{2,1,0:T(8,128)(2,1)} async-done(((bf16[64,16,1024]{2,1,0:T(8,128)(2,1)}), bf16[64,16,1024]{2,1,0:T(8,128)(2,1)}, u32[]{:S(2)}, u32[]{:S(2)}) %all-to-all-start) | async-done | bytes 2097184 | tf_op jit(solution)/shard_map/all_to_all | solution.py:650
  134.6 5.0 %trainer_step.1 = (f32[64,1024]{1,0:T(8,128)}, f32[64,1024]{1,0:T(8,128)}, bf16[80,1024]{1,0:T(8,128)(2,1)}, f32[1,128]{1,0:T(1,128)}) custom-call(bf16[1024,1024]{1,0:T(8,128)(2,1)} %bitcast.5.gap, bf16[64,1024]{1,0:T(8,128)(2,1)} %multiply_convert_fusion.lowered, bf16[64,1024]{1,0:T(8,128)(2,1)} %bitcast.35, f32[1024,128]{1,0:T(8,128)} %maximum_maximum_fusion.facts), custom_call_target="tpu_custom_call" | custom-call | flops 402653184 | bytes 4194304 | tf_op jit(solution)/shard_map/trainer_step/pallas_call | solution.py:528
  139.6 5.6 %collective-permute-done.10.got = bf16[80,1024]{1,0:T(8,128)(2,1)S(1)} collective-permute-done((bf16[80,1024]{1,0:T(8,128)(2,1)}, bf16[80,1024]{1,0:T(8,128)(2,1)S(1)}, u32[]{:S(2)}, u32[]{:S(2)}) %collective-permute-start.10) | collective-permute-done | bytes 163872 | tf_op jit(solution)/shard_map/ppermute | solution.py:26
  145.9 1.8 %pair_step.1 = (f32[64,1024]{1,0:T(8,128)}, f32[1,128]{1,0:T(1,128)}, bf16[80,1024]{1,0:T(8,128)(2,1)}) custom-call(f32[64,1024]{1,0:T(8,128)} %get-tuple-element.30.back, f32[1,128]{1,0:T(1,128)} %get-tuple-element.31.loss, bf16[80,1024]{1,0:T(8,128)(2,1)} %copy-done.6), custom_call_target="tpu_custom_call" | custom-call | flops 131072 | bytes 1048576 | tf_op jit(solution)/shard_map/pair_step/pallas_call | solution.py:574
  148.0 5.2 %collective-permute-done.11.got = bf16[80,1024]{1,0:T(8,128)(2,1)S(1)} collective-permute-done((bf16[80,1024]{1,0:T(8,128)(2,1)}, bf16[80,1024]{1,0:T(8,128)(2,1)S(1)}, u32[]{:S(2)}, u32[]{:S(2)}) %collective-permute-start.11) | collective-permute-done | bytes 163872 | tf_op jit(solution)/shard_map/ppermute | solution.py:26
  154.5 8.5 %all-to-all-start.2 = ((f32[64,1,16]{2,1,0:T(1,128)}), f32[64,1,16]{2,1,0:T(1,128)S(1)}, u32[]{:S(2)}, u32[]{:S(2)}) async-start(f32[64,1,16]{2,1,0:T(1,128)} %broadcast_in_dim.32), calls=%async_computation.2 | async-start | bytes 65536 | tf_op jit(solution)/shard_map/all_to_all | solution.py:684
  163.0 3.0 %down_step.1 = f32[64,1024]{1,0:T(8,128)} custom-call(f32[64,1024]{1,0:T(8,128)} %get-tuple-element.33.pair, bf16[80,1024]{1,0:T(8,128)(2,1)} %copy-done.5, bf16[1024,1024]{1,0:T(8,128)(2,1)} %get-tuple-element.35.normed), custom_call_target="tpu_custom_call" | custom-call | flops 134217728 | bytes 3145728 | tf_op jit(solution)/shard_map/down_step/pallas_call | solution.py:602
  166.0 6.3 %all-to-all-done.2 = f32[64,1,16]{2,1,0:T(1,128)S(1)} async-done(((f32[64,1,16]{2,1,0:T(1,128)}), f32[64,1,16]{2,1,0:T(1,128)S(1)}, u32[]{:S(2)}, u32[]{:S(2)}) %all-to-all-start.2) | async-done | bytes 4128 | tf_op jit(solution)/shard_map/all_to_all | solution.py:684
  172.4 1.2 fusion.10
  (48 shorter events, 9.7 us)
Async XLA Ops:
  7.6 13.3 %copy-start = (bf16[34,8,1024]{2,1,0:T(8,128)(2,1)S(1)}, bf16[34,8,1024]{2,1,0:T(8,128)(2,1)}, u32[]{:S(2)}) copy-start(bf16[34,8,1024]{2,1,0:T(8,128)(2,1)} %get-tuple-element.23) | copy-start | bytes 1671172
  7.6 14.7 %copy-start.3 = (bf16[32,8,1024]{2,1,0:T(8,128)(2,1)S(1)}, bf16[32,8,1024]{2,1,0:T(8,128)(2,1)}, u32[]{:S(2)}) copy-start(bf16[32,8,1024]{2,1,0:T(8,128)(2,1)} %get-tuple-element.22) | copy-start | bytes 1572868
  7.6 67.1 %all-to-all-start.1 = ((bf16[64,17,8,128]{3,2,1,0:T(8,128)(2,1)}), bf16[64,17,8,128]{3,2,1,0:T(8,128)(2,1)}, u32[]{:S(2)}, u32[]{:S(2)}) async-start(bf16[64,17,8,128]{3,2,1,0:T(8,128)(2,1)} %get-tuple-element.27), calls=%async_computation.1 | async-start | bytes 4456448 | tf_op jit(solution)/shard_map/all_to_all | solution.py:642
  20.9 13.9 %collective-permute-start.2 = (bf16[272,1024]{1,0:T(8,128)(2,1)S(1)}, bf16[272,1024]{1,0:T(8,128)(2,1)S(1)}, u32[]{:S(2)}, u32[]{:S(2)}) collective-permute-start(bf16[272,1024]{1,0:T(8,128)(2,1)S(1)} %bitcast.26), channel_id=1, source_target_pairs={{0,1},{1,0},{2,3},{3,2},{4,5},{5,4},{6,7},{7,6},{8,9},{9,8},{10,11... | collective-permute-start | bytes 1671176 | tf_op jit(solution)/shard_map/ppermute | solution.py:26
  22.3 15.2 %collective-permute-start = (bf16[256,1024]{1,0:T(8,128)(2,1)S(1)}, bf16[256,1024]{1,0:T(8,128)(2,1)}, u32[]{:S(2)}, u32[]{:S(2)}) collective-permute-start(bf16[256,1024]{1,0:T(8,128)(2,1)S(1)} %bitcast.30), channel_id=1, source_target_pairs={{0,3},{1,2},{2,1},{3,0},{4,7},{5,6},{6,5},{7,4},{8,11},{9,10},{10,... | collective-permute-start | bytes 1572872 | tf_op jit(solution)/shard_map/ppermute | solution.py:26
  24.2 26.1 %collective-permute-start.5 = (bf16[272,1024]{1,0:T(8,128)(2,1)S(1)}, bf16[272,1024]{1,0:T(8,128)(2,1)S(1)}, u32[]{:S(2)}, u32[]{:S(2)}) collective-permute-start(bf16[272,1024]{1,0:T(8,128)(2,1)S(1)} %bitcast.27), channel_id=1, source_target_pairs={{0,3},{1,2},{2,1},{3,0},{4,7},{5,6},{6,5},{7,4},{8,11},{9,10},{10,... | collective-permute-start | bytes 1671176 | tf_op jit(solution)/shard_map/ppermute | solution.py:26
  34.7 15.5 %copy-start.1 = (bf16[272,1024]{1,0:T(8,128)(2,1)}, bf16[272,1024]{1,0:T(8,128)(2,1)S(1)}, u32[]{:S(2)}) copy-start(bf16[272,1024]{1,0:T(8,128)(2,1)S(1)} %collective-permute-done.2.near_last) | copy-start | bytes 1671172
  34.7 25.9 %collective-permute-start.3 = (bf16[272,1024]{1,0:T(8,128)(2,1)S(1)}, bf16[272,1024]{1,0:T(8,128)(2,1)}, u32[]{:S(2)}, u32[]{:S(2)}) collective-permute-start(bf16[272,1024]{1,0:T(8,128)(2,1)S(1)} %collective-permute-done.2.near_last), channel_id=1, source_target_pairs={{0,3},{1,2},{2,1},{3,0},{4,7},{5,6},{6,5},{7,4},{8,11},{9,10},{10,... | collective-permute-start | bytes 1671176 | tf_op jit(solution)/shard_map/ppermute | solution.py:26
  37.5 12.0 %collective-permute-start.4 = (bf16[256,1024]{1,0:T(8,128)(2,1)S(1)}, bf16[256,1024]{1,0:T(8,128)(2,1)S(1)}, u32[]{:S(2)}, u32[]{:S(2)}) collective-permute-start(bf16[256,1024]{1,0:T(8,128)(2,1)S(1)} %bitcast.31), channel_id=1, source_target_pairs={{0,1},{1,0},{2,3},{3,2},{4,5},{5,4},{6,7},{7,6},{8,9},{9,8},{10,11... | collective-permute-start | bytes 1572872 | tf_op jit(solution)/shard_map/ppermute | solution.py:26
  37.5 23.2 %collective-permute-start.1 = (bf16[256,1024]{1,0:T(8,128)(2,1)}, bf16[256,1024]{1,0:T(8,128)(2,1)}, u32[]{:S(2)}, u32[]{:S(2)}) collective-permute-start(bf16[256,1024]{1,0:T(8,128)(2,1)} %collective-permute-done.other_first), channel_id=1, source_target_pairs={{0,1},{1,0},{2,3},{3,2},{4,5},{5,4},{6,7},{7,6},{8,9},{9,8},{10,11... | collective-permute-start | bytes 1572872 | tf_op jit(solution)/shard_map/ppermute | solution.py:26
  49.5 0.8 copy-start.4
  50.3 0.8 copy-start.2
  74.6 59.9 %all-to-all-start = ((bf16[64,16,1024]{2,1,0:T(8,128)(2,1)}), bf16[64,16,1024]{2,1,0:T(8,128)(2,1)}, u32[]{:S(2)}, u32[]{:S(2)}) async-start(bf16[64,16,1024]{2,1,0:T(8,128)(2,1)} %bitcast.23), calls=%async_computation | async-start | bytes 4194304 | tf_op jit(solution)/shard_map/all_to_all | solution.py:650
  88.4 3.1 %collective-permute-start.6 = (f32[1,1024]{1,0:T(1,128)}, f32[1,1024]{1,0:T(1,128)S(1)}, u32[]{:S(2)}, u32[]{:S(2)}) collective-permute-start(f32[1,1024]{1,0:T(1,128)} %row_squares.1), channel_id=1, source_target_pairs={{0,1},{1,0},{2,3},{3,2},{4,5},{5,4},{6,7},{7,6},{8,9},{9,8},{10,11... | collective-permute-start | bytes 12296 | tf_op jit(solution)/shard_map/ppermute | solution.py:26
  92.2 4.1 %collective-permute-start.7 = (f32[1,1024]{1,0:T(1,128)S(1)}, f32[1,1024]{1,0:T(1,128)S(1)}, u32[]{:S(2)}, u32[]{:S(2)}) collective-permute-start(f32[1,1024]{1,0:T(1,128)S(1)} %add.57), channel_id=1, source_target_pairs={{0,3},{1,2},{2,1},{3,0},{4,7},{5,6},{6,5},{7,4},{8,11},{9,10},{10,... | collective-permute-start | bytes 12296 | tf_op jit(solution)/shard_map/ppermute | solution.py:26
  101.2 6.1 %collective-permute-start.8 = (f32[64,1024]{1,0:T(8,128)}, f32[64,1024]{1,0:T(8,128)S(1)}, u32[]{:S(2)}, u32[]{:S(2)}) collective-permute-start(f32[64,1024]{1,0:T(8,128)} %get-tuple-element.29), channel_id=1, source_target_pairs={{0,1},{1,0},{2,3},{3,2},{4,5},{5,4},{6,7},{7,6},{8,9},{9,8},{10,11... | collective-permute-start | bytes 786440 | tf_op jit(solution)/shard_map/ppermute | solution.py:26
  108.3 6.9 %collective-permute-start.9 = (f32[64,1024]{1,0:T(8,128)S(1)}, f32[64,1024]{1,0:T(8,128)S(1)}, u32[]{:S(2)}, u32[]{:S(2)}) collective-permute-start(f32[64,1024]{1,0:T(8,128)S(1)} %add.59), channel_id=1, source_target_pairs={{0,3},{1,2},{2,1},{3,0},{4,7},{5,6},{6,5},{7,4},{8,11},{9,10},{10,... | collective-permute-start | bytes 786440 | tf_op jit(solution)/shard_map/ppermute | solution.py:26
  139.5 5.7 %collective-permute-start.10 = (bf16[80,1024]{1,0:T(8,128)(2,1)}, bf16[80,1024]{1,0:T(8,128)(2,1)S(1)}, u32[]{:S(2)}, u32[]{:S(2)}) collective-permute-start(bf16[80,1024]{1,0:T(8,128)(2,1)} %get-tuple-element.32), channel_id=1, source_target_pairs={{0,1},{1,0},{2,3},{3,2},{4,5},{5,4},{6,7},{7,6},{8,9},{9,8},{10,11... | collective-permute-start | bytes 491528 | tf_op jit(solution)/shard_map/ppermute | solution.py:26
  145.2 0.7 copy-start.6
  147.6 5.6 %collective-permute-start.11 = (bf16[80,1024]{1,0:T(8,128)(2,1)}, bf16[80,1024]{1,0:T(8,128)(2,1)S(1)}, u32[]{:S(2)}, u32[]{:S(2)}) collective-permute-start(bf16[80,1024]{1,0:T(8,128)(2,1)} %get-tuple-element.34), channel_id=1, source_target_pairs={{0,3},{1,2},{2,1},{3,0},{4,7},{5,6},{6,5},{7,4},{8,11},{9,10},{10,... | collective-permute-start | bytes 491528 | tf_op jit(solution)/shard_map/ppermute | solution.py:26
  153.2 9.8 %copy-start.5 = (bf16[80,1024]{1,0:T(8,128)(2,1)}, bf16[80,1024]{1,0:T(8,128)(2,1)S(1)}, u32[]{:S(2)}) copy-start(bf16[80,1024]{1,0:T(8,128)(2,1)S(1)} %collective-permute-done.11.got) | copy-start | bytes 491524
  154.5 17.8 %all-to-all-start.2 = ((f32[64,1,16]{2,1,0:T(1,128)}), f32[64,1,16]{2,1,0:T(1,128)S(1)}, u32[]{:S(2)}, u32[]{:S(2)}) async-start(f32[64,1,16]{2,1,0:T(1,128)} %broadcast_in_dim.32), calls=%async_computation.2 | async-start | bytes 65536 | tf_op jit(solution)/shard_map/all_to_all | solution.py:684

commit v11 on v10

--- a/solution.py
+++ b/solution.py
@@ -15,7 +15,7 @@
 ADAPTER_SCALING = 2.0
 PER_PAIR = 2
 TILES = 1
-LAST_CHUNK = 256
+LAST_CHUNK = 512
 VMEM_BYTES = 62 * 1024 * 1024
 CONTRACT_LAST = (((1,), (1,)), ((), ()))
 CONTRACT_FIRST = (((0,), (0,)), ((), ()))
@@ -161,8 +161,8 @@
         counts[b] = 0
         return carry
 
-    lax.fori_loop(0, trainers, clear, 0)
-    lax.fori_loop(0, NB, clear_counts, 0)
+    lax.fori_loop(0, trainers, clear, 0, unroll=8)
+    lax.fori_loop(0, NB, clear_counts, 0, unroll=8)
     for copy in copies:
         copy.wait()
 
@@ -184,36 +184,7 @@
         counts[bucket] = counts[bucket] + length
         return carry
 
-    lax.fori_loop(0, sampled, place, 0)
-
-    row = lax.broadcasted_iota(jnp.int32, (block_len, lanes), 0)
-    lane = lax.broadcasted_iota(jnp.int32, (block_len, lanes), 1)
-    holder = jnp.zeros((block_len, lanes), jnp.int32)
-    for b in range(NB):
-        count = counts[b]
-        holder = jnp.where((row == 1) & (lane == b), count // 16, holder)
-        holder = jnp.where((row == 2) & (lane == b), count % 16, holder)
-
-    def finish(k, found):
-        for s in range(PER_PAIR):
-            free = arrived[k] <= s
-
-            @pl.when(free)
-            def _():
-                slot_of[sampled + found] = k * PER_PAIR + s
-                for g in range(groups):
-                    send[k, s * groups + g] = jnp.zeros((block_len, lanes), send.dtype)
-
-            found = found + jnp.where(free, 1, 0)
-        facts = holder
-        for i in range(2 * PER_PAIR):
-            facts = jnp.where((row == 0) & (lane == i), info[i, k], facts)
-        send[k, pieces - 1] = facts.astype(jnp.float32).astype(send.dtype)
-        return found
-
-    lax.fori_loop(0, trainers, finish, 0)
-    send_copy = pltpu.make_async_copy(send, send_out, sem.at[0])
-    send_copy.start()
+    lax.fori_loop(0, sampled, place, 0, unroll=8)
     whole = gain[...]
     high = whole.astype(jnp.bfloat16).astype(jnp.float32)
     middle = (whole - high).astype(jnp.bfloat16).astype(jnp.float32)
@@ -228,6 +199,35 @@
     )
     for copy in own_copies:
         copy.start()
+
+    row = lax.broadcasted_iota(jnp.int32, (block_len, lanes), 0)
+    lane = lax.broadcasted_iota(jnp.int32, (block_len, lanes), 1)
+    holder = jnp.zeros((block_len, lanes), jnp.int32)
+    for b in range(NB):
+        count = counts[b]
+        holder = jnp.where((row == 1) & (lane == b), count // 16, holder)
+        holder = jnp.where((row == 2) & (lane == b), count % 16, holder)
+
+    def finish(k, found):
+        for s in range(PER_PAIR):
+            free = arrived[k] <= s
+
+            @pl.when(free)
+            def _():
+                slot_of[sampled + found] = k * PER_PAIR + s
+                for g in range(groups):
+                    send[k, s * groups + g] = jnp.zeros((block_len, lanes), send.dtype)
+
+            found = found + jnp.where(free, 1, 0)
+        facts = holder
+        for i in range(2 * PER_PAIR):
+            facts = jnp.where((row == 0) & (lane == i), info[i, k], facts)
+        send[k, pieces - 1] = facts.astype(jnp.float32).astype(send.dtype)
+        return found
+
+    lax.fori_loop(0, trainers, finish, 0, unroll=8)
+    send_copy = pltpu.make_async_copy(send, send_out, sem.at[0])
+    send_copy.start()
     for copy in own_copies:
         copy.wait()
     send_copy.wait()

time: 177 us -> 175 us (0.989)
  Pallas kernels: 40.2 us -> 38.3 us
where the time goes in v11:
time: 175 us; the launch traced here: 174 us
  waiting for transfers between devices  79.1 us (45%)
  starting transfers between devices  40 us (23%)
  Pallas kernels  38.3 us (22%)
  other arithmetic  8.9 us (5%)
  between operations  3.95 us (2%)
  local copies, waits for them, and re-layouts  3.92 us (2%)
    ppermute x12, waiting for transfers between devices, swap(): return lax.ppermute(value, axis, [(i, i ^ distance) for i in range(peers)])  50 us
    all_to_all x1, waiting for transfers between devices, on_device(): lax.all_to_all(send_gap.reshape(trainers, per_peer, part), DP, 0, 0, tile...  18.7 us
    all_to_all x1, starting transfers between devices, on_device(): got_x = lax.all_to_all(send_x, DP, 0, 0, tiled=True)  13.3 us
    pallas_call x1, Pallas kernels, base_gap_slots(): pl.pallas_call(gap_kernel, out_shape=(jax.ShapeDtypeStruct((slots, *block...  9.88 us
    ppermute x12, starting transfers between devices, swap(): return lax.ppermute(value, axis, [(i, i ^ distance) for i in range(peers)])  9.45 us
    all_to_all x1, starting transfers between devices, on_device(): lax.all_to_all(send_gap.reshape(trainers, per_peer, part), DP, 0, 0, tile...  8.75 us
    all_to_all x1, starting transfers between devices, on_device(): lax.all_to_all(jnp.broadcast_to(own_loss, (trainers, 1, NB)), DP, 0, 0, t...  8.51 us
    all_to_all x1, waiting for transfers between devices, on_device(): lax.all_to_all(jnp.broadcast_to(own_loss, (trainers, 1, NB)), DP, 0, 0, t...  6.33 us
  transfers between devices with their start and end apart: 15, of which 12 were waited for; matrix products, arithmetic and copies ran while one was open for 5% of the time, Pallas kernels for 15%

profile of v11, /device:TPU:1, one launch (start us, length us, event | category | flops | bytes accessed | tf_op | source)
XLA Modules:
  0.0 174.2 jit_solution(462042521102856778)
XLA Ops:
  0.6 5.7 %route.1 = (bf16[64,17,8,128]{3,2,1,0:T(8,128)(2,1)}, bf16[32,8,1024]{2,1,0:T(8,128)(2,1)}, bf16[34,8,1024]{2,1,0:T(8,128)(2,1)}, s32[128]{0:T(128)}) custom-call(s32[64]{0:T(128)} %ids.1, s32[64]{0:T(128)} %bitcast.39, s32[128]{0:T(128)} %buckets_in.1, s32[128]{0:T(128)} %lengths_in.1, bf16[128,8,1024]{2,1,0:T(8,128)(2,1)} %pool_in.1, f32[1,1024]{1,0:T(1,128)} %bitcast.36), custom_call_target="tpu_custom_call" | custom-call | bytes 5242880 | tf_op jit(solution)/shard_map/route/pallas_call | solution.py:244
  6.4 13.3 %all-to-all-start.1 = ((bf16[64,17,8,128]{3,2,1,0:T(8,128)(2,1)}), bf16[64,17,8,128]{3,2,1,0:T(8,128)(2,1)}, u32[]{:S(2)}, u32[]{:S(2)}) async-start(bf16[64,17,8,128]{3,2,1,0:T(8,128)(2,1)} %get-tuple-element.27), calls=%async_computation.1 | async-start | bytes 4456448 | tf_op jit(solution)/shard_map/all_to_all | solution.py:642
  19.7 1.4 collective-permute-start.2
  21.1 1.9 %collective-permute-start = (bf16[256,1024]{1,0:T(8,128)(2,1)S(1)}, bf16[256,1024]{1,0:T(8,128)(2,1)}, u32[]{:S(2)}, u32[]{:S(2)}) collective-permute-start(bf16[256,1024]{1,0:T(8,128)(2,1)S(1)} %bitcast.30), channel_id=1, source_target_pairs={{0,3},{1,2},{2,1},{3,0},{4,7},{5,6},{6,5},{7,4},{8,11},{9,10},{10,... | collective-permute-start | bytes 1572872 | tf_op jit(solution)/shard_map/ppermute | solution.py:26
  23.8 9.8 %collective-permute-done.2.near_last = bf16[272,1024]{1,0:T(8,128)(2,1)S(1)} collective-permute-done((bf16[272,1024]{1,0:T(8,128)(2,1)S(1)}, bf16[272,1024]{1,0:T(8,128)(2,1)S(1)}, u32[]{:S(2)}, u32[]{:S(2)}) %collective-permute-start.2) | collective-permute-done | bytes 557088 | tf_op jit(solution)/shard_map/ppermute | solution.py:26
  33.6 2.7 %collective-permute-start.3 = (bf16[272,1024]{1,0:T(8,128)(2,1)S(1)}, bf16[272,1024]{1,0:T(8,128)(2,1)}, u32[]{:S(2)}, u32[]{:S(2)}) collective-permute-start(bf16[272,1024]{1,0:T(8,128)(2,1)S(1)} %collective-permute-done.2.near_last), channel_id=1, source_target_pairs={{0,3},{1,2},{2,1},{3,0},{4,7},{5,6},{6,5},{7,4},{8,11},{9,10},{10,... | collective-permute-start | bytes 1671176 | tf_op jit(solution)/shard_map/ppermute | solution.py:26
  36.3 1.5 collective-permute-start.1
  38.3 10.0 %collective-permute-done.4.near_first = bf16[256,1024]{1,0:T(8,128)(2,1)S(1)} collective-permute-done((bf16[256,1024]{1,0:T(8,128)(2,1)S(1)}, bf16[256,1024]{1,0:T(8,128)(2,1)S(1)}, u32[]{:S(2)}, u32[]{:S(2)}) %collective-permute-start.4) | collective-permute-done | bytes 524320 | tf_op jit(solution)/shard_map/ppermute | solution.py:26
  49.1 0.8 copy-done.2
  49.9 5.1 %early_part.1 = (bf16[64,8,1024]{2,1,0:T(8,128)(2,1)}, f32[512,128]{1,0:T(8,128)}) custom-call(s32[64]{0:T(128)} %ids.1, bf16[256,1024]{1,0:T(8,128)(2,1)} %bitcast.28, bf16[272,1024]{1,0:T(8,128)(2,1)} %bitcast.24, bf16[256,1024]{1,0:T(8,128)(2,1)} %copy-done.4, bf16[272,1024]{1,0:T(8,128)(2,1)} %copy-done.1, ...), custom_call_target="tpu_custom_call" | custom-call | flops 6291456 | bytes 7340032 | tf_op jit(solution)/shard_map/early_part/pallas_call | solution.py:319
  55.0 4.5 %collective-permute-done.1.far_first = bf16[256,1024]{1,0:T(8,128)(2,1)} collective-permute-done((bf16[256,1024]{1,0:T(8,128)(2,1)}, bf16[256,1024]{1,0:T(8,128)(2,1)}, u32[]{:S(2)}, u32[]{:S(2)}) %collective-permute-start.1) | collective-permute-done | bytes 524320 | tf_op jit(solution)/shard_map/ppermute | solution.py:26
  59.5 9.9 %base_gap.1 = (bf16[128,8,1024]{2,1,0:T(8,128)(2,1)}, f32[1]{0:T(128)}) custom-call(s32[128]{0:T(128)} %get-tuple-element.21.slot_of, s32[4]{0:T(128)} %iota_xor_fusion.order, bf16[256,1024]{1,0:T(8,128)(2,1)} %collective-permute-done.1.far_first, bf16[272,1024]{1,0:T(8,128)(2,1)} %collective-permute-done.3.far_last, bf16[256,1024]{1,0:T(8,128)(2,1)} %bitcast.29, ...), custom_call_target="tpu_custom_call" | custom-call | flops 4294967296 | bytes 18874368 | tf_op jit(solution)/shard_map/base_gap/pallas_call | solution.py:458
  69.4 4.1 %all-to-all-done.1.packed = bf16[64,17,8,128]{3,2,1,0:T(8,128)(2,1)} async-done(((bf16[64,17,8,128]{3,2,1,0:T(8,128)(2,1)}), bf16[64,17,8,128]{3,2,1,0:T(8,128)(2,1)}, u32[]{:S(2)}, u32[]{:S(2)}) %all-to-all-start.1) | async-done | bytes 2228256 | tf_op jit(solution)/shard_map/all_to_all | solution.py:642
  73.5 8.8 %all-to-all-start = ((bf16[64,16,1024]{2,1,0:T(8,128)(2,1)}), bf16[64,16,1024]{2,1,0:T(8,128)(2,1)}, u32[]{:S(2)}, u32[]{:S(2)}) async-start(bf16[64,16,1024]{2,1,0:T(8,128)(2,1)} %bitcast.23), calls=%async_computation | async-start | bytes 4194304 | tf_op jit(solution)/shard_map/all_to_all | solution.py:650
  83.0 4.3 %row_squares.1 = f32[1,1024]{1,0:T(1,128)} custom-call(bf16[64,17,8,128]{3,2,1,0:T(8,128)(2,1)} %all-to-all-done.1.packed, f32[1]{0:T(128)} %get-tuple-element.28.done), custom_call_target="tpu_custom_call" | custom-call | flops 4194304 | bytes 2097152 | tf_op jit(solution)/shard_map/row_squares/pallas_call | solution.py:70
  87.3 0.9 fusion.2
  88.6 0.9 fusion.1
  91.4 3.6 %collective-permute-done.7 = f32[1,1024]{1,0:T(1,128)S(1)} collective-permute-done((f32[1,1024]{1,0:T(1,128)S(1)}, f32[1,1024]{1,0:T(1,128)S(1)}, u32[]{:S(2)}, u32[]{:S(2)}) %collective-permute-start.7) | collective-permute-done | bytes 4128 | tf_op jit(solution)/shard_map/ppermute | solution.py:26
  95.7 4.4 %latents.1 = (bf16[1024,1024]{1,0:T(8,128)(2,1)}, f32[64,1024]{1,0:T(8,128)}) custom-call(bf16[64,17,8,128]{3,2,1,0:T(8,128)(2,1)} %all-to-all-done.1.packed, f32[1,1024]{1,0:T(1,128)} %add_multiply_fusion.squares, f32[1,1024]{1,0:T(1,128)} %bitcast.37, bf16[64,1024]{1,0:T(8,128)(2,1)} %bitcast.34), custom_call_target="tpu_custom_call" | custom-call | flops 134217728 | bytes 4194304 | tf_op jit(solution)/shard_map/latents/pallas_call | solution.py:105
  100.9 5.2 %collective-permute-done.8 = f32[64,1024]{1,0:T(8,128)S(1)} collective-permute-done((f32[64,1024]{1,0:T(8,128)}, f32[64,1024]{1,0:T(8,128)S(1)}, u32[]{:S(2)}, u32[]{:S(2)}) %collective-permute-start.8) | collective-permute-done | bytes 262176 | tf_op jit(solution)/shard_map/ppermute | solution.py:26
  106.1 1.0 add.59
  107.8 1.0 maximum_maximum_fusion.facts
  108.8 5.2 %collective-permute-done.9 = f32[64,1024]{1,0:T(8,128)S(1)} collective-permute-done((f32[64,1024]{1,0:T(8,128)S(1)}, f32[64,1024]{1,0:T(8,128)S(1)}, u32[]{:S(2)}, u32[]{:S(2)}) %collective-permute-start.9) | collective-permute-done | bytes 262176 | tf_op jit(solution)/shard_map/ppermute | solution.py:26
  114.7 18.7 %all-to-all-done = bf16[64,16,1024]{2,1,0:T(8,128)(2,1)} async-done(((bf16[64,16,1024]{2,1,0:T(8,128)(2,1)}), bf16[64,16,1024]{2,1,0:T(8,128)(2,1)}, u32[]{:S(2)}, u32[]{:S(2)}) %all-to-all-start) | async-done | bytes 2097184 | tf_op jit(solution)/shard_map/all_to_all | solution.py:650
  133.4 4.3 %trainer_step.1 = (f32[64,1024]{1,0:T(8,128)}, f32[64,1024]{1,0:T(8,128)}, bf16[80,1024]{1,0:T(8,128)(2,1)}, f32[1,128]{1,0:T(1,128)}) custom-call(bf16[1024,1024]{1,0:T(8,128)(2,1)} %bitcast.5.gap, bf16[64,1024]{1,0:T(8,128)(2,1)} %multiply_convert_fusion.lowered, bf16[64,1024]{1,0:T(8,128)(2,1)} %bitcast.35, f32[1024,128]{1,0:T(8,128)} %maximum_maximum_fusion.facts), custom_call_target="tpu_custom_call" | custom-call | flops 402653184 | bytes 4194304 | tf_op jit(solution)/shard_map/trainer_step/pallas_call | solution.py:528
  137.7 5.6 %collective-permute-done.10.got = bf16[80,1024]{1,0:T(8,128)(2,1)S(1)} collective-permute-done((bf16[80,1024]{1,0:T(8,128)(2,1)}, bf16[80,1024]{1,0:T(8,128)(2,1)S(1)}, u32[]{:S(2)}, u32[]{:S(2)}) %collective-permute-start.10) | collective-permute-done | bytes 163872 | tf_op jit(solution)/shard_map/ppermute | solution.py:26
  143.9 1.8 %pair_step.1 = (f32[64,1024]{1,0:T(8,128)}, f32[1,128]{1,0:T(1,128)}, bf16[80,1024]{1,0:T(8,128)(2,1)}) custom-call(f32[64,1024]{1,0:T(8,128)} %get-tuple-element.30.back, f32[1,128]{1,0:T(1,128)} %get-tuple-element.31.loss, bf16[80,1024]{1,0:T(8,128)(2,1)} %copy-done.6), custom_call_target="tpu_custom_call" | custom-call | flops 131072 | bytes 1048576 | tf_op jit(solution)/shard_map/pair_step/pallas_call | solution.py:574
  146.1 5.2 %collective-permute-done.11.got = bf16[80,1024]{1,0:T(8,128)(2,1)S(1)} collective-permute-done((bf16[80,1024]{1,0:T(8,128)(2,1)}, bf16[80,1024]{1,0:T(8,128)(2,1)S(1)}, u32[]{:S(2)}, u32[]{:S(2)}) %collective-permute-start.11) | collective-permute-done | bytes 163872 | tf_op jit(solution)/shard_map/ppermute | solution.py:26
  152.6 8.5 %all-to-all-start.2 = ((f32[64,1,16]{2,1,0:T(1,128)}), f32[64,1,16]{2,1,0:T(1,128)S(1)}, u32[]{:S(2)}, u32[]{:S(2)}) async-start(f32[64,1,16]{2,1,0:T(1,128)} %broadcast_in_dim.32), calls=%async_computation.2 | async-start | bytes 65536 | tf_op jit(solution)/shard_map/all_to_all | solution.py:684
  161.1 3.0 %down_step.1 = f32[64,1024]{1,0:T(8,128)} custom-call(f32[64,1024]{1,0:T(8,128)} %get-tuple-element.33.pair, bf16[80,1024]{1,0:T(8,128)(2,1)} %copy-done.5, bf16[1024,1024]{1,0:T(8,128)(2,1)} %get-tuple-element.35.normed), custom_call_target="tpu_custom_call" | custom-call | flops 134217728 | bytes 3145728 | tf_op jit(solution)/shard_map/down_step/pallas_call | solution.py:602
  164.1 6.3 %all-to-all-done.2 = f32[64,1,16]{2,1,0:T(1,128)S(1)} async-done(((f32[64,1,16]{2,1,0:T(1,128)}), f32[64,1,16]{2,1,0:T(1,128)S(1)}, u32[]{:S(2)}, u32[]{:S(2)}) %all-to-all-start.2) | async-done | bytes 4128 | tf_op jit(solution)/shard_map/all_to_all | solution.py:684
  170.5 1.2 fusion.10
  (48 shorter events, 9.7 us)
Async XLA Ops:
  6.4 13.3 %copy-start = (bf16[34,8,1024]{2,1,0:T(8,128)(2,1)S(1)}, bf16[34,8,1024]{2,1,0:T(8,128)(2,1)}, u32[]{:S(2)}) copy-start(bf16[34,8,1024]{2,1,0:T(8,128)(2,1)} %get-tuple-element.23) | copy-start | bytes 1671172
  6.4 14.7 %copy-start.3 = (bf16[32,8,1024]{2,1,0:T(8,128)(2,1)S(1)}, bf16[32,8,1024]{2,1,0:T(8,128)(2,1)}, u32[]{:S(2)}) copy-start(bf16[32,8,1024]{2,1,0:T(8,128)(2,1)} %get-tuple-element.22) | copy-start | bytes 1572868
  6.4 67.1 %all-to-all-start.1 = ((bf16[64,17,8,128]{3,2,1,0:T(8,128)(2,1)}), bf16[64,17,8,128]{3,2,1,0:T(8,128)(2,1)}, u32[]{:S(2)}, u32[]{:S(2)}) async-start(bf16[64,17,8,128]{3,2,1,0:T(8,128)(2,1)} %get-tuple-element.27), calls=%async_computation.1 | async-start | bytes 4456448 | tf_op jit(solution)/shard_map/all_to_all | solution.py:642
  19.7 13.9 %collective-permute-start.2 = (bf16[272,1024]{1,0:T(8,128)(2,1)S(1)}, bf16[272,1024]{1,0:T(8,128)(2,1)S(1)}, u32[]{:S(2)}, u32[]{:S(2)}) collective-permute-start(bf16[272,1024]{1,0:T(8,128)(2,1)S(1)} %bitcast.26), channel_id=1, source_target_pairs={{0,1},{1,0},{2,3},{3,2},{4,5},{5,4},{6,7},{7,6},{8,9},{9,8},{10,11... | collective-permute-start | bytes 1671176 | tf_op jit(solution)/shard_map/ppermute | solution.py:26
  21.1 15.2 %collective-permute-start = (bf16[256,1024]{1,0:T(8,128)(2,1)S(1)}, bf16[256,1024]{1,0:T(8,128)(2,1)}, u32[]{:S(2)}, u32[]{:S(2)}) collective-permute-start(bf16[256,1024]{1,0:T(8,128)(2,1)S(1)} %bitcast.30), channel_id=1, source_target_pairs={{0,3},{1,2},{2,1},{3,0},{4,7},{5,6},{6,5},{7,4},{8,11},{9,10},{10,... | collective-permute-start | bytes 1572872 | tf_op jit(solution)/shard_map/ppermute | solution.py:26
  23.0 26.1 %collective-permute-start.5 = (bf16[272,1024]{1,0:T(8,128)(2,1)S(1)}, bf16[272,1024]{1,0:T(8,128)(2,1)S(1)}, u32[]{:S(2)}, u32[]{:S(2)}) collective-permute-start(bf16[272,1024]{1,0:T(8,128)(2,1)S(1)} %bitcast.27), channel_id=1, source_target_pairs={{0,3},{1,2},{2,1},{3,0},{4,7},{5,6},{6,5},{7,4},{8,11},{9,10},{10,... | collective-permute-start | bytes 1671176 | tf_op jit(solution)/shard_map/ppermute | solution.py:26
  33.6 15.5 %copy-start.1 = (bf16[272,1024]{1,0:T(8,128)(2,1)}, bf16[272,1024]{1,0:T(8,128)(2,1)S(1)}, u32[]{:S(2)}) copy-start(bf16[272,1024]{1,0:T(8,128)(2,1)S(1)} %collective-permute-done.2.near_last) | copy-start | bytes 1671172
  33.6 25.9 %collective-permute-start.3 = (bf16[272,1024]{1,0:T(8,128)(2,1)S(1)}, bf16[272,1024]{1,0:T(8,128)(2,1)}, u32[]{:S(2)}, u32[]{:S(2)}) collective-permute-start(bf16[272,1024]{1,0:T(8,128)(2,1)S(1)} %collective-permute-done.2.near_last), channel_id=1, source_target_pairs={{0,3},{1,2},{2,1},{3,0},{4,7},{5,6},{6,5},{7,4},{8,11},{9,10},{10,... | collective-permute-start | bytes 1671176 | tf_op jit(solution)/shard_map/ppermute | solution.py:26
  36.3 12.0 %collective-permute-start.4 = (bf16[256,1024]{1,0:T(8,128)(2,1)S(1)}, bf16[256,1024]{1,0:T(8,128)(2,1)S(1)}, u32[]{:S(2)}, u32[]{:S(2)}) collective-permute-start(bf16[256,1024]{1,0:T(8,128)(2,1)S(1)} %bitcast.31), channel_id=1, source_target_pairs={{0,1},{1,0},{2,3},{3,2},{4,5},{5,4},{6,7},{7,6},{8,9},{9,8},{10,11... | collective-permute-start | bytes 1572872 | tf_op jit(solution)/shard_map/ppermute | solution.py:26
  36.3 23.2 %collective-permute-start.1 = (bf16[256,1024]{1,0:T(8,128)(2,1)}, bf16[256,1024]{1,0:T(8,128)(2,1)}, u32[]{:S(2)}, u32[]{:S(2)}) collective-permute-start(bf16[256,1024]{1,0:T(8,128)(2,1)} %collective-permute-done.other_first), channel_id=1, source_target_pairs={{0,1},{1,0},{2,3},{3,2},{4,5},{5,4},{6,7},{7,6},{8,9},{9,8},{10,11... | collective-permute-start | bytes 1572872 | tf_op jit(solution)/shard_map/ppermute | solution.py:26
  48.3 0.8 copy-start.4
  49.1 0.8 copy-start.2
  73.5 59.9 %all-to-all-start = ((bf16[64,16,1024]{2,1,0:T(8,128)(2,1)}), bf16[64,16,1024]{2,1,0:T(8,128)(2,1)}, u32[]{:S(2)}, u32[]{:S(2)}) async-start(bf16[64,16,1024]{2,1,0:T(8,128)(2,1)} %bitcast.23), calls=%async_computation | async-start | bytes 4194304 | tf_op jit(solution)/shard_map/all_to_all | solution.py:650
  87.2 3.1 %collective-permute-start.6 = (f32[1,1024]{1,0:T(1,128)}, f32[1,1024]{1,0:T(1,128)S(1)}, u32[]{:S(2)}, u32[]{:S(2)}) collective-permute-start(f32[1,1024]{1,0:T(1,128)} %row_squares.1), channel_id=1, source_target_pairs={{0,1},{1,0},{2,3},{3,2},{4,5},{5,4},{6,7},{7,6},{8,9},{9,8},{10,11... | collective-permute-start | bytes 12296 | tf_op jit(solution)/shard_map/ppermute | solution.py:26
  91.0 4.1 %collective-permute-start.7 = (f32[1,1024]{1,0:T(1,128)S(1)}, f32[1,1024]{1,0:T(1,128)S(1)}, u32[]{:S(2)}, u32[]{:S(2)}) collective-permute-start(f32[1,1024]{1,0:T(1,128)S(1)} %add.57), channel_id=1, source_target_pairs={{0,3},{1,2},{2,1},{3,0},{4,7},{5,6},{6,5},{7,4},{8,11},{9,10},{10,... | collective-permute-start | bytes 12296 | tf_op jit(solution)/shard_map/ppermute | solution.py:26
  100.0 6.1 %collective-permute-start.8 = (f32[64,1024]{1,0:T(8,128)}, f32[64,1024]{1,0:T(8,128)S(1)}, u32[]{:S(2)}, u32[]{:S(2)}) collective-permute-start(f32[64,1024]{1,0:T(8,128)} %get-tuple-element.29), channel_id=1, source_target_pairs={{0,1},{1,0},{2,3},{3,2},{4,5},{5,4},{6,7},{7,6},{8,9},{9,8},{10,11... | collective-permute-start | bytes 786440 | tf_op jit(solution)/shard_map/ppermute | solution.py:26
  107.1 6.9 %collective-permute-start.9 = (f32[64,1024]{1,0:T(8,128)S(1)}, f32[64,1024]{1,0:T(8,128)S(1)}, u32[]{:S(2)}, u32[]{:S(2)}) collective-permute-start(f32[64,1024]{1,0:T(8,128)S(1)} %add.59), channel_id=1, source_target_pairs={{0,3},{1,2},{2,1},{3,0},{4,7},{5,6},{6,5},{7,4},{8,11},{9,10},{10,... | collective-permute-start | bytes 786440 | tf_op jit(solution)/shard_map/ppermute | solution.py:26
  137.6 5.6 %collective-permute-start.10 = (bf16[80,1024]{1,0:T(8,128)(2,1)}, bf16[80,1024]{1,0:T(8,128)(2,1)S(1)}, u32[]{:S(2)}, u32[]{:S(2)}) collective-permute-start(bf16[80,1024]{1,0:T(8,128)(2,1)} %get-tuple-element.32), channel_id=1, source_target_pairs={{0,1},{1,0},{2,3},{3,2},{4,5},{5,4},{6,7},{7,6},{8,9},{9,8},{10,11... | collective-permute-start | bytes 491528 | tf_op jit(solution)/shard_map/ppermute | solution.py:26
  143.3 0.7 copy-start.6
  145.7 5.6 %collective-permute-start.11 = (bf16[80,1024]{1,0:T(8,128)(2,1)}, bf16[80,1024]{1,0:T(8,128)(2,1)S(1)}, u32[]{:S(2)}, u32[]{:S(2)}) collective-permute-start(bf16[80,1024]{1,0:T(8,128)(2,1)} %get-tuple-element.34), channel_id=1, source_target_pairs={{0,3},{1,2},{2,1},{3,0},{4,7},{5,6},{6,5},{7,4},{8,11},{9,10},{10,... | collective-permute-start | bytes 491528 | tf_op jit(solution)/shard_map/ppermute | solution.py:26
  151.3 9.8 %copy-start.5 = (bf16[80,1024]{1,0:T(8,128)(2,1)}, bf16[80,1024]{1,0:T(8,128)(2,1)S(1)}, u32[]{:S(2)}) copy-start(bf16[80,1024]{1,0:T(8,128)(2,1)S(1)} %collective-permute-done.11.got) | copy-start | bytes 491524
  152.6 17.8 %all-to-all-start.2 = ((f32[64,1,16]{2,1,0:T(1,128)}), f32[64,1,16]{2,1,0:T(1,128)S(1)}, u32[]{:S(2)}, u32[]{:S(2)}) async-start(f32[64,1,16]{2,1,0:T(1,128)} %broadcast_in_dim.32), calls=%async_computation.2 | async-start | bytes 65536 | tf_op jit(solution)/shard_map/all_to_all | solution.py:684

commit v12 on v11

--- a/solution.py
+++ b/solution.py
@@ -225,12 +225,17 @@
         send[k, pieces - 1] = facts.astype(jnp.float32).astype(send.dtype)
         return found
 
-    lax.fori_loop(0, trainers, finish, 0, unroll=8)
-    send_copy = pltpu.make_async_copy(send, send_out, sem.at[0])
-    send_copy.start()
-    for copy in own_copies:
+    quarter = trainers // 4
+    found = 0
+    send_copies = []
+    for q in range(4):
+        found = lax.fori_loop(q * quarter, (q + 1) * quarter, finish, found, unroll=8)
+        part = pl.ds(q * quarter, quarter)
+        copy = pltpu.make_async_copy(send.at[part], send_out.at[part], sem.at[3 + q])
+        copy.start()
+        send_copies.append(copy)
+    for copy in (*own_copies, *send_copies):
         copy.wait()
-    send_copy.wait()
 
 
 def route(ids, dest, buckets, lengths, pool, gain, trainers):
@@ -263,7 +268,7 @@
             pltpu.SMEM((trainers,), jnp.int32),
             pltpu.SMEM((2 * PER_PAIR, trainers), jnp.int32),
             pltpu.SMEM((NB,), jnp.int32),
-            pltpu.SemaphoreType.DMA((6,)),
+            pltpu.SemaphoreType.DMA((7,)),
         ],
         compiler_params=pltpu.CompilerParams(vmem_limit_bytes=VMEM_BYTES),
         cost_estimate=pl.CostEstimate(flops=0, bytes_accessed=5 << 20, transcendentals=0),

time: 175 us -> 174 us (level)
  no operation moved by 1% of the time
where the time goes in v12:
time: 174 us
  waiting for transfers between devices  79.1 us (45%)
  starting transfers between devices  40 us (23%)
  Pallas kernels  37.8 us (22%)
  other arithmetic  8.9 us (5%)
  between operations  3.96 us (2%)
  local copies, waits for them, and re-layouts  3.92 us (2%)
    ppermute x12, waiting for transfers between devices, swap(): return lax.ppermute(value, axis, [(i, i ^ distance) for i in range(peers)])  50 us
    all_to_all x1, waiting for transfers between devices, on_device(): lax.all_to_all(send_gap.reshape(trainers, per_peer, part), DP, 0, 0, tile...  18.7 us
    all_to_all x1, starting transfers between devices, on_device(): got_x = lax.all_to_all(send_x, DP, 0, 0, tiled=True)  13.3 us
    pallas_call x1, Pallas kernels, base_gap_slots(): pl.pallas_call(gap_kernel, out_shape=(jax.ShapeDtypeStruct((slots, *block...  9.88 us
    ppermute x12, starting transfers between devices, swap(): return lax.ppermute(value, axis, [(i, i ^ distance) for i in range(peers)])  9.44 us
    all_to_all x1, starting transfers between devices, on_device(): lax.all_to_all(send_gap.reshape(trainers, per_peer, part), DP, 0, 0, tile...  8.76 us
    all_to_all x1, starting transfers between devices, on_device(): lax.all_to_all(jnp.broadcast_to(own_loss, (trainers, 1, NB)), DP, 0, 0, t...  8.51 us
    all_to_all x1, waiting for transfers between devices, on_device(): lax.all_to_all(jnp.broadcast_to(own_loss, (trainers, 1, NB)), DP, 0, 0, t...  6.33 us
  transfers between devices with their start and end apart: 15, of which 12 were waited for; matrix products, arithmetic and copies ran while one was open for 5% of the time, Pallas kernels for 15%

profile of v12, /device:TPU:1, one launch (start us, length us, event | category | flops | bytes accessed | tf_op | source)
XLA Modules:
  0.0 173.7 jit_solution(3739605736185921768)
XLA Ops:
  0.6 5.2 %route.1 = (bf16[64,17,8,128]{3,2,1,0:T(8,128)(2,1)}, bf16[32,8,1024]{2,1,0:T(8,128)(2,1)}, bf16[34,8,1024]{2,1,0:T(8,128)(2,1)}, s32[128]{0:T(128)}) custom-call(s32[64]{0:T(128)} %ids.1, s32[64]{0:T(128)} %bitcast.39, s32[128]{0:T(128)} %buckets_in.1, s32[128]{0:T(128)} %lengths_in.1, bf16[128,8,1024]{2,1,0:T(8,128)(2,1)} %pool_in.1, f32[1,1024]{1,0:T(1,128)} %bitcast.36), custom_call_target="tpu_custom_call" | custom-call | bytes 5242880 | tf_op jit(solution)/shard_map/route/pallas_call | solution.py:249
  5.8 13.3 %all-to-all-start.1 = ((bf16[64,17,8,128]{3,2,1,0:T(8,128)(2,1)}), bf16[64,17,8,128]{3,2,1,0:T(8,128)(2,1)}, u32[]{:S(2)}, u32[]{:S(2)}) async-start(bf16[64,17,8,128]{3,2,1,0:T(8,128)(2,1)} %get-tuple-element.27), calls=%async_computation.1 | async-start | bytes 4456448 | tf_op jit(solution)/shard_map/all_to_all | solution.py:647
  19.2 1.4 collective-permute-start.2
  20.5 1.9 %collective-permute-start = (bf16[256,1024]{1,0:T(8,128)(2,1)S(1)}, bf16[256,1024]{1,0:T(8,128)(2,1)}, u32[]{:S(2)}, u32[]{:S(2)}) collective-permute-start(bf16[256,1024]{1,0:T(8,128)(2,1)S(1)} %bitcast.30), channel_id=1, source_target_pairs={{0,3},{1,2},{2,1},{3,0},{4,7},{5,6},{6,5},{7,4},{8,11},{9,10},{10,... | collective-permute-start | bytes 1572872 | tf_op jit(solution)/shard_map/ppermute | solution.py:26
  23.2 9.8 %collective-permute-done.2.near_last = bf16[272,1024]{1,0:T(8,128)(2,1)S(1)} collective-permute-done((bf16[272,1024]{1,0:T(8,128)(2,1)S(1)}, bf16[272,1024]{1,0:T(8,128)(2,1)S(1)}, u32[]{:S(2)}, u32[]{:S(2)}) %collective-permute-start.2) | collective-permute-done | bytes 557088 | tf_op jit(solution)/shard_map/ppermute | solution.py:26
  33.0 2.7 %collective-permute-start.3 = (bf16[272,1024]{1,0:T(8,128)(2,1)S(1)}, bf16[272,1024]{1,0:T(8,128)(2,1)}, u32[]{:S(2)}, u32[]{:S(2)}) collective-permute-start(bf16[272,1024]{1,0:T(8,128)(2,1)S(1)} %collective-permute-done.2.near_last), channel_id=1, source_target_pairs={{0,3},{1,2},{2,1},{3,0},{4,7},{5,6},{6,5},{7,4},{8,11},{9,10},{10,... | collective-permute-start | bytes 1671176 | tf_op jit(solution)/shard_map/ppermute | solution.py:26
  35.8 1.5 collective-permute-start.1
  37.7 10.0 %collective-permute-done.4.near_first = bf16[256,1024]{1,0:T(8,128)(2,1)S(1)} collective-permute-done((bf16[256,1024]{1,0:T(8,128)(2,1)S(1)}, bf16[256,1024]{1,0:T(8,128)(2,1)S(1)}, u32[]{:S(2)}, u32[]{:S(2)}) %collective-permute-start.4) | collective-permute-done | bytes 524320 | tf_op jit(solution)/shard_map/ppermute | solution.py:26
  48.5 0.8 copy-done.2
  49.4 5.1 %early_part.1 = (bf16[64,8,1024]{2,1,0:T(8,128)(2,1)}, f32[512,128]{1,0:T(8,128)}) custom-call(s32[64]{0:T(128)} %ids.1, bf16[256,1024]{1,0:T(8,128)(2,1)} %bitcast.28, bf16[272,1024]{1,0:T(8,128)(2,1)} %bitcast.24, bf16[256,1024]{1,0:T(8,128)(2,1)} %copy-done.4, bf16[272,1024]{1,0:T(8,128)(2,1)} %copy-done.1, ...), custom_call_target="tpu_custom_call" | custom-call | flops 6291456 | bytes 7340032 | tf_op jit(solution)/shard_map/early_part/pallas_call | solution.py:324
  54.4 4.5 %collective-permute-done.1.far_first = bf16[256,1024]{1,0:T(8,128)(2,1)} collective-permute-done((bf16[256,1024]{1,0:T(8,128)(2,1)}, bf16[256,1024]{1,0:T(8,128)(2,1)}, u32[]{:S(2)}, u32[]{:S(2)}) %collective-permute-start.1) | collective-permute-done | bytes 524320 | tf_op jit(solution)/shard_map/ppermute | solution.py:26
  59.0 9.9 %base_gap.1 = (bf16[128,8,1024]{2,1,0:T(8,128)(2,1)}, f32[1]{0:T(128)}) custom-call(s32[128]{0:T(128)} %get-tuple-element.21.slot_of, s32[4]{0:T(128)} %iota_xor_fusion.order, bf16[256,1024]{1,0:T(8,128)(2,1)} %collective-permute-done.1.far_first, bf16[272,1024]{1,0:T(8,128)(2,1)} %collective-permute-done.3.far_last, bf16[256,1024]{1,0:T(8,128)(2,1)} %bitcast.29, ...), custom_call_target="tpu_custom_call" | custom-call | flops 4294967296 | bytes 18874368 | tf_op jit(solution)/shard_map/base_gap/pallas_call | solution.py:463
  68.9 4.1 %all-to-all-done.1.packed = bf16[64,17,8,128]{3,2,1,0:T(8,128)(2,1)} async-done(((bf16[64,17,8,128]{3,2,1,0:T(8,128)(2,1)}), bf16[64,17,8,128]{3,2,1,0:T(8,128)(2,1)}, u32[]{:S(2)}, u32[]{:S(2)}) %all-to-all-start.1) | async-done | bytes 2228256 | tf_op jit(solution)/shard_map/all_to_all | solution.py:647
  72.9 8.8 %all-to-all-start = ((bf16[64,16,1024]{2,1,0:T(8,128)(2,1)}), bf16[64,16,1024]{2,1,0:T(8,128)(2,1)}, u32[]{:S(2)}, u32[]{:S(2)}) async-start(bf16[64,16,1024]{2,1,0:T(8,128)(2,1)} %bitcast.23), calls=%async_computation | async-start | bytes 4194304 | tf_op jit(solution)/shard_map/all_to_all | solution.py:655
  82.4 4.3 %row_squares.1 = f32[1,1024]{1,0:T(1,128)} custom-call(bf16[64,17,8,128]{3,2,1,0:T(8,128)(2,1)} %all-to-all-done.1.packed, f32[1]{0:T(128)} %get-tuple-element.28.done), custom_call_target="tpu_custom_call" | custom-call | flops 4194304 | bytes 2097152 | tf_op jit(solution)/shard_map/row_squares/pallas_call | solution.py:70
  86.7 0.9 fusion.2
  88.0 0.9 fusion.1
  90.9 3.6 %collective-permute-done.7 = f32[1,1024]{1,0:T(1,128)S(1)} collective-permute-done((f32[1,1024]{1,0:T(1,128)S(1)}, f32[1,1024]{1,0:T(1,128)S(1)}, u32[]{:S(2)}, u32[]{:S(2)}) %collective-permute-start.7) | collective-permute-done | bytes 4128 | tf_op jit(solution)/shard_map/ppermute | solution.py:26
  95.1 4.4 %latents.1 = (bf16[1024,1024]{1,0:T(8,128)(2,1)}, f32[64,1024]{1,0:T(8,128)}) custom-call(bf16[64,17,8,128]{3,2,1,0:T(8,128)(2,1)} %all-to-all-done.1.packed, f32[1,1024]{1,0:T(1,128)} %add_multiply_fusion.squares, f32[1,1024]{1,0:T(1,128)} %bitcast.37, bf16[64,1024]{1,0:T(8,128)(2,1)} %bitcast.34), custom_call_target="tpu_custom_call" | custom-call | flops 134217728 | bytes 4194304 | tf_op jit(solution)/shard_map/latents/pallas_call | solution.py:105
  100.3 5.2 %collective-permute-done.8 = f32[64,1024]{1,0:T(8,128)S(1)} collective-permute-done((f32[64,1024]{1,0:T(8,128)}, f32[64,1024]{1,0:T(8,128)S(1)}, u32[]{:S(2)}, u32[]{:S(2)}) %collective-permute-start.8) | collective-permute-done | bytes 262176 | tf_op jit(solution)/shard_map/ppermute | solution.py:26
  105.6 1.0 add.59
  107.2 1.0 maximum_maximum_fusion.facts
  108.2 5.2 %collective-permute-done.9 = f32[64,1024]{1,0:T(8,128)S(1)} collective-permute-done((f32[64,1024]{1,0:T(8,128)S(1)}, f32[64,1024]{1,0:T(8,128)S(1)}, u32[]{:S(2)}, u32[]{:S(2)}) %collective-permute-start.9) | collective-permute-done | bytes 262176 | tf_op jit(solution)/shard_map/ppermute | solution.py:26
  114.2 18.7 %all-to-all-done = bf16[64,16,1024]{2,1,0:T(8,128)(2,1)} async-done(((bf16[64,16,1024]{2,1,0:T(8,128)(2,1)}), bf16[64,16,1024]{2,1,0:T(8,128)(2,1)}, u32[]{:S(2)}, u32[]{:S(2)}) %all-to-all-start) | async-done | bytes 2097184 | tf_op jit(solution)/shard_map/all_to_all | solution.py:655
  132.8 4.3 %trainer_step.1 = (f32[64,1024]{1,0:T(8,128)}, f32[64,1024]{1,0:T(8,128)}, bf16[80,1024]{1,0:T(8,128)(2,1)}, f32[1,128]{1,0:T(1,128)}) custom-call(bf16[1024,1024]{1,0:T(8,128)(2,1)} %bitcast.5.gap, bf16[64,1024]{1,0:T(8,128)(2,1)} %multiply_convert_fusion.lowered, bf16[64,1024]{1,0:T(8,128)(2,1)} %bitcast.35, f32[1024,128]{1,0:T(8,128)} %maximum_maximum_fusion.facts), custom_call_target="tpu_custom_call" | custom-call | flops 402653184 | bytes 4194304 | tf_op jit(solution)/shard_map/trainer_step/pallas_call | solution.py:533
  137.1 5.6 %collective-permute-done.10.got = bf16[80,1024]{1,0:T(8,128)(2,1)S(1)} collective-permute-done((bf16[80,1024]{1,0:T(8,128)(2,1)}, bf16[80,1024]{1,0:T(8,128)(2,1)S(1)}, u32[]{:S(2)}, u32[]{:S(2)}) %collective-permute-start.10) | collective-permute-done | bytes 163872 | tf_op jit(solution)/shard_map/ppermute | solution.py:26
  143.4 1.8 %pair_step.1 = (f32[64,1024]{1,0:T(8,128)}, f32[1,128]{1,0:T(1,128)}, bf16[80,1024]{1,0:T(8,128)(2,1)}) custom-call(f32[64,1024]{1,0:T(8,128)} %get-tuple-element.30.back, f32[1,128]{1,0:T(1,128)} %get-tuple-element.31.loss, bf16[80,1024]{1,0:T(8,128)(2,1)} %copy-done.6), custom_call_target="tpu_custom_call" | custom-call | flops 131072 | bytes 1048576 | tf_op jit(solution)/shard_map/pair_step/pallas_call | solution.py:579
  145.5 5.2 %collective-permute-done.11.got = bf16[80,1024]{1,0:T(8,128)(2,1)S(1)} collective-permute-done((bf16[80,1024]{1,0:T(8,128)(2,1)}, bf16[80,1024]{1,0:T(8,128)(2,1)S(1)}, u32[]{:S(2)}, u32[]{:S(2)}) %collective-permute-start.11) | collective-permute-done | bytes 163872 | tf_op jit(solution)/shard_map/ppermute | solution.py:26
  152.0 8.5 %all-to-all-start.2 = ((f32[64,1,16]{2,1,0:T(1,128)}), f32[64,1,16]{2,1,0:T(1,128)S(1)}, u32[]{:S(2)}, u32[]{:S(2)}) async-start(f32[64,1,16]{2,1,0:T(1,128)} %broadcast_in_dim.32), calls=%async_computation.2 | async-start | bytes 65536 | tf_op jit(solution)/shard_map/all_to_all | solution.py:689
  160.6 3.0 %down_step.1 = f32[64,1024]{1,0:T(8,128)} custom-call(f32[64,1024]{1,0:T(8,128)} %get-tuple-element.33.pair, bf16[80,1024]{1,0:T(8,128)(2,1)} %copy-done.5, bf16[1024,1024]{1,0:T(8,128)(2,1)} %get-tuple-element.35.normed), custom_call_target="tpu_custom_call" | custom-call | flops 134217728 | bytes 3145728 | tf_op jit(solution)/shard_map/down_step/pallas_call | solution.py:607
  163.5 6.3 %all-to-all-done.2 = f32[64,1,16]{2,1,0:T(1,128)S(1)} async-done(((f32[64,1,16]{2,1,0:T(1,128)}), f32[64,1,16]{2,1,0:T(1,128)S(1)}, u32[]{:S(2)}, u32[]{:S(2)}) %all-to-all-start.2) | async-done | bytes 4128 | tf_op jit(solution)/shard_map/all_to_all | solution.py:689
  169.9 1.2 fusion.10
  (48 shorter events, 9.7 us)
Async XLA Ops:
  5.8 13.3 %copy-start = (bf16[34,8,1024]{2,1,0:T(8,128)(2,1)S(1)}, bf16[34,8,1024]{2,1,0:T(8,128)(2,1)}, u32[]{:S(2)}) copy-start(bf16[34,8,1024]{2,1,0:T(8,128)(2,1)} %get-tuple-element.23) | copy-start | bytes 1671172
  5.8 14.7 %copy-start.3 = (bf16[32,8,1024]{2,1,0:T(8,128)(2,1)S(1)}, bf16[32,8,1024]{2,1,0:T(8,128)(2,1)}, u32[]{:S(2)}) copy-start(bf16[32,8,1024]{2,1,0:T(8,128)(2,1)} %get-tuple-element.22) | copy-start | bytes 1572868
  5.8 67.1 %all-to-all-start.1 = ((bf16[64,17,8,128]{3,2,1,0:T(8,128)(2,1)}), bf16[64,17,8,128]{3,2,1,0:T(8,128)(2,1)}, u32[]{:S(2)}, u32[]{:S(2)}) async-start(bf16[64,17,8,128]{3,2,1,0:T(8,128)(2,1)} %get-tuple-element.27), calls=%async_computation.1 | async-start | bytes 4456448 | tf_op jit(solution)/shard_map/all_to_all | solution.py:647
  19.2 13.9 %collective-permute-start.2 = (bf16[272,1024]{1,0:T(8,128)(2,1)S(1)}, bf16[272,1024]{1,0:T(8,128)(2,1)S(1)}, u32[]{:S(2)}, u32[]{:S(2)}) collective-permute-start(bf16[272,1024]{1,0:T(8,128)(2,1)S(1)} %bitcast.26), channel_id=1, source_target_pairs={{0,1},{1,0},{2,3},{3,2},{4,5},{5,4},{6,7},{7,6},{8,9},{9,8},{10,11... | collective-permute-start | bytes 1671176 | tf_op jit(solution)/shard_map/ppermute | solution.py:26
  20.5 15.2 %collective-permute-start = (bf16[256,1024]{1,0:T(8,128)(2,1)S(1)}, bf16[256,1024]{1,0:T(8,128)(2,1)}, u32[]{:S(2)}, u32[]{:S(2)}) collective-permute-start(bf16[256,1024]{1,0:T(8,128)(2,1)S(1)} %bitcast.30), channel_id=1, source_target_pairs={{0,3},{1,2},{2,1},{3,0},{4,7},{5,6},{6,5},{7,4},{8,11},{9,10},{10,... | collective-permute-start | bytes 1572872 | tf_op jit(solution)/shard_map/ppermute | solution.py:26
  22.4 26.1 %collective-permute-start.5 = (bf16[272,1024]{1,0:T(8,128)(2,1)S(1)}, bf16[272,1024]{1,0:T(8,128)(2,1)S(1)}, u32[]{:S(2)}, u32[]{:S(2)}) collective-permute-start(bf16[272,1024]{1,0:T(8,128)(2,1)S(1)} %bitcast.27), channel_id=1, source_target_pairs={{0,3},{1,2},{2,1},{3,0},{4,7},{5,6},{6,5},{7,4},{8,11},{9,10},{10,... | collective-permute-start | bytes 1671176 | tf_op jit(solution)/shard_map/ppermute | solution.py:26
  33.0 15.5 %copy-start.1 = (bf16[272,1024]{1,0:T(8,128)(2,1)}, bf16[272,1024]{1,0:T(8,128)(2,1)S(1)}, u32[]{:S(2)}) copy-start(bf16[272,1024]{1,0:T(8,128)(2,1)S(1)} %collective-permute-done.2.near_last) | copy-start | bytes 1671172
  33.0 25.9 %collective-permute-start.3 = (bf16[272,1024]{1,0:T(8,128)(2,1)S(1)}, bf16[272,1024]{1,0:T(8,128)(2,1)}, u32[]{:S(2)}, u32[]{:S(2)}) collective-permute-start(bf16[272,1024]{1,0:T(8,128)(2,1)S(1)} %collective-permute-done.2.near_last), channel_id=1, source_target_pairs={{0,3},{1,2},{2,1},{3,0},{4,7},{5,6},{6,5},{7,4},{8,11},{9,10},{10,... | collective-permute-start | bytes 1671176 | tf_op jit(solution)/shard_map/ppermute | solution.py:26
  35.8 12.0 %collective-permute-start.4 = (bf16[256,1024]{1,0:T(8,128)(2,1)S(1)}, bf16[256,1024]{1,0:T(8,128)(2,1)S(1)}, u32[]{:S(2)}, u32[]{:S(2)}) collective-permute-start(bf16[256,1024]{1,0:T(8,128)(2,1)S(1)} %bitcast.31), channel_id=1, source_target_pairs={{0,1},{1,0},{2,3},{3,2},{4,5},{5,4},{6,7},{7,6},{8,9},{9,8},{10,11... | collective-permute-start | bytes 1572872 | tf_op jit(solution)/shard_map/ppermute | solution.py:26
  35.8 23.2 %collective-permute-start.1 = (bf16[256,1024]{1,0:T(8,128)(2,1)}, bf16[256,1024]{1,0:T(8,128)(2,1)}, u32[]{:S(2)}, u32[]{:S(2)}) collective-permute-start(bf16[256,1024]{1,0:T(8,128)(2,1)} %collective-permute-done.other_first), channel_id=1, source_target_pairs={{0,1},{1,0},{2,3},{3,2},{4,5},{5,4},{6,7},{7,6},{8,9},{9,8},{10,11... | collective-permute-start | bytes 1572872 | tf_op jit(solution)/shard_map/ppermute | solution.py:26
  47.7 0.8 copy-start.4
  48.5 0.8 copy-start.2
  72.9 59.9 %all-to-all-start = ((bf16[64,16,1024]{2,1,0:T(8,128)(2,1)}), bf16[64,16,1024]{2,1,0:T(8,128)(2,1)}, u32[]{:S(2)}, u32[]{:S(2)}) async-start(bf16[64,16,1024]{2,1,0:T(8,128)(2,1)} %bitcast.23), calls=%async_computation | async-start | bytes 4194304 | tf_op jit(solution)/shard_map/all_to_all | solution.py:655
  86.7 3.1 %collective-permute-start.6 = (f32[1,1024]{1,0:T(1,128)}, f32[1,1024]{1,0:T(1,128)S(1)}, u32[]{:S(2)}, u32[]{:S(2)}) collective-permute-start(f32[1,1024]{1,0:T(1,128)} %row_squares.1), channel_id=1, source_target_pairs={{0,1},{1,0},{2,3},{3,2},{4,5},{5,4},{6,7},{7,6},{8,9},{9,8},{10,11... | collective-permute-start | bytes 12296 | tf_op jit(solution)/shard_map/ppermute | solution.py:26
  90.5 4.1 %collective-permute-start.7 = (f32[1,1024]{1,0:T(1,128)S(1)}, f32[1,1024]{1,0:T(1,128)S(1)}, u32[]{:S(2)}, u32[]{:S(2)}) collective-permute-start(f32[1,1024]{1,0:T(1,128)S(1)} %add.57), channel_id=1, source_target_pairs={{0,3},{1,2},{2,1},{3,0},{4,7},{5,6},{6,5},{7,4},{8,11},{9,10},{10,... | collective-permute-start | bytes 12296 | tf_op jit(solution)/shard_map/ppermute | solution.py:26
  99.5 6.1 %collective-permute-start.8 = (f32[64,1024]{1,0:T(8,128)}, f32[64,1024]{1,0:T(8,128)S(1)}, u32[]{:S(2)}, u32[]{:S(2)}) collective-permute-start(f32[64,1024]{1,0:T(8,128)} %get-tuple-element.29), channel_id=1, source_target_pairs={{0,1},{1,0},{2,3},{3,2},{4,5},{5,4},{6,7},{7,6},{8,9},{9,8},{10,11... | collective-permute-start | bytes 786440 | tf_op jit(solution)/shard_map/ppermute | solution.py:26
  106.6 6.9 %collective-permute-start.9 = (f32[64,1024]{1,0:T(8,128)S(1)}, f32[64,1024]{1,0:T(8,128)S(1)}, u32[]{:S(2)}, u32[]{:S(2)}) collective-permute-start(f32[64,1024]{1,0:T(8,128)S(1)} %add.59), channel_id=1, source_target_pairs={{0,3},{1,2},{2,1},{3,0},{4,7},{5,6},{6,5},{7,4},{8,11},{9,10},{10,... | collective-permute-start | bytes 786440 | tf_op jit(solution)/shard_map/ppermute | solution.py:26
  137.1 5.6 %collective-permute-start.10 = (bf16[80,1024]{1,0:T(8,128)(2,1)}, bf16[80,1024]{1,0:T(8,128)(2,1)S(1)}, u32[]{:S(2)}, u32[]{:S(2)}) collective-permute-start(bf16[80,1024]{1,0:T(8,128)(2,1)} %get-tuple-element.32), channel_id=1, source_target_pairs={{0,1},{1,0},{2,3},{3,2},{4,5},{5,4},{6,7},{7,6},{8,9},{9,8},{10,11... | collective-permute-start | bytes 491528 | tf_op jit(solution)/shard_map/ppermute | solution.py:26
  142.7 0.7 copy-start.6
  145.2 5.6 %collective-permute-start.11 = (bf16[80,1024]{1,0:T(8,128)(2,1)}, bf16[80,1024]{1,0:T(8,128)(2,1)S(1)}, u32[]{:S(2)}, u32[]{:S(2)}) collective-permute-start(bf16[80,1024]{1,0:T(8,128)(2,1)} %get-tuple-element.34), channel_id=1, source_target_pairs={{0,3},{1,2},{2,1},{3,0},{4,7},{5,6},{6,5},{7,4},{8,11},{9,10},{10,... | collective-permute-start | bytes 491528 | tf_op jit(solution)/shard_map/ppermute | solution.py:26
  150.8 9.8 %copy-start.5 = (bf16[80,1024]{1,0:T(8,128)(2,1)}, bf16[80,1024]{1,0:T(8,128)(2,1)S(1)}, u32[]{:S(2)}) copy-start(bf16[80,1024]{1,0:T(8,128)(2,1)S(1)} %collective-permute-done.11.got) | copy-start | bytes 491524
  152.0 17.8 %all-to-all-start.2 = ((f32[64,1,16]{2,1,0:T(1,128)}), f32[64,1,16]{2,1,0:T(1,128)S(1)}, u32[]{:S(2)}, u32[]{:S(2)}) async-start(f32[64,1,16]{2,1,0:T(1,128)} %broadcast_in_dim.32), calls=%async_computation.2 | async-start | bytes 65536 | tf_op jit(solution)/shard_map/all_to_all | solution.py:689

commit v13 on v12

--- a/solution.py
+++ b/solution.py
@@ -17,6 +17,7 @@
 TILES = 1
 LAST_CHUNK = 512
 VMEM_BYTES = 62 * 1024 * 1024
+SMALL_VMEM_BYTES = 16 * 1024 * 1024
 CONTRACT_LAST = (((1,), (1,)), ((), ()))
 CONTRACT_FIRST = (((0,), (0,)), ((), ()))
 
@@ -585,7 +586,7 @@
         ),
         in_specs=[vmem] * 3,
         out_specs=(vmem, vmem, vmem),
-        compiler_params=pltpu.CompilerParams(vmem_limit_bytes=VMEM_BYTES),
+        compiler_params=pltpu.CompilerParams(vmem_limit_bytes=SMALL_VMEM_BYTES),
         cost_estimate=pl.CostEstimate(flops=1 << 17, bytes_accessed=1 << 20, transcendentals=0),
         name="pair_step",
     )(back, loss, got)
@@ -609,7 +610,7 @@
         out_shape=jax.ShapeDtypeStruct((rank, columns), jnp.float32),
         in_specs=[vmem] * 3,
         out_specs=vmem,
-        compiler_params=pltpu.CompilerParams(vmem_limit_bytes=VMEM_BYTES),
+        compiler_params=pltpu.CompilerParams(vmem_limit_bytes=SMALL_VMEM_BYTES),
         cost_estimate=pl.CostEstimate(
             flops=2 * rows * rank * columns, bytes_accessed=3 << 20, transcendentals=0
         ),

time: 174 us -> 173 us (level)
  Pallas kernels: 37.8 us -> 34.3 us
  local copies, waits for them, and re-layouts: 3.92 us -> 6.46 us
    unnamed x14 -> x16, local copies, waits for them, and re-layouts: 2.29 us -> 4.81 us
    pallas_call x1, Pallas kernels: 2.95 us -> 1.18 us  [down_step(): pl.pallas_call(down_kernel, out_shape=jax.ShapeDtypeStruct((rank, columns...]
    pallas_call x1, Pallas kernels: 1.79 us -> 0.04 us  [pair_step(): pl.pallas_call(pair_kernel, out_shape=(jax.ShapeDtypeStruct(back.shape, j...]
  transfers between devices with their start and end apart: 15 -> 15, of which waited for: 12 -> 12; matrix products, arithmetic and copies ran while one was open for 5% -> 5% of each run, Pallas kernels for 15% -> 14%
where the time goes in v13:
time: 173 us; the launch traced here: 172 us
  waiting for transfers between devices  79.1 us (46%)
  starting transfers between devices  40.1 us (23%)
  Pallas kernels  34.3 us (20%)
  other arithmetic  8.16 us (5%)
  local copies, waits for them, and re-layouts  6.46 us (4%)
  between operations  3.82 us (2%)
    ppermute x12, waiting for transfers between devices, swap(): return lax.ppermute(value, axis, [(i, i ^ distance) for i in range(peers)])  49.8 us
    all_to_all x1, waiting for transfers between devices, on_device(): lax.all_to_all(send_gap.reshape(trainers, per_peer, part), DP, 0, 0, tile...  18.7 us
    all_to_all x1, starting transfers between devices, on_device(): got_x = lax.all_to_all(send_x, DP, 0, 0, tiled=True)  13.3 us
    pallas_call x1, Pallas kernels, base_gap_slots(): pl.pallas_call(gap_kernel, out_shape=(jax.ShapeDtypeStruct((slots, *block...  9.89 us
    ppermute x12, starting transfers between devices, swap(): return lax.ppermute(value, axis, [(i, i ^ distance) for i in range(peers)])  9.55 us
    all_to_all x1, starting transfers between devices, on_device(): lax.all_to_all(send_gap.reshape(trainers, per_peer, part), DP, 0, 0, tile...  8.77 us
    all_to_all x1, starting transfers between devices, on_device(): lax.all_to_all(jnp.broadcast_to(own_loss, (trainers, 1, NB)), DP, 0, 0, t...  8.51 us
    all_to_all x1, waiting for transfers between devices, on_device(): lax.all_to_all(jnp.broadcast_to(own_loss, (trainers, 1, NB)), DP, 0, 0, t...  6.51 us
  transfers between devices with their start and end apart: 15, of which 12 were waited for; matrix products, arithmetic and copies ran while one was open for 5% of the time, Pallas kernels for 14%

profile of v13, /device:TPU:1, one launch (start us, length us, event | category | flops | bytes accessed | tf_op | source)
XLA Modules:
  0.0 171.9 jit_solution(15048637495438456276)
XLA Ops:
  0.6 5.2 %route.1 = (bf16[64,17,8,128]{3,2,1,0:T(8,128)(2,1)}, bf16[32,8,1024]{2,1,0:T(8,128)(2,1)}, bf16[34,8,1024]{2,1,0:T(8,128)(2,1)}, s32[128]{0:T(128)}) custom-call(s32[64]{0:T(128)} %ids.1, s32[64]{0:T(128)} %bitcast.39, s32[128]{0:T(128)} %buckets_in.1, s32[128]{0:T(128)} %lengths_in.1, bf16[128,8,1024]{2,1,0:T(8,128)(2,1)} %pool_in.1, f32[1,1024]{1,0:T(1,128)} %bitcast.36), custom_call_target="tpu_custom_call" | custom-call | bytes 5242880 | tf_op jit(solution)/shard_map/route/pallas_call | solution.py:250
  5.9 13.3 %all-to-all-start.1 = ((bf16[64,17,8,128]{3,2,1,0:T(8,128)(2,1)}), bf16[64,17,8,128]{3,2,1,0:T(8,128)(2,1)}, u32[]{:S(2)}, u32[]{:S(2)}) async-start(bf16[64,17,8,128]{3,2,1,0:T(8,128)(2,1)} %get-tuple-element.27), calls=%async_computation.1 | async-start | bytes 4456448 | tf_op jit(solution)/shard_map/all_to_all | solution.py:648
  19.2 1.4 collective-permute-start.2
  20.6 1.9 %collective-permute-start = (bf16[256,1024]{1,0:T(8,128)(2,1)S(1)}, bf16[256,1024]{1,0:T(8,128)(2,1)}, u32[]{:S(2)}, u32[]{:S(2)}) collective-permute-start(bf16[256,1024]{1,0:T(8,128)(2,1)S(1)} %bitcast.30), channel_id=1, source_target_pairs={{0,3},{1,2},{2,1},{3,0},{4,7},{5,6},{6,5},{7,4},{8,11},{9,10},{10,... | collective-permute-start | bytes 1572872 | tf_op jit(solution)/shard_map/ppermute | solution.py:27
  23.2 9.8 %collective-permute-done.2.near_last = bf16[272,1024]{1,0:T(8,128)(2,1)S(1)} collective-permute-done((bf16[272,1024]{1,0:T(8,128)(2,1)S(1)}, bf16[272,1024]{1,0:T(8,128)(2,1)S(1)}, u32[]{:S(2)}, u32[]{:S(2)}) %collective-permute-start.2) | collective-permute-done | bytes 557088 | tf_op jit(solution)/shard_map/ppermute | solution.py:27
  33.0 2.7 %collective-permute-start.3 = (bf16[272,1024]{1,0:T(8,128)(2,1)S(1)}, bf16[272,1024]{1,0:T(8,128)(2,1)}, u32[]{:S(2)}, u32[]{:S(2)}) collective-permute-start(bf16[272,1024]{1,0:T(8,128)(2,1)S(1)} %collective-permute-done.2.near_last), channel_id=1, source_target_pairs={{0,3},{1,2},{2,1},{3,0},{4,7},{5,6},{6,5},{7,4},{8,11},{9,10},{10,... | collective-permute-start | bytes 1671176 | tf_op jit(solution)/shard_map/ppermute | solution.py:27
  35.8 1.5 collective-permute-start.1
  37.8 10.0 %collective-permute-done.4.near_first = bf16[256,1024]{1,0:T(8,128)(2,1)S(1)} collective-permute-done((bf16[256,1024]{1,0:T(8,128)(2,1)S(1)}, bf16[256,1024]{1,0:T(8,128)(2,1)S(1)}, u32[]{:S(2)}, u32[]{:S(2)}) %collective-permute-start.4) | collective-permute-done | bytes 524320 | tf_op jit(solution)/shard_map/ppermute | solution.py:27
  49.4 5.1 %early_part.1 = (bf16[64,8,1024]{2,1,0:T(8,128)(2,1)}, f32[512,128]{1,0:T(8,128)}) custom-call(s32[64]{0:T(128)} %ids.1, bf16[256,1024]{1,0:T(8,128)(2,1)} %bitcast.28, bf16[272,1024]{1,0:T(8,128)(2,1)} %bitcast.24, bf16[256,1024]{1,0:T(8,128)(2,1)} %copy-done.7, bf16[272,1024]{1,0:T(8,128)(2,1)} %copy-done.4, ...), custom_call_target="tpu_custom_call" | custom-call | flops 6291456 | bytes 7340032 | tf_op jit(solution)/shard_map/early_part/pallas_call | solution.py:325
  54.4 4.5 %collective-permute-done.1.far_first = bf16[256,1024]{1,0:T(8,128)(2,1)} collective-permute-done((bf16[256,1024]{1,0:T(8,128)(2,1)}, bf16[256,1024]{1,0:T(8,128)(2,1)}, u32[]{:S(2)}, u32[]{:S(2)}) %collective-permute-start.1) | collective-permute-done | bytes 524320 | tf_op jit(solution)/shard_map/ppermute | solution.py:27
  59.0 9.9 %base_gap.1 = (bf16[128,8,1024]{2,1,0:T(8,128)(2,1)}, f32[1]{0:T(128)}) custom-call(s32[128]{0:T(128)} %get-tuple-element.21.slot_of, s32[4]{0:T(128)} %iota_xor_fusion.order, bf16[256,1024]{1,0:T(8,128)(2,1)} %collective-permute-done.1.far_first, bf16[272,1024]{1,0:T(8,128)(2,1)} %collective-permute-done.3.far_last, bf16[256,1024]{1,0:T(8,128)(2,1)} %bitcast.29, ...), custom_call_target="tpu_custom_call" | custom-call | flops 4294967296 | bytes 18874368 | tf_op jit(solution)/shard_map/base_gap/pallas_call | solution.py:464
  68.9 4.1 %all-to-all-done.1.packed = bf16[64,17,8,128]{3,2,1,0:T(8,128)(2,1)} async-done(((bf16[64,17,8,128]{3,2,1,0:T(8,128)(2,1)}), bf16[64,17,8,128]{3,2,1,0:T(8,128)(2,1)}, u32[]{:S(2)}, u32[]{:S(2)}) %all-to-all-start.1) | async-done | bytes 2228256 | tf_op jit(solution)/shard_map/all_to_all | solution.py:648
  72.9 8.8 %all-to-all-start = ((bf16[64,16,1024]{2,1,0:T(8,128)(2,1)}), bf16[64,16,1024]{2,1,0:T(8,128)(2,1)}, u32[]{:S(2)}, u32[]{:S(2)}) async-start(bf16[64,16,1024]{2,1,0:T(8,128)(2,1)} %bitcast.23), calls=%async_computation | async-start | bytes 4194304 | tf_op jit(solution)/shard_map/all_to_all | solution.py:656
  82.4 4.3 %row_squares.1 = f32[1,1024]{1,0:T(1,128)} custom-call(bf16[64,17,8,128]{3,2,1,0:T(8,128)(2,1)} %all-to-all-done.1.packed, f32[1]{0:T(128)} %get-tuple-element.28.done), custom_call_target="tpu_custom_call" | custom-call | flops 4194304 | bytes 2097152 | tf_op jit(solution)/shard_map/row_squares/pallas_call | solution.py:71
  86.7 0.9 fusion.2
  88.1 0.9 fusion.1
  90.9 3.6 %collective-permute-done.7 = f32[1,1024]{1,0:T(1,128)S(1)} collective-permute-done((f32[1,1024]{1,0:T(1,128)S(1)}, f32[1,1024]{1,0:T(1,128)S(1)}, u32[]{:S(2)}, u32[]{:S(2)}) %collective-permute-start.7) | collective-permute-done | bytes 4128 | tf_op jit(solution)/shard_map/ppermute | solution.py:27
  95.2 4.4 %latents.1 = (bf16[1024,1024]{1,0:T(8,128)(2,1)}, f32[64,1024]{1,0:T(8,128)}) custom-call(bf16[64,17,8,128]{3,2,1,0:T(8,128)(2,1)} %all-to-all-done.1.packed, f32[1,1024]{1,0:T(1,128)} %add_multiply_fusion.squares, f32[1,1024]{1,0:T(1,128)} %bitcast.37, bf16[64,1024]{1,0:T(8,128)(2,1)} %bitcast.34), custom_call_target="tpu_custom_call" | custom-call | flops 134217728 | bytes 4194304 | tf_op jit(solution)/shard_map/latents/pallas_call | solution.py:106
  100.4 5.2 %collective-permute-done.8 = f32[64,1024]{1,0:T(8,128)S(1)} collective-permute-done((f32[64,1024]{1,0:T(8,128)}, f32[64,1024]{1,0:T(8,128)S(1)}, u32[]{:S(2)}, u32[]{:S(2)}) %collective-permute-start.8) | collective-permute-done | bytes 262176 | tf_op jit(solution)/shard_map/ppermute | solution.py:27
  105.6 1.0 add.59
  107.3 1.0 maximum_maximum_fusion.facts
  108.3 5.2 %collective-permute-done.9 = f32[64,1024]{1,0:T(8,128)S(1)} collective-permute-done((f32[64,1024]{1,0:T(8,128)S(1)}, f32[64,1024]{1,0:T(8,128)S(1)}, u32[]{:S(2)}, u32[]{:S(2)}) %collective-permute-start.9) | collective-permute-done | bytes 262176 | tf_op jit(solution)/shard_map/ppermute | solution.py:27
  114.2 18.7 %all-to-all-done = bf16[64,16,1024]{2,1,0:T(8,128)(2,1)} async-done(((bf16[64,16,1024]{2,1,0:T(8,128)(2,1)}), bf16[64,16,1024]{2,1,0:T(8,128)(2,1)}, u32[]{:S(2)}, u32[]{:S(2)}) %all-to-all-start) | async-done | bytes 2097184 | tf_op jit(solution)/shard_map/all_to_all | solution.py:656
  132.9 4.3 %trainer_step.1 = (f32[64,1024]{1,0:T(8,128)}, f32[64,1024]{1,0:T(8,128)}, bf16[80,1024]{1,0:T(8,128)(2,1)}, f32[1,128]{1,0:T(1,128)}) custom-call(bf16[1024,1024]{1,0:T(8,128)(2,1)} %bitcast.5.gap, bf16[64,1024]{1,0:T(8,128)(2,1)} %multiply_convert_fusion.lowered, bf16[64,1024]{1,0:T(8,128)(2,1)} %bitcast.35, f32[1024,128]{1,0:T(8,128)} %maximum_maximum_fusion.facts), custom_call_target="tpu_custom_call" | custom-call | flops 402653184 | bytes 4194304 | tf_op jit(solution)/shard_map/trainer_step/pallas_call | solution.py:534
  137.2 5.6 %collective-permute-done.10.got = bf16[80,1024]{1,0:T(8,128)(2,1)S(1)} collective-permute-done((bf16[80,1024]{1,0:T(8,128)(2,1)}, bf16[80,1024]{1,0:T(8,128)(2,1)S(1)}, u32[]{:S(2)}, u32[]{:S(2)}) %collective-permute-start.10) | collective-permute-done | bytes 163872 | tf_op jit(solution)/shard_map/ppermute | solution.py:27
  142.7 0.9 copy-done.1
  144.8 5.0 %collective-permute-done.11.got = bf16[80,1024]{1,0:T(8,128)(2,1)S(1)} collective-permute-done((bf16[80,1024]{1,0:T(8,128)(2,1)S(1)}, bf16[80,1024]{1,0:T(8,128)(2,1)S(1)}, u32[]{:S(2)}, u32[]{:S(2)}) %collective-permute-start.11) | collective-permute-done | bytes 163872 | tf_op jit(solution)/shard_map/ppermute | solution.py:27
  150.5 8.5 %all-to-all-start.2 = ((f32[64,1,16]{2,1,0:T(1,128)}), f32[64,1,16]{2,1,0:T(1,128)S(1)}, u32[]{:S(2)}, u32[]{:S(2)}) async-start(f32[64,1,16]{2,1,0:T(1,128)} %broadcast_in_dim.32), calls=%async_computation.2 | async-start | bytes 65536 | tf_op jit(solution)/shard_map/all_to_all | solution.py:690
  159.0 1.6 copy-done
  160.6 1.2 down_step.1
  161.8 6.5 %all-to-all-done.2 = f32[64,1,16]{2,1,0:T(1,128)S(1)} async-done(((f32[64,1,16]{2,1,0:T(1,128)}), f32[64,1,16]{2,1,0:T(1,128)S(1)}, u32[]{:S(2)}, u32[]{:S(2)}) %all-to-all-start.2) | async-done | bytes 4128 | tf_op jit(solution)/shard_map/all_to_all | solution.py:690
  168.4 1.1 fusion.10
  (50 shorter events, 10.0 us)
Async XLA Ops:
  5.8 13.3 %copy-start.3 = (bf16[34,8,1024]{2,1,0:T(8,128)(2,1)S(1)}, bf16[34,8,1024]{2,1,0:T(8,128)(2,1)}, u32[]{:S(2)}) copy-start(bf16[34,8,1024]{2,1,0:T(8,128)(2,1)} %get-tuple-element.23) | copy-start | bytes 1671172
  5.8 14.7 %copy-start.6 = (bf16[32,8,1024]{2,1,0:T(8,128)(2,1)S(1)}, bf16[32,8,1024]{2,1,0:T(8,128)(2,1)}, u32[]{:S(2)}) copy-start(bf16[32,8,1024]{2,1,0:T(8,128)(2,1)} %get-tuple-element.22) | copy-start | bytes 1572868
  5.9 67.1 %all-to-all-start.1 = ((bf16[64,17,8,128]{3,2,1,0:T(8,128)(2,1)}), bf16[64,17,8,128]{3,2,1,0:T(8,128)(2,1)}, u32[]{:S(2)}, u32[]{:S(2)}) async-start(bf16[64,17,8,128]{3,2,1,0:T(8,128)(2,1)} %get-tuple-element.27), calls=%async_computation.1 | async-start | bytes 4456448 | tf_op jit(solution)/shard_map/all_to_all | solution.py:648
  19.2 13.9 %collective-permute-start.2 = (bf16[272,1024]{1,0:T(8,128)(2,1)S(1)}, bf16[272,1024]{1,0:T(8,128)(2,1)S(1)}, u32[]{:S(2)}, u32[]{:S(2)}) collective-permute-start(bf16[272,1024]{1,0:T(8,128)(2,1)S(1)} %bitcast.26), channel_id=1, source_target_pairs={{0,1},{1,0},{2,3},{3,2},{4,5},{5,4},{6,7},{7,6},{8,9},{9,8},{10,11... | collective-permute-start | bytes 1671176 | tf_op jit(solution)/shard_map/ppermute | solution.py:27
  20.6 15.2 %collective-permute-start = (bf16[256,1024]{1,0:T(8,128)(2,1)S(1)}, bf16[256,1024]{1,0:T(8,128)(2,1)}, u32[]{:S(2)}, u32[]{:S(2)}) collective-permute-start(bf16[256,1024]{1,0:T(8,128)(2,1)S(1)} %bitcast.30), channel_id=1, source_target_pairs={{0,3},{1,2},{2,1},{3,0},{4,7},{5,6},{6,5},{7,4},{8,11},{9,10},{10,... | collective-permute-start | bytes 1572872 | tf_op jit(solution)/shard_map/ppermute | solution.py:27
  22.5 26.1 %collective-permute-start.5 = (bf16[272,1024]{1,0:T(8,128)(2,1)S(1)}, bf16[272,1024]{1,0:T(8,128)(2,1)S(1)}, u32[]{:S(2)}, u32[]{:S(2)}) collective-permute-start(bf16[272,1024]{1,0:T(8,128)(2,1)S(1)} %bitcast.27), channel_id=1, source_target_pairs={{0,3},{1,2},{2,1},{3,0},{4,7},{5,6},{6,5},{7,4},{8,11},{9,10},{10,... | collective-permute-start | bytes 1671176 | tf_op jit(solution)/shard_map/ppermute | solution.py:27
  33.0 15.5 %copy-start.4 = (bf16[272,1024]{1,0:T(8,128)(2,1)}, bf16[272,1024]{1,0:T(8,128)(2,1)S(1)}, u32[]{:S(2)}) copy-start(bf16[272,1024]{1,0:T(8,128)(2,1)S(1)} %collective-permute-done.2.near_last) | copy-start | bytes 1671172
  33.0 25.9 %collective-permute-start.3 = (bf16[272,1024]{1,0:T(8,128)(2,1)S(1)}, bf16[272,1024]{1,0:T(8,128)(2,1)}, u32[]{:S(2)}, u32[]{:S(2)}) collective-permute-start(bf16[272,1024]{1,0:T(8,128)(2,1)S(1)} %collective-permute-done.2.near_last), channel_id=1, source_target_pairs={{0,3},{1,2},{2,1},{3,0},{4,7},{5,6},{6,5},{7,4},{8,11},{9,10},{10,... | collective-permute-start | bytes 1671176 | tf_op jit(solution)/shard_map/ppermute | solution.py:27
  35.8 12.0 %collective-permute-start.4 = (bf16[256,1024]{1,0:T(8,128)(2,1)S(1)}, bf16[256,1024]{1,0:T(8,128)(2,1)S(1)}, u32[]{:S(2)}, u32[]{:S(2)}) collective-permute-start(bf16[256,1024]{1,0:T(8,128)(2,1)S(1)} %bitcast.31), channel_id=1, source_target_pairs={{0,1},{1,0},{2,3},{3,2},{4,5},{5,4},{6,7},{7,6},{8,9},{9,8},{10,11... | collective-permute-start | bytes 1572872 | tf_op jit(solution)/shard_map/ppermute | solution.py:27
  35.8 23.2 %collective-permute-start.1 = (bf16[256,1024]{1,0:T(8,128)(2,1)}, bf16[256,1024]{1,0:T(8,128)(2,1)}, u32[]{:S(2)}, u32[]{:S(2)}) collective-permute-start(bf16[256,1024]{1,0:T(8,128)(2,1)} %collective-permute-done.other_first), channel_id=1, source_target_pairs={{0,1},{1,0},{2,3},{3,2},{4,5},{5,4},{6,7},{7,6},{8,9},{9,8},{10,11... | collective-permute-start | bytes 1572872 | tf_op jit(solution)/shard_map/ppermute | solution.py:27
  47.7 0.8 copy-start.7
  48.5 0.8 copy-start.5
  72.9 59.9 %all-to-all-start = ((bf16[64,16,1024]{2,1,0:T(8,128)(2,1)}), bf16[64,16,1024]{2,1,0:T(8,128)(2,1)}, u32[]{:S(2)}, u32[]{:S(2)}) async-start(bf16[64,16,1024]{2,1,0:T(8,128)(2,1)} %bitcast.23), calls=%async_computation | async-start | bytes 4194304 | tf_op jit(solution)/shard_map/all_to_all | solution.py:656
  86.7 3.1 %collective-permute-start.6 = (f32[1,1024]{1,0:T(1,128)}, f32[1,1024]{1,0:T(1,128)S(1)}, u32[]{:S(2)}, u32[]{:S(2)}) collective-permute-start(f32[1,1024]{1,0:T(1,128)} %row_squares.1), channel_id=1, source_target_pairs={{0,1},{1,0},{2,3},{3,2},{4,5},{5,4},{6,7},{7,6},{8,9},{9,8},{10,11... | collective-permute-start | bytes 12296 | tf_op jit(solution)/shard_map/ppermute | solution.py:27
  90.5 4.1 %collective-permute-start.7 = (f32[1,1024]{1,0:T(1,128)S(1)}, f32[1,1024]{1,0:T(1,128)S(1)}, u32[]{:S(2)}, u32[]{:S(2)}) collective-permute-start(f32[1,1024]{1,0:T(1,128)S(1)} %add.57), channel_id=1, source_target_pairs={{0,3},{1,2},{2,1},{3,0},{4,7},{5,6},{6,5},{7,4},{8,11},{9,10},{10,... | collective-permute-start | bytes 12296 | tf_op jit(solution)/shard_map/ppermute | solution.py:27
  99.5 6.1 %collective-permute-start.8 = (f32[64,1024]{1,0:T(8,128)}, f32[64,1024]{1,0:T(8,128)S(1)}, u32[]{:S(2)}, u32[]{:S(2)}) collective-permute-start(f32[64,1024]{1,0:T(8,128)} %get-tuple-element.29), channel_id=1, source_target_pairs={{0,1},{1,0},{2,3},{3,2},{4,5},{5,4},{6,7},{7,6},{8,9},{9,8},{10,11... | collective-permute-start | bytes 786440 | tf_op jit(solution)/shard_map/ppermute | solution.py:27
  106.6 6.9 %collective-permute-start.9 = (f32[64,1024]{1,0:T(8,128)S(1)}, f32[64,1024]{1,0:T(8,128)S(1)}, u32[]{:S(2)}, u32[]{:S(2)}) collective-permute-start(f32[64,1024]{1,0:T(8,128)S(1)} %add.59), channel_id=1, source_target_pairs={{0,3},{1,2},{2,1},{3,0},{4,7},{5,6},{6,5},{7,4},{8,11},{9,10},{10,... | collective-permute-start | bytes 786440 | tf_op jit(solution)/shard_map/ppermute | solution.py:27
  137.1 5.6 %collective-permute-start.10 = (bf16[80,1024]{1,0:T(8,128)(2,1)}, bf16[80,1024]{1,0:T(8,128)(2,1)S(1)}, u32[]{:S(2)}, u32[]{:S(2)}) collective-permute-start(bf16[80,1024]{1,0:T(8,128)(2,1)} %get-tuple-element.32), channel_id=1, source_target_pairs={{0,1},{1,0},{2,3},{3,2},{4,5},{5,4},{6,7},{7,6},{8,9},{9,8},{10,11... | collective-permute-start | bytes 491528 | tf_op jit(solution)/shard_map/ppermute | solution.py:27
  142.7 1.0 copy-start.1
  143.7 0.7 copy-start.2
  144.4 5.5 %collective-permute-start.11 = (bf16[80,1024]{1,0:T(8,128)(2,1)S(1)}, bf16[80,1024]{1,0:T(8,128)(2,1)S(1)}, u32[]{:S(2)}, u32[]{:S(2)}) collective-permute-start(bf16[80,1024]{1,0:T(8,128)(2,1)S(1)} %get-tuple-element.34), channel_id=1, source_target_pairs={{0,3},{1,2},{2,1},{3,0},{4,7},{5,6},{6,5},{7,4},{8,11},{9,10},{10,... | collective-permute-start | bytes 491528 | tf_op jit(solution)/shard_map/ppermute | solution.py:27
  150.5 17.8 %all-to-all-start.2 = ((f32[64,1,16]{2,1,0:T(1,128)}), f32[64,1,16]{2,1,0:T(1,128)S(1)}, u32[]{:S(2)}, u32[]{:S(2)}) async-start(f32[64,1,16]{2,1,0:T(1,128)} %broadcast_in_dim.32), calls=%async_computation.2 | async-start | bytes 65536 | tf_op jit(solution)/shard_map/all_to_all | solution.py:690
  159.0 1.6 copy-start
